TPU v7x, 32 devices: a whole 2x2x4 slice. The times are simulated.
32 devices in a mesh: parts: 2 (over y), col: 16 (over z, x, core).
Axes of the slice: x: 2, y: 2, z: 4, core: 2. Of those that a mesh axis runs over, the one named last changes fastest.
Arguments:
- counts: int32 [1024, 8192], P('parts', 'col'), parts along dimension 0, may hold values from 0 to 4095, as said below
- row_totals: int32 [1024], P('parts'), parts along dimension 0, may hold values from 1000 to 999999
- column_totals: int32 [16384], P(('parts', 'col')), parts along dimension 0, may hold values from 1000 to 999999
- row_master: float32 [1024, 256], P(('parts', 'col')), parts along dimension 0, may hold values from -1.5 to 1.5
- row_history: float32 [1024, 256], P(('parts', 'col')), parts along dimension 0, may hold values from 0.01 to 0.1
- column_master: float32 [16384, 256], P(('parts', 'col')), parts along dimension 0, may hold values from -1.5 to 1.5
- column_history: float32 [16384, 256], P(('parts', 'col')), parts along dimension 0, may hold values from 0.01 to 0.1
Outputs:
- grid_rows: bfloat16 [1024, 256], P('parts'), parts along dimension 0
- new_row_master: float32 [1024, 256], P(('parts', 'col')), parts along dimension 0
- new_row_history: float32 [1024, 256], P(('parts', 'col')), parts along dimension 0
- new_column_master: float32 [16384, 256], P(('parts', 'col')), parts along dimension 0
- new_column_history: float32 [16384, 256], P(('parts', 'col')), parts along dimension 0
There are 2 independent parts, one for each index of `parts`. A program takes and returns all parts, laid end to end along the dimension named above; each array names one. Nothing has to cross between parts.
Inputs may be any that keep to these rules, and one draw needn't show every extreme that they name: Co-occurrence counts; some are zero, and their sizes spread over several powers of two.
All inputs are finite; a program needn't handle non-finite values.
Results may differ from a plain program's by a relative error of at most 0.0075.
Values may be sent and summed in bfloat16 or wider, within the bound.
No kernel may reach another device: no remote copies, remote signals or barrier semaphores. Data moves between devices by JAX's collectives and lax.ppermute only.
A program may use at most 64 MiB of HBM per device.

v0:
```python
import jax
import jax.numpy as jnp
from jax import lax
from jax.sharding import PartitionSpec as P

step_size = 2.0


def slope_terms(scores, counts, log_rows, log_columns, log_total):
    amounts = counts.astype(jnp.float32)
    log_count = jnp.log(jnp.maximum(amounts, 1.0))
    log_ratio = log_count + log_total - log_rows[:, None] - log_columns[None, :]
    confidence = 0.1 + 0.25 * jnp.sqrt(amounts)
    fitted = confidence * (scores - log_ratio)
    hinged = jax.nn.sigmoid(scores - log_ratio)
    return jnp.where(counts > 0, fitted, hinged).astype(jnp.bfloat16)


def adagrad(master, history, gradient):
    updated = history + gradient * gradient
    return (master - step_size * gradient / jnp.sqrt(updated), updated)


def per_device(
    counts, row_totals, column_totals, row_master, row_history, column_master, column_history
):
    total_rows = counts.shape[0]
    all_columns = counts.shape[1] * lax.axis_size("col")
    row_floats = row_totals.astype(jnp.float32)
    log_total = jnp.log(jnp.sum(row_floats))
    log_rows = jnp.log(row_floats)
    log_columns = jnp.log(column_totals.astype(jnp.float32))
    column_copy = column_master.astype(jnp.bfloat16)
    portion = lax.all_gather(row_master.astype(jnp.bfloat16), "col", axis=0, tiled=True)
    scores = jnp.dot(portion, column_copy.T, preferred_element_type=jnp.float32)
    slopes = slope_terms(scores, counts, log_rows, log_columns, log_total)
    column_sum = jnp.dot(slopes.T, portion, preferred_element_type=jnp.float32)
    slope_store, column_sum = (slopes, column_sum)
    row_grad = (
        lax.psum_scatter(
            jnp.dot(slope_store, column_copy, preferred_element_type=jnp.float32),
            "col",
            scatter_dimension=0,
            tiled=True,
        )
        / all_columns
    )
    new_rows, new_row_hist = adagrad(row_master, row_history, row_grad)
    grid_rows = lax.all_gather(new_rows.astype(jnp.bfloat16), "col", axis=0, tiled=True)
    column_grad = column_sum / total_rows
    new_columns, new_column_hist = adagrad(column_master, column_history, column_grad)
    return (grid_rows, new_rows, new_row_hist, new_columns, new_column_hist)


def solution(mesh):
    return jax.shard_map(
        per_device,
        mesh=mesh,
        in_specs=(
            P("parts", "col"),
            P("parts"),
            P(("parts", "col")),
            P(("parts", "col"), None),
            P(("parts", "col"), None),
            P(("parts", "col"), None),
            P(("parts", "col"), None),
        ),
        out_specs=(
            P("parts", None),
            P(("parts", "col"), None),
            P(("parts", "col"), None),
            P(("parts", "col"), None),
            P(("parts", "col"), None),
        ),
        check_vma=False,
    )
```

profile of v0, /device:TPU:0, one launch (start us, length us, event | category | flops | bytes accessed | tf_op | source)
XLA Modules:
  0.0 119.9 jit_solution(1236787541807811656)
XLA Ops:
  7.2 0.0 reduce-scatter.2.cloned.1.call-start
  7.2 1.3 %convert_reduce_fusion = (f32[]{:T(128)}, f32[512]{0:T(512)S(1)}, f32[512]{0:T(512)S(1)}) fusion(s32[512]{0:T(512)} %param.8, s32[512]{0:T(512)} %param.9), kind=kLoop, calls=%fused_computation.11 | loop fusion | flops 1535 | bytes 8196 | tf_op jit(solution)/shard_map/reduce_sum | solution.py:30
  9.2 0.8 convert_element_type.22
  10.0 23.8 %all_gather.6 = bf16[512,256]{1,0:T(8,128)(2,1)S(1)} all-gather(bf16[32,256]{1,0:T(8,128)(2,1)S(1)} %convert_element_type.22), channel_id=1, replica_groups=mesh['parts'=2,'col'=16] {'col'}, dimensions={0}, use_global_device_ids=true | all-gather | bytes 278528 | tf_op jit(solution)/shard_map/all_gather | solution.py:34
  33.7 0.0 copy-start
  33.7 2.7 %select_convert_fusion = bf16[512,512]{1,0:T(8,128)(2,1)S(1)} fusion(bf16[512,256]{1,0:T(8,128)(2,1)S(1)} %all_gather.6, s32[512,512]{1,0:T(8,128)} %param.7, f32[512]{0:T(512)S(1)} %get-tuple-element.12, f32[512]{0:T(512)S(1)} %get-tuple-element.11, f32[]{:T(128)S(6)} %log.13, f32[512,256]{1,0:T(8,128)} %param.12), kind=kOutput, calls=%fused_computation.1 | convolution fusion | flops 138280960 | bytes 2363396 | tf_op jit(solution)/shard_map/dot_general | solution.py:35
  36.5 0.0 copy-done
  36.5 1.1 fusion
  37.6 0.0 copy-start.1
  37.6 0.0 reduce-scatter.2.cloned.1.call-update
  37.6 1.0 copy-done.1
  38.6 0.0 copy-start.2
  38.6 0.0 copy-start.3
  38.6 1.3 %multiply_subtract_fusion = (f32[512,256]{1,0:T(8,128)}, f32[512,256]{1,0:T(8,128)}) fusion(f32[512,256]{1,0:T(8,128)S(1)} %copy-done, f32[512,256]{1,0:T(8,128)S(1)} %copy-done.1, bf16[512,512]{1,0:T(8,128)(2,1)S(1)} %select_convert_fusion, bf16[512,256]{1,0:T(8,128)(2,1)S(1)} %all_gather.6), kind=kOutput, calls=%fused_computation.2 | convolution fusion | flops 135004160 | bytes 2883584 | tf_op jit(solution)/shard_map/dot_general | solution.py:37
  39.9 50.9 %reduce-scatter.2.cloned.1.call-done = f32[32,256]{1,0:T(8,128)} async-done(((f32[512,256]{1,0:T(8,128)}), f32[32,256]{1,0:T(8,128)}) %reduce-scatter.2.cloned.1.call-update) | async-done | bytes 32784 | tf_op jit(solution)/shard_map/reduce_scatter | solution.py:40
  90.8 0.0 copy-done.2
  90.8 0.0 copy-done.3
  90.8 1.4 %fusion.3 = (bf16[32,256]{1,0:T(8,128)(2,1)S(1)}, f32[32,256]{1,0:T(8,128)}, f32[32,256]{1,0:T(8,128)}) fusion(f32[32,256]{1,0:T(8,128)S(1)} %copy-done.2, f32[32,256]{1,0:T(8,128)} %reduce-scatter.2.cloned.1.call-done, f32[32,256]{1,0:T(8,128)S(1)} %copy-done.3), kind=kLoop, calls=%fused_computation.12 | loop fusion | flops 57344 | bytes 180224 | tf_op jit(solution)/shard_map/convert_element_type | solution.py:49
  92.2 20.1 %all_gather.7 = bf16[512,256]{1,0:T(8,128)(2,1)S(1)} all-gather(bf16[32,256]{1,0:T(8,128)(2,1)S(1)} %get-tuple-element.7), channel_id=1, replica_groups=mesh['parts'=2,'col'=16] {'col'}, dimensions={0}, use_global_device_ids=true | all-gather | bytes 278528 | tf_op jit(solution)/shard_map/all_gather | solution.py:49
  112.3 0.7 copy.13
Async XLA Ops:
  7.2 83.7 %reduce-scatter.2.cloned.1.call-start = ((), (), s32[]{:S(2)}) async-start(), calls=%async_computation.1 | async-start | bytes 557056 | tf_op jit(solution)/shard_map/reduce_scatter | solution.py:40
  33.7 2.7 %copy-start = (f32[512,256]{1,0:T(8,128)S(1)}, f32[512,256]{1,0:T(8,128)}, u32[]{:S(2)}) copy-start(f32[512,256]{1,0:T(8,128)} %param.12) | copy-start | bytes 1572868
  37.6 1.0 copy-start.1
  38.6 52.2 %copy-start.2 = (f32[32,256]{1,0:T(8,128)S(1)}, f32[32,256]{1,0:T(8,128)}, u32[]{:S(2)}) copy-start(f32[32,256]{1,0:T(8,128)} %param.10) | copy-start | bytes 98308
  38.6 52.2 %copy-start.3 = (f32[32,256]{1,0:T(8,128)S(1)}, f32[32,256]{1,0:T(8,128)}, u32[]{:S(2)}) copy-start(f32[32,256]{1,0:T(8,128)} %param.11) | copy-start | bytes 98308
Sparse Core Ops, SparseCore 0:
  37.7 53.0 reduce-scatter.1
where the time goes:
time: 120 us
  waiting for transfers between devices  50.9 us (42%)
  blocking collectives  43.9 us (37%)
  between operations  14.7 us (12%)
  matrix products  5.13 us (4%)
  other arithmetic  3.46 us (3%)
  local copies, waits for them, and re-layouts  1.73 us (1%)
    reduce_scatter x1, waiting for transfers between devices, per_device(): lax.psum_scatter(jnp.dot(slope_store, column_copy, preferred_element_type...  50.9 us
    all_gather x1, blocking collectives, per_device(): lax.all_gather(row_master.astype(jnp.bfloat16), 'col', axis=0, tiled=True)  23.8 us
    all_gather x1, blocking collectives, per_device(): lax.all_gather(new_rows.astype(jnp.bfloat16), 'col', axis=0, tiled=True)  20.1 us
    dot_general x1, matrix products, per_device(): scores = jnp.dot(portion, column_copy.T, preferred_element_type=jnp.float32)  2.73 us
  transfers between devices with their start and end apart: 1, of which 1 were waited for; matrix products, arithmetic and copies ran while one was open for 1% of the time, Pallas kernels for 0%

commit v1 on v0

v1 whole, which is shorter than its diff:
```python
import functools

import jax
import jax.numpy as jnp
from jax import lax
from jax.experimental import pallas as pl
from jax.experimental.pallas import tpu as pltpu
from jax.sharding import PartitionSpec as P

step_size = 2.0
VMEM = pl.BlockSpec(memory_space=pltpu.VMEM)
ANY = pl.BlockSpec(memory_space=pl.ANY)
LIMIT = 56 * 1024 * 1024


def hop(value, bit, size):
    return lax.ppermute(value, "col", [(i, i ^ bit) for i in range(size)])


def slopes_kernel(chunk, counts, row_term, column_term, columns, *refs):
    pieces, (sent, kept, slopes, column_copy) = refs[:4], refs[4:]
    me = lax.axis_index("col")
    column_copy[...] = columns[...].astype(jnp.bfloat16)
    own_rows = counts.shape[3]
    group = chunk // own_rows
    steps = pieces[0].shape[0] // chunk
    for place in range(4):
        high, low = place // 2, place % 2
        at_x = lax.rem(lax.div(me, 2) + low, 2)
        at_core = lax.rem(me + high, 2)
        target = sent if high else kept

        def body(step, _, place=place, low=low, at_x=at_x, at_core=at_core, target=target):
            first = pl.multiple_of(step * chunk, chunk)
            rows = pieces[place][pl.ds(first, chunk), :]
            scores = lax.dot_general(
                rows, column_copy[...], (((1,), (1,)), ((), ())), preferred_element_type=jnp.float32
            )
            block = counts[pl.ds(step * group, group), at_x, at_core]
            amounts = block.reshape(chunk, block.shape[-1]).astype(jnp.float32)
            terms = row_term[pl.ds(place * steps * group + step * group, group)].reshape(chunk, 1)
            ratio = jnp.log(jnp.maximum(amounts, 1.0)) + terms - column_term[...]
            gap = scores - ratio
            fitted = (0.1 + 0.25 * jnp.sqrt(amounts)) * gap
            slope = jnp.where(amounts > 0, fitted, jax.nn.sigmoid(gap)).astype(jnp.bfloat16)
            slopes[place, pl.ds(first, chunk), :] = slope
            target[pl.ds(low * steps * chunk + first, chunk), :] = jnp.dot(
                slope, column_copy[...], preferred_element_type=jnp.float32
            ).astype(target.dtype)
            return 0

        if steps == 1:
            body(0, 0)
        else:
            lax.fori_loop(0, steps, body, 0)


def columns_kernel(total_rows, chunk, slopes, master, history, *refs):
    pieces, (new_master, new_history, total) = refs[:4], refs[4:]
    steps = pieces[0].shape[0] // chunk
    for place in range(4):

        def body(step, _, place=place):
            first = pl.multiple_of(step * chunk, chunk)
            part = lax.dot_general(
                slopes[place, pl.ds(first, chunk), :],
                pieces[place][pl.ds(first, chunk), :],
                (((0,), (0,)), ((), ())),
                preferred_element_type=jnp.float32,
            )
            total[...] = part if place == 0 and steps == 1 else total[...] + part
            return 0

        if steps == 1:
            body(0, 0)
        else:
            if place == 0:
                total[...] = jnp.zeros_like(total)
            lax.fori_loop(0, steps, body, 0)
    gradient = total[...] / total_rows
    updated = history[...] + gradient * gradient
    new_history[...] = updated
    new_master[...] = master[...] - step_size * gradient * lax.rsqrt(updated)


def place_kernel(*refs):
    pieces, out, sems = refs[:4], refs[4], refs[5]
    me = lax.axis_index("col")
    copies = []
    for place in range(4):
        at_x = lax.rem(lax.div(me, 2) + place % 2, 2)
        at_core = lax.rem(me + place // 2, 2)
        copies.append(pltpu.make_async_copy(pieces[place], out.at[:, at_x, at_core], sems.at[place]))
    for copy in copies:
        copy.start()
    for copy in copies:
        copy.wait()


def gather_group(value, size):
    me = lax.axis_index("col")
    held = [value]
    bit = size // 2
    while bit >= 4:
        held = held + [hop(v, bit, size) for v in held]
        bit //= 2
    group = size // 4
    bits = group.bit_length() - 1
    flip = [int(format(k, "b").zfill(bits)[::-1], 2) if bits else 0 for k in range(group)]
    by_offset = [held[flip[k]] for k in range(group)]
    place = lax.div(me, 4)
    for b in range(bits):
        turned = lax.rem(lax.div(place, 1 << b), 2) == 1
        by_offset = [jnp.where(turned, by_offset[k ^ (1 << b)], by_offset[k]) for k in range(group)]
    return jnp.stack(by_offset)


def per_device(
    counts, row_totals, column_totals, row_master, row_history, column_master, column_history
):
    size = lax.axis_size("col")
    me = lax.axis_index("col")
    total_rows, block_columns = counts.shape
    all_columns = block_columns * size
    own, width = row_master.shape
    group = size // 4
    group_rows = group * own
    chunk = 128

    row_floats = row_totals.astype(jnp.float32)
    row_term = (jnp.log(jnp.sum(row_floats)) - jnp.log(row_floats)).reshape(group, 2, 2, own)
    x_bit, core_bit = lax.rem(lax.div(me, 2), 2), lax.rem(me, 2)
    row_term = jnp.where(x_bit == 1, row_term[:, ::-1], row_term)
    row_term = jnp.where(core_bit == 1, row_term[:, :, ::-1], row_term)
    row_term = row_term.transpose(2, 1, 0, 3).reshape(4 * group, own, 1)
    column_term = jnp.log(column_totals.astype(jnp.float32)).reshape(1, block_columns)

    master = gather_group(row_master, size)
    history = gather_group(row_history, size)
    mine = master.reshape(group_rows, width).astype(jnp.bfloat16)
    beside = hop(mine, 2, size)
    pieces = (mine, beside, hop(mine, 1, size), hop(beside, 1, size))

    half = jax.ShapeDtypeStruct((2 * group_rows, width), jnp.bfloat16)
    kept_half = jax.ShapeDtypeStruct((2 * group_rows, width), jnp.float32)
    sent, kept, slopes = pl.pallas_call(
        functools.partial(slopes_kernel, chunk),
        out_shape=(half, kept_half, jax.ShapeDtypeStruct((4, group_rows, block_columns), jnp.bfloat16)),
        in_specs=[VMEM] * 8,
        out_specs=[VMEM] * 3,
        scratch_shapes=[pltpu.VMEM(column_master.shape, jnp.bfloat16)],
        compiler_params=pltpu.CompilerParams(vmem_limit_bytes=LIMIT),
        name="slopes",
    )(counts.reshape(group, 2, 2, own, block_columns), row_term, column_term, column_master, *pieces)

    part = kept + hop(sent, 1, size).astype(jnp.float32)
    part = part[:group_rows] + hop(part[group_rows:].astype(jnp.bfloat16), 2, size).astype(jnp.float32)
    bit = 4
    while bit < size:
        rounded = part.astype(jnp.bfloat16)
        part = rounded.astype(jnp.float32) + hop(rounded, bit, size).astype(jnp.float32)
        bit *= 2

    struct = jax.ShapeDtypeStruct(column_master.shape, jnp.float32)
    new_columns, new_column_history = pl.pallas_call(
        functools.partial(columns_kernel, total_rows, chunk),
        out_shape=(struct, struct),
        in_specs=[VMEM] * 7,
        out_specs=[VMEM] * 2,
        scratch_shapes=[pltpu.VMEM(column_master.shape, jnp.float32)],
        compiler_params=pltpu.CompilerParams(vmem_limit_bytes=LIMIT),
        cost_estimate=pl.CostEstimate(flops=4 * total_rows * block_columns * width, bytes_accessed=8 * 512 * 1024, transcendentals=0),
        name="columns",
    )(slopes, column_master, column_history, *pieces)

    gradient = part.reshape(group, own, width) / all_columns
    updated = history + gradient * gradient
    new_group = master - step_size * gradient / jnp.sqrt(updated)
    place = lax.div(me, 4)
    new_rows = lax.dynamic_index_in_dim(new_group, place, 0, keepdims=False)
    new_row_history = lax.dynamic_index_in_dim(updated, place, 0, keepdims=False)
    copy = new_group.astype(jnp.bfloat16)
    beside = hop(copy, 2, size)
    grid_rows = pl.pallas_call(
        place_kernel,
        out_shape=jax.ShapeDtypeStruct((group, 2, 2, own, width), jnp.bfloat16),
        in_specs=[ANY] * 4,
        out_specs=ANY,
        scratch_shapes=[pltpu.SemaphoreType.DMA((4,))],
        name="place",
    )(copy, beside, hop(copy, 1, size), hop(beside, 1, size))
    return (grid_rows.reshape(total_rows, width), new_rows, new_row_history, new_columns, new_column_history)


def solution(mesh):
    return jax.shard_map(
        per_device,
        mesh=mesh,
        in_specs=(
            P("parts", "col"),
            P("parts"),
            P(("parts", "col")),
            P(("parts", "col"), None),
            P(("parts", "col"), None),
            P(("parts", "col"), None),
            P(("parts", "col"), None),
        ),
        out_specs=(
            P("parts", None),
            P(("parts", "col"), None),
            P(("parts", "col"), None),
            P(("parts", "col"), None),
            P(("parts", "col"), None),
        ),
        check_vma=False,
    )
```

time: 120 us -> 58.6 us (0.49)
  blocking collectives: 43.9 us -> 0 us
  waiting for transfers between devices: 50.9 us -> 16.7 us
  starting transfers between devices: 0.04 us -> 18.5 us
  Pallas kernels: 0 us -> 15.2 us
  between operations: 14.7 us -> 1.52 us
  matrix products: 5.13 us -> 0 us
  local copies, waits for them, and re-layouts: 1.73 us -> 3.38 us
    reduce_scatter x1 -> x0, waiting for transfers between devices: 50.9 us -> none  [per_device(): lax.psum_scatter(jnp.dot(slope_store, column_copy, preferred_element_type...]
    all_gather x2 -> x0, blocking collectives: 43.9 us -> none  [the longest x1 23.8 us: per_device(): lax.all_gather(row_master.astype(jnp.bfloat16), 'col', axis=0, tiled=True)]
    ppermute x0 -> x16, starting transfers between devices: none -> 18.5 us  [hop(): return lax.ppermute(value, 'col', [(i, i ^ bit) for i in range(size)])]
    ppermute x0 -> x16, waiting for transfers between devices: none -> 16.7 us  [hop(): return lax.ppermute(value, 'col', [(i, i ^ bit) for i in range(size)])]
    pallas_call x0 -> x3, Pallas kernels: none -> 15.2 us  [the longest x1 9.08 us: per_device(): pl.pallas_call(place_kernel, out_shape=jax.ShapeDtypeStruct((group, 2, 2,...]
    dot_general x3 -> x0, matrix products: 5.13 us -> none  [the longest x1 2.73 us: per_device(): scores = jnp.dot(portion, column_copy.T, preferred_element_type=jnp.float32)]
    convert_element_type x2 -> x4, other arithmetic: 2.15 us -> 0.09 us  [the longest x1 0.04 us: per_device(): copy = new_group.astype(jnp.bfloat16)]
  transfers between devices with their start and end apart: 1 -> 16, of which waited for: 1 -> 9; matrix products, arithmetic and copies ran while one was open for 1% -> 6% of each run, Pallas kernels for 0% -> 5%
where the time goes in v1:
time: 58.6 us; the launch traced here: 58.4 us
  starting transfers between devices  18.5 us (32%)
  waiting for transfers between devices  16.7 us (28%)
  Pallas kernels  15.2 us (26%)
  local copies, waits for them, and re-layouts  3.38 us (6%)
  other arithmetic  3.01 us (5%)
  between operations  1.52 us (3%)
    ppermute x16, starting transfers between devices, hop(): return lax.ppermute(value, 'col', [(i, i ^ bit) for i in range(size)])  18.5 us
    ppermute x16, waiting for transfers between devices, hop(): return lax.ppermute(value, 'col', [(i, i ^ bit) for i in range(size)])  16.7 us
    pallas_call x1, Pallas kernels, per_device(): pl.pallas_call(place_kernel, out_shape=jax.ShapeDtypeStruct((group, 2, 2,...  9.08 us
    pallas_call x1, Pallas kernels, per_device(): pl.pallas_call(functools.partial(slopes_kernel, chunk), out_shape=(half,...  3.33 us
    pallas_call x1, Pallas kernels, per_device(): pl.pallas_call(functools.partial(columns_kernel, total_rows, chunk), out_...  2.84 us
    unnamed x24, local copies, waits for them, and re-layouts  1.74 us
    reduce_sum x1, other arithmetic, per_device(): jnp.sum(row_floats)  1.29 us
  transfers between devices with their start and end apart: 16, of which 9 were waited for; matrix products, arithmetic and copies ran while one was open for 6% of the time, Pallas kernels for 5%

profile of v1, /device:TPU:0, one launch (start us, length us, event | category | flops | bytes accessed | tf_op | source)
XLA Modules:
  0.0 58.4 jit_solution(16033229211020684702)
XLA Ops:
  0.6 4.1 %collective-permute-start = (f32[32,256]{1,0:T(8,128)}, f32[32,256]{1,0:T(8,128)S(1)}, u32[]{:S(2)}, u32[]{:S(2)}) collective-permute-start(f32[32,256]{1,0:T(8,128)} %param.10), channel_id=1, source_target_pairs={{0,8},{1,9},{2,10},{3,11},{4,12},{5,13},{6,14},{7,15},{8,0},{9,1},... | collective-permute-start | bytes 98312 | tf_op jit(solution)/shard_map/ppermute | solution.py:17
  4.7 1.6 %collective-permute-start.2 = (f32[32,256]{1,0:T(8,128)}, f32[32,256]{1,0:T(8,128)S(1)}, u32[]{:S(2)}, u32[]{:S(2)}) collective-permute-start(f32[32,256]{1,0:T(8,128)} %param.10), channel_id=1, source_target_pairs={{0,4},{1,5},{2,6},{3,7},{4,0},{5,1},{6,2},{7,3},{8,12},{9,13},{10,... | collective-permute-start | bytes 98312 | tf_op jit(solution)/shard_map/ppermute | solution.py:17
  6.3 1.3 %convert_reduce_fusion = f32[]{:T(128)} fusion(s32[512]{0:T(512)} %param.8), kind=kLoop, calls=%fused_computation.34 | loop fusion | flops 1023 | bytes 2052 | tf_op jit(solution)/shard_map/reduce_sum | solution.py:131
  8.3 0.1 reshape.34
  8.4 0.0 collective-permute-done
  8.4 0.5 collective-permute-start.1
  9.0 0.0 collective-permute-done.2
  9.0 3.4 %collective-permute-done.1 = f32[32,256]{1,0:T(8,128)S(1)} collective-permute-done((f32[32,256]{1,0:T(8,128)S(1)}, f32[32,256]{1,0:T(8,128)S(1)}, u32[]{:S(2)}, u32[]{:S(2)}) %collective-permute-start.1) | collective-permute-done | bytes 32800 | tf_op jit(solution)/shard_map/ppermute | solution.py:17
  12.5 0.0 copy-start.11
  12.5 1.6 %collective-permute-start.3 = (bf16[128,256]{1,0:T(8,128)(2,1)S(1)}, bf16[128,256]{1,0:T(8,128)(2,1)S(1)}, u32[]{:S(2)}, u32[]{:S(2)}) collective-permute-start(bf16[128,256]{1,0:T(8,128)(2,1)S(1)} %bitcast.30), channel_id=1, source_target_pairs={{0,2},{1,3},{2,0},{3,1},{4,6},{5,7},{6,4},{7,5},{8,10},{9,11},{10,... | collective-permute-start | bytes 196616 | tf_op jit(solution)/shard_map/ppermute | solution.py:17
  14.0 0.0 collective-permute-start.4
  14.0 2.8 %collective-permute-done.3.refs_1_ = bf16[128,256]{1,0:T(8,128)(2,1)S(1)} collective-permute-done((bf16[128,256]{1,0:T(8,128)(2,1)S(1)}, bf16[128,256]{1,0:T(8,128)(2,1)S(1)}, u32[]{:S(2)}, u32[]{:S(2)}) %collective-permute-start.3) | collective-permute-done | bytes 65568 | tf_op jit(solution)/shard_map/ppermute | solution.py:17
  16.8 0.0 collective-permute-start.5
  16.8 0.6 %convert_log_fusion = f32[512]{0:T(512)} fusion(s32[512]{0:T(512)S(1)} %copy-done.11), kind=kLoop, calls=%fused_computation.32 | loop fusion | flops 512 | bytes 4096 | tf_op jit(solution)/shard_map/log | solution.py:136
  17.4 0.9 %copy.13.row_term = f32[16,32,1]{2,1,0:T(8,128)} copy(f32[16,32,1]{1,0,2:T(8,128)S(1)} %bitcast.37) | data formatting | bytes 4096 | tf_op jit(solution)/shard_map/reshape | solution.py:135
  18.3 0.0 copy-done
  18.3 0.0 collective-permute-done.4.refs_2_
  18.3 0.0 collective-permute-done.5.refs_3_
  18.3 0.6 %copy-done.2 = bf16[128,256]{1,0:T(8,128)(2,1)} copy-done((bf16[128,256]{1,0:T(8,128)(2,1)}, bf16[128,256]{1,0:T(8,128)(2,1)S(1)}, u32[]{:S(2)}) %copy-start.2) | copy-done | bytes 65560
  18.9 0.0 copy-done.3
  18.9 3.3 %slopes.1 = (bf16[256,256]{1,0:T(8,128)(2,1)}, f32[256,256]{1,0:T(8,128)}, bf16[4,128,512]{2,1,0:T(8,128)(2,1)}) custom-call(s32[4,2,2,32,512]{4,3,2,1,0:T(8,128)} %bitcast.29, f32[16,32,1]{2,1,0:T(8,128)} %copy.13.row_term, f32[1,512]{1,0:T(1,128)} %bitcast.38, f32[512,256]{1,0:T(8,128)} %master.1, bf16[128,256]{1,0:T(8,128)(2,1)} %bitcast.32, ...), custom_call_target="tpu_custom_call" | custom-call | tf_op jit(solution)/shard_map/slopes/pallas_call | solution.py:146
  22.3 0.5 collective-permute-start.6
  22.8 1.2 %collective-permute-done.6 = bf16[256,256]{1,0:T(8,128)(2,1)S(1)} collective-permute-done((bf16[256,256]{1,0:T(8,128)(2,1)}, bf16[256,256]{1,0:T(8,128)(2,1)S(1)}, u32[]{:S(2)}, u32[]{:S(2)}) %collective-permute-start.6) | collective-permute-done | bytes 131104 | tf_op jit(solution)/shard_map/ppermute | solution.py:17
  24.0 1.0 %convert_add_fusion = f32[256,256]{1,0:T(8,128)S(1)} fusion(f32[256,256]{1,0:T(8,128)} %get-tuple-element.10, bf16[256,256]{1,0:T(8,128)(2,1)S(1)} %collective-permute-done.6), kind=kLoop, calls=%fused_computation | loop fusion | flops 131072 | bytes 655360 | tf_op jit(solution)/shard_map/add | solution.py:156
  25.0 0.0 copy-start.9
  25.0 1.6 %collective-permute-start.7 = (bf16[128,256]{1,0:T(8,128)(2,1)S(1)}, bf16[128,256]{1,0:T(8,128)(2,1)S(1)}, u32[]{:S(2)}, u32[]{:S(2)}) collective-permute-start(bf16[128,256]{1,0:T(8,128)(2,1)S(1)} %slice.15), channel_id=1, source_target_pairs={{0,2},{1,3},{2,0},{3,1},{4,6},{5,7},{6,4},{7,5},{8,10},{9,11},{10,... | collective-permute-start | bytes 196616 | tf_op jit(solution)/shard_map/ppermute | solution.py:17
  26.6 2.8 %collective-permute-done.7 = bf16[128,256]{1,0:T(8,128)(2,1)S(1)} collective-permute-done((bf16[128,256]{1,0:T(8,128)(2,1)S(1)}, bf16[128,256]{1,0:T(8,128)(2,1)S(1)}, u32[]{:S(2)}, u32[]{:S(2)}) %collective-permute-start.7) | collective-permute-done | bytes 65568 | tf_op jit(solution)/shard_map/ppermute | solution.py:17
  29.4 0.5 collective-permute-start.8
  29.9 2.6 %collective-permute-start.10 = (f32[32,256]{1,0:T(8,128)S(1)}, f32[32,256]{1,0:T(8,128)S(1)}, u32[]{:S(2)}, u32[]{:S(2)}) collective-permute-start(f32[32,256]{1,0:T(8,128)S(1)} %copy-done.9), channel_id=1, source_target_pairs={{0,8},{1,9},{2,10},{3,11},{4,12},{5,13},{6,14},{7,15},{8,0},{9,1},... | collective-permute-start | bytes 98312 | tf_op jit(solution)/shard_map/ppermute | solution.py:17
  32.6 0.4 collective-permute-start.12
  33.0 1.9 %collective-permute-done.10 = f32[32,256]{1,0:T(8,128)S(1)} collective-permute-done((f32[32,256]{1,0:T(8,128)S(1)}, f32[32,256]{1,0:T(8,128)S(1)}, u32[]{:S(2)}, u32[]{:S(2)}) %collective-permute-start.10) | collective-permute-done | bytes 32800 | tf_op jit(solution)/shard_map/ppermute | solution.py:17
  34.9 1.5 %collective-permute-start.11 = (f32[32,256]{1,0:T(8,128)S(1)}, f32[32,256]{1,0:T(8,128)S(1)}, u32[]{:S(2)}, u32[]{:S(2)}) collective-permute-start(f32[32,256]{1,0:T(8,128)S(1)} %collective-permute-done.10), channel_id=1, source_target_pairs={{0,4},{1,5},{2,6},{3,7},{4,0},{5,1},{6,2},{7,3},{8,12},{9,13},{10,... | collective-permute-start | bytes 98312 | tf_op jit(solution)/shard_map/ppermute | solution.py:17
  36.3 0.0 collective-permute-done.8
  36.4 1.5 %collective-permute-start.9 = (bf16[128,256]{1,0:T(8,128)(2,1)S(1)}, bf16[128,256]{1,0:T(8,128)(2,1)S(1)}, u32[]{:S(2)}, u32[]{:S(2)}) collective-permute-start(bf16[128,256]{1,0:T(8,128)(2,1)S(1)} %add_convert_fusion), channel_id=1, source_target_pairs={{0,8},{1,9},{2,10},{3,11},{4,12},{5,13},{6,14},{7,15},{8,0},{9,1},... | collective-permute-start | bytes 196616 | tf_op jit(solution)/shard_map/ppermute | solution.py:17
  37.9 0.0 collective-permute-done.12
  37.9 0.9 %collective-permute-done.11 = f32[32,256]{1,0:T(8,128)S(1)} collective-permute-done((f32[32,256]{1,0:T(8,128)S(1)}, f32[32,256]{1,0:T(8,128)S(1)}, u32[]{:S(2)}, u32[]{:S(2)}) %collective-permute-start.11) | collective-permute-done | bytes 32800 | tf_op jit(solution)/shard_map/ppermute | solution.py:17
  38.8 3.5 %collective-permute-done.9 = bf16[128,256]{1,0:T(8,128)(2,1)S(1)} collective-permute-done((bf16[128,256]{1,0:T(8,128)(2,1)S(1)}, bf16[128,256]{1,0:T(8,128)(2,1)S(1)}, u32[]{:S(2)}, u32[]{:S(2)}) %collective-permute-start.9) | collective-permute-done | bytes 65568 | tf_op jit(solution)/shard_map/ppermute | solution.py:17
  42.4 1.6 %collective-permute-start.13 = (bf16[4,32,256]{2,1,0:T(8,128)(2,1)S(1)}, bf16[4,32,256]{2,1,0:T(8,128)(2,1)S(1)}, u32[]{:S(2)}, u32[]{:S(2)}) collective-permute-start(bf16[4,32,256]{2,1,0:T(8,128)(2,1)S(1)} %get-tuple-element.15.refs_0_), channel_id=1, source_target_pairs={{0,2},{1,3},{2,0},{3,1},{4,6},{5,7},{6,4},{7,5},{8,10},{9,11},{10,... | collective-permute-start | bytes 196616 | tf_op jit(solution)/shard_map/ppermute | solution.py:17
  43.9 2.8 %columns.3 = (f32[512,256]{1,0:T(8,128)}, f32[512,256]{1,0:T(8,128)}) custom-call(bf16[4,128,512]{2,1,0:T(8,128)(2,1)} %get-tuple-element.12.slopes, f32[512,256]{1,0:T(8,128)} %master.1, f32[512,256]{1,0:T(8,128)} %history.1, bf16[128,256]{1,0:T(8,128)(2,1)} %bitcast.33, bf16[128,256]{1,0:T(8,128)(2,1)} %copy-done.1, bf16[128,256]{1,0:T(8,128)(2,1)} %copy-done.2, ...), custom_call_target="tpu_custom_call" | custom-call | flops 268435456 | bytes 4194304 | tf_op jit(solution)/shard_map/columns/pallas_call | solution.py:165
  46.8 0.0 collective-permute-start.14
  46.8 0.0 collective-permute-done.13.refs_1_
  46.8 0.5 collective-permute-start.15
  47.3 0.6 %dynamic-slice_bitcast_fusion = (f32[32,256]{1,0:T(8,128)}, f32[32,256]{1,0:T(8,128)}) fusion(f32[4,32,256]{2,1,0:T(8,128)S(1)} %get-tuple-element.17, s32[]{:T(128)S(6)} %select_n.111, f32[4,32,256]{2,1,0:T(8,128)S(1)} %get-tuple-element.16), kind=kLoop, calls=%fused_computation.12 | loop fusion | bytes 131076 | tf_op jit(solution)/shard_map/jit(dynamic_index_in_dim)/squeeze | solution.py:181
  47.9 0.1 collective-permute-done.14.refs_2_
  48.0 0.2 collective-permute-done.15.refs_3_
  48.2 0.5 copy-done.6
  48.7 0.6 %copy-done.7 = bf16[4,32,256]{2,1,0:T(8,128)(2,1)} copy-done((bf16[4,32,256]{2,1,0:T(8,128)(2,1)}, bf16[4,32,256]{2,1,0:T(8,128)(2,1)S(1)}, u32[]{:S(2)}) %copy-start.7) | copy-done | bytes 65560
  49.3 9.1 %place.1 = bf16[4,2,2,32,256]{4,3,2,1,0:T(8,128)(2,1)} custom-call(bf16[4,32,256]{2,1,0:T(8,128)(2,1)} %copy-done.4, bf16[4,32,256]{2,1,0:T(8,128)(2,1)} %copy-done.5, bf16[4,32,256]{2,1,0:T(8,128)(2,1)} %copy-done.6, bf16[4,32,256]{2,1,0:T(8,128)(2,1)} %copy-done.7), custom_call_target="tpu_custom_call" | custom-call | tf_op jit(solution)/shard_map/place/pallas_call | solution.py:184
  (30 shorter events, 0.2 us)
Async XLA Ops:
  0.6 7.7 %copy-start.10 = (s32[512]{0:T(512)S(1)}, s32[512]{0:T(512)}, u32[]{:S(2)}) copy-start(s32[512]{0:T(512)} %param.8) | copy-start | bytes 6148
  0.6 7.8 %collective-permute-start = (f32[32,256]{1,0:T(8,128)}, f32[32,256]{1,0:T(8,128)S(1)}, u32[]{:S(2)}, u32[]{:S(2)}) collective-permute-start(f32[32,256]{1,0:T(8,128)} %param.10), channel_id=1, source_target_pairs={{0,8},{1,9},{2,10},{3,11},{4,12},{5,13},{6,14},{7,15},{8,0},{9,1},... | collective-permute-start | bytes 98312 | tf_op jit(solution)/shard_map/ppermute | solution.py:17
  4.7 4.2 %collective-permute-start.2 = (f32[32,256]{1,0:T(8,128)}, f32[32,256]{1,0:T(8,128)S(1)}, u32[]{:S(2)}, u32[]{:S(2)}) collective-permute-start(f32[32,256]{1,0:T(8,128)} %param.10), channel_id=1, source_target_pairs={{0,4},{1,5},{2,6},{3,7},{4,0},{5,1},{6,2},{7,3},{8,12},{9,13},{10,... | collective-permute-start | bytes 98312 | tf_op jit(solution)/shard_map/ppermute | solution.py:17
  8.4 4.0 %collective-permute-start.1 = (f32[32,256]{1,0:T(8,128)S(1)}, f32[32,256]{1,0:T(8,128)S(1)}, u32[]{:S(2)}, u32[]{:S(2)}) collective-permute-start(f32[32,256]{1,0:T(8,128)S(1)} %collective-permute-done), channel_id=1, source_target_pairs={{0,4},{1,5},{2,6},{3,7},{4,0},{5,1},{6,2},{7,3},{8,12},{9,13},{10,... | collective-permute-start | bytes 98312 | tf_op jit(solution)/shard_map/ppermute | solution.py:17
  8.9 3.5 %copy-start.8 = (f32[32,256]{1,0:T(8,128)S(1)}, f32[32,256]{1,0:T(8,128)}, u32[]{:S(2)}) copy-start(f32[32,256]{1,0:T(8,128)} %param.10) | copy-start | bytes 98308
  12.4 5.8 %copy-start = (bf16[4,32,256]{2,1,0:T(8,128)(2,1)}, bf16[4,32,256]{2,1,0:T(8,128)(2,1)S(1)}, u32[]{:S(2)}) copy-start(bf16[4,32,256]{2,1,0:T(8,128)(2,1)S(1)} %fusion.2) | copy-start | bytes 196612
  12.5 4.4 %copy-start.11 = (s32[512]{0:T(512)S(1)}, s32[512]{0:T(512)}, u32[]{:S(2)}) copy-start(s32[512]{0:T(512)} %param.9) | copy-start | bytes 6148
  12.5 4.3 %collective-permute-start.3 = (bf16[128,256]{1,0:T(8,128)(2,1)S(1)}, bf16[128,256]{1,0:T(8,128)(2,1)S(1)}, u32[]{:S(2)}, u32[]{:S(2)}) collective-permute-start(bf16[128,256]{1,0:T(8,128)(2,1)S(1)} %bitcast.30), channel_id=1, source_target_pairs={{0,2},{1,3},{2,0},{3,1},{4,6},{5,7},{6,4},{7,5},{8,10},{9,11},{10,... | collective-permute-start | bytes 196616 | tf_op jit(solution)/shard_map/ppermute | solution.py:17
  14.0 4.3 %collective-permute-start.4 = (bf16[128,256]{1,0:T(8,128)(2,1)S(1)}, bf16[128,256]{1,0:T(8,128)(2,1)S(1)}, u32[]{:S(2)}, u32[]{:S(2)}) collective-permute-start(bf16[128,256]{1,0:T(8,128)(2,1)S(1)} %bitcast.31), channel_id=1, source_target_pairs={{0,1},{1,0},{2,3},{3,2},{4,5},{5,4},{6,7},{7,6},{8,9},{9,8},{10,11... | collective-permute-start | bytes 196616 | tf_op jit(solution)/shard_map/ppermute | solution.py:17
  16.8 1.5 %copy-start.1 = (bf16[128,256]{1,0:T(8,128)(2,1)}, bf16[128,256]{1,0:T(8,128)(2,1)S(1)}, u32[]{:S(2)}) copy-start(bf16[128,256]{1,0:T(8,128)(2,1)S(1)} %collective-permute-done.3.refs_1_) | copy-start | bytes 196612
  16.8 1.5 %collective-permute-start.5 = (bf16[128,256]{1,0:T(8,128)(2,1)S(1)}, bf16[128,256]{1,0:T(8,128)(2,1)S(1)}, u32[]{:S(2)}, u32[]{:S(2)}) collective-permute-start(bf16[128,256]{1,0:T(8,128)(2,1)S(1)} %collective-permute-done.3.refs_1_), channel_id=1, source_target_pairs={{0,1},{1,0},{2,3},{3,2},{4,5},{5,4},{6,7},{7,6},{8,9},{9,8},{10,11... | collective-permute-start | bytes 196616 | tf_op jit(solution)/shard_map/ppermute | solution.py:17
  18.3 0.6 %copy-start.2 = (bf16[128,256]{1,0:T(8,128)(2,1)}, bf16[128,256]{1,0:T(8,128)(2,1)S(1)}, u32[]{:S(2)}) copy-start(bf16[128,256]{1,0:T(8,128)(2,1)S(1)} %collective-permute-done.4.refs_2_) | copy-start | bytes 196612
  18.3 0.6 %copy-start.3 = (bf16[128,256]{1,0:T(8,128)(2,1)}, bf16[128,256]{1,0:T(8,128)(2,1)S(1)}, u32[]{:S(2)}) copy-start(bf16[128,256]{1,0:T(8,128)(2,1)S(1)} %collective-permute-done.5.refs_3_) | copy-start | bytes 196612
  22.3 1.7 %collective-permute-start.6 = (bf16[256,256]{1,0:T(8,128)(2,1)}, bf16[256,256]{1,0:T(8,128)(2,1)S(1)}, u32[]{:S(2)}, u32[]{:S(2)}) collective-permute-start(bf16[256,256]{1,0:T(8,128)(2,1)} %get-tuple-element.11), channel_id=1, source_target_pairs={{0,1},{1,0},{2,3},{3,2},{4,5},{5,4},{6,7},{7,6},{8,9},{9,8},{10,11... | collective-permute-start | bytes 393224 | tf_op jit(solution)/shard_map/ppermute | solution.py:17
  25.0 5.0 %copy-start.9 = (f32[32,256]{1,0:T(8,128)S(1)}, f32[32,256]{1,0:T(8,128)}, u32[]{:S(2)}) copy-start(f32[32,256]{1,0:T(8,128)} %param.11) | copy-start | bytes 98308
  25.0 4.4 %collective-permute-start.7 = (bf16[128,256]{1,0:T(8,128)(2,1)S(1)}, bf16[128,256]{1,0:T(8,128)(2,1)S(1)}, u32[]{:S(2)}, u32[]{:S(2)}) collective-permute-start(bf16[128,256]{1,0:T(8,128)(2,1)S(1)} %slice.15), channel_id=1, source_target_pairs={{0,2},{1,3},{2,0},{3,1},{4,6},{5,7},{6,4},{7,5},{8,10},{9,11},{10,... | collective-permute-start | bytes 196616 | tf_op jit(solution)/shard_map/ppermute | solution.py:17
  29.4 6.9 %collective-permute-start.8 = (bf16[128,256]{1,0:T(8,128)(2,1)S(1)}, bf16[128,256]{1,0:T(8,128)(2,1)S(1)}, u32[]{:S(2)}, u32[]{:S(2)}) collective-permute-start(bf16[128,256]{1,0:T(8,128)(2,1)S(1)} %fusion), channel_id=1, source_target_pairs={{0,4},{1,5},{2,6},{3,7},{4,0},{5,1},{6,2},{7,3},{8,12},{9,13},{10,... | collective-permute-start | bytes 196616 | tf_op jit(solution)/shard_map/ppermute | solution.py:17
  29.9 4.9 %collective-permute-start.10 = (f32[32,256]{1,0:T(8,128)S(1)}, f32[32,256]{1,0:T(8,128)S(1)}, u32[]{:S(2)}, u32[]{:S(2)}) collective-permute-start(f32[32,256]{1,0:T(8,128)S(1)} %copy-done.9), channel_id=1, source_target_pairs={{0,8},{1,9},{2,10},{3,11},{4,12},{5,13},{6,14},{7,15},{8,0},{9,1},... | collective-permute-start | bytes 98312 | tf_op jit(solution)/shard_map/ppermute | solution.py:17
  32.6 5.3 %collective-permute-start.12 = (f32[32,256]{1,0:T(8,128)S(1)}, f32[32,256]{1,0:T(8,128)S(1)}, u32[]{:S(2)}, u32[]{:S(2)}) collective-permute-start(f32[32,256]{1,0:T(8,128)S(1)} %copy-done.9), channel_id=1, source_target_pairs={{0,4},{1,5},{2,6},{3,7},{4,0},{5,1},{6,2},{7,3},{8,12},{9,13},{10,... | collective-permute-start | bytes 98312 | tf_op jit(solution)/shard_map/ppermute | solution.py:17
  34.9 3.9 %collective-permute-start.11 = (f32[32,256]{1,0:T(8,128)S(1)}, f32[32,256]{1,0:T(8,128)S(1)}, u32[]{:S(2)}, u32[]{:S(2)}) collective-permute-start(f32[32,256]{1,0:T(8,128)S(1)} %collective-permute-done.10), channel_id=1, source_target_pairs={{0,4},{1,5},{2,6},{3,7},{4,0},{5,1},{6,2},{7,3},{8,12},{9,13},{10,... | collective-permute-start | bytes 98312 | tf_op jit(solution)/shard_map/ppermute | solution.py:17
  36.4 5.9 %collective-permute-start.9 = (bf16[128,256]{1,0:T(8,128)(2,1)S(1)}, bf16[128,256]{1,0:T(8,128)(2,1)S(1)}, u32[]{:S(2)}, u32[]{:S(2)}) collective-permute-start(bf16[128,256]{1,0:T(8,128)(2,1)S(1)} %add_convert_fusion), channel_id=1, source_target_pairs={{0,8},{1,9},{2,10},{3,11},{4,12},{5,13},{6,14},{7,15},{8,0},{9,1},... | collective-permute-start | bytes 196616 | tf_op jit(solution)/shard_map/ppermute | solution.py:17
  42.4 4.4 %copy-start.4 = (bf16[4,32,256]{2,1,0:T(8,128)(2,1)}, bf16[4,32,256]{2,1,0:T(8,128)(2,1)S(1)}, u32[]{:S(2)}) copy-start(bf16[4,32,256]{2,1,0:T(8,128)(2,1)S(1)} %get-tuple-element.15.refs_0_) | copy-start | bytes 196612
  42.4 4.4 %collective-permute-start.13 = (bf16[4,32,256]{2,1,0:T(8,128)(2,1)S(1)}, bf16[4,32,256]{2,1,0:T(8,128)(2,1)S(1)}, u32[]{:S(2)}, u32[]{:S(2)}) collective-permute-start(bf16[4,32,256]{2,1,0:T(8,128)(2,1)S(1)} %get-tuple-element.15.refs_0_), channel_id=1, source_target_pairs={{0,2},{1,3},{2,0},{3,1},{4,6},{5,7},{6,4},{7,5},{8,10},{9,11},{10,... | collective-permute-start | bytes 196616 | tf_op jit(solution)/shard_map/ppermute | solution.py:17
  46.8 1.3 %collective-permute-start.14 = (bf16[4,32,256]{2,1,0:T(8,128)(2,1)S(1)}, bf16[4,32,256]{2,1,0:T(8,128)(2,1)S(1)}, u32[]{:S(2)}, u32[]{:S(2)}) collective-permute-start(bf16[4,32,256]{2,1,0:T(8,128)(2,1)S(1)} %get-tuple-element.15.refs_0_), channel_id=1, source_target_pairs={{0,1},{1,0},{2,3},{3,2},{4,5},{5,4},{6,7},{7,6},{8,9},{9,8},{10,11... | collective-permute-start | bytes 196616 | tf_op jit(solution)/shard_map/ppermute | solution.py:17
  46.8 1.1 %copy-start.5 = (bf16[4,32,256]{2,1,0:T(8,128)(2,1)}, bf16[4,32,256]{2,1,0:T(8,128)(2,1)S(1)}, u32[]{:S(2)}) copy-start(bf16[4,32,256]{2,1,0:T(8,128)(2,1)S(1)} %collective-permute-done.13.refs_1_) | copy-start | bytes 196612
  46.8 1.4 %collective-permute-start.15 = (bf16[4,32,256]{2,1,0:T(8,128)(2,1)S(1)}, bf16[4,32,256]{2,1,0:T(8,128)(2,1)S(1)}, u32[]{:S(2)}, u32[]{:S(2)}) collective-permute-start(bf16[4,32,256]{2,1,0:T(8,128)(2,1)S(1)} %collective-permute-done.13.refs_1_), channel_id=1, source_target_pairs={{0,1},{1,0},{2,3},{3,2},{4,5},{5,4},{6,7},{7,6},{8,9},{9,8},{10,11... | collective-permute-start | bytes 196616 | tf_op jit(solution)/shard_map/ppermute | solution.py:17
  48.0 0.6 %copy-start.6 = (bf16[4,32,256]{2,1,0:T(8,128)(2,1)}, bf16[4,32,256]{2,1,0:T(8,128)(2,1)S(1)}, u32[]{:S(2)}) copy-start(bf16[4,32,256]{2,1,0:T(8,128)(2,1)S(1)} %collective-permute-done.14.refs_2_) | copy-start | bytes 196612
  48.7 0.6 %copy-start.7 = (bf16[4,32,256]{2,1,0:T(8,128)(2,1)}, bf16[4,32,256]{2,1,0:T(8,128)(2,1)S(1)}, u32[]{:S(2)}) copy-start(bf16[4,32,256]{2,1,0:T(8,128)(2,1)S(1)} %collective-permute-done.15.refs_3_) | copy-start | bytes 196612

commit v2 on v1

v2 whole, which is shorter than its diff:
```python
import functools

import jax
import jax.numpy as jnp
from jax import lax
from jax.experimental import pallas as pl
from jax.experimental.pallas import tpu as pltpu
from jax.sharding import PartitionSpec as P

step_size = 2.0
VMEM = pl.BlockSpec(memory_space=pltpu.VMEM)
ANY = pl.BlockSpec(memory_space=pl.ANY)
PARAMS = pltpu.CompilerParams(vmem_limit_bytes=12 * 1024 * 1024)


def hop(value, bit, size):
    return lax.ppermute(value, "col", [(i, i ^ bit) for i in range(size)])


def near(value):
    return pltpu.with_memory_space_constraint(value, pltpu.VMEM)


def place_at(me, place):
    return lax.rem(lax.div(me, 2) + place % 2, 2), lax.rem(me + place // 2, 2)


def steps_of(count, body):
    if count == 1:
        body(0)
    else:
        pl.loop(0, count)(body)


def prepare_kernel(chunk, counts, row_totals, column_totals, columns, ratio, weight, column_copy):
    me = lax.axis_index("col")
    groups, own, owners = counts.shape[0], counts.shape[3], row_totals.shape[1]
    column_copy[...] = columns[...].astype(jnp.bfloat16)
    row_floats = row_totals[...].astype(jnp.float32)
    total = jnp.sum(jnp.sum(row_floats, axis=1, keepdims=True), axis=0, keepdims=True)
    row_terms = jnp.log(total) - jnp.log(row_floats)
    column_term = jnp.log(column_totals[...].astype(jnp.float32))
    owner = lax.broadcasted_iota(jnp.int32, row_terms.shape, 1)
    for place in range(4):
        at_x, at_core = place_at(me, place)

        def body(z, place=place, at_x=at_x, at_core=at_core):
            amounts = counts[z, at_x, at_core].astype(jnp.float32)
            here = owner == z * 4 + at_x * 2 + at_core
            row_term = jnp.sum(jnp.where(here, row_terms, 0.0), axis=1, keepdims=True)
            ratio[place, z] = jnp.log(jnp.maximum(amounts, 1.0)) + row_term - column_term
            weight[place, z] = jnp.where(amounts > 0, 0.1 + 0.25 * jnp.sqrt(amounts), 0.0)

        if groups <= 4:
            for z in range(groups):
                body(z)
        else:
            pl.loop(0, groups)(body)


def slopes_kernel(chunk, places, ratio, weight, column_copy, kept_rows, sent_rows, *refs):
    kept, sent, slopes = refs[-3:]
    group = chunk // ratio.shape[2]
    count = kept_rows.shape[0] // chunk
    for k, (place, source, target) in enumerate(zip(places, (kept_rows, sent_rows), (kept, sent))):

        def body(step, k=k, place=place, source=source, target=target):
            first = pl.multiple_of(step * chunk, chunk)
            scores = lax.dot_general(
                source[pl.ds(first, chunk), :],
                column_copy[...],
                (((1,), (1,)), ((), ())),
                preferred_element_type=jnp.float32,
            )
            at = pl.ds(step * group, group)
            gap = scores - ratio[place, at].reshape(scores.shape)
            confidence = weight[place, at].reshape(scores.shape)
            slope = jnp.where(confidence > 0, confidence * gap, jax.nn.sigmoid(gap)).astype(jnp.bfloat16)
            slopes[k, pl.ds(first, chunk), :] = slope
            target[pl.ds(first, chunk), :] = jnp.dot(
                slope, column_copy[...], preferred_element_type=jnp.float32
            ).astype(target.dtype)

        steps_of(count, body)


def columns_kernel(total_rows, chunk, early, late, master, history, *refs):
    pieces, (new_master, new_history, total) = refs[:4], refs[4:]
    count = pieces[0].shape[0] // chunk
    for place in range(4):
        slopes, k = (early, late)[place % 2], place // 2

        def body(step, place=place, slopes=slopes, k=k):
            first = pl.multiple_of(step * chunk, chunk)
            part = lax.dot_general(
                slopes[k, pl.ds(first, chunk), :],
                pieces[place][pl.ds(first, chunk), :],
                (((0,), (0,)), ((), ())),
                preferred_element_type=jnp.float32,
            )
            total[...] = part if place == 0 and count == 1 else total[...] + part

        if place == 0 and count > 1:
            total[...] = jnp.zeros_like(total)
        steps_of(count, body)
    gradient = total[...] / total_rows
    updated = history[...] + gradient * gradient
    new_history[...] = updated
    new_master[...] = master[...] - step_size * gradient * lax.rsqrt(updated)


def place_kernel(*refs):
    pieces, out = refs[:4], refs[4]
    me = lax.axis_index("col")
    for place in range(4):
        at_x, at_core = place_at(me, place)
        for z in range(out.shape[0]):
            out[z, at_x, at_core] = pieces[place][z]


def gather_group(value, size):
    place = lax.div(lax.axis_index("col"), 4)
    held = value[None]
    bit = size // 2
    while bit >= 4:
        other = hop(held, bit, size)
        upper = lax.rem(lax.div(place, bit // 4), 2) == 1
        low, high = jnp.where(upper, other, held), jnp.where(upper, held, other)
        held = jnp.stack([low, high], axis=1).reshape((2 * held.shape[0],) + held.shape[1:])
        bit //= 2
    return held


def per_device(
    counts, row_totals, column_totals, row_master, row_history, column_master, column_history
):
    size = lax.axis_size("col")
    me = lax.axis_index("col")
    total_rows, block_columns = counts.shape
    all_columns = block_columns * size
    own, width = row_master.shape
    group = size // 4
    group_rows = group * own
    chunk = 128
    ratio_type = pltpu.VMEM((4, group, own, block_columns), jnp.float32)

    master = gather_group(row_master, size)
    history = gather_group(row_history, size)
    mine = master.reshape(group_rows, width).astype(jnp.bfloat16)
    beside = hop(mine, 2, size)
    opposite = hop(mine, 1, size)
    corner = hop(beside, 1, size)

    ratio, weight, column_copy = pl.pallas_call(
        functools.partial(prepare_kernel, chunk),
        out_shape=(ratio_type, ratio_type, pltpu.VMEM(column_master.shape, jnp.bfloat16)),
        in_specs=[VMEM] * 4,
        out_specs=[VMEM] * 3,
        compiler_params=PARAMS,
        cost_estimate=pl.CostEstimate(flops=8 * counts.size, bytes_accessed=4 * counts.size, transcendentals=2 * counts.size),
        name="prepare",
    )(
        near(counts.reshape(group, 2, 2, own, block_columns)),
        near(row_totals.reshape(size, own).T),
        near(column_totals.reshape(1, block_columns)),
        near(column_master),
    )

    def slopes_of(places, kept_rows, sent_rows, *wait_for):
        return pl.pallas_call(
            functools.partial(slopes_kernel, chunk, places),
            out_shape=(
                pltpu.VMEM((group_rows, width), jnp.float32),
                pltpu.VMEM((group_rows, width), jnp.bfloat16),
                pltpu.VMEM((2, group_rows, block_columns), jnp.bfloat16),
            ),
            in_specs=[VMEM] * 5 + [ANY] * len(wait_for),
            out_specs=[VMEM] * 3,
            compiler_params=PARAMS,
            cost_estimate=pl.CostEstimate(flops=8 * group_rows * block_columns * width, bytes_accessed=0, transcendentals=4 * group_rows * block_columns),
            name="slopes",
        )(ratio, weight, column_copy, near(kept_rows), near(sent_rows), *wait_for)

    kept_early, sent_early, early = slopes_of((0, 2), mine, opposite)
    kept_late, sent_late, late = slopes_of((1, 3), beside, corner, history)

    part = kept_late + hop(sent_late, 1, size).astype(jnp.float32)
    other = hop(part.astype(jnp.bfloat16), 2, size)
    part = kept_early + hop(sent_early, 1, size).astype(jnp.float32) + other.astype(jnp.float32)
    bit = 4
    while bit < size:
        rounded = part.astype(jnp.bfloat16)
        part = rounded.astype(jnp.float32) + hop(rounded, bit, size).astype(jnp.float32)
        bit *= 2

    struct = jax.ShapeDtypeStruct(column_master.shape, jnp.float32)
    new_columns, new_column_history = pl.pallas_call(
        functools.partial(columns_kernel, total_rows, chunk),
        out_shape=(struct, struct),
        in_specs=[VMEM] * 8,
        out_specs=[VMEM] * 2,
        scratch_shapes=[pltpu.VMEM(column_master.shape, jnp.float32)],
        compiler_params=PARAMS,
        cost_estimate=pl.CostEstimate(flops=2 * total_rows * block_columns * width, bytes_accessed=4 * column_master.size * 4, transcendentals=0),
        name="columns",
    )(near(early), near(late), near(column_master), near(column_history), near(mine), near(beside), near(opposite), near(corner))

    gradient = part.reshape(group, own, width) / all_columns
    updated = history + gradient * gradient
    new_group = master - step_size * gradient / jnp.sqrt(updated)
    place = lax.div(me, 4)
    new_rows = lax.dynamic_index_in_dim(new_group, place, 0, keepdims=False)
    new_row_history = lax.dynamic_index_in_dim(updated, place, 0, keepdims=False)
    copy = new_group.astype(jnp.bfloat16)
    beside = hop(copy, 2, size)
    grid_rows = pl.pallas_call(
        place_kernel,
        out_shape=jax.ShapeDtypeStruct((group, 2, 2, own, width), jnp.bfloat16),
        in_specs=[VMEM] * 4,
        out_specs=VMEM,
        compiler_params=PARAMS,
        name="place",
    )(near(copy), near(beside), near(hop(copy, 1, size)), near(hop(beside, 1, size)))
    return (grid_rows.reshape(total_rows, width), new_rows, new_row_history, new_columns, new_column_history)


def solution(mesh):
    return jax.shard_map(
        per_device,
        mesh=mesh,
        in_specs=(
            P("parts", "col"),
            P("parts"),
            P(("parts", "col")),
            P(("parts", "col"), None),
            P(("parts", "col"), None),
            P(("parts", "col"), None),
            P(("parts", "col"), None),
        ),
        out_specs=(
            P("parts", None),
            P(("parts", "col"), None),
            P(("parts", "col"), None),
            P(("parts", "col"), None),
            P(("parts", "col"), None),
        ),
        check_vma=False,
    )
```

time: 58.6 us -> 42.5 us (0.73)
  Pallas kernels: 15.2 us -> 4.06 us
  other arithmetic: 3.01 us -> 0.2 us
  starting transfers between devices: 18.5 us -> 15.7 us
  local copies, waits for them, and re-layouts: 3.38 us -> 5.06 us
  between operations: 1.52 us -> 0.78 us
    pallas_call x1, Pallas kernels: 9.08 us -> 0.72 us  [per_device(): pl.pallas_call(place_kernel, out_shape=jax.ShapeDtypeStruct((group, 2, 2,...]
    ppermute x16 -> x15, starting transfers between devices: 18.5 us -> 15.7 us  [hop(): return lax.ppermute(value, 'col', [(i, i ^ bit) for i in range(size)])]
    unnamed x24 -> x16, local copies, waits for them, and re-layouts: 1.74 us -> 3.65 us
    pallas_call x1 -> x3, Pallas kernels: 3.33 us -> 1.9 us  [the longest x2 1.19 us: slopes_of(): pl.pallas_call(functools.partial(slopes_kernel, chunk, places), out_shape...]
    pallas_call x1, Pallas kernels: 2.84 us -> 1.44 us  [per_device(): pl.pallas_call(functools.partial(columns_kernel, total_rows, chunk), out_...]
    reduce_sum x1 -> x0, other arithmetic: 1.29 us -> none  [per_device(): jnp.sum(row_floats)]
    add x1 -> x0, other arithmetic: 0.97 us -> none  [per_device(): part = kept + hop(sent, 1, size).astype(jnp.float32)]
    reshape x2, local copies, waits for them, and re-layouts: 0.96 us -> 0.15 us  [per_device(): row_totals.reshape(size, own)]
  transfers between devices with their start and end apart: 16 -> 15, of which waited for: 9 -> 10; matrix products, arithmetic and copies ran while one was open for 6% -> 4% of each run, Pallas kernels for 5% -> 8%
where the time goes in v2:
time: 42.5 us; the launch traced here: 42.2 us
  waiting for transfers between devices  16.5 us (39%)
  starting transfers between devices  15.7 us (37%)
  local copies, waits for them, and re-layouts  5.06 us (12%)
  Pallas kernels  4.06 us (10%)
  between operations  0.78 us (2%)
    ppermute x15, waiting for transfers between devices, hop(): return lax.ppermute(value, 'col', [(i, i ^ bit) for i in range(size)])  16.5 us
    ppermute x15, starting transfers between devices, hop(): return lax.ppermute(value, 'col', [(i, i ^ bit) for i in range(size)])  15.7 us
    unnamed x16, local copies, waits for them, and re-layouts  3.65 us
    pallas_call x1, Pallas kernels, per_device(): pl.pallas_call(functools.partial(columns_kernel, total_rows, chunk), out_...  1.44 us
    pallas_call x2, Pallas kernels, slopes_of(): pl.pallas_call(functools.partial(slopes_kernel, chunk, places), out_shape...  1.19 us
  transfers between devices with their start and end apart: 15, of which 10 were waited for; matrix products, arithmetic and copies ran while one was open for 4% of the time, Pallas kernels for 8%

profile of v2, /device:TPU:0, one launch (start us, length us, event | category | flops | bytes accessed | tf_op | source)
XLA Modules:
  0.0 42.2 jit_solution(10219401597608979118)
XLA Ops:
  0.6 4.1 %collective-permute-start.6 = (f32[1,32,256]{2,1,0:T(8,128)}, f32[1,32,256]{2,1,0:T(8,128)S(1)}, u32[]{:S(2)}, u32[]{:S(2)}) collective-permute-start(f32[1,32,256]{2,1,0:T(8,128)} %bitcast.62), channel_id=1, source_target_pairs={{0,8},{1,9},{2,10},{3,11},{4,12},{5,13},{6,14},{7,15},{8,0},{9,1},... | collective-permute-start | bytes 98312 | tf_op jit(solution)/shard_map/ppermute | solution.py:17
  4.7 0.1 collective-permute-start
  4.8 0.0 copy-start.7
  4.8 0.7 %copy-done.7 = s32[512]{0:T(512)S(1)} copy-done((s32[512]{0:T(512)S(1)}, s32[512]{0:T(512)}, u32[]{:S(2)}) %copy-start.7) | copy-done | bytes 2072
  5.5 0.1 reshape.44
  5.6 0.1 copy.16
  5.7 0.7 %copy-done.4 = s32[512]{0:T(512)S(1)} copy-done((s32[512]{0:T(512)S(1)}, s32[512]{0:T(512)}, u32[]{:S(2)}) %copy-start.4) | copy-done | bytes 2072
  6.3 1.0 %copy-done = f32[512,256]{1,0:T(8,128)S(1)} copy-done((f32[512,256]{1,0:T(8,128)S(1)}, f32[512,256]{1,0:T(8,128)}, u32[]{:S(2)}) %copy-start) | copy-done | bytes 524312
  7.4 1.2 %copy-done.2 = s32[512,512]{1,0:T(8,128)S(1)} copy-done((s32[512,512]{1,0:T(8,128)S(1)}, s32[512,512]{1,0:T(8,128)}, u32[]{:S(2)}) %copy-start.2) | copy-done | bytes 1048600
  8.6 0.7 %prepare.1 = (f32[4,4,32,512]{3,2,1,0:T(8,128)S(1)}, f32[4,4,32,512]{3,2,1,0:T(8,128)S(1)}, bf16[512,256]{1,0:T(8,128)(2,1)S(1)}) custom-call(s32[4,2,2,32,512]{4,3,2,1,0:T(8,128)S(1)} %bitcast.52, s32[32,16]{1,0:T(8,128)S(1)} %bitcast.57, s32[1,512]{1,0:T(1,128)S(1)} %bitcast.58, f32[512,256]{1,0:T(8,128)S(1)} %copy-done), custom_call_target="tpu_custom_call" | custom-call | flops 2097152 | bytes 1048576 | tf_op jit(solution)/shard_map/prepare/pallas_call | solution.py:154
  9.3 0.0 collective-permute-done.6
  9.3 0.4 %collective-permute-done = f32[1,32,256]{2,1,0:T(8,128)S(1)} collective-permute-done((f32[1,32,256]{2,1,0:T(8,128)}, f32[1,32,256]{2,1,0:T(8,128)S(1)}, u32[]{:S(2)}, u32[]{:S(2)}) %collective-permute-start) | collective-permute-done | bytes 32800 | tf_op jit(solution)/shard_map/ppermute | solution.py:17
  9.8 0.0 copy-done.5
  9.8 0.0 copy-done.6
  9.8 1.6 %collective-permute-start.1 = (f32[2,32,256]{2,1,0:T(8,128)S(1)}, f32[2,32,256]{2,1,0:T(8,128)S(1)}, u32[]{:S(2)}, u32[]{:S(2)}) collective-permute-start(f32[2,32,256]{2,1,0:T(8,128)S(1)} %maximum_bitcast_fusion), channel_id=1, source_target_pairs={{0,4},{1,5},{2,6},{3,7},{4,0},{5,1},{6,2},{7,3},{8,12},{9,13},{10,... | collective-permute-start | bytes 196616 | tf_op jit(solution)/shard_map/ppermute | solution.py:17
  11.4 0.4 %collective-permute-start.7 = (f32[2,32,256]{2,1,0:T(8,128)S(1)}, f32[2,32,256]{2,1,0:T(8,128)S(1)}, u32[]{:S(2)}, u32[]{:S(2)}) collective-permute-start(f32[2,32,256]{2,1,0:T(8,128)S(1)} %maximum_bitcast_fusion.1), channel_id=1, source_target_pairs={{0,4},{1,5},{2,6},{3,7},{4,0},{5,1},{6,2},{7,3},{8,12},{9,13},{10,... | collective-permute-start | bytes 196616 | tf_op jit(solution)/shard_map/ppermute | solution.py:17
  11.9 2.4 %collective-permute-done.1 = f32[2,32,256]{2,1,0:T(8,128)S(1)} collective-permute-done((f32[2,32,256]{2,1,0:T(8,128)S(1)}, f32[2,32,256]{2,1,0:T(8,128)S(1)}, u32[]{:S(2)}, u32[]{:S(2)}) %collective-permute-start.1) | collective-permute-done | bytes 65568 | tf_op jit(solution)/shard_map/ppermute | solution.py:17
  14.4 1.6 %collective-permute-start.4 = (bf16[128,256]{1,0:T(8,128)(2,1)S(1)}, bf16[128,256]{1,0:T(8,128)(2,1)S(1)}, u32[]{:S(2)}, u32[]{:S(2)}) collective-permute-start(bf16[128,256]{1,0:T(8,128)(2,1)S(1)} %bitcast.53), channel_id=1, source_target_pairs={{0,2},{1,3},{2,0},{3,1},{4,6},{5,7},{6,4},{7,5},{8,10},{9,11},{10,... | collective-permute-start | bytes 196616 | tf_op jit(solution)/shard_map/ppermute | solution.py:17
  15.9 0.0 collective-permute-start.2
  15.9 0.0 collective-permute-done.7
  16.0 2.8 %collective-permute-done.4.kept_rows.refs_1_ = bf16[128,256]{1,0:T(8,128)(2,1)S(1)} collective-permute-done((bf16[128,256]{1,0:T(8,128)(2,1)S(1)}, bf16[128,256]{1,0:T(8,128)(2,1)S(1)}, u32[]{:S(2)}, u32[]{:S(2)}) %collective-permute-start.4) | collective-permute-done | bytes 65568 | tf_op jit(solution)/shard_map/ppermute | solution.py:17
  18.7 0.0 collective-permute-start.5
  18.7 1.2 %collective-permute-done.5.sent_rows.refs_3_ = bf16[128,256]{1,0:T(8,128)(2,1)S(1)} collective-permute-done((bf16[128,256]{1,0:T(8,128)(2,1)S(1)}, bf16[128,256]{1,0:T(8,128)(2,1)S(1)}, u32[]{:S(2)}, u32[]{:S(2)}) %collective-permute-start.5) | collective-permute-done | bytes 65568 | tf_op jit(solution)/shard_map/ppermute | solution.py:17
  20.0 0.6 %slopes.3 = (f32[128,256]{1,0:T(8,128)S(1)}, bf16[128,256]{1,0:T(8,128)(2,1)S(1)}, bf16[2,128,512]{2,1,0:T(8,128)(2,1)S(1)}) custom-call(f32[4,4,32,512]{3,2,1,0:T(8,128)S(1)} %get-tuple-element.16.ratio, f32[4,4,32,512]{3,2,1,0:T(8,128)S(1)} %get-tuple-element.17.weight, bf16[512,256]{1,0:T(8,128)(2,1)S(1)} %get-tuple-element.18.column_copy, ...), custom_call_target="tpu_custom_call" | custom-call | flops 134217728 | tf_op jit(solution)/shard_map/slopes/pallas_call | solution.py:170
  20.6 0.2 collective-permute-start.8
  20.8 0.0 collective-permute-done.2.sent_rows.refs_2_
  20.8 0.6 %slopes.2 = (f32[128,256]{1,0:T(8,128)S(1)}, bf16[128,256]{1,0:T(8,128)(2,1)S(1)}, bf16[2,128,512]{2,1,0:T(8,128)(2,1)S(1)}) custom-call(f32[4,4,32,512]{3,2,1,0:T(8,128)S(1)} %get-tuple-element.16.ratio, f32[4,4,32,512]{3,2,1,0:T(8,128)S(1)} %get-tuple-element.17.weight, bf16[512,256]{1,0:T(8,128)(2,1)S(1)} %get-tuple-element.18.column_copy, ...), custom_call_target="tpu_custom_call" | custom-call | flops 134217728 | tf_op jit(solution)/shard_map/slopes/pallas_call | solution.py:170
  21.4 0.4 collective-permute-start.3
  21.8 0.1 collective-permute-done.8
  21.9 1.6 %collective-permute-start.9 = (bf16[128,256]{1,0:T(8,128)(2,1)S(1)}, bf16[128,256]{1,0:T(8,128)(2,1)S(1)}, u32[]{:S(2)}, u32[]{:S(2)}) collective-permute-start(bf16[128,256]{1,0:T(8,128)(2,1)S(1)} %add_convert_fusion.2), channel_id=1, source_target_pairs={{0,2},{1,3},{2,0},{3,1},{4,6},{5,7},{6,4},{7,5},{8,10},{9,11},{10,... | collective-permute-start | bytes 196616 | tf_op jit(solution)/shard_map/ppermute | solution.py:17
  23.5 0.0 collective-permute-done.3
  23.5 2.8 %collective-permute-done.9 = bf16[128,256]{1,0:T(8,128)(2,1)S(1)} collective-permute-done((bf16[128,256]{1,0:T(8,128)(2,1)S(1)}, bf16[128,256]{1,0:T(8,128)(2,1)S(1)}, u32[]{:S(2)}, u32[]{:S(2)}) %collective-permute-start.9) | collective-permute-done | bytes 65568 | tf_op jit(solution)/shard_map/ppermute | solution.py:17
  26.3 1.4 %collective-permute-start.10 = (bf16[128,256]{1,0:T(8,128)(2,1)S(1)}, bf16[128,256]{1,0:T(8,128)(2,1)S(1)}, u32[]{:S(2)}, u32[]{:S(2)}) collective-permute-start(bf16[128,256]{1,0:T(8,128)(2,1)S(1)} %add_convert_fusion.1), channel_id=1, source_target_pairs={{0,4},{1,5},{2,6},{3,7},{4,0},{5,1},{6,2},{7,3},{8,12},{9,13},{10,... | collective-permute-start | bytes 196616 | tf_op jit(solution)/shard_map/ppermute | solution.py:17
  27.7 2.9 %collective-permute-done.10 = bf16[128,256]{1,0:T(8,128)(2,1)S(1)} collective-permute-done((bf16[128,256]{1,0:T(8,128)(2,1)S(1)}, bf16[128,256]{1,0:T(8,128)(2,1)S(1)}, u32[]{:S(2)}, u32[]{:S(2)}) %collective-permute-start.10) | collective-permute-done | bytes 65568 | tf_op jit(solution)/shard_map/ppermute | solution.py:17
  30.6 2.6 %collective-permute-start.11 = (bf16[128,256]{1,0:T(8,128)(2,1)S(1)}, bf16[128,256]{1,0:T(8,128)(2,1)S(1)}, u32[]{:S(2)}, u32[]{:S(2)}) collective-permute-start(bf16[128,256]{1,0:T(8,128)(2,1)S(1)} %add_convert_fusion), channel_id=1, source_target_pairs={{0,8},{1,9},{2,10},{3,11},{4,12},{5,13},{6,14},{7,15},{8,0},{9,1},... | collective-permute-start | bytes 196616 | tf_op jit(solution)/shard_map/ppermute | solution.py:17
  33.3 0.0 copy-done.1
  33.3 0.0 copy-done.3
  33.3 1.4 %columns.3 = (f32[512,256]{1,0:T(8,128)}, f32[512,256]{1,0:T(8,128)}) custom-call(bf16[2,128,512]{2,1,0:T(8,128)(2,1)S(1)} %get-tuple-element.23.early, bf16[2,128,512]{2,1,0:T(8,128)(2,1)S(1)} %get-tuple-element.24.late, f32[512,256]{1,0:T(8,128)S(1)} %copy-done.1, f32[512,256]{1,0:T(8,128)S(1)} %copy-done.3, bf16[128,256]{1,0:T(8,128)(2,1)S(1)} %bitcast.56, ...), custom_call_target="tpu_custom_call" | custom-call | flops 134217728 | bytes 2097152 | tf_op jit(solution)/shard_map/columns/pallas_call | solution.py:197
  34.7 1.1 %collective-permute-done.11 = bf16[128,256]{1,0:T(8,128)(2,1)S(1)} collective-permute-done((bf16[128,256]{1,0:T(8,128)(2,1)S(1)}, bf16[128,256]{1,0:T(8,128)(2,1)S(1)}, u32[]{:S(2)}, u32[]{:S(2)}) %collective-permute-start.11) | collective-permute-done | bytes 65568 | tf_op jit(solution)/shard_map/ppermute | solution.py:17
  35.9 1.6 %collective-permute-start.12 = (bf16[4,32,256]{2,1,0:T(8,128)(2,1)S(1)}, bf16[4,32,256]{2,1,0:T(8,128)(2,1)S(1)}, u32[]{:S(2)}, u32[]{:S(2)}) collective-permute-start(bf16[4,32,256]{2,1,0:T(8,128)(2,1)S(1)} %get-tuple-element.27.refs_0_), channel_id=1, source_target_pairs={{0,2},{1,3},{2,0},{3,1},{4,6},{5,7},{6,4},{7,5},{8,10},{9,11},{10,... | collective-permute-start | bytes 196616 | tf_op jit(solution)/shard_map/ppermute | solution.py:17
  37.5 0.0 collective-permute-start.13
  37.5 0.6 %dynamic-slice_bitcast_fusion.1 = f32[32,256]{1,0:T(8,128)} fusion(f32[4,32,256]{2,1,0:T(8,128)S(1)} %get-tuple-element.28, s32[]{:T(128)S(6)} %select_n.55), kind=kLoop, calls=%fused_computation.16 | loop fusion | bytes 65540 | tf_op jit(solution)/shard_map/jit(dynamic_index_in_dim)/squeeze | solution.py:212
  38.1 2.2 %collective-permute-done.12.refs_1_ = bf16[4,32,256]{2,1,0:T(8,128)(2,1)S(1)} collective-permute-done((bf16[4,32,256]{2,1,0:T(8,128)(2,1)S(1)}, bf16[4,32,256]{2,1,0:T(8,128)(2,1)S(1)}, u32[]{:S(2)}, u32[]{:S(2)}) %collective-permute-start.12) | collective-permute-done | bytes 65568 | tf_op jit(solution)/shard_map/ppermute | solution.py:17
  40.3 0.0 collective-permute-start.14
  40.3 0.6 %dynamic-slice_bitcast_fusion = f32[32,256]{1,0:T(8,128)} fusion(f32[4,32,256]{2,1,0:T(8,128)S(1)} %get-tuple-element.29, s32[]{:T(128)S(6)} %select_n.55), kind=kLoop, calls=%fused_computation.15 | loop fusion | bytes 65540 | tf_op jit(solution)/shard_map/jit(dynamic_index_in_dim)/squeeze | solution.py:213
  40.9 0.0 collective-permute-done.13.refs_2_
  40.9 0.6 %collective-permute-done.14.refs_3_ = bf16[4,32,256]{2,1,0:T(8,128)(2,1)S(1)} collective-permute-done((bf16[4,32,256]{2,1,0:T(8,128)(2,1)S(1)}, bf16[4,32,256]{2,1,0:T(8,128)(2,1)S(1)}, u32[]{:S(2)}, u32[]{:S(2)}) %collective-permute-start.14) | collective-permute-done | bytes 65568 | tf_op jit(solution)/shard_map/ppermute | solution.py:17
  41.5 0.7 %place.1 = bf16[4,2,2,32,256]{4,3,2,1,0:T(8,128)(2,1)} custom-call(bf16[4,32,256]{2,1,0:T(8,128)(2,1)S(1)} %get-tuple-element.27.refs_0_, bf16[4,32,256]{2,1,0:T(8,128)(2,1)S(1)} %collective-permute-done.12.refs_1_, bf16[4,32,256]{2,1,0:T(8,128)(2,1)S(1)} %collective-permute-done.13.refs_2_, bf16[4,32,256]{2,1,0:T(8,128)(2,1)S(1)} %collective-permute-done.14.refs_3_), custom_call_target="tpu_custom_call" | custom-call | tf_op jit(solution)/shard_map/place/pallas_call | solution.py:216
  (23 shorter events, 0.2 us)
Async XLA Ops:
  0.6 8.7 %collective-permute-start.6 = (f32[1,32,256]{2,1,0:T(8,128)}, f32[1,32,256]{2,1,0:T(8,128)S(1)}, u32[]{:S(2)}, u32[]{:S(2)}) collective-permute-start(f32[1,32,256]{2,1,0:T(8,128)} %bitcast.62), channel_id=1, source_target_pairs={{0,8},{1,9},{2,10},{3,11},{4,12},{5,13},{6,14},{7,15},{8,0},{9,1},... | collective-permute-start | bytes 98312 | tf_op jit(solution)/shard_map/ppermute | solution.py:17
  4.7 5.0 %collective-permute-start = (f32[1,32,256]{2,1,0:T(8,128)}, f32[1,32,256]{2,1,0:T(8,128)S(1)}, u32[]{:S(2)}, u32[]{:S(2)}) collective-permute-start(f32[1,32,256]{2,1,0:T(8,128)} %bitcast.63), channel_id=1, source_target_pairs={{0,8},{1,9},{2,10},{3,11},{4,12},{5,13},{6,14},{7,15},{8,0},{9,1},... | collective-permute-start | bytes 98312 | tf_op jit(solution)/shard_map/ppermute | solution.py:17
  4.8 0.7 %copy-start.7 = (s32[512]{0:T(512)S(1)}, s32[512]{0:T(512)}, u32[]{:S(2)}) copy-start(s32[512]{0:T(512)} %param.8) | copy-start | bytes 6148
  5.7 0.7 %copy-start.4 = (s32[512]{0:T(512)S(1)}, s32[512]{0:T(512)}, u32[]{:S(2)}) copy-start(s32[512]{0:T(512)} %param.9) | copy-start | bytes 6148
  6.3 1.0 %copy-start = (f32[512,256]{1,0:T(8,128)S(1)}, f32[512,256]{1,0:T(8,128)}, u32[]{:S(2)}) copy-start(f32[512,256]{1,0:T(8,128)} %master.1) | copy-start | bytes 1572868
  7.4 1.2 %copy-start.2 = (s32[512,512]{1,0:T(8,128)S(1)}, s32[512,512]{1,0:T(8,128)}, u32[]{:S(2)}) copy-start(s32[512,512]{1,0:T(8,128)} %param.7) | copy-start | bytes 3145732
  8.6 1.2 %copy-start.5 = (f32[32,256]{1,0:T(8,128)S(1)}, f32[32,256]{1,0:T(8,128)}, u32[]{:S(2)}) copy-start(f32[32,256]{1,0:T(8,128)} %param.11) | copy-start | bytes 98308
  8.6 1.2 %copy-start.6 = (f32[32,256]{1,0:T(8,128)S(1)}, f32[32,256]{1,0:T(8,128)}, u32[]{:S(2)}) copy-start(f32[32,256]{1,0:T(8,128)} %param.10) | copy-start | bytes 98308
  9.8 4.5 %collective-permute-start.1 = (f32[2,32,256]{2,1,0:T(8,128)S(1)}, f32[2,32,256]{2,1,0:T(8,128)S(1)}, u32[]{:S(2)}, u32[]{:S(2)}) collective-permute-start(f32[2,32,256]{2,1,0:T(8,128)S(1)} %maximum_bitcast_fusion), channel_id=1, source_target_pairs={{0,4},{1,5},{2,6},{3,7},{4,0},{5,1},{6,2},{7,3},{8,12},{9,13},{10,... | collective-permute-start | bytes 196616 | tf_op jit(solution)/shard_map/ppermute | solution.py:17
  11.4 4.5 %collective-permute-start.7 = (f32[2,32,256]{2,1,0:T(8,128)S(1)}, f32[2,32,256]{2,1,0:T(8,128)S(1)}, u32[]{:S(2)}, u32[]{:S(2)}) collective-permute-start(f32[2,32,256]{2,1,0:T(8,128)S(1)} %maximum_bitcast_fusion.1), channel_id=1, source_target_pairs={{0,4},{1,5},{2,6},{3,7},{4,0},{5,1},{6,2},{7,3},{8,12},{9,13},{10,... | collective-permute-start | bytes 196616 | tf_op jit(solution)/shard_map/ppermute | solution.py:17
  14.4 4.3 %collective-permute-start.4 = (bf16[128,256]{1,0:T(8,128)(2,1)S(1)}, bf16[128,256]{1,0:T(8,128)(2,1)S(1)}, u32[]{:S(2)}, u32[]{:S(2)}) collective-permute-start(bf16[128,256]{1,0:T(8,128)(2,1)S(1)} %bitcast.53), channel_id=1, source_target_pairs={{0,2},{1,3},{2,0},{3,1},{4,6},{5,7},{6,4},{7,5},{8,10},{9,11},{10,... | collective-permute-start | bytes 196616 | tf_op jit(solution)/shard_map/ppermute | solution.py:17
  15.9 4.9 %collective-permute-start.2 = (bf16[128,256]{1,0:T(8,128)(2,1)S(1)}, bf16[128,256]{1,0:T(8,128)(2,1)S(1)}, u32[]{:S(2)}, u32[]{:S(2)}) collective-permute-start(bf16[128,256]{1,0:T(8,128)(2,1)S(1)} %bitcast.54), channel_id=1, source_target_pairs={{0,1},{1,0},{2,3},{3,2},{4,5},{5,4},{6,7},{7,6},{8,9},{9,8},{10,11... | collective-permute-start | bytes 196616 | tf_op jit(solution)/shard_map/ppermute | solution.py:17
  18.7 1.3 %collective-permute-start.5 = (bf16[128,256]{1,0:T(8,128)(2,1)S(1)}, bf16[128,256]{1,0:T(8,128)(2,1)S(1)}, u32[]{:S(2)}, u32[]{:S(2)}) collective-permute-start(bf16[128,256]{1,0:T(8,128)(2,1)S(1)} %collective-permute-done.4.kept_rows.refs_1_), channel_id=1, source_target_pairs={{0,1},{1,0},{2,3},{3,2},{4,5},{5,4},{6,7},{7,6},{8,9},{9,8},{10,11... | collective-permute-start | bytes 196616 | tf_op jit(solution)/shard_map/ppermute | solution.py:17
  20.6 1.3 %collective-permute-start.8 = (bf16[128,256]{1,0:T(8,128)(2,1)S(1)}, bf16[128,256]{1,0:T(8,128)(2,1)S(1)}, u32[]{:S(2)}, u32[]{:S(2)}) collective-permute-start(bf16[128,256]{1,0:T(8,128)(2,1)S(1)} %get-tuple-element.22), channel_id=1, source_target_pairs={{0,1},{1,0},{2,3},{3,2},{4,5},{5,4},{6,7},{7,6},{8,9},{9,8},{10,11... | collective-permute-start | bytes 196616 | tf_op jit(solution)/shard_map/ppermute | solution.py:17
  21.4 2.1 %collective-permute-start.3 = (bf16[128,256]{1,0:T(8,128)(2,1)S(1)}, bf16[128,256]{1,0:T(8,128)(2,1)S(1)}, u32[]{:S(2)}, u32[]{:S(2)}) collective-permute-start(bf16[128,256]{1,0:T(8,128)(2,1)S(1)} %get-tuple-element.20), channel_id=1, source_target_pairs={{0,1},{1,0},{2,3},{3,2},{4,5},{5,4},{6,7},{7,6},{8,9},{9,8},{10,11... | collective-permute-start | bytes 196616 | tf_op jit(solution)/shard_map/ppermute | solution.py:17
  21.9 4.3 %collective-permute-start.9 = (bf16[128,256]{1,0:T(8,128)(2,1)S(1)}, bf16[128,256]{1,0:T(8,128)(2,1)S(1)}, u32[]{:S(2)}, u32[]{:S(2)}) collective-permute-start(bf16[128,256]{1,0:T(8,128)(2,1)S(1)} %add_convert_fusion.2), channel_id=1, source_target_pairs={{0,2},{1,3},{2,0},{3,1},{4,6},{5,7},{6,4},{7,5},{8,10},{9,11},{10,... | collective-permute-start | bytes 196616 | tf_op jit(solution)/shard_map/ppermute | solution.py:17
  26.2 7.0 %copy-start.1 = (f32[512,256]{1,0:T(8,128)S(1)}, f32[512,256]{1,0:T(8,128)}, u32[]{:S(2)}) copy-start(f32[512,256]{1,0:T(8,128)} %master.1) | copy-start | bytes 1572868
  26.2 7.1 %copy-start.3 = (f32[512,256]{1,0:T(8,128)S(1)}, f32[512,256]{1,0:T(8,128)}, u32[]{:S(2)}) copy-start(f32[512,256]{1,0:T(8,128)} %history.1) | copy-start | bytes 1572868
  26.3 4.3 %collective-permute-start.10 = (bf16[128,256]{1,0:T(8,128)(2,1)S(1)}, bf16[128,256]{1,0:T(8,128)(2,1)S(1)}, u32[]{:S(2)}, u32[]{:S(2)}) collective-permute-start(bf16[128,256]{1,0:T(8,128)(2,1)S(1)} %add_convert_fusion.1), channel_id=1, source_target_pairs={{0,4},{1,5},{2,6},{3,7},{4,0},{5,1},{6,2},{7,3},{8,12},{9,13},{10,... | collective-permute-start | bytes 196616 | tf_op jit(solution)/shard_map/ppermute | solution.py:17
  30.6 5.2 %collective-permute-start.11 = (bf16[128,256]{1,0:T(8,128)(2,1)S(1)}, bf16[128,256]{1,0:T(8,128)(2,1)S(1)}, u32[]{:S(2)}, u32[]{:S(2)}) collective-permute-start(bf16[128,256]{1,0:T(8,128)(2,1)S(1)} %add_convert_fusion), channel_id=1, source_target_pairs={{0,8},{1,9},{2,10},{3,11},{4,12},{5,13},{6,14},{7,15},{8,0},{9,1},... | collective-permute-start | bytes 196616 | tf_op jit(solution)/shard_map/ppermute | solution.py:17
  35.9 4.3 %collective-permute-start.12 = (bf16[4,32,256]{2,1,0:T(8,128)(2,1)S(1)}, bf16[4,32,256]{2,1,0:T(8,128)(2,1)S(1)}, u32[]{:S(2)}, u32[]{:S(2)}) collective-permute-start(bf16[4,32,256]{2,1,0:T(8,128)(2,1)S(1)} %get-tuple-element.27.refs_0_), channel_id=1, source_target_pairs={{0,2},{1,3},{2,0},{3,1},{4,6},{5,7},{6,4},{7,5},{8,10},{9,11},{10,... | collective-permute-start | bytes 196616 | tf_op jit(solution)/shard_map/ppermute | solution.py:17
  37.5 3.4 %collective-permute-start.13 = (bf16[4,32,256]{2,1,0:T(8,128)(2,1)S(1)}, bf16[4,32,256]{2,1,0:T(8,128)(2,1)S(1)}, u32[]{:S(2)}, u32[]{:S(2)}) collective-permute-start(bf16[4,32,256]{2,1,0:T(8,128)(2,1)S(1)} %get-tuple-element.27.refs_0_), channel_id=1, source_target_pairs={{0,1},{1,0},{2,3},{3,2},{4,5},{5,4},{6,7},{7,6},{8,9},{9,8},{10,11... | collective-permute-start | bytes 196616 | tf_op jit(solution)/shard_map/ppermute | solution.py:17
  40.3 1.3 %collective-permute-start.14 = (bf16[4,32,256]{2,1,0:T(8,128)(2,1)S(1)}, bf16[4,32,256]{2,1,0:T(8,128)(2,1)S(1)}, u32[]{:S(2)}, u32[]{:S(2)}) collective-permute-start(bf16[4,32,256]{2,1,0:T(8,128)(2,1)S(1)} %collective-permute-done.12.refs_1_), channel_id=1, source_target_pairs={{0,1},{1,0},{2,3},{3,2},{4,5},{5,4},{6,7},{7,6},{8,9},{9,8},{10,11... | collective-permute-start | bytes 196616 | tf_op jit(solution)/shard_map/ppermute | solution.py:17

commit v3 on v2

--- a/solution.py
+++ b/solution.py
@@ -9,8 +9,9 @@
 
 step_size = 2.0
 VMEM = pl.BlockSpec(memory_space=pltpu.VMEM)
+HBM = pl.BlockSpec(memory_space=pltpu.HBM)
 ANY = pl.BlockSpec(memory_space=pl.ANY)
-PARAMS = pltpu.CompilerParams(vmem_limit_bytes=12 * 1024 * 1024)
+PARAMS = pltpu.CompilerParams(vmem_limit_bytes=16 * 1024 * 1024)
 
 
 def hop(value, bit, size):
@@ -19,6 +20,10 @@
 
 def near(value):
     return pltpu.with_memory_space_constraint(value, pltpu.VMEM)
+
+
+def far(value):
+    return pltpu.with_memory_space_constraint(value, pltpu.HBM)
 
 
 def place_at(me, place):
@@ -32,23 +37,33 @@
         pl.loop(0, count)(body)
 
 
-def prepare_kernel(chunk, counts, row_totals, column_totals, columns, ratio, weight, column_copy):
+def prepare_kernel(counts, row_totals, column_totals, columns, _, ratio, weight, column_copy, *scratch):
+    near_counts, near_rows, near_columns, near_copy, row_terms, sems = scratch
     me = lax.axis_index("col")
-    groups, own, owners = counts.shape[0], counts.shape[3], row_totals.shape[1]
-    column_copy[...] = columns[...].astype(jnp.bfloat16)
-    row_floats = row_totals[...].astype(jnp.float32)
-    total = jnp.sum(jnp.sum(row_floats, axis=1, keepdims=True), axis=0, keepdims=True)
-    row_terms = jnp.log(total) - jnp.log(row_floats)
-    column_term = jnp.log(column_totals[...].astype(jnp.float32))
-    owner = lax.broadcasted_iota(jnp.int32, row_terms.shape, 1)
+    groups, own = counts.shape[0], counts.shape[3]
+    copies = [
+        pltpu.make_async_copy(row_totals, near_rows, sems.at[0]),
+        pltpu.make_async_copy(column_totals, near_columns, sems.at[1]),
+        pltpu.make_async_copy(counts, near_counts, sems.at[2]),
+        pltpu.make_async_copy(columns, near_copy, sems.at[3]),
+    ]
+    for copy in copies:
+        copy.start()
+    copies[0].wait()
+    row_floats = near_rows[...].astype(jnp.float32)
+    terms = jnp.log(jnp.sum(row_floats, axis=1, keepdims=True)) - jnp.log(row_floats)
+    row_terms[...] = jnp.broadcast_to(terms, (128, terms.shape[1])).T.reshape(row_terms.shape)
+    copies[1].wait()
+    column_term = jnp.log(near_columns[...].astype(jnp.float32))
+    copies[2].wait()
     for place in range(4):
         at_x, at_core = place_at(me, place)
 
         def body(z, place=place, at_x=at_x, at_core=at_core):
-            amounts = counts[z, at_x, at_core].astype(jnp.float32)
-            here = owner == z * 4 + at_x * 2 + at_core
-            row_term = jnp.sum(jnp.where(here, row_terms, 0.0), axis=1, keepdims=True)
-            ratio[place, z] = jnp.log(jnp.maximum(amounts, 1.0)) + row_term - column_term
+            amounts = near_counts[z, at_x, at_core].astype(jnp.float32)
+            term = row_terms[z, at_x, at_core]
+            term = jnp.concatenate([term] * (amounts.shape[1] // 128), axis=1)
+            ratio[place, z] = jnp.log(jnp.maximum(amounts, 1.0)) + (term - column_term)
             weight[place, z] = jnp.where(amounts > 0, 0.1 + 0.25 * jnp.sqrt(amounts), 0.0)
 
         if groups <= 4:
@@ -56,6 +71,8 @@
                 body(z)
         else:
             pl.loop(0, groups)(body)
+    copies[3].wait()
+    column_copy[...] = near_copy[...].astype(jnp.bfloat16)
 
 
 def slopes_kernel(chunk, places, ratio, weight, column_copy, kept_rows, sent_rows, *refs):
@@ -118,17 +135,10 @@
             out[z, at_x, at_core] = pieces[place][z]
 
 
-def gather_group(value, size):
-    place = lax.div(lax.axis_index("col"), 4)
-    held = value[None]
-    bit = size // 2
-    while bit >= 4:
-        other = hop(held, bit, size)
-        upper = lax.rem(lax.div(place, bit // 4), 2) == 1
-        low, high = jnp.where(upper, other, held), jnp.where(upper, held, other)
-        held = jnp.stack([low, high], axis=1).reshape((2 * held.shape[0],) + held.shape[1:])
-        bit //= 2
-    return held
+def joined(held, other, bit):
+    upper = lax.rem(lax.div(lax.axis_index("col"), bit), 2) == 1
+    low, high = jnp.where(upper, other, held), jnp.where(upper, held, other)
+    return jnp.stack([low, high], axis=1).reshape((2 * held.shape[0],) + held.shape[1:])
 
 
 def per_device(
@@ -144,27 +154,42 @@
     chunk = 128
     ratio_type = pltpu.VMEM((4, group, own, block_columns), jnp.float32)
 
-    master = gather_group(row_master, size)
-    history = gather_group(row_history, size)
-    mine = master.reshape(group_rows, width).astype(jnp.bfloat16)
-    beside = hop(mine, 2, size)
-    opposite = hop(mine, 1, size)
-    corner = hop(beside, 1, size)
-
+    bits = [size >> k for k in range(1, size.bit_length() - 2)]
+    master, first_hop = row_master[None], None
+    for bit in bits:
+        other = hop(master, bit, size)
+        first_hop = other if first_hop is None else first_hop
+        master = joined(master, other, bit).astype(jnp.bfloat16)
+    grid = (group, 2, 2, own)
     ratio, weight, column_copy = pl.pallas_call(
-        functools.partial(prepare_kernel, chunk),
+        prepare_kernel,
         out_shape=(ratio_type, ratio_type, pltpu.VMEM(column_master.shape, jnp.bfloat16)),
-        in_specs=[VMEM] * 4,
+        in_specs=[HBM] * 4 + [ANY],
         out_specs=[VMEM] * 3,
+        scratch_shapes=[
+            pltpu.VMEM(grid + (block_columns,), jnp.int32),
+            pltpu.VMEM((1, total_rows), jnp.int32),
+            pltpu.VMEM((1, block_columns), jnp.int32),
+            pltpu.VMEM(column_master.shape, jnp.float32),
+            pltpu.VMEM(grid + (128,), jnp.float32),
+            pltpu.SemaphoreType.DMA((4,)),
+        ],
         compiler_params=PARAMS,
         cost_estimate=pl.CostEstimate(flops=8 * counts.size, bytes_accessed=4 * counts.size, transcendentals=2 * counts.size),
         name="prepare",
     )(
-        near(counts.reshape(group, 2, 2, own, block_columns)),
-        near(row_totals.reshape(size, own).T),
-        near(column_totals.reshape(1, block_columns)),
-        near(column_master),
+        far(counts.reshape(grid + (block_columns,))),
+        far(row_totals.reshape(1, total_rows)),
+        far(column_totals.reshape(1, block_columns)),
+        far(column_master),
+        first_hop,
     )
+
+    master, column_copy = lax.optimization_barrier((master, column_copy))
+    mine = master.reshape(group_rows, width)
+    beside = hop(mine, 2, size)
+    opposite = hop(mine, 1, size)
+    corner = hop(beside, 1, size)
 
     def slopes_of(places, kept_rows, sent_rows, *wait_for):
         return pl.pallas_call(
@@ -182,16 +207,17 @@
         )(ratio, weight, column_copy, near(kept_rows), near(sent_rows), *wait_for)
 
     kept_early, sent_early, early = slopes_of((0, 2), mine, opposite)
-    kept_late, sent_late, late = slopes_of((1, 3), beside, corner, history)
+    kept_late, sent_late, late = slopes_of((1, 3), beside, corner, early)
 
     part = kept_late + hop(sent_late, 1, size).astype(jnp.float32)
     other = hop(part.astype(jnp.bfloat16), 2, size)
     part = kept_early + hop(sent_early, 1, size).astype(jnp.float32) + other.astype(jnp.float32)
-    bit = 4
-    while bit < size:
+    history = row_history.astype(jnp.bfloat16)[None]
+    for bit in bits:
         rounded = part.astype(jnp.bfloat16)
-        part = rounded.astype(jnp.float32) + hop(rounded, bit, size).astype(jnp.float32)
-        bit *= 2
+        other = hop(jnp.concatenate([rounded, history.reshape(-1, width)]), bit, size)
+        part = rounded.astype(jnp.float32) + other[:group_rows].astype(jnp.float32)
+        history = joined(history, other[group_rows:].reshape(history.shape), bit)
 
     struct = jax.ShapeDtypeStruct(column_master.shape, jnp.float32)
     new_columns, new_column_history = pl.pallas_call(
@@ -205,13 +231,14 @@
         name="columns",
     )(near(early), near(late), near(column_master), near(column_history), near(mine), near(beside), near(opposite), near(corner))
 
+    def adagrad(master, history, gradient):
+        updated = history + gradient * gradient
+        return master - step_size * gradient * lax.rsqrt(updated), updated
+
     gradient = part.reshape(group, own, width) / all_columns
-    updated = history + gradient * gradient
-    new_group = master - step_size * gradient / jnp.sqrt(updated)
-    place = lax.div(me, 4)
-    new_rows = lax.dynamic_index_in_dim(new_group, place, 0, keepdims=False)
-    new_row_history = lax.dynamic_index_in_dim(updated, place, 0, keepdims=False)
-    copy = new_group.astype(jnp.bfloat16)
+    own_gradient = lax.dynamic_index_in_dim(gradient, lax.div(me, 4), 0, keepdims=False)
+    new_rows, new_row_history = adagrad(row_master, row_history, own_gradient)
+    copy = adagrad(master.astype(jnp.float32), history.astype(jnp.float32), gradient)[0].astype(jnp.bfloat16)
     beside = hop(copy, 2, size)
     grid_rows = pl.pallas_call(
         place_kernel,

time: 42.5 us -> 40.1 us (0.944)
  local copies, waits for them, and re-layouts: 5.06 us -> 0.04 us
  Pallas kernels: 4.06 us -> 5.24 us
  waiting for transfers between devices: 16.5 us -> 17.2 us
  other arithmetic: 0.2 us -> 0.85 us
    unnamed x16 -> x8, local copies, waits for them, and re-layouts: 3.65 us -> 0.02 us
    squeeze x2 -> x0, local copies, waits for them, and re-layouts: 1.24 us -> none  [the longest x1 0.62 us: per_device(): lax.dynamic_index_in_dim(updated, place, 0, keepdims=False)]
    pallas_call x1, Pallas kernels: 0.71 us -> 1.9 us  [per_device(): pl.pallas_call(prepare_kernel, out_shape=(ratio_type, ratio_type, pltpu.V...]
    ppermute x15 -> x13, waiting for transfers between devices: 16.5 us -> 17.2 us  [hop(): return lax.ppermute(value, 'col', [(i, i ^ bit) for i in range(size)])]
    sub x0 -> x1, other arithmetic: none -> 0.63 us  [adagrad(): return (master - step_size * gradient * lax.rsqrt(updated), updated)]
    ppermute x15 -> x13, starting transfers between devices: 15.7 us -> 15.7 us  [hop(): return lax.ppermute(value, 'col', [(i, i ^ bit) for i in range(size)])]
  transfers between devices with their start and end apart: 15 -> 13, of which waited for: 10 -> 10; matrix products, arithmetic and copies ran while one was open for 4% -> 2% of each run, Pallas kernels for 8% -> 10%
where the time goes in v3:
time: 40.1 us; the launch traced here: 39.9 us
  waiting for transfers between devices  17.2 us (43%)
  starting transfers between devices  15.7 us (39%)
  Pallas kernels  5.24 us (13%)
  other arithmetic  0.85 us (2%)
  between operations  0.79 us (2%)
    ppermute x13, waiting for transfers between devices, hop(): return lax.ppermute(value, 'col', [(i, i ^ bit) for i in range(size)])  17.2 us
    ppermute x13, starting transfers between devices, hop(): return lax.ppermute(value, 'col', [(i, i ^ bit) for i in range(size)])  15.7 us
    pallas_call x1, Pallas kernels, per_device(): pl.pallas_call(prepare_kernel, out_shape=(ratio_type, ratio_type, pltpu.V...  1.9 us
    pallas_call x1, Pallas kernels, per_device(): pl.pallas_call(functools.partial(columns_kernel, total_rows, chunk), out_...  1.44 us
    pallas_call x2, Pallas kernels, slopes_of(): pl.pallas_call(functools.partial(slopes_kernel, chunk, places), out_shape...  1.18 us
  transfers between devices with their start and end apart: 13, of which 10 were waited for; matrix products, arithmetic and copies ran while one was open for 2% of the time, Pallas kernels for 10%

profile of v3, /device:TPU:0, one launch (start us, length us, event | category | flops | bytes accessed | tf_op | source)
XLA Modules:
  0.0 39.9 jit_solution(781081320172685947)
XLA Ops:
  0.6 0.0 copy-start.3
  0.6 4.1 %collective-permute-start = (f32[1,32,256]{2,1,0:T(8,128)}, f32[1,32,256]{2,1,0:T(8,128)S(1)}, u32[]{:S(2)}, u32[]{:S(2)}) collective-permute-start(f32[1,32,256]{2,1,0:T(8,128)} %bitcast.61), channel_id=1, source_target_pairs={{0,8},{1,9},{2,10},{3,11},{4,12},{5,13},{6,14},{7,15},{8,0},{9,1},... | collective-permute-start | bytes 98312 | tf_op jit(solution)/shard_map/ppermute | solution.py:18
  4.7 2.5 %collective-permute-done._ = f32[1,32,256]{2,1,0:T(8,128)S(1)} collective-permute-done((f32[1,32,256]{2,1,0:T(8,128)}, f32[1,32,256]{2,1,0:T(8,128)S(1)}, u32[]{:S(2)}, u32[]{:S(2)}) %collective-permute-start) | collective-permute-done | bytes 32800 | tf_op jit(solution)/shard_map/ppermute | solution.py:18
  7.2 0.0 copy-done.3
  7.2 1.6 %collective-permute-start.1 = (bf16[2,32,256]{2,1,0:T(8,128)(2,1)S(1)}, bf16[2,32,256]{2,1,0:T(8,128)(2,1)S(1)}, u32[]{:S(2)}, u32[]{:S(2)}) collective-permute-start(bf16[2,32,256]{2,1,0:T(8,128)(2,1)S(1)} %maximum_bitcast_fusion), channel_id=1, source_target_pairs={{0,4},{1,5},{2,6},{3,7},{4,0},{5,1},{6,2},{7,3},{8,12},{9,13},{10,... | collective-permute-start | bytes 98312 | tf_op jit(solution)/shard_map/ppermute | solution.py:18
  8.8 1.9 %prepare.1 = (f32[4,4,32,512]{3,2,1,0:T(8,128)S(1)}, f32[4,4,32,512]{3,2,1,0:T(8,128)S(1)}, bf16[512,256]{1,0:T(8,128)(2,1)S(1)}) custom-call(s32[4,2,2,32,512]{4,3,2,1,0:T(8,128)} %bitcast.56, s32[1,512]{1,0:T(1,128)} %bitcast.64, s32[1,512]{1,0:T(1,128)} %bitcast.65, f32[512,256]{1,0:T(8,128)} %master.1, f32[1,32,256]{2,1,0:T(8,128)S(1)} %collective-permute-done._), custom_call_target="tpu_custom_call" | custom-call | flops 2097152 | bytes 1048576 | tf_op jit(solution)/shard_map/prepare/pallas_call | solution.py:164
  10.8 0.4 %collective-permute-done.1 = bf16[2,32,256]{2,1,0:T(8,128)(2,1)S(1)} collective-permute-done((bf16[2,32,256]{2,1,0:T(8,128)(2,1)S(1)}, bf16[2,32,256]{2,1,0:T(8,128)(2,1)S(1)}, u32[]{:S(2)}, u32[]{:S(2)}) %collective-permute-start.1) | collective-permute-done | bytes 32800 | tf_op jit(solution)/shard_map/ppermute | solution.py:18
  11.3 1.8 %collective-permute-start.4 = (bf16[128,256]{1,0:T(8,128)(2,1)S(1)}, bf16[128,256]{1,0:T(8,128)(2,1)S(1)}, u32[]{:S(2)}, u32[]{:S(2)}) collective-permute-start(bf16[128,256]{1,0:T(8,128)(2,1)S(1)} %bitcast.51), channel_id=1, source_target_pairs={{0,2},{1,3},{2,0},{3,1},{4,6},{5,7},{6,4},{7,5},{8,10},{9,11},{10,... | collective-permute-start | bytes 196616 | tf_op jit(solution)/shard_map/ppermute | solution.py:18
  13.0 0.0 collective-permute-start.2
  13.0 2.6 %collective-permute-done.4.kept_rows.refs_1_ = bf16[128,256]{1,0:T(8,128)(2,1)S(1)} collective-permute-done((bf16[128,256]{1,0:T(8,128)(2,1)S(1)}, bf16[128,256]{1,0:T(8,128)(2,1)S(1)}, u32[]{:S(2)}, u32[]{:S(2)}) %collective-permute-start.4) | collective-permute-done | bytes 65568 | tf_op jit(solution)/shard_map/ppermute | solution.py:18
  15.6 0.0 collective-permute-start.5
  15.6 0.0 collective-permute-done.2.sent_rows.refs_2_
  15.6 0.6 %slopes.2 = (f32[128,256]{1,0:T(8,128)S(1)}, bf16[128,256]{1,0:T(8,128)(2,1)S(1)}, bf16[2,128,512]{2,1,0:T(8,128)(2,1)S(1)}) custom-call(f32[4,4,32,512]{3,2,1,0:T(8,128)S(1)} %get-tuple-element.20.ratio, f32[4,4,32,512]{3,2,1,0:T(8,128)S(1)} %get-tuple-element.21.weight, bf16[512,256]{1,0:T(8,128)(2,1)S(1)} %get-tuple-element.22.column_copy, ...), custom_call_target="tpu_custom_call" | custom-call | flops 134217728 | tf_op jit(solution)/shard_map/slopes/pallas_call | solution.py:195
  16.2 0.6 %collective-permute-done.5.sent_rows.refs_3_ = bf16[128,256]{1,0:T(8,128)(2,1)S(1)} collective-permute-done((bf16[128,256]{1,0:T(8,128)(2,1)S(1)}, bf16[128,256]{1,0:T(8,128)(2,1)S(1)}, u32[]{:S(2)}, u32[]{:S(2)}) %collective-permute-start.5) | collective-permute-done | bytes 65568 | tf_op jit(solution)/shard_map/ppermute | solution.py:18
  16.8 0.6 %slopes.3 = (f32[128,256]{1,0:T(8,128)S(1)}, bf16[128,256]{1,0:T(8,128)(2,1)S(1)}, bf16[2,128,512]{2,1,0:T(8,128)(2,1)S(1)}) custom-call(f32[4,4,32,512]{3,2,1,0:T(8,128)S(1)} %get-tuple-element.20.ratio, f32[4,4,32,512]{3,2,1,0:T(8,128)S(1)} %get-tuple-element.21.weight, bf16[512,256]{1,0:T(8,128)(2,1)S(1)} %get-tuple-element.22.column_copy, ...), custom_call_target="tpu_custom_call" | custom-call | flops 134217728 | tf_op jit(solution)/shard_map/slopes/pallas_call | solution.py:195
  17.4 0.2 collective-permute-start.6
  17.7 0.4 collective-permute-start.3
  18.0 0.7 %collective-permute-done.6 = bf16[128,256]{1,0:T(8,128)(2,1)S(1)} collective-permute-done((bf16[128,256]{1,0:T(8,128)(2,1)S(1)}, bf16[128,256]{1,0:T(8,128)(2,1)S(1)}, u32[]{:S(2)}, u32[]{:S(2)}) %collective-permute-start.6) | collective-permute-done | bytes 65568 | tf_op jit(solution)/shard_map/ppermute | solution.py:18
  18.8 0.0 copy-start.2
  18.8 1.8 %collective-permute-start.7 = (bf16[128,256]{1,0:T(8,128)(2,1)S(1)}, bf16[128,256]{1,0:T(8,128)(2,1)S(1)}, u32[]{:S(2)}, u32[]{:S(2)}) collective-permute-start(bf16[128,256]{1,0:T(8,128)(2,1)S(1)} %add_convert_fusion.2), channel_id=1, source_target_pairs={{0,2},{1,3},{2,0},{3,1},{4,6},{5,7},{6,4},{7,5},{8,10},{9,11},{10,... | collective-permute-start | bytes 196616 | tf_op jit(solution)/shard_map/ppermute | solution.py:18
  20.5 0.0 copy-done.2
  20.5 0.0 collective-permute-done.3
  20.6 2.6 %collective-permute-done.7 = bf16[128,256]{1,0:T(8,128)(2,1)S(1)} collective-permute-done((bf16[128,256]{1,0:T(8,128)(2,1)S(1)}, bf16[128,256]{1,0:T(8,128)(2,1)S(1)}, u32[]{:S(2)}, u32[]{:S(2)}) %collective-permute-start.7) | collective-permute-done | bytes 65568 | tf_op jit(solution)/shard_map/ppermute | solution.py:18
  23.2 2.7 %collective-permute-start.8 = (bf16[160,256]{1,0:T(8,128)(2,1)S(1)}, bf16[160,256]{1,0:T(8,128)(2,1)S(1)}, u32[]{:S(2)}, u32[]{:S(2)}) collective-permute-start(bf16[160,256]{1,0:T(8,128)(2,1)S(1)} %pad_maximum_fusion.1), channel_id=1, source_target_pairs={{0,8},{1,9},{2,10},{3,11},{4,12},{5,13},{6,14},{7,15},{8,0},{9,1},... | collective-permute-start | bytes 245768 | tf_op jit(solution)/shard_map/ppermute | solution.py:18
  25.8 2.8 %collective-permute-done.8 = bf16[160,256]{1,0:T(8,128)(2,1)S(1)} collective-permute-done((bf16[160,256]{1,0:T(8,128)(2,1)S(1)}, bf16[160,256]{1,0:T(8,128)(2,1)S(1)}, u32[]{:S(2)}, u32[]{:S(2)}) %collective-permute-start.8) | collective-permute-done | bytes 81952 | tf_op jit(solution)/shard_map/ppermute | solution.py:18
  28.7 1.5 %collective-permute-start.9 = (bf16[192,256]{1,0:T(8,128)(2,1)S(1)}, bf16[192,256]{1,0:T(8,128)(2,1)S(1)}, u32[]{:S(2)}, u32[]{:S(2)}) collective-permute-start(bf16[192,256]{1,0:T(8,128)(2,1)S(1)} %pad_maximum_fusion), channel_id=1, source_target_pairs={{0,4},{1,5},{2,6},{3,7},{4,0},{5,1},{6,2},{7,3},{8,12},{9,13},{10,... | collective-permute-start | bytes 294920 | tf_op jit(solution)/shard_map/ppermute | solution.py:18
  30.2 3.2 %collective-permute-done.9 = bf16[192,256]{1,0:T(8,128)(2,1)S(1)} collective-permute-done((bf16[192,256]{1,0:T(8,128)(2,1)S(1)}, bf16[192,256]{1,0:T(8,128)(2,1)S(1)}, u32[]{:S(2)}, u32[]{:S(2)}) %collective-permute-start.9) | collective-permute-done | bytes 98336 | tf_op jit(solution)/shard_map/ppermute | solution.py:18
  33.4 0.0 copy-start.1
  33.5 0.0 copy-start
  33.6 1.7 %collective-permute-start.10 = (bf16[4,32,256]{2,1,0:T(8,128)(2,1)S(1)}, bf16[4,32,256]{2,1,0:T(8,128)(2,1)S(1)}, u32[]{:S(2)}, u32[]{:S(2)}) collective-permute-start(bf16[4,32,256]{2,1,0:T(8,128)(2,1)S(1)} %fusion.3.refs_0_), channel_id=1, source_target_pairs={{0,2},{1,3},{2,0},{3,1},{4,6},{5,7},{6,4},{7,5},{8,10},{9,11},{10,... | collective-permute-start | bytes 196616 | tf_op jit(solution)/shard_map/ppermute | solution.py:18
  35.2 0.0 copy-done.1
  35.2 0.0 copy-done
  35.2 1.4 %columns.3 = (f32[512,256]{1,0:T(8,128)}, f32[512,256]{1,0:T(8,128)}) custom-call(bf16[2,128,512]{2,1,0:T(8,128)(2,1)S(1)} %get-tuple-element.25.refs_0_.early, bf16[2,128,512]{2,1,0:T(8,128)(2,1)S(1)} %get-tuple-element.28.late, f32[512,256]{1,0:T(8,128)S(1)} %copy-done, f32[512,256]{1,0:T(8,128)S(1)} %copy-done.1, bf16[128,256]{1,0:T(8,128)(2,1)S(1)} %bitcast.55, ...), custom_call_target="tpu_custom_call" | custom-call | flops 134217728 | bytes 2097152 | tf_op jit(solution)/shard_map/columns/pallas_call | solution.py:223
  36.7 0.0 collective-permute-start.11
  36.7 1.2 %collective-permute-done.10.refs_1_ = bf16[4,32,256]{2,1,0:T(8,128)(2,1)S(1)} collective-permute-done((bf16[4,32,256]{2,1,0:T(8,128)(2,1)S(1)}, bf16[4,32,256]{2,1,0:T(8,128)(2,1)S(1)}, u32[]{:S(2)}, u32[]{:S(2)}) %collective-permute-start.10) | collective-permute-done | bytes 65568 | tf_op jit(solution)/shard_map/ppermute | solution.py:18
  37.9 0.0 collective-permute-start.12
  37.9 0.6 %fusion.6 = (f32[32,256]{1,0:T(8,128)}, f32[32,256]{1,0:T(8,128)}) fusion(f32[32,256]{1,0:T(8,128)S(1)} %copy-done.3, f32[4,32,256]{2,1,0:T(8,128)S(1)} %bitcast.58, s32[]{:T(128)S(6)} %select_n.78, f32[32,256]{1,0:T(8,128)S(1)} %copy-done.2), kind=kLoop, calls=%fused_computation.19 | loop fusion | flops 40960 | bytes 163844 | tf_op jit(solution)/shard_map/sub | solution.py:236
  38.5 0.0 collective-permute-done.11.refs_2_
  38.5 0.6 %collective-permute-done.12.refs_3_ = bf16[4,32,256]{2,1,0:T(8,128)(2,1)S(1)} collective-permute-done((bf16[4,32,256]{2,1,0:T(8,128)(2,1)S(1)}, bf16[4,32,256]{2,1,0:T(8,128)(2,1)S(1)}, u32[]{:S(2)}, u32[]{:S(2)}) %collective-permute-start.12) | collective-permute-done | bytes 65568 | tf_op jit(solution)/shard_map/ppermute | solution.py:18
  39.1 0.7 %place.1 = bf16[4,2,2,32,256]{4,3,2,1,0:T(8,128)(2,1)} custom-call(bf16[4,32,256]{2,1,0:T(8,128)(2,1)S(1)} %fusion.3.refs_0_, bf16[4,32,256]{2,1,0:T(8,128)(2,1)S(1)} %collective-permute-done.10.refs_1_, bf16[4,32,256]{2,1,0:T(8,128)(2,1)S(1)} %collective-permute-done.11.refs_2_, bf16[4,32,256]{2,1,0:T(8,128)(2,1)S(1)} %collective-permute-done.12.refs_3_), custom_call_target="tpu_custom_call" | custom-call | tf_op jit(solution)/shard_map/place/pallas_call | solution.py:243
  (19 shorter events, 0.2 us)
Async XLA Ops:
  0.6 6.6 %copy-start.3 = (f32[32,256]{1,0:T(8,128)S(1)}, f32[32,256]{1,0:T(8,128)}, u32[]{:S(2)}) copy-start(f32[32,256]{1,0:T(8,128)} %param.10) | copy-start | bytes 98308
  0.6 6.6 %collective-permute-start = (f32[1,32,256]{2,1,0:T(8,128)}, f32[1,32,256]{2,1,0:T(8,128)S(1)}, u32[]{:S(2)}, u32[]{:S(2)}) collective-permute-start(f32[1,32,256]{2,1,0:T(8,128)} %bitcast.61), channel_id=1, source_target_pairs={{0,8},{1,9},{2,10},{3,11},{4,12},{5,13},{6,14},{7,15},{8,0},{9,1},... | collective-permute-start | bytes 98312 | tf_op jit(solution)/shard_map/ppermute | solution.py:18
  7.2 4.0 %collective-permute-start.1 = (bf16[2,32,256]{2,1,0:T(8,128)(2,1)S(1)}, bf16[2,32,256]{2,1,0:T(8,128)(2,1)S(1)}, u32[]{:S(2)}, u32[]{:S(2)}) collective-permute-start(bf16[2,32,256]{2,1,0:T(8,128)(2,1)S(1)} %maximum_bitcast_fusion), channel_id=1, source_target_pairs={{0,4},{1,5},{2,6},{3,7},{4,0},{5,1},{6,2},{7,3},{8,12},{9,13},{10,... | collective-permute-start | bytes 98312 | tf_op jit(solution)/shard_map/ppermute | solution.py:18
  11.3 4.3 %collective-permute-start.4 = (bf16[128,256]{1,0:T(8,128)(2,1)S(1)}, bf16[128,256]{1,0:T(8,128)(2,1)S(1)}, u32[]{:S(2)}, u32[]{:S(2)}) collective-permute-start(bf16[128,256]{1,0:T(8,128)(2,1)S(1)} %bitcast.51), channel_id=1, source_target_pairs={{0,2},{1,3},{2,0},{3,1},{4,6},{5,7},{6,4},{7,5},{8,10},{9,11},{10,... | collective-permute-start | bytes 196616 | tf_op jit(solution)/shard_map/ppermute | solution.py:18
  13.0 2.6 %collective-permute-start.2 = (bf16[128,256]{1,0:T(8,128)(2,1)S(1)}, bf16[128,256]{1,0:T(8,128)(2,1)S(1)}, u32[]{:S(2)}, u32[]{:S(2)}) collective-permute-start(bf16[128,256]{1,0:T(8,128)(2,1)S(1)} %bitcast.52), channel_id=1, source_target_pairs={{0,1},{1,0},{2,3},{3,2},{4,5},{5,4},{6,7},{7,6},{8,9},{9,8},{10,11... | collective-permute-start | bytes 196616 | tf_op jit(solution)/shard_map/ppermute | solution.py:18
  15.6 1.3 %collective-permute-start.5 = (bf16[128,256]{1,0:T(8,128)(2,1)S(1)}, bf16[128,256]{1,0:T(8,128)(2,1)S(1)}, u32[]{:S(2)}, u32[]{:S(2)}) collective-permute-start(bf16[128,256]{1,0:T(8,128)(2,1)S(1)} %collective-permute-done.4.kept_rows.refs_1_), channel_id=1, source_target_pairs={{0,1},{1,0},{2,3},{3,2},{4,5},{5,4},{6,7},{7,6},{8,9},{9,8},{10,11... | collective-permute-start | bytes 196616 | tf_op jit(solution)/shard_map/ppermute | solution.py:18
  17.4 1.3 %collective-permute-start.6 = (bf16[128,256]{1,0:T(8,128)(2,1)S(1)}, bf16[128,256]{1,0:T(8,128)(2,1)S(1)}, u32[]{:S(2)}, u32[]{:S(2)}) collective-permute-start(bf16[128,256]{1,0:T(8,128)(2,1)S(1)} %get-tuple-element.27), channel_id=1, source_target_pairs={{0,1},{1,0},{2,3},{3,2},{4,5},{5,4},{6,7},{7,6},{8,9},{9,8},{10,11... | collective-permute-start | bytes 196616 | tf_op jit(solution)/shard_map/ppermute | solution.py:18
  17.7 2.9 %collective-permute-start.3 = (bf16[128,256]{1,0:T(8,128)(2,1)S(1)}, bf16[128,256]{1,0:T(8,128)(2,1)S(1)}, u32[]{:S(2)}, u32[]{:S(2)}) collective-permute-start(bf16[128,256]{1,0:T(8,128)(2,1)S(1)} %get-tuple-element.24), channel_id=1, source_target_pairs={{0,1},{1,0},{2,3},{3,2},{4,5},{5,4},{6,7},{7,6},{8,9},{9,8},{10,11... | collective-permute-start | bytes 196616 | tf_op jit(solution)/shard_map/ppermute | solution.py:18
  18.8 1.8 %copy-start.2 = (f32[32,256]{1,0:T(8,128)S(1)}, f32[32,256]{1,0:T(8,128)}, u32[]{:S(2)}) copy-start(f32[32,256]{1,0:T(8,128)} %param.11) | copy-start | bytes 98308
  18.8 4.3 %collective-permute-start.7 = (bf16[128,256]{1,0:T(8,128)(2,1)S(1)}, bf16[128,256]{1,0:T(8,128)(2,1)S(1)}, u32[]{:S(2)}, u32[]{:S(2)}) collective-permute-start(bf16[128,256]{1,0:T(8,128)(2,1)S(1)} %add_convert_fusion.2), channel_id=1, source_target_pairs={{0,2},{1,3},{2,0},{3,1},{4,6},{5,7},{6,4},{7,5},{8,10},{9,11},{10,... | collective-permute-start | bytes 196616 | tf_op jit(solution)/shard_map/ppermute | solution.py:18
  23.2 5.5 %collective-permute-start.8 = (bf16[160,256]{1,0:T(8,128)(2,1)S(1)}, bf16[160,256]{1,0:T(8,128)(2,1)S(1)}, u32[]{:S(2)}, u32[]{:S(2)}) collective-permute-start(bf16[160,256]{1,0:T(8,128)(2,1)S(1)} %pad_maximum_fusion.1), channel_id=1, source_target_pairs={{0,8},{1,9},{2,10},{3,11},{4,12},{5,13},{6,14},{7,15},{8,0},{9,1},... | collective-permute-start | bytes 245768 | tf_op jit(solution)/shard_map/ppermute | solution.py:18
  28.7 4.7 %collective-permute-start.9 = (bf16[192,256]{1,0:T(8,128)(2,1)S(1)}, bf16[192,256]{1,0:T(8,128)(2,1)S(1)}, u32[]{:S(2)}, u32[]{:S(2)}) collective-permute-start(bf16[192,256]{1,0:T(8,128)(2,1)S(1)} %pad_maximum_fusion), channel_id=1, source_target_pairs={{0,4},{1,5},{2,6},{3,7},{4,0},{5,1},{6,2},{7,3},{8,12},{9,13},{10,... | collective-permute-start | bytes 294920 | tf_op jit(solution)/shard_map/ppermute | solution.py:18
  33.4 1.8 %copy-start.1 = (f32[512,256]{1,0:T(8,128)S(1)}, f32[512,256]{1,0:T(8,128)}, u32[]{:S(2)}) copy-start(f32[512,256]{1,0:T(8,128)} %history.1) | copy-start | bytes 1572868
  33.5 1.8 %copy-start = (f32[512,256]{1,0:T(8,128)S(1)}, f32[512,256]{1,0:T(8,128)}, u32[]{:S(2)}) copy-start(f32[512,256]{1,0:T(8,128)} %master.1) | copy-start | bytes 1572868
  33.6 4.3 %collective-permute-start.10 = (bf16[4,32,256]{2,1,0:T(8,128)(2,1)S(1)}, bf16[4,32,256]{2,1,0:T(8,128)(2,1)S(1)}, u32[]{:S(2)}, u32[]{:S(2)}) collective-permute-start(bf16[4,32,256]{2,1,0:T(8,128)(2,1)S(1)} %fusion.3.refs_0_), channel_id=1, source_target_pairs={{0,2},{1,3},{2,0},{3,1},{4,6},{5,7},{6,4},{7,5},{8,10},{9,11},{10,... | collective-permute-start | bytes 196616 | tf_op jit(solution)/shard_map/ppermute | solution.py:18
  36.7 1.8 %collective-permute-start.11 = (bf16[4,32,256]{2,1,0:T(8,128)(2,1)S(1)}, bf16[4,32,256]{2,1,0:T(8,128)(2,1)S(1)}, u32[]{:S(2)}, u32[]{:S(2)}) collective-permute-start(bf16[4,32,256]{2,1,0:T(8,128)(2,1)S(1)} %fusion.3.refs_0_), channel_id=1, source_target_pairs={{0,1},{1,0},{2,3},{3,2},{4,5},{5,4},{6,7},{7,6},{8,9},{9,8},{10,11... | collective-permute-start | bytes 196616 | tf_op jit(solution)/shard_map/ppermute | solution.py:18
  37.9 1.3 %collective-permute-start.12 = (bf16[4,32,256]{2,1,0:T(8,128)(2,1)S(1)}, bf16[4,32,256]{2,1,0:T(8,128)(2,1)S(1)}, u32[]{:S(2)}, u32[]{:S(2)}) collective-permute-start(bf16[4,32,256]{2,1,0:T(8,128)(2,1)S(1)} %collective-permute-done.10.refs_1_), channel_id=1, source_target_pairs={{0,1},{1,0},{2,3},{3,2},{4,5},{5,4},{6,7},{7,6},{8,9},{9,8},{10,11... | collective-permute-start | bytes 196616 | tf_op jit(solution)/shard_map/ppermute | solution.py:18

commit v4 on v3

--- a/solution.py
+++ b/solution.py
@@ -15,7 +15,13 @@
 
 
 def hop(value, bit, size):
-    return lax.ppermute(value, "col", [(i, i ^ bit) for i in range(size)])
+    return lax.ppermute(value, "col", [(i, i ^ (bit | 1)) for i in range(size)])
+
+
+def parity(value):
+    for shift in (8, 4, 2, 1):
+        value = value ^ (value >> shift)
+    return value & 1
 
 
 def near(value):
@@ -26,8 +32,10 @@
     return pltpu.with_memory_space_constraint(value, pltpu.HBM)
 
 
-def place_at(me, place):
-    return lax.rem(lax.div(me, 2) + place % 2, 2), lax.rem(me + place // 2, 2)
+def place_at(place, z):
+    me = lax.axis_index("col")
+    at_x = ((me >> 1) + place) & 1
+    return at_x, (parity(me) + (place >> 1) + at_x + parity(z)) & 1
 
 
 def steps_of(count, body):
@@ -39,7 +47,6 @@
 
 def prepare_kernel(counts, row_totals, column_totals, columns, _, ratio, weight, column_copy, *scratch):
     near_counts, near_rows, near_columns, near_copy, row_terms, sems = scratch
-    me = lax.axis_index("col")
     groups, own = counts.shape[0], counts.shape[3]
     copies = [
         pltpu.make_async_copy(row_totals, near_rows, sems.at[0]),
@@ -57,9 +64,9 @@
     column_term = jnp.log(near_columns[...].astype(jnp.float32))
     copies[2].wait()
     for place in range(4):
-        at_x, at_core = place_at(me, place)
-
-        def body(z, place=place, at_x=at_x, at_core=at_core):
+
+        def body(z, place=place):
+            at_x, at_core = place_at(place, z)
             amounts = near_counts[z, at_x, at_core].astype(jnp.float32)
             term = row_terms[z, at_x, at_core]
             term = jnp.concatenate([term] * (amounts.shape[1] // 128), axis=1)
@@ -128,10 +135,9 @@
 
 def place_kernel(*refs):
     pieces, out = refs[:4], refs[4]
-    me = lax.axis_index("col")
     for place in range(4):
-        at_x, at_core = place_at(me, place)
         for z in range(out.shape[0]):
+            at_x, at_core = place_at(place, z)
             out[z, at_x, at_core] = pieces[place][z]
 
 

time: 40.1 us -> 39.7 us (0.990)
  waiting for transfers between devices: 17.2 us -> 14.6 us
  starting transfers between devices: 15.7 us -> 17.6 us
    ppermute x13, waiting for transfers between devices: 17.2 us -> 14.6 us  [hop(): return lax.ppermute(value, 'col', [(i, i ^ (bit | 1)) for i in range(size)])]
    ppermute x13, starting transfers between devices: 15.7 us -> 17.6 us  [hop(): return lax.ppermute(value, 'col', [(i, i ^ (bit | 1)) for i in range(size)])]
  transfers between devices with their start and end apart: 13 -> 13, of which waited for: 10 -> 9; matrix products, arithmetic and copies ran while one was open for 2% -> 2% of each run, Pallas kernels for 10% -> 10%
where the time goes in v4:
time: 39.7 us; the launch traced here: 39.1 us
  starting transfers between devices  17.6 us (44%)
  waiting for transfers between devices  14.6 us (37%)
  Pallas kernels  5.24 us (13%)
  other arithmetic  0.85 us (2%)
  between operations  0.8 us (2%)
    ppermute x13, starting transfers between devices, hop(): return lax.ppermute(value, 'col', [(i, i ^ (bit | 1)) for i in range(size)])  17.6 us
    ppermute x13, waiting for transfers between devices, hop(): return lax.ppermute(value, 'col', [(i, i ^ (bit | 1)) for i in range(size)])  14.6 us
    pallas_call x1, Pallas kernels, per_device(): pl.pallas_call(prepare_kernel, out_shape=(ratio_type, ratio_type, pltpu.V...  1.9 us
    pallas_call x1, Pallas kernels, per_device(): pl.pallas_call(functools.partial(columns_kernel, total_rows, chunk), out_...  1.44 us
    pallas_call x2, Pallas kernels, slopes_of(): pl.pallas_call(functools.partial(slopes_kernel, chunk, places), out_shape...  1.18 us
  transfers between devices with their start and end apart: 13, of which 9 were waited for; matrix products, arithmetic and copies ran while one was open for 2% of the time, Pallas kernels for 10%

profile of v4, /device:TPU:0, one launch (start us, length us, event | category | flops | bytes accessed | tf_op | source)
XLA Modules:
  0.0 39.1 jit_solution(13278483862346432362)
XLA Ops:
  0.6 0.0 copy-start.3
  0.6 3.5 %collective-permute-start = (f32[1,32,256]{2,1,0:T(8,128)}, f32[1,32,256]{2,1,0:T(8,128)S(1)}, u32[]{:S(2)}, u32[]{:S(2)}) collective-permute-start(f32[1,32,256]{2,1,0:T(8,128)} %bitcast.61), channel_id=1, source_target_pairs={{0,9},{1,8},{2,11},{3,10},{4,13},{5,12},{6,15},{7,14},{8,1},{9,0},... | collective-permute-start | bytes 98312 | tf_op jit(solution)/shard_map/ppermute | solution.py:18
  4.2 2.1 %collective-permute-done._ = f32[1,32,256]{2,1,0:T(8,128)S(1)} collective-permute-done((f32[1,32,256]{2,1,0:T(8,128)}, f32[1,32,256]{2,1,0:T(8,128)S(1)}, u32[]{:S(2)}, u32[]{:S(2)}) %collective-permute-start) | collective-permute-done | bytes 32800 | tf_op jit(solution)/shard_map/ppermute | solution.py:18
  6.3 0.0 copy-done.3
  6.3 1.8 %collective-permute-start.1 = (bf16[2,32,256]{2,1,0:T(8,128)(2,1)S(1)}, bf16[2,32,256]{2,1,0:T(8,128)(2,1)S(1)}, u32[]{:S(2)}, u32[]{:S(2)}) collective-permute-start(bf16[2,32,256]{2,1,0:T(8,128)(2,1)S(1)} %maximum_bitcast_fusion), channel_id=1, source_target_pairs={{0,5},{1,4},{2,7},{3,6},{4,1},{5,0},{6,3},{7,2},{8,13},{9,12},{10,... | collective-permute-start | bytes 98312 | tf_op jit(solution)/shard_map/ppermute | solution.py:18
  8.1 1.9 %prepare.1 = (f32[4,4,32,512]{3,2,1,0:T(8,128)S(1)}, f32[4,4,32,512]{3,2,1,0:T(8,128)S(1)}, bf16[512,256]{1,0:T(8,128)(2,1)S(1)}) custom-call(s32[4,2,2,32,512]{4,3,2,1,0:T(8,128)} %bitcast.56, s32[1,512]{1,0:T(1,128)} %bitcast.64, s32[1,512]{1,0:T(1,128)} %bitcast.65, f32[512,256]{1,0:T(8,128)} %master.1, f32[1,32,256]{2,1,0:T(8,128)S(1)} %collective-permute-done._), custom_call_target="tpu_custom_call" | custom-call | flops 2097152 | bytes 1048576 | tf_op jit(solution)/shard_map/prepare/pallas_call | solution.py:170
  10.0 0.0 collective-permute-done.1
  10.1 1.5 %collective-permute-start.4 = (bf16[128,256]{1,0:T(8,128)(2,1)S(1)}, bf16[128,256]{1,0:T(8,128)(2,1)S(1)}, u32[]{:S(2)}, u32[]{:S(2)}) collective-permute-start(bf16[128,256]{1,0:T(8,128)(2,1)S(1)} %bitcast.51), channel_id=1, source_target_pairs={{0,3},{1,2},{2,1},{3,0},{4,7},{5,6},{6,5},{7,4},{8,11},{9,10},{10,... | collective-permute-start | bytes 196616 | tf_op jit(solution)/shard_map/ppermute | solution.py:18
  11.6 0.3 collective-permute-start.2
  11.9 2.2 %collective-permute-done.4.kept_rows.refs_1_ = bf16[128,256]{1,0:T(8,128)(2,1)S(1)} collective-permute-done((bf16[128,256]{1,0:T(8,128)(2,1)S(1)}, bf16[128,256]{1,0:T(8,128)(2,1)S(1)}, u32[]{:S(2)}, u32[]{:S(2)}) %collective-permute-start.4) | collective-permute-done | bytes 65568 | tf_op jit(solution)/shard_map/ppermute | solution.py:18
  14.1 0.3 collective-permute-start.5
  14.4 0.0 collective-permute-done.2.sent_rows.refs_2_
  14.4 0.6 %slopes.2 = (f32[128,256]{1,0:T(8,128)S(1)}, bf16[128,256]{1,0:T(8,128)(2,1)S(1)}, bf16[2,128,512]{2,1,0:T(8,128)(2,1)S(1)}) custom-call(f32[4,4,32,512]{3,2,1,0:T(8,128)S(1)} %get-tuple-element.20.ratio, f32[4,4,32,512]{3,2,1,0:T(8,128)S(1)} %get-tuple-element.21.weight, bf16[512,256]{1,0:T(8,128)(2,1)S(1)} %get-tuple-element.22.column_copy, ...), custom_call_target="tpu_custom_call" | custom-call | flops 134217728 | tf_op jit(solution)/shard_map/slopes/pallas_call | solution.py:201
  15.0 0.4 collective-permute-done.5.sent_rows.refs_3_
  15.3 0.6 %slopes.3 = (f32[128,256]{1,0:T(8,128)S(1)}, bf16[128,256]{1,0:T(8,128)(2,1)S(1)}, bf16[2,128,512]{2,1,0:T(8,128)(2,1)S(1)}) custom-call(f32[4,4,32,512]{3,2,1,0:T(8,128)S(1)} %get-tuple-element.20.ratio, f32[4,4,32,512]{3,2,1,0:T(8,128)S(1)} %get-tuple-element.21.weight, bf16[512,256]{1,0:T(8,128)(2,1)S(1)} %get-tuple-element.22.column_copy, ...), custom_call_target="tpu_custom_call" | custom-call | flops 134217728 | tf_op jit(solution)/shard_map/slopes/pallas_call | solution.py:201
  15.9 0.4 collective-permute-start.6
  16.3 0.2 collective-permute-start.3
  16.5 0.7 %collective-permute-done.6 = bf16[128,256]{1,0:T(8,128)(2,1)S(1)} collective-permute-done((bf16[128,256]{1,0:T(8,128)(2,1)S(1)}, bf16[128,256]{1,0:T(8,128)(2,1)S(1)}, u32[]{:S(2)}, u32[]{:S(2)}) %collective-permute-start.6) | collective-permute-done | bytes 65568 | tf_op jit(solution)/shard_map/ppermute | solution.py:18
  17.3 0.0 copy-start.2
  17.3 1.6 %collective-permute-start.7 = (bf16[128,256]{1,0:T(8,128)(2,1)S(1)}, bf16[128,256]{1,0:T(8,128)(2,1)S(1)}, u32[]{:S(2)}, u32[]{:S(2)}) collective-permute-start(bf16[128,256]{1,0:T(8,128)(2,1)S(1)} %add_convert_fusion.2), channel_id=1, source_target_pairs={{0,3},{1,2},{2,1},{3,0},{4,7},{5,6},{6,5},{7,4},{8,11},{9,10},{10,... | collective-permute-start | bytes 196616 | tf_op jit(solution)/shard_map/ppermute | solution.py:18
  18.9 0.0 copy-done.2
  18.9 0.0 collective-permute-done.3
  18.9 2.4 %collective-permute-done.7 = bf16[128,256]{1,0:T(8,128)(2,1)S(1)} collective-permute-done((bf16[128,256]{1,0:T(8,128)(2,1)S(1)}, bf16[128,256]{1,0:T(8,128)(2,1)S(1)}, u32[]{:S(2)}, u32[]{:S(2)}) %collective-permute-start.7) | collective-permute-done | bytes 65568 | tf_op jit(solution)/shard_map/ppermute | solution.py:18
  21.4 3.2 %collective-permute-start.8 = (bf16[160,256]{1,0:T(8,128)(2,1)S(1)}, bf16[160,256]{1,0:T(8,128)(2,1)S(1)}, u32[]{:S(2)}, u32[]{:S(2)}) collective-permute-start(bf16[160,256]{1,0:T(8,128)(2,1)S(1)} %pad_maximum_fusion.1), channel_id=1, source_target_pairs={{0,9},{1,8},{2,11},{3,10},{4,13},{5,12},{6,15},{7,14},{8,1},{9,0},... | collective-permute-start | bytes 245768 | tf_op jit(solution)/shard_map/ppermute | solution.py:18
  24.6 2.7 %collective-permute-done.8 = bf16[160,256]{1,0:T(8,128)(2,1)S(1)} collective-permute-done((bf16[160,256]{1,0:T(8,128)(2,1)S(1)}, bf16[160,256]{1,0:T(8,128)(2,1)S(1)}, u32[]{:S(2)}, u32[]{:S(2)}) %collective-permute-start.8) | collective-permute-done | bytes 81952 | tf_op jit(solution)/shard_map/ppermute | solution.py:18
  27.3 2.7 %collective-permute-start.9 = (bf16[192,256]{1,0:T(8,128)(2,1)S(1)}, bf16[192,256]{1,0:T(8,128)(2,1)S(1)}, u32[]{:S(2)}, u32[]{:S(2)}) collective-permute-start(bf16[192,256]{1,0:T(8,128)(2,1)S(1)} %pad_maximum_fusion), channel_id=1, source_target_pairs={{0,5},{1,4},{2,7},{3,6},{4,1},{5,0},{6,3},{7,2},{8,13},{9,12},{10,... | collective-permute-start | bytes 294920 | tf_op jit(solution)/shard_map/ppermute | solution.py:18
  30.0 3.0 %collective-permute-done.9 = bf16[192,256]{1,0:T(8,128)(2,1)S(1)} collective-permute-done((bf16[192,256]{1,0:T(8,128)(2,1)S(1)}, bf16[192,256]{1,0:T(8,128)(2,1)S(1)}, u32[]{:S(2)}, u32[]{:S(2)}) %collective-permute-start.9) | collective-permute-done | bytes 98336 | tf_op jit(solution)/shard_map/ppermute | solution.py:18
  33.0 0.0 copy-start.1
  33.0 0.0 copy-start
  33.1 1.6 %collective-permute-start.10 = (bf16[4,32,256]{2,1,0:T(8,128)(2,1)S(1)}, bf16[4,32,256]{2,1,0:T(8,128)(2,1)S(1)}, u32[]{:S(2)}, u32[]{:S(2)}) collective-permute-start(bf16[4,32,256]{2,1,0:T(8,128)(2,1)S(1)} %fusion.3.refs_0_), channel_id=1, source_target_pairs={{0,3},{1,2},{2,1},{3,0},{4,7},{5,6},{6,5},{7,4},{8,11},{9,10},{10,... | collective-permute-start | bytes 196616 | tf_op jit(solution)/shard_map/ppermute | solution.py:18
  34.7 0.0 copy-done.1
  34.7 0.0 copy-done
  34.7 1.4 %columns.3 = (f32[512,256]{1,0:T(8,128)}, f32[512,256]{1,0:T(8,128)}) custom-call(bf16[2,128,512]{2,1,0:T(8,128)(2,1)S(1)} %get-tuple-element.25.refs_0_.early, bf16[2,128,512]{2,1,0:T(8,128)(2,1)S(1)} %get-tuple-element.28.late, f32[512,256]{1,0:T(8,128)S(1)} %copy-done, f32[512,256]{1,0:T(8,128)S(1)} %copy-done.1, bf16[128,256]{1,0:T(8,128)(2,1)S(1)} %bitcast.55, ...), custom_call_target="tpu_custom_call" | custom-call | flops 134217728 | bytes 2097152 | tf_op jit(solution)/shard_map/columns/pallas_call | solution.py:229
  36.1 0.1 collective-permute-start.11
  36.3 0.9 %collective-permute-done.10.refs_1_ = bf16[4,32,256]{2,1,0:T(8,128)(2,1)S(1)} collective-permute-done((bf16[4,32,256]{2,1,0:T(8,128)(2,1)S(1)}, bf16[4,32,256]{2,1,0:T(8,128)(2,1)S(1)}, u32[]{:S(2)}, u32[]{:S(2)}) %collective-permute-start.10) | collective-permute-done | bytes 65568 | tf_op jit(solution)/shard_map/ppermute | solution.py:18
  37.1 0.3 collective-permute-start.12
  37.4 0.6 %fusion.6 = (f32[32,256]{1,0:T(8,128)}, f32[32,256]{1,0:T(8,128)}) fusion(f32[32,256]{1,0:T(8,128)S(1)} %copy-done.3, f32[4,32,256]{2,1,0:T(8,128)S(1)} %bitcast.58, s32[]{:T(128)S(6)} %select_n.78, f32[32,256]{1,0:T(8,128)S(1)} %copy-done.2), kind=kLoop, calls=%fused_computation.19 | loop fusion | flops 40960 | bytes 163844 | tf_op jit(solution)/shard_map/sub | solution.py:242
  38.1 0.0 collective-permute-done.11.refs_2_
  38.1 0.3 collective-permute-done.12.refs_3_
  38.4 0.7 %place.1 = bf16[4,2,2,32,256]{4,3,2,1,0:T(8,128)(2,1)} custom-call(bf16[4,32,256]{2,1,0:T(8,128)(2,1)S(1)} %fusion.3.refs_0_, bf16[4,32,256]{2,1,0:T(8,128)(2,1)S(1)} %collective-permute-done.10.refs_1_, bf16[4,32,256]{2,1,0:T(8,128)(2,1)S(1)} %collective-permute-done.11.refs_2_, bf16[4,32,256]{2,1,0:T(8,128)(2,1)S(1)} %collective-permute-done.12.refs_3_), custom_call_target="tpu_custom_call" | custom-call | tf_op jit(solution)/shard_map/place/pallas_call | solution.py:249
  (19 shorter events, 0.2 us)
Async XLA Ops:
  0.6 5.6 %copy-start.3 = (f32[32,256]{1,0:T(8,128)S(1)}, f32[32,256]{1,0:T(8,128)}, u32[]{:S(2)}) copy-start(f32[32,256]{1,0:T(8,128)} %param.10) | copy-start | bytes 98308
  0.6 5.6 %collective-permute-start = (f32[1,32,256]{2,1,0:T(8,128)}, f32[1,32,256]{2,1,0:T(8,128)S(1)}, u32[]{:S(2)}, u32[]{:S(2)}) collective-permute-start(f32[1,32,256]{2,1,0:T(8,128)} %bitcast.61), channel_id=1, source_target_pairs={{0,9},{1,8},{2,11},{3,10},{4,13},{5,12},{6,15},{7,14},{8,1},{9,0},... | collective-permute-start | bytes 98312 | tf_op jit(solution)/shard_map/ppermute | solution.py:18
  6.3 3.7 %collective-permute-start.1 = (bf16[2,32,256]{2,1,0:T(8,128)(2,1)S(1)}, bf16[2,32,256]{2,1,0:T(8,128)(2,1)S(1)}, u32[]{:S(2)}, u32[]{:S(2)}) collective-permute-start(bf16[2,32,256]{2,1,0:T(8,128)(2,1)S(1)} %maximum_bitcast_fusion), channel_id=1, source_target_pairs={{0,5},{1,4},{2,7},{3,6},{4,1},{5,0},{6,3},{7,2},{8,13},{9,12},{10,... | collective-permute-start | bytes 98312 | tf_op jit(solution)/shard_map/ppermute | solution.py:18
  10.1 4.0 %collective-permute-start.4 = (bf16[128,256]{1,0:T(8,128)(2,1)S(1)}, bf16[128,256]{1,0:T(8,128)(2,1)S(1)}, u32[]{:S(2)}, u32[]{:S(2)}) collective-permute-start(bf16[128,256]{1,0:T(8,128)(2,1)S(1)} %bitcast.51), channel_id=1, source_target_pairs={{0,3},{1,2},{2,1},{3,0},{4,7},{5,6},{6,5},{7,4},{8,11},{9,10},{10,... | collective-permute-start | bytes 196616 | tf_op jit(solution)/shard_map/ppermute | solution.py:18
  11.6 2.8 %collective-permute-start.2 = (bf16[128,256]{1,0:T(8,128)(2,1)S(1)}, bf16[128,256]{1,0:T(8,128)(2,1)S(1)}, u32[]{:S(2)}, u32[]{:S(2)}) collective-permute-start(bf16[128,256]{1,0:T(8,128)(2,1)S(1)} %bitcast.52), channel_id=1, source_target_pairs={{0,1},{1,0},{2,3},{3,2},{4,5},{5,4},{6,7},{7,6},{8,9},{9,8},{10,11... | collective-permute-start | bytes 196616 | tf_op jit(solution)/shard_map/ppermute | solution.py:18
  14.1 1.3 %collective-permute-start.5 = (bf16[128,256]{1,0:T(8,128)(2,1)S(1)}, bf16[128,256]{1,0:T(8,128)(2,1)S(1)}, u32[]{:S(2)}, u32[]{:S(2)}) collective-permute-start(bf16[128,256]{1,0:T(8,128)(2,1)S(1)} %collective-permute-done.4.kept_rows.refs_1_), channel_id=1, source_target_pairs={{0,1},{1,0},{2,3},{3,2},{4,5},{5,4},{6,7},{7,6},{8,9},{9,8},{10,11... | collective-permute-start | bytes 196616 | tf_op jit(solution)/shard_map/ppermute | solution.py:18
  15.9 1.3 %collective-permute-start.6 = (bf16[128,256]{1,0:T(8,128)(2,1)S(1)}, bf16[128,256]{1,0:T(8,128)(2,1)S(1)}, u32[]{:S(2)}, u32[]{:S(2)}) collective-permute-start(bf16[128,256]{1,0:T(8,128)(2,1)S(1)} %get-tuple-element.27), channel_id=1, source_target_pairs={{0,1},{1,0},{2,3},{3,2},{4,5},{5,4},{6,7},{7,6},{8,9},{9,8},{10,11... | collective-permute-start | bytes 196616 | tf_op jit(solution)/shard_map/ppermute | solution.py:18
  16.3 2.6 %collective-permute-start.3 = (bf16[128,256]{1,0:T(8,128)(2,1)S(1)}, bf16[128,256]{1,0:T(8,128)(2,1)S(1)}, u32[]{:S(2)}, u32[]{:S(2)}) collective-permute-start(bf16[128,256]{1,0:T(8,128)(2,1)S(1)} %get-tuple-element.24), channel_id=1, source_target_pairs={{0,1},{1,0},{2,3},{3,2},{4,5},{5,4},{6,7},{7,6},{8,9},{9,8},{10,11... | collective-permute-start | bytes 196616 | tf_op jit(solution)/shard_map/ppermute | solution.py:18
  17.3 1.6 %copy-start.2 = (f32[32,256]{1,0:T(8,128)S(1)}, f32[32,256]{1,0:T(8,128)}, u32[]{:S(2)}) copy-start(f32[32,256]{1,0:T(8,128)} %param.11) | copy-start | bytes 98308
  17.3 4.1 %collective-permute-start.7 = (bf16[128,256]{1,0:T(8,128)(2,1)S(1)}, bf16[128,256]{1,0:T(8,128)(2,1)S(1)}, u32[]{:S(2)}, u32[]{:S(2)}) collective-permute-start(bf16[128,256]{1,0:T(8,128)(2,1)S(1)} %add_convert_fusion.2), channel_id=1, source_target_pairs={{0,3},{1,2},{2,1},{3,0},{4,7},{5,6},{6,5},{7,4},{8,11},{9,10},{10,... | collective-permute-start | bytes 196616 | tf_op jit(solution)/shard_map/ppermute | solution.py:18
  21.4 5.9 %collective-permute-start.8 = (bf16[160,256]{1,0:T(8,128)(2,1)S(1)}, bf16[160,256]{1,0:T(8,128)(2,1)S(1)}, u32[]{:S(2)}, u32[]{:S(2)}) collective-permute-start(bf16[160,256]{1,0:T(8,128)(2,1)S(1)} %pad_maximum_fusion.1), channel_id=1, source_target_pairs={{0,9},{1,8},{2,11},{3,10},{4,13},{5,12},{6,15},{7,14},{8,1},{9,0},... | collective-permute-start | bytes 245768 | tf_op jit(solution)/shard_map/ppermute | solution.py:18
  27.3 5.6 %collective-permute-start.9 = (bf16[192,256]{1,0:T(8,128)(2,1)S(1)}, bf16[192,256]{1,0:T(8,128)(2,1)S(1)}, u32[]{:S(2)}, u32[]{:S(2)}) collective-permute-start(bf16[192,256]{1,0:T(8,128)(2,1)S(1)} %pad_maximum_fusion), channel_id=1, source_target_pairs={{0,5},{1,4},{2,7},{3,6},{4,1},{5,0},{6,3},{7,2},{8,13},{9,12},{10,... | collective-permute-start | bytes 294920 | tf_op jit(solution)/shard_map/ppermute | solution.py:18
  33.0 1.7 %copy-start.1 = (f32[512,256]{1,0:T(8,128)S(1)}, f32[512,256]{1,0:T(8,128)}, u32[]{:S(2)}) copy-start(f32[512,256]{1,0:T(8,128)} %history.1) | copy-start | bytes 1572868
  33.0 1.7 %copy-start = (f32[512,256]{1,0:T(8,128)S(1)}, f32[512,256]{1,0:T(8,128)}, u32[]{:S(2)}) copy-start(f32[512,256]{1,0:T(8,128)} %master.1) | copy-start | bytes 1572868
  33.1 4.0 %collective-permute-start.10 = (bf16[4,32,256]{2,1,0:T(8,128)(2,1)S(1)}, bf16[4,32,256]{2,1,0:T(8,128)(2,1)S(1)}, u32[]{:S(2)}, u32[]{:S(2)}) collective-permute-start(bf16[4,32,256]{2,1,0:T(8,128)(2,1)S(1)} %fusion.3.refs_0_), channel_id=1, source_target_pairs={{0,3},{1,2},{2,1},{3,0},{4,7},{5,6},{6,5},{7,4},{8,11},{9,10},{10,... | collective-permute-start | bytes 196616 | tf_op jit(solution)/shard_map/ppermute | solution.py:18
  36.1 1.9 %collective-permute-start.11 = (bf16[4,32,256]{2,1,0:T(8,128)(2,1)S(1)}, bf16[4,32,256]{2,1,0:T(8,128)(2,1)S(1)}, u32[]{:S(2)}, u32[]{:S(2)}) collective-permute-start(bf16[4,32,256]{2,1,0:T(8,128)(2,1)S(1)} %fusion.3.refs_0_), channel_id=1, source_target_pairs={{0,1},{1,0},{2,3},{3,2},{4,5},{5,4},{6,7},{7,6},{8,9},{9,8},{10,11... | collective-permute-start | bytes 196616 | tf_op jit(solution)/shard_map/ppermute | solution.py:18
  37.1 1.3 %collective-permute-start.12 = (bf16[4,32,256]{2,1,0:T(8,128)(2,1)S(1)}, bf16[4,32,256]{2,1,0:T(8,128)(2,1)S(1)}, u32[]{:S(2)}, u32[]{:S(2)}) collective-permute-start(bf16[4,32,256]{2,1,0:T(8,128)(2,1)S(1)} %collective-permute-done.10.refs_1_), channel_id=1, source_target_pairs={{0,1},{1,0},{2,3},{3,2},{4,5},{5,4},{6,7},{7,6},{8,9},{9,8},{10,11... | collective-permute-start | bytes 196616 | tf_op jit(solution)/shard_map/ppermute | solution.py:18

commit v5 on v4

v5 whole, which is shorter than its diff:
```python
import functools

import jax
import jax.numpy as jnp
from jax import lax
from jax.experimental import pallas as pl
from jax.experimental.pallas import tpu as pltpu
from jax.sharding import PartitionSpec as P

step_size = 2.0
VMEM = pl.BlockSpec(memory_space=pltpu.VMEM)
HBM = pl.BlockSpec(memory_space=pltpu.HBM)
ANY = pl.BlockSpec(memory_space=pl.ANY)
PARAMS = pltpu.CompilerParams(vmem_limit_bytes=16 * 1024 * 1024)


def parity(value):
    for shift in (8, 4, 2, 1):
        value = value ^ (value >> shift)
    return value & 1


def hop(value, bits, size):
    pairs = [(i, i ^ (bits[parity(i)] | 1)) for i in range(size)]
    return lax.ppermute(value, "col", pairs)


CORE, SPLIT, SUM = (1, 1), (2, 4), (4, 2)


def near(value):
    return pltpu.with_memory_space_constraint(value, pltpu.VMEM)


def far(value):
    return pltpu.with_memory_space_constraint(value, pltpu.HBM)


def place_at(place, g):
    me = lax.axis_index("col")
    odd = parity(me) ^ (place >> 1)
    one, two = (me >> 1) & 1, (me >> 2) & 1
    split, last, rest = (one + odd * (two - one)) ^ (place & 1), g & 1, g >> 1
    bit_one, bit_two = split + odd * (last - split), last + odd * (split - last)
    return rest, bit_two, bit_one, odd ^ bit_one ^ bit_two ^ parity(rest)


def steps_of(count, body):
    if count == 1:
        body(0)
    else:
        pl.loop(0, count)(body)


def prepare_kernel(counts, row_totals, column_totals, columns, _, ratio, weight, column_copy, *scratch):
    near_counts, near_rows, near_columns, near_copy, row_terms, sems = scratch
    groups = ratio.shape[1]
    copies = [
        pltpu.make_async_copy(row_totals, near_rows, sems.at[0]),
        pltpu.make_async_copy(column_totals, near_columns, sems.at[1]),
        pltpu.make_async_copy(counts, near_counts, sems.at[2]),
        pltpu.make_async_copy(columns, near_copy, sems.at[3]),
    ]
    for copy in copies:
        copy.start()
    copies[0].wait()
    row_floats = near_rows[...].astype(jnp.float32)
    terms = jnp.log(jnp.sum(row_floats, axis=1, keepdims=True)) - jnp.log(row_floats)
    row_terms[...] = jnp.broadcast_to(terms, (128, terms.shape[1])).T.reshape(row_terms.shape)
    copies[1].wait()
    column_term = jnp.log(near_columns[...].astype(jnp.float32))
    copies[2].wait()
    for place in range(4):

        def body(g, place=place):
            at = place_at(place, g)
            amounts = near_counts[at].astype(jnp.float32)
            term = row_terms[at]
            term = jnp.concatenate([term] * (amounts.shape[1] // 128), axis=1)
            ratio[place, g] = jnp.log(jnp.maximum(amounts, 1.0)) + (term - column_term)
            weight[place, g] = jnp.where(amounts > 0, 0.1 + 0.25 * jnp.sqrt(amounts), 0.0)

        if groups <= 4:
            for g in range(groups):
                body(g)
        else:
            pl.loop(0, groups)(body)
    copies[3].wait()
    column_copy[...] = near_copy[...].astype(jnp.bfloat16)


def slopes_kernel(chunk, places, ratio, weight, column_copy, *refs):
    rows, outs = refs[: len(places)], refs[len(places) :]
    group = chunk // ratio.shape[2]
    count = rows[0].shape[0] // chunk
    for k, place in enumerate(places):

        def body(step, place=place, source=rows[k], target=outs[2 * k], slopes=outs[2 * k + 1]):
            first = pl.multiple_of(step * chunk, chunk)
            scores = lax.dot_general(
                source[pl.ds(first, chunk), :],
                column_copy[...],
                (((1,), (1,)), ((), ())),
                preferred_element_type=jnp.float32,
            )
            at = pl.ds(step * group, group)
            gap = scores - ratio[place, at].reshape(scores.shape)
            confidence = weight[place, at].reshape(scores.shape)
            slope = jnp.where(confidence > 0, confidence * gap, jax.nn.sigmoid(gap)).astype(jnp.bfloat16)
            slopes[pl.ds(first, chunk), :] = slope
            target[pl.ds(first, chunk), :] = jnp.dot(
                slope, column_copy[...], preferred_element_type=jnp.float32
            ).astype(target.dtype)

        steps_of(count, body)


def columns_kernel(total_rows, chunk, master, history, *refs):
    pieces, slopes, (new_master, new_history, total) = refs[:4], refs[4:8], refs[8:]
    count = pieces[0].shape[0] // chunk
    for place in range(4):

        def body(step, place=place):
            first = pl.multiple_of(step * chunk, chunk)
            part = lax.dot_general(
                slopes[place][pl.ds(first, chunk), :],
                pieces[place][pl.ds(first, chunk), :],
                (((0,), (0,)), ((), ())),
                preferred_element_type=jnp.float32,
            )
            total[...] = part if place == 0 and count == 1 else total[...] + part

        if place == 0 and count > 1:
            total[...] = jnp.zeros_like(total)
        steps_of(count, body)
    gradient = total[...] / total_rows
    updated = history[...] + gradient * gradient
    new_history[...] = updated
    new_master[...] = master[...] - step_size * gradient * lax.rsqrt(updated)


def place_kernel(*refs):
    pieces, out = refs[:4], refs[4]
    for place in range(4):
        for g in range(pieces[0].shape[0]):
            out[place_at(place, g)] = pieces[place][g]


def joined(held, other, upper):
    low, high = jnp.where(upper, other, held), jnp.where(upper, held, other)
    return jnp.stack([low, high], axis=1).reshape((2 * held.shape[0],) + held.shape[1:])


def per_device(
    counts, row_totals, column_totals, row_master, row_history, column_master, column_history
):
    size = lax.axis_size("col")
    me = lax.axis_index("col")
    total_rows, block_columns = counts.shape
    all_columns = block_columns * size
    own, width = row_master.shape
    group = size // 4
    group_rows = group * own
    chunk = 128
    ratio_type = pltpu.VMEM((4, group, own, block_columns), jnp.float32)

    odd = parity(me)
    last = jnp.where(odd == 1, me >> 1, me >> 2) & 1
    place = (me >> 3) * 2 + last
    top = [size >> k for k in range(1, size.bit_length() - 3)]
    steps = [((bit, bit), (me & bit) != 0) for bit in top] + [(SUM, last != 0)]
    master, first_hop = row_master[None], None
    for bits, upper in steps:
        other = hop(master, bits, size)
        first_hop = other if first_hop is None else first_hop
        master = joined(master, other, upper).astype(jnp.bfloat16)
    grid = (group // 2, 2, 2, 2, own)
    ratio, weight, column_copy = pl.pallas_call(
        prepare_kernel,
        out_shape=(ratio_type, ratio_type, pltpu.VMEM(column_master.shape, jnp.bfloat16)),
        in_specs=[HBM] * 4 + [ANY],
        out_specs=[VMEM] * 3,
        scratch_shapes=[
            pltpu.VMEM(grid + (block_columns,), jnp.int32),
            pltpu.VMEM((1, total_rows), jnp.int32),
            pltpu.VMEM((1, block_columns), jnp.int32),
            pltpu.VMEM(column_master.shape, jnp.float32),
            pltpu.VMEM(grid + (128,), jnp.float32),
            pltpu.SemaphoreType.DMA((4,)),
        ],
        compiler_params=PARAMS,
        cost_estimate=pl.CostEstimate(flops=8 * counts.size, bytes_accessed=4 * counts.size, transcendentals=2 * counts.size),
        name="prepare",
    )(
        far(counts.reshape(grid + (block_columns,))),
        far(row_totals.reshape(1, total_rows)),
        far(column_totals.reshape(1, block_columns)),
        far(column_master),
        first_hop,
    )

    master, column_copy = lax.optimization_barrier((master, column_copy))
    mine = master.reshape(group_rows, width)
    beside = hop(mine, SPLIT, size)
    opposite = hop(mine, CORE, size)

    def slopes_of(places, *rows):
        types = [(pltpu.VMEM((group_rows, width), jnp.float32 if place < 2 else jnp.bfloat16), pltpu.VMEM((group_rows, block_columns), jnp.bfloat16)) for place in places]
        return pl.pallas_call(
            functools.partial(slopes_kernel, chunk, places),
            out_shape=sum(types, ()),
            in_specs=[VMEM] * (3 + len(places)),
            out_specs=[VMEM] * (2 * len(places)),
            compiler_params=PARAMS,
            cost_estimate=pl.CostEstimate(flops=4 * len(places) * group_rows * block_columns * width, bytes_accessed=0, transcendentals=2 * len(places) * group_rows * block_columns),
            name="slopes",
        )(ratio, weight, column_copy, *[near(r) for r in rows])

    kept_early, slopes_0, sent_early, slopes_2 = slopes_of((0, 2), mine, opposite)
    beside, kept_early = lax.optimization_barrier((beside, kept_early))
    corner = hop(beside, CORE, size)
    kept_late, slopes_1 = slopes_of((1,), beside)
    sent_late, slopes_3 = slopes_of((3,), corner)

    part = kept_late + hop(sent_late, CORE, size).astype(jnp.float32)
    other = hop(part.astype(jnp.bfloat16), SPLIT, size)
    part = kept_early + hop(sent_early, CORE, size).astype(jnp.float32) + other.astype(jnp.float32)
    history = row_history.astype(jnp.bfloat16)[None]
    for bits, upper in steps:
        rounded = part.astype(jnp.bfloat16)
        other = hop(jnp.concatenate([rounded, history.reshape(-1, width)]), bits, size)
        part = rounded.astype(jnp.float32) + other[:group_rows].astype(jnp.float32)
        history = joined(history, other[group_rows:].reshape(history.shape), upper)

    struct = jax.ShapeDtypeStruct(column_master.shape, jnp.float32)
    new_columns, new_column_history = pl.pallas_call(
        functools.partial(columns_kernel, total_rows, chunk),
        out_shape=(struct, struct),
        in_specs=[VMEM] * 10,
        out_specs=[VMEM] * 2,
        scratch_shapes=[pltpu.VMEM(column_master.shape, jnp.float32)],
        compiler_params=PARAMS,
        cost_estimate=pl.CostEstimate(flops=2 * total_rows * block_columns * width, bytes_accessed=4 * column_master.size * 4, transcendentals=0),
        name="columns",
    )(*[near(v) for v in (column_master, column_history, mine, beside, opposite, corner, slopes_0, slopes_1, slopes_2, slopes_3)])

    def adagrad(master, history, gradient):
        updated = history + gradient * gradient
        return master - step_size * gradient * lax.rsqrt(updated), updated

    gradient = part.reshape(group, own, width) / all_columns
    own_gradient = lax.dynamic_index_in_dim(gradient, place, 0, keepdims=False)
    new_rows, new_row_history = adagrad(row_master, row_history, own_gradient)
    copy = adagrad(master.astype(jnp.float32), history.astype(jnp.float32), gradient)[0].astype(jnp.bfloat16)
    beside = hop(copy, SPLIT, size)
    grid_rows = pl.pallas_call(
        place_kernel,
        out_shape=jax.ShapeDtypeStruct(grid + (width,), jnp.bfloat16),
        in_specs=[VMEM] * 4,
        out_specs=VMEM,
        compiler_params=PARAMS,
        name="place",
    )(near(copy), near(beside), near(hop(copy, CORE, size)), near(hop(beside, CORE, size)))
    return (grid_rows.reshape(total_rows, width), new_rows, new_row_history, new_columns, new_column_history)


def solution(mesh):
    return jax.shard_map(
        per_device,
        mesh=mesh,
        in_specs=(
            P("parts", "col"),
            P("parts"),
            P(("parts", "col")),
            P(("parts", "col"), None),
            P(("parts", "col"), None),
            P(("parts", "col"), None),
            P(("parts", "col"), None),
        ),
        out_specs=(
            P("parts", None),
            P(("parts", "col"), None),
            P(("parts", "col"), None),
            P(("parts", "col"), None),
            P(("parts", "col"), None),
        ),
        check_vma=False,
    )
```

time: 39.7 us -> 39.6 us (level)
  starting transfers between devices: 17.6 us -> 15.8 us
  waiting for transfers between devices: 14.6 us -> 15.7 us
  other arithmetic: 0.85 us -> 1.61 us
    ppermute x13, starting transfers between devices: 17.6 us -> 15.8 us  [hop(): return lax.ppermute(value, 'col', pairs)]
    ppermute x13, waiting for transfers between devices: 14.6 us -> 15.7 us  [hop(): return lax.ppermute(value, 'col', pairs)]
    another operation x5, other arithmetic: 0.04 us -> 0.8 us  [joined(): jnp.stack([low, high], axis=1)]
    pallas_call x2 -> x3, Pallas kernels: 1.18 us -> 1.34 us  [slopes_of(): pl.pallas_call(functools.partial(slopes_kernel, chunk, places), out_shape...]
  transfers between devices with their start and end apart: 13 -> 13, of which waited for: 9 -> 9; matrix products, arithmetic and copies ran while one was open for 2% -> 2% of each run, Pallas kernels for 10% -> 11%
where the time goes in v5:
time: 39.6 us; the launch traced here: 39.3 us
  starting transfers between devices  15.8 us (40%)
  waiting for transfers between devices  15.7 us (40%)
  Pallas kernels  5.39 us (14%)
  other arithmetic  1.61 us (4%)
  between operations  0.79 us (2%)
    ppermute x13, starting transfers between devices, hop(): return lax.ppermute(value, 'col', pairs)  15.8 us
    ppermute x13, waiting for transfers between devices, hop(): return lax.ppermute(value, 'col', pairs)  15.7 us
    pallas_call x1, Pallas kernels, per_device(): pl.pallas_call(prepare_kernel, out_shape=(ratio_type, ratio_type, pltpu.V...  1.9 us
    pallas_call x1, Pallas kernels, per_device(): pl.pallas_call(functools.partial(columns_kernel, total_rows, chunk), out_...  1.43 us
    pallas_call x3, Pallas kernels, slopes_of(): pl.pallas_call(functools.partial(slopes_kernel, chunk, places), out_shape...  1.34 us
    another operation x5, other arithmetic, joined(): jnp.stack([low, high], axis=1)  0.8 us
  transfers between devices with their start and end apart: 13, of which 9 were waited for; matrix products, arithmetic and copies ran while one was open for 2% of the time, Pallas kernels for 11%

profile of v5, /device:TPU:0, one launch (start us, length us, event | category | flops | bytes accessed | tf_op | source)
XLA Modules:
  0.0 39.3 jit_solution(3635126392950888311)
XLA Ops:
  0.6 3.5 %collective-permute-start = (f32[1,32,256]{2,1,0:T(8,128)}, f32[1,32,256]{2,1,0:T(8,128)S(1)}, u32[]{:S(2)}, u32[]{:S(2)}) collective-permute-start(f32[1,32,256]{2,1,0:T(8,128)} %bitcast.61), channel_id=1, source_target_pairs={{0,9},{1,8},{2,11},{3,10},{4,13},{5,12},{6,15},{7,14},{8,1},{9,0},... | collective-permute-start | bytes 98312 | tf_op jit(solution)/shard_map/ppermute | solution.py:25
  4.2 2.1 %collective-permute-done._ = f32[1,32,256]{2,1,0:T(8,128)S(1)} collective-permute-done((f32[1,32,256]{2,1,0:T(8,128)}, f32[1,32,256]{2,1,0:T(8,128)S(1)}, u32[]{:S(2)}, u32[]{:S(2)}) %collective-permute-start) | collective-permute-done | bytes 32800 | tf_op jit(solution)/shard_map/ppermute | solution.py:25
  6.3 0.8 %fusion.7 = (bf16[1,1,32,256]{3,2,1,0:T(8,128)(2,1)S(1)}, bf16[1,1,32,256]{3,2,1,0:T(8,128)(2,1)S(1)}) fusion(f32[1,32,256]{2,1,0:T(8,128)S(1)} %collective-permute-done._, pred[]{:T(512)S(6)} %ne.7, f32[32,256]{1,0:T(8,128)} %param.10), kind=kLoop, calls=%fused_computation.26 | loop fusion | flops 16384 | bytes 98305 | tf_op jit(solution)/shard_map/stack | solution.py:151
  7.0 1.8 %collective-permute-start.1 = (bf16[2,32,256]{2,1,0:T(8,128)(2,1)S(1)}, bf16[2,32,256]{2,1,0:T(8,128)(2,1)S(1)}, u32[]{:S(2)}, u32[]{:S(2)}) collective-permute-start(bf16[2,32,256]{2,1,0:T(8,128)(2,1)S(1)} %maximum_bitcast_fusion), channel_id=1, source_target_pairs={{0,5},{1,2},{2,1},{3,6},{4,7},{5,0},{6,3},{7,4},{8,11},{9,12},{10,... | collective-permute-start | bytes 98312 | tf_op jit(solution)/shard_map/ppermute | solution.py:25
  8.8 1.9 %prepare.1 = (f32[4,4,32,512]{3,2,1,0:T(8,128)S(1)}, f32[4,4,32,512]{3,2,1,0:T(8,128)S(1)}, bf16[512,256]{1,0:T(8,128)(2,1)S(1)}) custom-call(s32[2,2,2,2,32,512]{5,4,3,2,1,0:T(8,128)} %bitcast.56, s32[1,512]{1,0:T(1,128)} %bitcast.64, s32[1,512]{1,0:T(1,128)} %bitcast.65, f32[512,256]{1,0:T(8,128)} %master.1, f32[1,32,256]{2,1,0:T(8,128)S(1)} %collective-permute-done._), custom_call_target="tpu_custom_call" | custom-call | flops 2097152 | bytes 1048576 | tf_op jit(solution)/shard_map/prepare/pallas_call | solution.py:178
  10.7 0.0 collective-permute-done.1
  10.8 0.4 collective-permute-start.3
  11.2 1.4 %collective-permute-start.2 = (bf16[128,256]{1,0:T(8,128)(2,1)S(1)}, bf16[128,256]{1,0:T(8,128)(2,1)S(1)}, u32[]{:S(2)}, u32[]{:S(2)}) collective-permute-start(bf16[128,256]{1,0:T(8,128)(2,1)S(1)} %bitcast.52), channel_id=1, source_target_pairs={{0,3},{1,4},{2,7},{3,0},{4,1},{5,6},{6,5},{7,2},{8,13},{9,10},{10,... | collective-permute-start | bytes 196616 | tf_op jit(solution)/shard_map/ppermute | solution.py:25
  12.6 0.0 collective-permute-done.3.refs_1_.refs_2_
  12.6 0.6 %slopes.3 = (f32[128,256]{1,0:T(8,128)S(1)}, bf16[128,512]{1,0:T(8,128)(2,1)S(1)}, bf16[128,256]{1,0:T(8,128)(2,1)S(1)}, bf16[128,512]{1,0:T(8,128)(2,1)S(1)}) custom-call(f32[4,4,32,512]{3,2,1,0:T(8,128)S(1)} %get-tuple-element.24.ratio, f32[4,4,32,512]{3,2,1,0:T(8,128)S(1)} %get-tuple-element.25.weight, ...), custom_call_target="tpu_custom_call" | custom-call | flops 134217728 | tf_op jit(solution)/shard_map/slopes/pallas_call | solution.py:209
  13.2 1.7 %collective-permute-done.2.refs_0_.refs_1_ = bf16[128,256]{1,0:T(8,128)(2,1)S(1)} collective-permute-done((bf16[128,256]{1,0:T(8,128)(2,1)S(1)}, bf16[128,256]{1,0:T(8,128)(2,1)S(1)}, u32[]{:S(2)}, u32[]{:S(2)}) %collective-permute-start.2) | collective-permute-done | bytes 65568 | tf_op jit(solution)/shard_map/ppermute | solution.py:25
  14.9 0.2 collective-permute-start.5
  15.1 1.0 %collective-permute-done.5.refs_0_.refs_3_ = bf16[128,256]{1,0:T(8,128)(2,1)S(1)} collective-permute-done((bf16[128,256]{1,0:T(8,128)(2,1)S(1)}, bf16[128,256]{1,0:T(8,128)(2,1)S(1)}, u32[]{:S(2)}, u32[]{:S(2)}) %collective-permute-start.5) | collective-permute-done | bytes 65568 | tf_op jit(solution)/shard_map/ppermute | solution.py:25
  16.1 0.4 slopes.5
  16.5 0.3 collective-permute-start.6
  16.8 0.3 collective-permute-start.4
  17.1 0.4 slopes.4
  17.5 0.4 collective-permute-done.6
  17.8 0.0 copy-start.2
  17.8 1.5 %collective-permute-start.7 = (bf16[128,256]{1,0:T(8,128)(2,1)S(1)}, bf16[128,256]{1,0:T(8,128)(2,1)S(1)}, u32[]{:S(2)}, u32[]{:S(2)}) collective-permute-start(bf16[128,256]{1,0:T(8,128)(2,1)S(1)} %add_convert_fusion.2), channel_id=1, source_target_pairs={{0,3},{1,4},{2,7},{3,0},{4,1},{5,6},{6,5},{7,2},{8,13},{9,10},{10,... | collective-permute-start | bytes 196616 | tf_op jit(solution)/shard_map/ppermute | solution.py:25
  19.3 0.0 copy-done.2
  19.3 0.0 collective-permute-done.4
  19.3 2.3 %collective-permute-done.7 = bf16[128,256]{1,0:T(8,128)(2,1)S(1)} collective-permute-done((bf16[128,256]{1,0:T(8,128)(2,1)S(1)}, bf16[128,256]{1,0:T(8,128)(2,1)S(1)}, u32[]{:S(2)}, u32[]{:S(2)}) %collective-permute-start.7) | collective-permute-done | bytes 65568 | tf_op jit(solution)/shard_map/ppermute | solution.py:25
  21.6 3.3 %collective-permute-start.8 = (bf16[160,256]{1,0:T(8,128)(2,1)S(1)}, bf16[160,256]{1,0:T(8,128)(2,1)S(1)}, u32[]{:S(2)}, u32[]{:S(2)}) collective-permute-start(bf16[160,256]{1,0:T(8,128)(2,1)S(1)} %pad_maximum_fusion.1), channel_id=1, source_target_pairs={{0,9},{1,8},{2,11},{3,10},{4,13},{5,12},{6,15},{7,14},{8,1},{9,0},... | collective-permute-start | bytes 245768 | tf_op jit(solution)/shard_map/ppermute | solution.py:25
  25.0 4.3 %collective-permute-done.8 = bf16[160,256]{1,0:T(8,128)(2,1)S(1)} collective-permute-done((bf16[160,256]{1,0:T(8,128)(2,1)S(1)}, bf16[160,256]{1,0:T(8,128)(2,1)S(1)}, u32[]{:S(2)}, u32[]{:S(2)}) %collective-permute-start.8) | collective-permute-done | bytes 81952 | tf_op jit(solution)/shard_map/ppermute | solution.py:25
  29.3 1.2 %collective-permute-start.9 = (bf16[192,256]{1,0:T(8,128)(2,1)S(1)}, bf16[192,256]{1,0:T(8,128)(2,1)S(1)}, u32[]{:S(2)}, u32[]{:S(2)}) collective-permute-start(bf16[192,256]{1,0:T(8,128)(2,1)S(1)} %pad_maximum_fusion), channel_id=1, source_target_pairs={{0,5},{1,2},{2,1},{3,6},{4,7},{5,0},{6,3},{7,4},{8,11},{9,12},{10,... | collective-permute-start | bytes 294920 | tf_op jit(solution)/shard_map/ppermute | solution.py:25
  30.5 2.9 %collective-permute-done.9 = bf16[192,256]{1,0:T(8,128)(2,1)S(1)} collective-permute-done((bf16[192,256]{1,0:T(8,128)(2,1)S(1)}, bf16[192,256]{1,0:T(8,128)(2,1)S(1)}, u32[]{:S(2)}, u32[]{:S(2)}) %collective-permute-start.9) | collective-permute-done | bytes 98336 | tf_op jit(solution)/shard_map/ppermute | solution.py:25
  33.5 0.0 copy-start.1
  33.5 0.0 copy-start
  33.6 1.4 %collective-permute-start.10 = (bf16[4,32,256]{2,1,0:T(8,128)(2,1)S(1)}, bf16[4,32,256]{2,1,0:T(8,128)(2,1)S(1)}, u32[]{:S(2)}, u32[]{:S(2)}) collective-permute-start(bf16[4,32,256]{2,1,0:T(8,128)(2,1)S(1)} %fusion.3.refs_0_), channel_id=1, source_target_pairs={{0,3},{1,4},{2,7},{3,0},{4,1},{5,6},{6,5},{7,2},{8,13},{9,10},{10,... | collective-permute-start | bytes 196616 | tf_op jit(solution)/shard_map/ppermute | solution.py:25
  35.0 0.0 copy-done.1
  35.0 0.0 copy-done
  35.0 0.0 copy-start.3
  35.0 1.4 %columns.3 = (f32[512,256]{1,0:T(8,128)}, f32[512,256]{1,0:T(8,128)}) custom-call(f32[512,256]{1,0:T(8,128)S(1)} %copy-done, f32[512,256]{1,0:T(8,128)S(1)} %copy-done.1, bf16[128,256]{1,0:T(8,128)(2,1)S(1)} %bitcast.55, bf16[128,256]{1,0:T(8,128)(2,1)S(1)} %collective-permute-done.2.refs_0_.refs_1_, ...), custom_call_target="tpu_custom_call" | custom-call | flops 134217728 | bytes 2097152 | tf_op jit(solution)/shard_map/columns/pallas_call | solution.py:236
  36.4 0.2 collective-permute-start.11
  36.7 0.7 %collective-permute-done.10.refs_1_ = bf16[4,32,256]{2,1,0:T(8,128)(2,1)S(1)} collective-permute-done((bf16[4,32,256]{2,1,0:T(8,128)(2,1)S(1)}, bf16[4,32,256]{2,1,0:T(8,128)(2,1)S(1)}, u32[]{:S(2)}, u32[]{:S(2)}) %collective-permute-start.10) | collective-permute-done | bytes 65568 | tf_op jit(solution)/shard_map/ppermute | solution.py:25
  37.4 0.3 collective-permute-start.12
  37.6 0.0 copy-done.3
  37.6 0.6 %fusion.6 = (f32[32,256]{1,0:T(8,128)}, f32[32,256]{1,0:T(8,128)}) fusion(f32[32,256]{1,0:T(8,128)S(1)} %copy-done.3, f32[4,32,256]{2,1,0:T(8,128)S(1)} %bitcast.58, s32[]{:T(128)S(6)} %select_n.83, f32[32,256]{1,0:T(8,128)S(1)} %copy-done.2), kind=kLoop, calls=%fused_computation.19 | loop fusion | flops 40960 | bytes 163844 | tf_op jit(solution)/shard_map/sub | solution.py:249
  38.3 0.0 collective-permute-done.11.refs_2_
  38.3 0.3 collective-permute-done.12.refs_3_
  38.6 0.7 %place.1 = bf16[2,2,2,2,32,256]{5,4,3,2,1,0:T(8,128)(2,1)} custom-call(bf16[4,32,256]{2,1,0:T(8,128)(2,1)S(1)} %fusion.3.refs_0_, bf16[4,32,256]{2,1,0:T(8,128)(2,1)S(1)} %collective-permute-done.10.refs_1_, bf16[4,32,256]{2,1,0:T(8,128)(2,1)S(1)} %collective-permute-done.11.refs_2_, bf16[4,32,256]{2,1,0:T(8,128)(2,1)S(1)} %collective-permute-done.12.refs_3_), custom_call_target="tpu_custom_call" | custom-call | tf_op jit(solution)/shard_map/place/pallas_call | solution.py:256
  (18 shorter events, 0.2 us)
Async XLA Ops:
  0.6 5.6 %collective-permute-start = (f32[1,32,256]{2,1,0:T(8,128)}, f32[1,32,256]{2,1,0:T(8,128)S(1)}, u32[]{:S(2)}, u32[]{:S(2)}) collective-permute-start(f32[1,32,256]{2,1,0:T(8,128)} %bitcast.61), channel_id=1, source_target_pairs={{0,9},{1,8},{2,11},{3,10},{4,13},{5,12},{6,15},{7,14},{8,1},{9,0},... | collective-permute-start | bytes 98312 | tf_op jit(solution)/shard_map/ppermute | solution.py:25
  7.0 3.7 %collective-permute-start.1 = (bf16[2,32,256]{2,1,0:T(8,128)(2,1)S(1)}, bf16[2,32,256]{2,1,0:T(8,128)(2,1)S(1)}, u32[]{:S(2)}, u32[]{:S(2)}) collective-permute-start(bf16[2,32,256]{2,1,0:T(8,128)(2,1)S(1)} %maximum_bitcast_fusion), channel_id=1, source_target_pairs={{0,5},{1,2},{2,1},{3,6},{4,7},{5,0},{6,3},{7,4},{8,11},{9,12},{10,... | collective-permute-start | bytes 98312 | tf_op jit(solution)/shard_map/ppermute | solution.py:25
  10.8 1.8 %collective-permute-start.3 = (bf16[128,256]{1,0:T(8,128)(2,1)S(1)}, bf16[128,256]{1,0:T(8,128)(2,1)S(1)}, u32[]{:S(2)}, u32[]{:S(2)}) collective-permute-start(bf16[128,256]{1,0:T(8,128)(2,1)S(1)} %bitcast.51), channel_id=1, source_target_pairs={{0,1},{1,0},{2,3},{3,2},{4,5},{5,4},{6,7},{7,6},{8,9},{9,8},{10,11... | collective-permute-start | bytes 196616 | tf_op jit(solution)/shard_map/ppermute | solution.py:25
  11.2 3.7 %collective-permute-start.2 = (bf16[128,256]{1,0:T(8,128)(2,1)S(1)}, bf16[128,256]{1,0:T(8,128)(2,1)S(1)}, u32[]{:S(2)}, u32[]{:S(2)}) collective-permute-start(bf16[128,256]{1,0:T(8,128)(2,1)S(1)} %bitcast.52), channel_id=1, source_target_pairs={{0,3},{1,4},{2,7},{3,0},{4,1},{5,6},{6,5},{7,2},{8,13},{9,10},{10,... | collective-permute-start | bytes 196616 | tf_op jit(solution)/shard_map/ppermute | solution.py:25
  14.9 1.3 %collective-permute-start.5 = (bf16[128,256]{1,0:T(8,128)(2,1)S(1)}, bf16[128,256]{1,0:T(8,128)(2,1)S(1)}, u32[]{:S(2)}, u32[]{:S(2)}) collective-permute-start(bf16[128,256]{1,0:T(8,128)(2,1)S(1)} %collective-permute-done.2.refs_0_.refs_1_), channel_id=1, source_target_pairs={{0,1},{1,0},{2,3},{3,2},{4,5},{5,4},{6,7},{7,6},{8,9},{9,8},{10,11... | collective-permute-start | bytes 196616 | tf_op jit(solution)/shard_map/ppermute | solution.py:25
  16.5 1.3 %collective-permute-start.6 = (bf16[128,256]{1,0:T(8,128)(2,1)S(1)}, bf16[128,256]{1,0:T(8,128)(2,1)S(1)}, u32[]{:S(2)}, u32[]{:S(2)}) collective-permute-start(bf16[128,256]{1,0:T(8,128)(2,1)S(1)} %get-tuple-element.32), channel_id=1, source_target_pairs={{0,1},{1,0},{2,3},{3,2},{4,5},{5,4},{6,7},{7,6},{8,9},{9,8},{10,11... | collective-permute-start | bytes 196616 | tf_op jit(solution)/shard_map/ppermute | solution.py:25
  16.8 2.6 %collective-permute-start.4 = (bf16[128,256]{1,0:T(8,128)(2,1)S(1)}, bf16[128,256]{1,0:T(8,128)(2,1)S(1)}, u32[]{:S(2)}, u32[]{:S(2)}) collective-permute-start(bf16[128,256]{1,0:T(8,128)(2,1)S(1)} %get-tuple-element.29), channel_id=1, source_target_pairs={{0,1},{1,0},{2,3},{3,2},{4,5},{5,4},{6,7},{7,6},{8,9},{9,8},{10,11... | collective-permute-start | bytes 196616 | tf_op jit(solution)/shard_map/ppermute | solution.py:25
  17.8 1.5 %copy-start.2 = (f32[32,256]{1,0:T(8,128)S(1)}, f32[32,256]{1,0:T(8,128)}, u32[]{:S(2)}) copy-start(f32[32,256]{1,0:T(8,128)} %param.11) | copy-start | bytes 98308
  17.8 3.8 %collective-permute-start.7 = (bf16[128,256]{1,0:T(8,128)(2,1)S(1)}, bf16[128,256]{1,0:T(8,128)(2,1)S(1)}, u32[]{:S(2)}, u32[]{:S(2)}) collective-permute-start(bf16[128,256]{1,0:T(8,128)(2,1)S(1)} %add_convert_fusion.2), channel_id=1, source_target_pairs={{0,3},{1,4},{2,7},{3,0},{4,1},{5,6},{6,5},{7,2},{8,13},{9,10},{10,... | collective-permute-start | bytes 196616 | tf_op jit(solution)/shard_map/ppermute | solution.py:25
  21.6 7.6 %collective-permute-start.8 = (bf16[160,256]{1,0:T(8,128)(2,1)S(1)}, bf16[160,256]{1,0:T(8,128)(2,1)S(1)}, u32[]{:S(2)}, u32[]{:S(2)}) collective-permute-start(bf16[160,256]{1,0:T(8,128)(2,1)S(1)} %pad_maximum_fusion.1), channel_id=1, source_target_pairs={{0,9},{1,8},{2,11},{3,10},{4,13},{5,12},{6,15},{7,14},{8,1},{9,0},... | collective-permute-start | bytes 245768 | tf_op jit(solution)/shard_map/ppermute | solution.py:25
  29.3 4.1 %collective-permute-start.9 = (bf16[192,256]{1,0:T(8,128)(2,1)S(1)}, bf16[192,256]{1,0:T(8,128)(2,1)S(1)}, u32[]{:S(2)}, u32[]{:S(2)}) collective-permute-start(bf16[192,256]{1,0:T(8,128)(2,1)S(1)} %pad_maximum_fusion), channel_id=1, source_target_pairs={{0,5},{1,2},{2,1},{3,6},{4,7},{5,0},{6,3},{7,4},{8,11},{9,12},{10,... | collective-permute-start | bytes 294920 | tf_op jit(solution)/shard_map/ppermute | solution.py:25
  33.5 1.5 %copy-start.1 = (f32[512,256]{1,0:T(8,128)S(1)}, f32[512,256]{1,0:T(8,128)}, u32[]{:S(2)}) copy-start(f32[512,256]{1,0:T(8,128)} %history.1) | copy-start | bytes 1572868
  33.5 1.5 %copy-start = (f32[512,256]{1,0:T(8,128)S(1)}, f32[512,256]{1,0:T(8,128)}, u32[]{:S(2)}) copy-start(f32[512,256]{1,0:T(8,128)} %master.1) | copy-start | bytes 1572868
  33.6 3.8 %collective-permute-start.10 = (bf16[4,32,256]{2,1,0:T(8,128)(2,1)S(1)}, bf16[4,32,256]{2,1,0:T(8,128)(2,1)S(1)}, u32[]{:S(2)}, u32[]{:S(2)}) collective-permute-start(bf16[4,32,256]{2,1,0:T(8,128)(2,1)S(1)} %fusion.3.refs_0_), channel_id=1, source_target_pairs={{0,3},{1,4},{2,7},{3,0},{4,1},{5,6},{6,5},{7,2},{8,13},{9,10},{10,... | collective-permute-start | bytes 196616 | tf_op jit(solution)/shard_map/ppermute | solution.py:25
  35.0 2.6 %copy-start.3 = (f32[32,256]{1,0:T(8,128)S(1)}, f32[32,256]{1,0:T(8,128)}, u32[]{:S(2)}) copy-start(f32[32,256]{1,0:T(8,128)} %param.10) | copy-start | bytes 98308
  36.4 1.8 %collective-permute-start.11 = (bf16[4,32,256]{2,1,0:T(8,128)(2,1)S(1)}, bf16[4,32,256]{2,1,0:T(8,128)(2,1)S(1)}, u32[]{:S(2)}, u32[]{:S(2)}) collective-permute-start(bf16[4,32,256]{2,1,0:T(8,128)(2,1)S(1)} %fusion.3.refs_0_), channel_id=1, source_target_pairs={{0,1},{1,0},{2,3},{3,2},{4,5},{5,4},{6,7},{7,6},{8,9},{9,8},{10,11... | collective-permute-start | bytes 196616 | tf_op jit(solution)/shard_map/ppermute | solution.py:25
  37.4 1.3 %collective-permute-start.12 = (bf16[4,32,256]{2,1,0:T(8,128)(2,1)S(1)}, bf16[4,32,256]{2,1,0:T(8,128)(2,1)S(1)}, u32[]{:S(2)}, u32[]{:S(2)}) collective-permute-start(bf16[4,32,256]{2,1,0:T(8,128)(2,1)S(1)} %collective-permute-done.10.refs_1_), channel_id=1, source_target_pairs={{0,1},{1,0},{2,3},{3,2},{4,5},{5,4},{6,7},{7,6},{8,9},{9,8},{10,11... | collective-permute-start | bytes 196616 | tf_op jit(solution)/shard_map/ppermute | solution.py:25

commit v6 on v5

--- a/solution.py
+++ b/solution.py
@@ -11,7 +11,7 @@
 VMEM = pl.BlockSpec(memory_space=pltpu.VMEM)
 HBM = pl.BlockSpec(memory_space=pltpu.HBM)
 ANY = pl.BlockSpec(memory_space=pl.ANY)
-PARAMS = pltpu.CompilerParams(vmem_limit_bytes=16 * 1024 * 1024)
+PARAMS = pltpu.CompilerParams(vmem_limit_bytes=20 * 1024 * 1024)
 
 
 def parity(value):
@@ -52,9 +52,9 @@
         pl.loop(0, count)(body)
 
 
-def prepare_kernel(counts, row_totals, column_totals, columns, _, ratio, weight, column_copy, *scratch):
+def prepare_kernel(counts, row_totals, column_totals, columns, _, kept_0, kept_1, sent_0, sent_1, column_copy, *scratch):
     near_counts, near_rows, near_columns, near_copy, row_terms, sems = scratch
-    groups = ratio.shape[1]
+    groups = kept_0.shape[1]
     copies = [
         pltpu.make_async_copy(row_totals, near_rows, sems.at[0]),
         pltpu.make_async_copy(column_totals, near_columns, sems.at[1]),
@@ -77,8 +77,9 @@
             amounts = near_counts[at].astype(jnp.float32)
             term = row_terms[at]
             term = jnp.concatenate([term] * (amounts.shape[1] // 128), axis=1)
-            ratio[place, g] = jnp.log(jnp.maximum(amounts, 1.0)) + (term - column_term)
-            weight[place, g] = jnp.where(amounts > 0, 0.1 + 0.25 * jnp.sqrt(amounts), 0.0)
+            target = (kept_0, kept_1, sent_0, sent_1)[place]
+            target[0, g] = jnp.log(jnp.maximum(amounts, 1.0)) + (term - column_term)
+            target[1, g] = jnp.where(amounts > 0, 0.1 + 0.25 * jnp.sqrt(amounts), 0.0)
 
         if groups <= 4:
             for g in range(groups):
@@ -89,50 +90,46 @@
     column_copy[...] = near_copy[...].astype(jnp.bfloat16)
 
 
-def slopes_kernel(chunk, places, ratio, weight, column_copy, *refs):
-    rows, outs = refs[: len(places)], refs[len(places) :]
-    group = chunk // ratio.shape[2]
-    count = rows[0].shape[0] // chunk
-    for k, place in enumerate(places):
-
-        def body(step, place=place, source=rows[k], target=outs[2 * k], slopes=outs[2 * k + 1]):
-            first = pl.multiple_of(step * chunk, chunk)
-            scores = lax.dot_general(
-                source[pl.ds(first, chunk), :],
-                column_copy[...],
-                (((1,), (1,)), ((), ())),
-                preferred_element_type=jnp.float32,
-            )
-            at = pl.ds(step * group, group)
-            gap = scores - ratio[place, at].reshape(scores.shape)
-            confidence = weight[place, at].reshape(scores.shape)
-            slope = jnp.where(confidence > 0, confidence * gap, jax.nn.sigmoid(gap)).astype(jnp.bfloat16)
-            slopes[pl.ds(first, chunk), :] = slope
-            target[pl.ds(first, chunk), :] = jnp.dot(
-                slope, column_copy[...], preferred_element_type=jnp.float32
-            ).astype(target.dtype)
-
-        steps_of(count, body)
-
-
-def columns_kernel(total_rows, chunk, master, history, *refs):
-    pieces, slopes, (new_master, new_history, total) = refs[:4], refs[4:8], refs[8:]
-    count = pieces[0].shape[0] // chunk
-    for place in range(4):
-
-        def body(step, place=place):
-            first = pl.multiple_of(step * chunk, chunk)
-            part = lax.dot_general(
-                slopes[place][pl.ds(first, chunk), :],
-                pieces[place][pl.ds(first, chunk), :],
-                (((0,), (0,)), ((), ())),
-                preferred_element_type=jnp.float32,
-            )
-            total[...] = part if place == 0 and count == 1 else total[...] + part
-
-        if place == 0 and count > 1:
-            total[...] = jnp.zeros_like(total)
-        steps_of(count, body)
+def slopes_of(rows, columns, terms, step, chunk):
+    group = chunk // terms.shape[2]
+    at = pl.ds(step * group, group)
+    scores = lax.dot_general(rows, columns, (((1,), (1,)), ((), ())), preferred_element_type=jnp.float32)
+    gap = scores - terms[0, at].reshape(scores.shape)
+    confidence = terms[1, at].reshape(scores.shape)
+    return jnp.where(confidence > 0, confidence * gap, jax.nn.sigmoid(gap)).astype(jnp.bfloat16)
+
+
+def rows_kernel(chunk, rows, kept, received, columns, other_columns, gradient, slopes):
+    def body(step):
+        at = pl.ds(pl.multiple_of(step * chunk, chunk), chunk)
+        own = slopes_of(rows[at, :], columns[...], kept, step, chunk)
+        slopes[at, :] = own
+        gradient[at, :] = jnp.dot(own, columns[...], preferred_element_type=jnp.float32)
+        other = slopes_of(rows[at, :], other_columns[...], received, step, chunk)
+        gradient[at, :] += jnp.dot(other, other_columns[...], preferred_element_type=jnp.float32)
+
+    steps_of(rows.shape[0] // chunk, body)
+
+
+def columns_kernel(total_rows, chunk, master, history, columns, sent_0, sent_1, mine, beside, others, slopes_0, slopes_1, *outs):
+    new_master, new_history, total = outs
+    group_rows = mine.shape[0]
+    total[...] = jnp.zeros_like(total)
+
+    def body(step):
+        first = pl.multiple_of(step * chunk, chunk)
+        at = pl.ds(first, chunk)
+        part = total[...]
+        for place in range(2):
+            rows = (mine, beside)[place][at, :]
+            own = (slopes_0, slopes_1)[place][at, :]
+            part += lax.dot_general(own, rows, (((0,), (0,)), ((), ())), preferred_element_type=jnp.float32)
+            rows = others[pl.ds(place * group_rows + first, chunk), :]
+            own = slopes_of(rows, columns[...], (sent_0, sent_1)[place], step, chunk)
+            part += lax.dot_general(own, rows, (((0,), (0,)), ((), ())), preferred_element_type=jnp.float32)
+        total[...] = part
+
+    steps_of(group_rows // chunk, body)
     gradient = total[...] / total_rows
     updated = history[...] + gradient * gradient
     new_history[...] = updated
@@ -162,24 +159,25 @@
     group = size // 4
     group_rows = group * own
     chunk = 128
-    ratio_type = pltpu.VMEM((4, group, own, block_columns), jnp.float32)
+    terms_type = pltpu.VMEM((2, group, own, block_columns), jnp.float32)
 
     odd = parity(me)
     last = jnp.where(odd == 1, me >> 1, me >> 2) & 1
     place = (me >> 3) * 2 + last
     top = [size >> k for k in range(1, size.bit_length() - 3)]
     steps = [((bit, bit), (me & bit) != 0) for bit in top] + [(SUM, last != 0)]
-    master, first_hop = row_master[None], None
-    for bits, upper in steps:
-        other = hop(master, bits, size)
-        first_hop = other if first_hop is None else first_hop
-        master = joined(master, other, upper).astype(jnp.bfloat16)
+    other = first_hop = hop(row_master[None], steps[0][0], size)
+    master = lax.optimization_barrier(row_master.astype(jnp.bfloat16))[None]
+    for k, (bits, upper) in enumerate(steps):
+        if k > 0:
+            other = hop(master, bits, size)
+        master = joined(master, other.astype(jnp.bfloat16), upper)
     grid = (group // 2, 2, 2, 2, own)
-    ratio, weight, column_copy = pl.pallas_call(
+    kept_0, kept_1, sent_0, sent_1, column_copy = pl.pallas_call(
         prepare_kernel,
-        out_shape=(ratio_type, ratio_type, pltpu.VMEM(column_master.shape, jnp.bfloat16)),
+        out_shape=(terms_type,) * 4 + (pltpu.VMEM(column_master.shape, jnp.bfloat16),),
         in_specs=[HBM] * 4 + [ANY],
-        out_specs=[VMEM] * 3,
+        out_specs=[VMEM] * 5,
         scratch_shapes=[
             pltpu.VMEM(grid + (block_columns,), jnp.int32),
             pltpu.VMEM((1, total_rows), jnp.int32),
@@ -198,33 +196,28 @@
         far(column_master),
         first_hop,
     )
-
-    master, column_copy = lax.optimization_barrier((master, column_copy))
+    other_columns = hop(column_copy, CORE, size)
+    received_0, received_1 = hop(sent_0, CORE, size), hop(sent_1, CORE, size)
     mine = master.reshape(group_rows, width)
     beside = hop(mine, SPLIT, size)
-    opposite = hop(mine, CORE, size)
-
-    def slopes_of(places, *rows):
-        types = [(pltpu.VMEM((group_rows, width), jnp.float32 if place < 2 else jnp.bfloat16), pltpu.VMEM((group_rows, block_columns), jnp.bfloat16)) for place in places]
+
+    def gradient_of(rows, kept, received):
         return pl.pallas_call(
-            functools.partial(slopes_kernel, chunk, places),
-            out_shape=sum(types, ()),
-            in_specs=[VMEM] * (3 + len(places)),
-            out_specs=[VMEM] * (2 * len(places)),
+            functools.partial(rows_kernel, chunk),
+            out_shape=(pltpu.VMEM((group_rows, width), jnp.float32), pltpu.VMEM((group_rows, block_columns), jnp.bfloat16)),
+            in_specs=[VMEM] * 5,
+            out_specs=[VMEM] * 2,
             compiler_params=PARAMS,
-            cost_estimate=pl.CostEstimate(flops=4 * len(places) * group_rows * block_columns * width, bytes_accessed=0, transcendentals=2 * len(places) * group_rows * block_columns),
-            name="slopes",
-        )(ratio, weight, column_copy, *[near(r) for r in rows])
-
-    kept_early, slopes_0, sent_early, slopes_2 = slopes_of((0, 2), mine, opposite)
-    beside, kept_early = lax.optimization_barrier((beside, kept_early))
-    corner = hop(beside, CORE, size)
-    kept_late, slopes_1 = slopes_of((1,), beside)
-    sent_late, slopes_3 = slopes_of((3,), corner)
-
-    part = kept_late + hop(sent_late, CORE, size).astype(jnp.float32)
-    other = hop(part.astype(jnp.bfloat16), SPLIT, size)
-    part = kept_early + hop(sent_early, CORE, size).astype(jnp.float32) + other.astype(jnp.float32)
+            cost_estimate=pl.CostEstimate(flops=8 * group_rows * block_columns * width, bytes_accessed=0, transcendentals=4 * group_rows * block_columns),
+            name="rows",
+        )(*[near(v) for v in (rows, kept, received, column_copy, other_columns)])
+
+    part_early, slopes_0 = gradient_of(mine, kept_0, received_0)
+    part_late, slopes_1 = gradient_of(beside, kept_1, received_1)
+    own_rows, part_late = lax.optimization_barrier((jnp.concatenate([mine, beside]), part_late))
+    others = hop(own_rows, CORE, size)
+
+    part = part_early + hop(part_late.astype(jnp.bfloat16), SPLIT, size).astype(jnp.float32)
     history = row_history.astype(jnp.bfloat16)[None]
     for bits, upper in steps:
         rounded = part.astype(jnp.bfloat16)
@@ -242,7 +235,7 @@
         compiler_params=PARAMS,
         cost_estimate=pl.CostEstimate(flops=2 * total_rows * block_columns * width, bytes_accessed=4 * column_master.size * 4, transcendentals=0),
         name="columns",
-    )(*[near(v) for v in (column_master, column_history, mine, beside, opposite, corner, slopes_0, slopes_1, slopes_2, slopes_3)])
+    )(*[near(v) for v in (column_master, column_history, column_copy, sent_0, sent_1, mine, beside, others, slopes_0, slopes_1)])
 
     def adagrad(master, history, gradient):
         updated = history + gradient * gradient
@@ -252,6 +245,7 @@
     own_gradient = lax.dynamic_index_in_dim(gradient, place, 0, keepdims=False)
     new_rows, new_row_history = adagrad(row_master, row_history, own_gradient)
     copy = adagrad(master.astype(jnp.float32), history.astype(jnp.float32), gradient)[0].astype(jnp.bfloat16)
+    copy, new_columns = lax.optimization_barrier((copy, new_columns))
     beside = hop(copy, SPLIT, size)
     grid_rows = pl.pallas_call(
         place_kernel,

time: 39.6 us -> 37 us (0.934)
  waiting for transfers between devices: 15.7 us -> 12.6 us
    ppermute x13, waiting for transfers between devices: 15.7 us -> 12.6 us  [hop(): return lax.ppermute(value, 'col', pairs)]
    convert_element_type x2 -> x3, other arithmetic: 0.02 us -> 0.82 us  [the longest x1 0.79 us: per_device(): master = lax.optimization_barrier(row_master.astype(jnp.bfloat16))[None]]
    another operation x5 -> x4, other arithmetic: 0.8 us -> 0.03 us  [joined(): jnp.stack([low, high], axis=1)]
    pallas_call x1, Pallas kernels: 1.43 us -> 1.88 us  [per_device(): pl.pallas_call(functools.partial(columns_kernel, total_rows, chunk), out_...]
    pallas_call x4 -> x3, Pallas kernels: 3.23 us -> 3.11 us  [the longest x1 1.9 us: per_device(): pl.pallas_call(prepare_kernel, out_shape=(terms_type,) * 4 + (pltpu.VMEM(...]
  transfers between devices with their start and end apart: 13 -> 13, of which waited for: 9 -> 7; matrix products, arithmetic and copies ran while one was open for 2% -> 4% of each run, Pallas kernels for 11% -> 14%
where the time goes in v6:
time: 37 us; the launch traced here: 36.7 us
  starting transfers between devices  15.9 us (43%)
  waiting for transfers between devices  12.6 us (34%)
  Pallas kernels  5.71 us (15%)
  other arithmetic  1.65 us (4%)
  between operations  0.82 us (2%)
    ppermute x13, starting transfers between devices, hop(): return lax.ppermute(value, 'col', pairs)  15.9 us
    ppermute x13, waiting for transfers between devices, hop(): return lax.ppermute(value, 'col', pairs)  12.6 us
    pallas_call x1, Pallas kernels, per_device(): pl.pallas_call(prepare_kernel, out_shape=(terms_type,) * 4 + (pltpu.VMEM(...  1.9 us
    pallas_call x1, Pallas kernels, per_device(): pl.pallas_call(functools.partial(columns_kernel, total_rows, chunk), out_...  1.88 us
    pallas_call x2, Pallas kernels, gradient_of(): pl.pallas_call(functools.partial(rows_kernel, chunk), out_shape=(pltpu.VM...  1.21 us
    convert_element_type x1, other arithmetic, per_device(): master = lax.optimization_barrier(row_master.astype(jnp.bfloat16))[None]  0.79 us
  transfers between devices with their start and end apart: 13, of which 7 were waited for; matrix products, arithmetic and copies ran while one was open for 4% of the time, Pallas kernels for 14%

profile of v6, /device:TPU:0, one launch (start us, length us, event | category | flops | bytes accessed | tf_op | source)
XLA Modules:
  0.0 36.7 jit_solution(1098569754551387448)
XLA Ops:
  0.6 3.5 %collective-permute-start = (f32[1,32,256]{2,1,0:T(8,128)}, f32[1,32,256]{2,1,0:T(8,128)S(1)}, u32[]{:S(2)}, u32[]{:S(2)}) collective-permute-start(f32[1,32,256]{2,1,0:T(8,128)} %bitcast.66), channel_id=1, source_target_pairs={{0,9},{1,8},{2,11},{3,10},{4,13},{5,12},{6,15},{7,14},{8,1},{9,0},... | collective-permute-start | bytes 98312 | tf_op jit(solution)/shard_map/ppermute | solution.py:25
  4.2 0.8 %convert_element_type.49 = bf16[32,256]{1,0:T(8,128)(2,1)S(1)} convert(f32[32,256]{1,0:T(8,128)} %param.10) | non-fusion elementwise | flops 8192 | bytes 49152 | tf_op jit(solution)/shard_map/convert_element_type | solution.py:170
  5.0 1.3 %collective-permute-done._ = f32[1,32,256]{2,1,0:T(8,128)S(1)} collective-permute-done((f32[1,32,256]{2,1,0:T(8,128)}, f32[1,32,256]{2,1,0:T(8,128)S(1)}, u32[]{:S(2)}, u32[]{:S(2)}) %collective-permute-start) | collective-permute-done | bytes 32800 | tf_op jit(solution)/shard_map/ppermute | solution.py:25
  6.3 1.8 %collective-permute-start.1 = (bf16[2,32,256]{2,1,0:T(8,128)(2,1)S(1)}, bf16[2,32,256]{2,1,0:T(8,128)(2,1)S(1)}, u32[]{:S(2)}, u32[]{:S(2)}) collective-permute-start(bf16[2,32,256]{2,1,0:T(8,128)(2,1)S(1)} %maximum_bitcast_fusion), channel_id=1, source_target_pairs={{0,5},{1,2},{2,1},{3,6},{4,7},{5,0},{6,3},{7,4},{8,11},{9,12},{10,... | collective-permute-start | bytes 98312 | tf_op jit(solution)/shard_map/ppermute | solution.py:25
  8.1 1.9 %prepare.1 = (f32[2,4,32,512]{3,2,1,0:T(8,128)S(1)}, f32[2,4,32,512]{3,2,1,0:T(8,128)S(1)}, f32[2,4,32,512]{3,2,1,0:T(8,128)S(1)}, f32[2,4,32,512]{3,2,1,0:T(8,128)S(1)}, bf16[512,256]{1,0:T(8,128)(2,1)S(1)}) custom-call(s32[2,2,2,2,32,512]{5,4,3,2,1,0:T(8,128)} %bitcast.61, s32[1,512]{1,0:T(1,128)} %bitcast.69, s32[1,512]{1,0:T(1,128)} %bitcast.70, ...), custom_call_target="tpu_custom_call" | custom-call | flops 2097152 | bytes 1048576 | tf_op jit(solution)/shard_map/prepare/pallas_call | solution.py:176
  10.0 0.4 %collective-permute-start.2 = (f32[2,4,32,512]{3,2,1,0:T(8,128)S(1)}, f32[2,4,32,512]{3,2,1,0:T(8,128)S(1)}, u32[]{:S(2)}, u32[]{:S(2)}) collective-permute-start(f32[2,4,32,512]{3,2,1,0:T(8,128)S(1)} %get-tuple-element.21.sent_0), channel_id=1, source_target_pairs={{0,1},{1,0},{2,3},{3,2},{4,5},{5,4},{6,7},{7,6},{8,9},{9,8},{10,11... | collective-permute-start | bytes 1572872 | tf_op jit(solution)/shard_map/ppermute | solution.py:25
  10.4 0.2 collective-permute-start.3
  10.6 0.3 collective-permute-start.5
  10.9 0.0 collective-permute-done.1
  10.9 1.3 %collective-permute-start.4 = (bf16[128,256]{1,0:T(8,128)(2,1)S(1)}, bf16[128,256]{1,0:T(8,128)(2,1)S(1)}, u32[]{:S(2)}, u32[]{:S(2)}) collective-permute-start(bf16[128,256]{1,0:T(8,128)(2,1)S(1)} %bitcast.57), channel_id=1, source_target_pairs={{0,3},{1,4},{2,7},{3,0},{4,1},{5,6},{6,5},{7,2},{8,13},{9,10},{10,... | collective-permute-start | bytes 196616 | tf_op jit(solution)/shard_map/ppermute | solution.py:25
  12.2 2.4 %collective-permute-done.4.rows.beside = bf16[128,256]{1,0:T(8,128)(2,1)S(1)} collective-permute-done((bf16[128,256]{1,0:T(8,128)(2,1)S(1)}, bf16[128,256]{1,0:T(8,128)(2,1)S(1)}, u32[]{:S(2)}, u32[]{:S(2)}) %collective-permute-start.4) | collective-permute-done | bytes 65568 | tf_op jit(solution)/shard_map/ppermute | solution.py:25
  14.7 0.0 collective-permute-done.3.other_columns
  14.7 0.0 collective-permute-done.5.received
  14.7 0.6 %rows.3 = (f32[128,256]{1,0:T(8,128)S(1)}, bf16[128,512]{1,0:T(8,128)(2,1)S(1)}) custom-call(bf16[128,256]{1,0:T(8,128)(2,1)S(1)} %collective-permute-done.4.rows.beside, f32[2,4,32,512]{3,2,1,0:T(8,128)S(1)} %get-tuple-element.24.kept, f32[2,4,32,512]{3,2,1,0:T(8,128)S(1)} %collective-permute-done.5.received, ...), custom_call_target="tpu_custom_call" | custom-call | flops 134217728 | tf_op jit(solution)/shard_map/rows/pallas_call | solution.py:205
  15.3 0.0 copy-start.2
  15.4 1.4 %collective-permute-start.6 = (bf16[128,256]{1,0:T(8,128)(2,1)S(1)}, bf16[128,256]{1,0:T(8,128)(2,1)S(1)}, u32[]{:S(2)}, u32[]{:S(2)}) collective-permute-start(bf16[128,256]{1,0:T(8,128)(2,1)S(1)} %convert_element_type.52), channel_id=1, source_target_pairs={{0,3},{1,4},{2,7},{3,0},{4,1},{5,6},{6,5},{7,2},{8,13},{9,10},{10,... | collective-permute-start | bytes 196616 | tf_op jit(solution)/shard_map/ppermute | solution.py:25
  16.7 0.0 copy-done.2
  16.7 0.0 collective-permute-done.2.received
  16.7 0.6 %rows.2 = (f32[128,256]{1,0:T(8,128)S(1)}, bf16[128,512]{1,0:T(8,128)(2,1)S(1)}) custom-call(bf16[128,256]{1,0:T(8,128)(2,1)S(1)} %bitcast.59, f32[2,4,32,512]{3,2,1,0:T(8,128)S(1)} %get-tuple-element.20.kept, f32[2,4,32,512]{3,2,1,0:T(8,128)S(1)} %collective-permute-done.2.received, bf16[512,256]{1,0:T(8,128)(2,1)S(1)} %get-tuple-element.22.columns, ...), custom_call_target="tpu_custom_call" | custom-call | flops 134217728 | tf_op jit(solution)/shard_map/rows/pallas_call | solution.py:205
  17.3 1.8 %collective-permute-done.6 = bf16[128,256]{1,0:T(8,128)(2,1)S(1)} collective-permute-done((bf16[128,256]{1,0:T(8,128)(2,1)S(1)}, bf16[128,256]{1,0:T(8,128)(2,1)S(1)}, u32[]{:S(2)}, u32[]{:S(2)}) %collective-permute-start.6) | collective-permute-done | bytes 65568 | tf_op jit(solution)/shard_map/ppermute | solution.py:25
  19.1 0.0 copy-start.1
  19.1 0.0 copy-start
  19.2 3.3 %collective-permute-start.7 = (bf16[160,256]{1,0:T(8,128)(2,1)S(1)}, bf16[160,256]{1,0:T(8,128)(2,1)S(1)}, u32[]{:S(2)}, u32[]{:S(2)}) collective-permute-start(bf16[160,256]{1,0:T(8,128)(2,1)S(1)} %pad_maximum_fusion.2), channel_id=1, source_target_pairs={{0,9},{1,8},{2,11},{3,10},{4,13},{5,12},{6,15},{7,14},{8,1},{9,0},... | collective-permute-start | bytes 245768 | tf_op jit(solution)/shard_map/ppermute | solution.py:25
  22.5 0.4 %collective-permute-start.9 = (bf16[256,256]{1,0:T(8,128)(2,1)S(1)}, bf16[256,256]{1,0:T(8,128)(2,1)S(1)}, u32[]{:S(2)}, u32[]{:S(2)}) collective-permute-start(bf16[256,256]{1,0:T(8,128)(2,1)S(1)} %pad_maximum_fusion), channel_id=1, source_target_pairs={{0,1},{1,0},{2,3},{3,2},{4,5},{5,4},{6,7},{7,6},{8,9},{9,8},{10,11... | collective-permute-start | bytes 393224 | tf_op jit(solution)/shard_map/ppermute | solution.py:25
  22.8 3.8 %collective-permute-done.7 = bf16[160,256]{1,0:T(8,128)(2,1)S(1)} collective-permute-done((bf16[160,256]{1,0:T(8,128)(2,1)S(1)}, bf16[160,256]{1,0:T(8,128)(2,1)S(1)}, u32[]{:S(2)}, u32[]{:S(2)}) %collective-permute-start.7) | collective-permute-done | bytes 81952 | tf_op jit(solution)/shard_map/ppermute | solution.py:25
  26.8 1.3 %collective-permute-start.8 = (bf16[192,256]{1,0:T(8,128)(2,1)S(1)}, bf16[192,256]{1,0:T(8,128)(2,1)S(1)}, u32[]{:S(2)}, u32[]{:S(2)}) collective-permute-start(bf16[192,256]{1,0:T(8,128)(2,1)S(1)} %pad_maximum_fusion.1), channel_id=1, source_target_pairs={{0,5},{1,2},{2,1},{3,6},{4,7},{5,0},{6,3},{7,4},{8,11},{9,12},{10,... | collective-permute-start | bytes 294920 | tf_op jit(solution)/shard_map/ppermute | solution.py:25
  28.0 0.0 collective-permute-done.9.others
  28.1 0.0 copy-done.1
  28.1 0.0 copy-done
  28.1 1.9 %columns.3 = (f32[512,256]{1,0:T(8,128)}, f32[512,256]{1,0:T(8,128)}) custom-call(f32[512,256]{1,0:T(8,128)S(1)} %copy-done, f32[512,256]{1,0:T(8,128)S(1)} %copy-done.1, bf16[512,256]{1,0:T(8,128)(2,1)S(1)} %get-tuple-element.22.columns, f32[2,4,32,512]{3,2,1,0:T(8,128)S(1)} %get-tuple-element.21.sent_0, f32[2,4,32,512]{3,2,1,0:T(8,128)S(1)} %get-tuple-element.25.sent_1, ...), custom_call_target="tpu_custom_call" | custom-call | flops 134217728 | bytes 2097152 | tf_op jit(solution)/shard_map/columns/pallas_call | solution.py:229
  30.0 0.9 %collective-permute-done.8 = bf16[192,256]{1,0:T(8,128)(2,1)S(1)} collective-permute-done((bf16[192,256]{1,0:T(8,128)(2,1)S(1)}, bf16[192,256]{1,0:T(8,128)(2,1)S(1)}, u32[]{:S(2)}, u32[]{:S(2)}) %collective-permute-start.8) | collective-permute-done | bytes 98336 | tf_op jit(solution)/shard_map/ppermute | solution.py:25
  31.0 0.0 copy-start.3
  31.0 1.5 %collective-permute-start.10 = (bf16[4,32,256]{2,1,0:T(8,128)(2,1)S(1)}, bf16[4,32,256]{2,1,0:T(8,128)(2,1)S(1)}, u32[]{:S(2)}, u32[]{:S(2)}) collective-permute-start(bf16[4,32,256]{2,1,0:T(8,128)(2,1)S(1)} %fusion.3.refs_0_), channel_id=1, source_target_pairs={{0,3},{1,4},{2,7},{3,0},{4,1},{5,6},{6,5},{7,2},{8,13},{9,10},{10,... | collective-permute-start | bytes 196616 | tf_op jit(solution)/shard_map/ppermute | solution.py:25
  32.5 0.2 collective-permute-start.11
  32.7 2.0 %collective-permute-done.10.refs_1_ = bf16[4,32,256]{2,1,0:T(8,128)(2,1)S(1)} collective-permute-done((bf16[4,32,256]{2,1,0:T(8,128)(2,1)S(1)}, bf16[4,32,256]{2,1,0:T(8,128)(2,1)S(1)}, u32[]{:S(2)}, u32[]{:S(2)}) %collective-permute-start.10) | collective-permute-done | bytes 65568 | tf_op jit(solution)/shard_map/ppermute | solution.py:25
  34.8 0.3 collective-permute-start.12
  35.1 0.0 copy-done.3
  35.1 0.6 %fusion.6 = (f32[32,256]{1,0:T(8,128)}, f32[32,256]{1,0:T(8,128)}) fusion(f32[32,256]{1,0:T(8,128)S(1)} %copy-done.3, f32[4,32,256]{2,1,0:T(8,128)S(1)} %bitcast.63, s32[]{:T(128)S(6)} %select_n.81, f32[32,256]{1,0:T(8,128)S(1)} %copy-done.2), kind=kLoop, calls=%fused_computation.19 | loop fusion | flops 40960 | bytes 163844 | tf_op jit(solution)/shard_map/sub | solution.py:242
  35.7 0.0 collective-permute-done.11.refs_2_
  35.7 0.3 collective-permute-done.12.refs_3_
  36.0 0.7 %place.1 = bf16[2,2,2,2,32,256]{5,4,3,2,1,0:T(8,128)(2,1)} custom-call(bf16[4,32,256]{2,1,0:T(8,128)(2,1)S(1)} %fusion.3.refs_0_, bf16[4,32,256]{2,1,0:T(8,128)(2,1)S(1)} %collective-permute-done.10.refs_1_, bf16[4,32,256]{2,1,0:T(8,128)(2,1)S(1)} %collective-permute-done.11.refs_2_, bf16[4,32,256]{2,1,0:T(8,128)(2,1)S(1)} %collective-permute-done.12.refs_3_), custom_call_target="tpu_custom_call" | custom-call | tf_op jit(solution)/shard_map/place/pallas_call | solution.py:250
  (21 shorter events, 0.2 us)
Async XLA Ops:
  0.6 5.6 %collective-permute-start = (f32[1,32,256]{2,1,0:T(8,128)}, f32[1,32,256]{2,1,0:T(8,128)S(1)}, u32[]{:S(2)}, u32[]{:S(2)}) collective-permute-start(f32[1,32,256]{2,1,0:T(8,128)} %bitcast.66), channel_id=1, source_target_pairs={{0,9},{1,8},{2,11},{3,10},{4,13},{5,12},{6,15},{7,14},{8,1},{9,0},... | collective-permute-start | bytes 98312 | tf_op jit(solution)/shard_map/ppermute | solution.py:25
  6.3 4.6 %collective-permute-start.1 = (bf16[2,32,256]{2,1,0:T(8,128)(2,1)S(1)}, bf16[2,32,256]{2,1,0:T(8,128)(2,1)S(1)}, u32[]{:S(2)}, u32[]{:S(2)}) collective-permute-start(bf16[2,32,256]{2,1,0:T(8,128)(2,1)S(1)} %maximum_bitcast_fusion), channel_id=1, source_target_pairs={{0,5},{1,2},{2,1},{3,6},{4,7},{5,0},{6,3},{7,4},{8,11},{9,12},{10,... | collective-permute-start | bytes 98312 | tf_op jit(solution)/shard_map/ppermute | solution.py:25
  10.0 6.7 %collective-permute-start.2 = (f32[2,4,32,512]{3,2,1,0:T(8,128)S(1)}, f32[2,4,32,512]{3,2,1,0:T(8,128)S(1)}, u32[]{:S(2)}, u32[]{:S(2)}) collective-permute-start(f32[2,4,32,512]{3,2,1,0:T(8,128)S(1)} %get-tuple-element.21.sent_0), channel_id=1, source_target_pairs={{0,1},{1,0},{2,3},{3,2},{4,5},{5,4},{6,7},{7,6},{8,9},{9,8},{10,11... | collective-permute-start | bytes 1572872 | tf_op jit(solution)/shard_map/ppermute | solution.py:25
  10.4 4.3 %collective-permute-start.3 = (bf16[512,256]{1,0:T(8,128)(2,1)S(1)}, bf16[512,256]{1,0:T(8,128)(2,1)S(1)}, u32[]{:S(2)}, u32[]{:S(2)}) collective-permute-start(bf16[512,256]{1,0:T(8,128)(2,1)S(1)} %get-tuple-element.22.columns), channel_id=1, source_target_pairs={{0,1},{1,0},{2,3},{3,2},{4,5},{5,4},{6,7},{7,6},{8,9},{9,8},{10,11... | collective-permute-start | bytes 786440 | tf_op jit(solution)/shard_map/ppermute | solution.py:25
  10.6 4.1 %collective-permute-start.5 = (f32[2,4,32,512]{3,2,1,0:T(8,128)S(1)}, f32[2,4,32,512]{3,2,1,0:T(8,128)S(1)}, u32[]{:S(2)}, u32[]{:S(2)}) collective-permute-start(f32[2,4,32,512]{3,2,1,0:T(8,128)S(1)} %get-tuple-element.25.sent_1), channel_id=1, source_target_pairs={{0,1},{1,0},{2,3},{3,2},{4,5},{5,4},{6,7},{7,6},{8,9},{9,8},{10,11... | collective-permute-start | bytes 1572872 | tf_op jit(solution)/shard_map/ppermute | solution.py:25
  10.9 3.8 %collective-permute-start.4 = (bf16[128,256]{1,0:T(8,128)(2,1)S(1)}, bf16[128,256]{1,0:T(8,128)(2,1)S(1)}, u32[]{:S(2)}, u32[]{:S(2)}) collective-permute-start(bf16[128,256]{1,0:T(8,128)(2,1)S(1)} %bitcast.57), channel_id=1, source_target_pairs={{0,3},{1,4},{2,7},{3,0},{4,1},{5,6},{6,5},{7,2},{8,13},{9,10},{10,... | collective-permute-start | bytes 196616 | tf_op jit(solution)/shard_map/ppermute | solution.py:25
  15.3 1.4 %copy-start.2 = (f32[32,256]{1,0:T(8,128)S(1)}, f32[32,256]{1,0:T(8,128)}, u32[]{:S(2)}) copy-start(f32[32,256]{1,0:T(8,128)} %param.11) | copy-start | bytes 98308
  15.4 3.8 %collective-permute-start.6 = (bf16[128,256]{1,0:T(8,128)(2,1)S(1)}, bf16[128,256]{1,0:T(8,128)(2,1)S(1)}, u32[]{:S(2)}, u32[]{:S(2)}) collective-permute-start(bf16[128,256]{1,0:T(8,128)(2,1)S(1)} %convert_element_type.52), channel_id=1, source_target_pairs={{0,3},{1,4},{2,7},{3,0},{4,1},{5,6},{6,5},{7,2},{8,13},{9,10},{10,... | collective-permute-start | bytes 196616 | tf_op jit(solution)/shard_map/ppermute | solution.py:25
  19.1 8.9 %copy-start.1 = (f32[512,256]{1,0:T(8,128)S(1)}, f32[512,256]{1,0:T(8,128)}, u32[]{:S(2)}) copy-start(f32[512,256]{1,0:T(8,128)} %history.1) | copy-start | bytes 1572868
  19.1 8.9 %copy-start = (f32[512,256]{1,0:T(8,128)S(1)}, f32[512,256]{1,0:T(8,128)}, u32[]{:S(2)}) copy-start(f32[512,256]{1,0:T(8,128)} %master.1) | copy-start | bytes 1572868
  19.2 7.5 %collective-permute-start.7 = (bf16[160,256]{1,0:T(8,128)(2,1)S(1)}, bf16[160,256]{1,0:T(8,128)(2,1)S(1)}, u32[]{:S(2)}, u32[]{:S(2)}) collective-permute-start(bf16[160,256]{1,0:T(8,128)(2,1)S(1)} %pad_maximum_fusion.2), channel_id=1, source_target_pairs={{0,9},{1,8},{2,11},{3,10},{4,13},{5,12},{6,15},{7,14},{8,1},{9,0},... | collective-permute-start | bytes 245768 | tf_op jit(solution)/shard_map/ppermute | solution.py:25
  22.5 5.6 %collective-permute-start.9 = (bf16[256,256]{1,0:T(8,128)(2,1)S(1)}, bf16[256,256]{1,0:T(8,128)(2,1)S(1)}, u32[]{:S(2)}, u32[]{:S(2)}) collective-permute-start(bf16[256,256]{1,0:T(8,128)(2,1)S(1)} %pad_maximum_fusion), channel_id=1, source_target_pairs={{0,1},{1,0},{2,3},{3,2},{4,5},{5,4},{6,7},{7,6},{8,9},{9,8},{10,11... | collective-permute-start | bytes 393224 | tf_op jit(solution)/shard_map/ppermute | solution.py:25
  26.8 4.1 %collective-permute-start.8 = (bf16[192,256]{1,0:T(8,128)(2,1)S(1)}, bf16[192,256]{1,0:T(8,128)(2,1)S(1)}, u32[]{:S(2)}, u32[]{:S(2)}) collective-permute-start(bf16[192,256]{1,0:T(8,128)(2,1)S(1)} %pad_maximum_fusion.1), channel_id=1, source_target_pairs={{0,5},{1,2},{2,1},{3,6},{4,7},{5,0},{6,3},{7,4},{8,11},{9,12},{10,... | collective-permute-start | bytes 294920 | tf_op jit(solution)/shard_map/ppermute | solution.py:25
  31.0 4.1 %copy-start.3 = (f32[32,256]{1,0:T(8,128)S(1)}, f32[32,256]{1,0:T(8,128)}, u32[]{:S(2)}) copy-start(f32[32,256]{1,0:T(8,128)} %param.10) | copy-start | bytes 98308
  31.0 3.8 %collective-permute-start.10 = (bf16[4,32,256]{2,1,0:T(8,128)(2,1)S(1)}, bf16[4,32,256]{2,1,0:T(8,128)(2,1)S(1)}, u32[]{:S(2)}, u32[]{:S(2)}) collective-permute-start(bf16[4,32,256]{2,1,0:T(8,128)(2,1)S(1)} %fusion.3.refs_0_), channel_id=1, source_target_pairs={{0,3},{1,4},{2,7},{3,0},{4,1},{5,6},{6,5},{7,2},{8,13},{9,10},{10,... | collective-permute-start | bytes 196616 | tf_op jit(solution)/shard_map/ppermute | solution.py:25
  32.5 3.2 %collective-permute-start.11 = (bf16[4,32,256]{2,1,0:T(8,128)(2,1)S(1)}, bf16[4,32,256]{2,1,0:T(8,128)(2,1)S(1)}, u32[]{:S(2)}, u32[]{:S(2)}) collective-permute-start(bf16[4,32,256]{2,1,0:T(8,128)(2,1)S(1)} %fusion.3.refs_0_), channel_id=1, source_target_pairs={{0,1},{1,0},{2,3},{3,2},{4,5},{5,4},{6,7},{7,6},{8,9},{9,8},{10,11... | collective-permute-start | bytes 196616 | tf_op jit(solution)/shard_map/ppermute | solution.py:25
  34.8 1.3 %collective-permute-start.12 = (bf16[4,32,256]{2,1,0:T(8,128)(2,1)S(1)}, bf16[4,32,256]{2,1,0:T(8,128)(2,1)S(1)}, u32[]{:S(2)}, u32[]{:S(2)}) collective-permute-start(bf16[4,32,256]{2,1,0:T(8,128)(2,1)S(1)} %collective-permute-done.10.refs_1_), channel_id=1, source_target_pairs={{0,1},{1,0},{2,3},{3,2},{4,5},{5,4},{6,7},{7,6},{8,9},{9,8},{10,11... | collective-permute-start | bytes 196616 | tf_op jit(solution)/shard_map/ppermute | solution.py:25

commit v7 on v6

--- a/solution.py
+++ b/solution.py
@@ -52,14 +52,16 @@
         pl.loop(0, count)(body)
 
 
-def prepare_kernel(counts, row_totals, column_totals, columns, _, kept_0, kept_1, sent_0, sent_1, column_copy, *scratch):
-    near_counts, near_rows, near_columns, near_copy, row_terms, sems = scratch
+def prepare_kernel(counts, row_totals, column_totals, columns, rows, *refs):
+    kept_0, kept_1, sent_0, sent_1, column_copy, row_copy = refs[:6]
+    near_counts, near_rows, near_columns, near_copy, row_terms, sems = refs[6:]
     groups = kept_0.shape[1]
     copies = [
         pltpu.make_async_copy(row_totals, near_rows, sems.at[0]),
         pltpu.make_async_copy(column_totals, near_columns, sems.at[1]),
         pltpu.make_async_copy(counts, near_counts, sems.at[2]),
         pltpu.make_async_copy(columns, near_copy, sems.at[3]),
+        pltpu.make_async_copy(rows, row_copy, sems.at[4]),
     ]
     for copy in copies:
         copy.start()
@@ -88,6 +90,7 @@
             pl.loop(0, groups)(body)
     copies[3].wait()
     column_copy[...] = near_copy[...].astype(jnp.bfloat16)
+    copies[4].wait()
 
 
 def slopes_of(rows, columns, terms, step, chunk):
@@ -99,7 +102,9 @@
     return jnp.where(confidence > 0, confidence * gap, jax.nn.sigmoid(gap)).astype(jnp.bfloat16)
 
 
-def rows_kernel(chunk, rows, kept, received, columns, other_columns, gradient, slopes):
+def rows_kernel(chunk, rows, kept, received, columns, other_columns, *refs):
+    gradient, slopes = refs[-2:]
+
     def body(step):
         at = pl.ds(pl.multiple_of(step * chunk, chunk), chunk)
         own = slopes_of(rows[at, :], columns[...], kept, step, chunk)
@@ -166,25 +171,19 @@
     place = (me >> 3) * 2 + last
     top = [size >> k for k in range(1, size.bit_length() - 3)]
     steps = [((bit, bit), (me & bit) != 0) for bit in top] + [(SUM, last != 0)]
-    other = first_hop = hop(row_master[None], steps[0][0], size)
-    master = lax.optimization_barrier(row_master.astype(jnp.bfloat16))[None]
-    for k, (bits, upper) in enumerate(steps):
-        if k > 0:
-            other = hop(master, bits, size)
-        master = joined(master, other.astype(jnp.bfloat16), upper)
     grid = (group // 2, 2, 2, 2, own)
-    kept_0, kept_1, sent_0, sent_1, column_copy = pl.pallas_call(
+    kept_0, kept_1, sent_0, sent_1, column_copy, row_copy = pl.pallas_call(
         prepare_kernel,
-        out_shape=(terms_type,) * 4 + (pltpu.VMEM(column_master.shape, jnp.bfloat16),),
-        in_specs=[HBM] * 4 + [ANY],
-        out_specs=[VMEM] * 5,
+        out_shape=(terms_type,) * 4 + (pltpu.VMEM(column_master.shape, jnp.bfloat16), pltpu.VMEM(row_master.shape, jnp.float32)),
+        in_specs=[HBM] * 5,
+        out_specs=[VMEM] * 6,
         scratch_shapes=[
             pltpu.VMEM(grid + (block_columns,), jnp.int32),
             pltpu.VMEM((1, total_rows), jnp.int32),
             pltpu.VMEM((1, block_columns), jnp.int32),
             pltpu.VMEM(column_master.shape, jnp.float32),
             pltpu.VMEM(grid + (128,), jnp.float32),
-            pltpu.SemaphoreType.DMA((4,)),
+            pltpu.SemaphoreType.DMA((5,)),
         ],
         compiler_params=PARAMS,
         cost_estimate=pl.CostEstimate(flops=8 * counts.size, bytes_accessed=4 * counts.size, transcendentals=2 * counts.size),
@@ -194,25 +193,31 @@
         far(row_totals.reshape(1, total_rows)),
         far(column_totals.reshape(1, block_columns)),
         far(column_master),
-        first_hop,
+        far(row_master),
     )
     other_columns = hop(column_copy, CORE, size)
     received_0, received_1 = hop(sent_0, CORE, size), hop(sent_1, CORE, size)
+    first_hop = hop(row_master[None], steps[0][0], size)
+    master, other = row_copy[None], first_hop
+    for k, (bits, upper) in enumerate(steps):
+        if k > 0:
+            other = hop(master, bits, size)
+        master = joined(master, other, upper).astype(jnp.bfloat16)
     mine = master.reshape(group_rows, width)
     beside = hop(mine, SPLIT, size)
 
-    def gradient_of(rows, kept, received):
+    def gradient_of(rows, kept, received, *after):
         return pl.pallas_call(
             functools.partial(rows_kernel, chunk),
             out_shape=(pltpu.VMEM((group_rows, width), jnp.float32), pltpu.VMEM((group_rows, block_columns), jnp.bfloat16)),
-            in_specs=[VMEM] * 5,
+            in_specs=[VMEM] * 5 + [ANY] * len(after),
             out_specs=[VMEM] * 2,
             compiler_params=PARAMS,
             cost_estimate=pl.CostEstimate(flops=8 * group_rows * block_columns * width, bytes_accessed=0, transcendentals=4 * group_rows * block_columns),
             name="rows",
-        )(*[near(v) for v in (rows, kept, received, column_copy, other_columns)])
-
-    part_early, slopes_0 = gradient_of(mine, kept_0, received_0)
+        )(*[near(v) for v in (rows, kept, received, column_copy, other_columns)], *after)
+
+    part_early, slopes_0 = gradient_of(mine, kept_0, received_0, first_hop)
     part_late, slopes_1 = gradient_of(beside, kept_1, received_1)
     own_rows, part_late = lax.optimization_barrier((jnp.concatenate([mine, beside]), part_late))
     others = hop(own_rows, CORE, size)

time: 37 us -> 35.9 us (0.970)
  waiting for transfers between devices: 12.6 us -> 9.1 us
  Pallas kernels: 5.71 us -> 7.58 us
  starting transfers between devices: 15.9 us -> 17.3 us
  other arithmetic: 1.65 us -> 0.85 us
    ppermute x13, waiting for transfers between devices: 12.6 us -> 9.1 us  [hop(): return lax.ppermute(value, 'col', pairs)]
    ppermute x13, starting transfers between devices: 15.9 us -> 17.3 us  [hop(): return lax.ppermute(value, 'col', pairs)]
    pallas_call x1, Pallas kernels: 1.88 us -> 2.92 us  [per_device(): pl.pallas_call(functools.partial(columns_kernel, total_rows, chunk), out_...]
    pallas_call x1, Pallas kernels: 1.9 us -> 2.72 us  [per_device(): pl.pallas_call(prepare_kernel, out_shape=(terms_type,) * 4 + (pltpu.VMEM(...]
    convert_element_type x1, other arithmetic: 0.79 us -> 0.01 us  [per_device(): master = joined(master, other, upper).astype(jnp.bfloat16)]
  transfers between devices with their start and end apart: 13 -> 13, of which waited for: 7 -> 6; matrix products, arithmetic and copies ran while one was open for 4% -> 2% of each run, Pallas kernels for 14% -> 19%
where the time goes in v7:
time: 35.9 us; the launch traced here: 35.7 us
  starting transfers between devices  17.3 us (48%)
  waiting for transfers between devices  9.1 us (25%)
  Pallas kernels  7.58 us (21%)
  other arithmetic  0.85 us (2%)
  between operations  0.85 us (2%)
    ppermute x13, starting transfers between devices, hop(): return lax.ppermute(value, 'col', pairs)  17.3 us
    ppermute x13, waiting for transfers between devices, hop(): return lax.ppermute(value, 'col', pairs)  9.1 us
    pallas_call x1, Pallas kernels, per_device(): pl.pallas_call(functools.partial(columns_kernel, total_rows, chunk), out_...  2.92 us
    pallas_call x1, Pallas kernels, per_device(): pl.pallas_call(prepare_kernel, out_shape=(terms_type,) * 4 + (pltpu.VMEM(...  2.72 us
    pallas_call x2, Pallas kernels, gradient_of(): pl.pallas_call(functools.partial(rows_kernel, chunk), out_shape=(pltpu.VM...  1.21 us
    pallas_call x1, Pallas kernels, per_device(): pl.pallas_call(place_kernel, out_shape=jax.ShapeDtypeStruct(grid + (width...  0.72 us
  transfers between devices with their start and end apart: 13, of which 6 were waited for; matrix products, arithmetic and copies ran while one was open for 2% of the time, Pallas kernels for 19%

profile of v7, /device:TPU:0, one launch (start us, length us, event | category | flops | bytes accessed | tf_op | source)
XLA Modules:
  0.0 35.7 jit_solution(5082638556800157512)
XLA Ops:
  0.6 3.5 %collective-permute-start = (f32[1,32,256]{2,1,0:T(8,128)}, f32[1,32,256]{2,1,0:T(8,128)S(1)}, u32[]{:S(2)}, u32[]{:S(2)}) collective-permute-start(f32[1,32,256]{2,1,0:T(8,128)} %bitcast.70), channel_id=1, source_target_pairs={{0,9},{1,8},{2,11},{3,10},{4,13},{5,12},{6,15},{7,14},{8,1},{9,0},... | collective-permute-start | bytes 98312 | tf_op jit(solution)/shard_map/ppermute | solution.py:25
  4.2 2.7 %prepare.1 = (f32[2,4,32,512]{3,2,1,0:T(8,128)S(1)}, f32[2,4,32,512]{3,2,1,0:T(8,128)S(1)}, f32[2,4,32,512]{3,2,1,0:T(8,128)S(1)}, f32[2,4,32,512]{3,2,1,0:T(8,1...) custom-call(s32[2,2,2,2,32,512]{5,4,3,2,1,0:T(8,128)} %bitcast.65, s32[1,512]{1,0:T(1,128)} %bitcast.73, ...), custom_call_target="tpu_custom_call" | custom-call | flops 2097152 | bytes 1048576 | tf_op jit(solution)/shard_map/prepare/pallas_call | solution.py:175
  6.9 0.0 collective-permute-done.refs_0_
  6.9 1.9 %collective-permute-start.1 = (bf16[2,32,256]{2,1,0:T(8,128)(2,1)S(1)}, bf16[2,32,256]{2,1,0:T(8,128)(2,1)S(1)}, u32[]{:S(2)}, u32[]{:S(2)}) collective-permute-start(bf16[2,32,256]{2,1,0:T(8,128)(2,1)S(1)} %maximum_bitcast_fusion), channel_id=1, source_target_pairs={{0,5},{1,2},{2,1},{3,6},{4,7},{5,0},{6,3},{7,4},{8,11},{9,12},{10,... | collective-permute-start | bytes 98312 | tf_op jit(solution)/shard_map/ppermute | solution.py:25
  8.9 0.0 collective-permute-start.2
  8.9 0.5 %collective-permute-start.3 = (bf16[512,256]{1,0:T(8,128)(2,1)S(1)}, bf16[512,256]{1,0:T(8,128)(2,1)S(1)}, u32[]{:S(2)}, u32[]{:S(2)}) collective-permute-start(bf16[512,256]{1,0:T(8,128)(2,1)S(1)} %get-tuple-element.24.columns), channel_id=1, source_target_pairs={{0,1},{1,0},{2,3},{3,2},{4,5},{5,4},{6,7},{7,6},{8,9},{9,8},{10,11... | collective-permute-start | bytes 786440 | tf_op jit(solution)/shard_map/ppermute | solution.py:25
  9.4 0.0 collective-permute-start.5
  9.4 1.1 %collective-permute-done.1 = bf16[2,32,256]{2,1,0:T(8,128)(2,1)S(1)} collective-permute-done((bf16[2,32,256]{2,1,0:T(8,128)(2,1)S(1)}, bf16[2,32,256]{2,1,0:T(8,128)(2,1)S(1)}, u32[]{:S(2)}, u32[]{:S(2)}) %collective-permute-start.1) | collective-permute-done | bytes 32800 | tf_op jit(solution)/shard_map/ppermute | solution.py:25
  10.5 1.7 %collective-permute-start.4 = (bf16[128,256]{1,0:T(8,128)(2,1)S(1)}, bf16[128,256]{1,0:T(8,128)(2,1)S(1)}, u32[]{:S(2)}, u32[]{:S(2)}) collective-permute-start(bf16[128,256]{1,0:T(8,128)(2,1)S(1)} %bitcast.61), channel_id=1, source_target_pairs={{0,3},{1,4},{2,7},{3,0},{4,1},{5,6},{6,5},{7,2},{8,13},{9,10},{10,... | collective-permute-start | bytes 196616 | tf_op jit(solution)/shard_map/ppermute | solution.py:25
  12.2 2.0 %collective-permute-done.4.rows.beside = bf16[128,256]{1,0:T(8,128)(2,1)S(1)} collective-permute-done((bf16[128,256]{1,0:T(8,128)(2,1)S(1)}, bf16[128,256]{1,0:T(8,128)(2,1)S(1)}, u32[]{:S(2)}, u32[]{:S(2)}) %collective-permute-start.4) | collective-permute-done | bytes 65568 | tf_op jit(solution)/shard_map/ppermute | solution.py:25
  14.3 0.0 collective-permute-done.3.other_columns
  14.3 0.0 collective-permute-done.5.received
  14.3 0.6 %rows.5 = (f32[128,256]{1,0:T(8,128)S(1)}, bf16[128,512]{1,0:T(8,128)(2,1)S(1)}) custom-call(bf16[128,256]{1,0:T(8,128)(2,1)S(1)} %collective-permute-done.4.rows.beside, f32[2,4,32,512]{3,2,1,0:T(8,128)S(1)} %get-tuple-element.26.kept, f32[2,4,32,512]{3,2,1,0:T(8,128)S(1)} %collective-permute-done.5.received, ...), custom_call_target="tpu_custom_call" | custom-call | flops 134217728 | tf_op jit(solution)/shard_map/rows/pallas_call | solution.py:210
  14.9 0.0 copy-start.2
  14.9 1.7 %collective-permute-start.6 = (bf16[128,256]{1,0:T(8,128)(2,1)S(1)}, bf16[128,256]{1,0:T(8,128)(2,1)S(1)}, u32[]{:S(2)}, u32[]{:S(2)}) collective-permute-start(bf16[128,256]{1,0:T(8,128)(2,1)S(1)} %convert_element_type.49), channel_id=1, source_target_pairs={{0,3},{1,4},{2,7},{3,0},{4,1},{5,6},{6,5},{7,2},{8,13},{9,10},{10,... | collective-permute-start | bytes 196616 | tf_op jit(solution)/shard_map/ppermute | solution.py:25
  16.7 0.0 copy-done.2
  16.7 0.0 collective-permute-done.2.received
  16.7 0.6 %rows.4 = (f32[128,256]{1,0:T(8,128)S(1)}, bf16[128,512]{1,0:T(8,128)(2,1)S(1)}) custom-call(bf16[128,256]{1,0:T(8,128)(2,1)S(1)} %bitcast.63, f32[2,4,32,512]{3,2,1,0:T(8,128)S(1)} %get-tuple-element.22.kept, f32[2,4,32,512]{3,2,1,0:T(8,128)S(1)} %collective-permute-done.2.received, bf16[512,256]{1,0:T(8,128)(2,1)S(1)} %get-tuple-element.24.columns, ...), custom_call_target="tpu_custom_call" | custom-call | flops 134217728 | tf_op jit(solution)/shard_map/rows/pallas_call | solution.py:210
  17.3 1.4 %collective-permute-done.6 = bf16[128,256]{1,0:T(8,128)(2,1)S(1)} collective-permute-done((bf16[128,256]{1,0:T(8,128)(2,1)S(1)}, bf16[128,256]{1,0:T(8,128)(2,1)S(1)}, u32[]{:S(2)}, u32[]{:S(2)}) %collective-permute-start.6) | collective-permute-done | bytes 65568 | tf_op jit(solution)/shard_map/ppermute | solution.py:25
  18.7 0.0 copy-start.1
  18.7 0.0 copy-start
  18.7 2.7 %collective-permute-start.7 = (bf16[160,256]{1,0:T(8,128)(2,1)S(1)}, bf16[160,256]{1,0:T(8,128)(2,1)S(1)}, u32[]{:S(2)}, u32[]{:S(2)}) collective-permute-start(bf16[160,256]{1,0:T(8,128)(2,1)S(1)} %pad_maximum_fusion.2), channel_id=1, source_target_pairs={{0,9},{1,8},{2,11},{3,10},{4,13},{5,12},{6,15},{7,14},{8,1},{9,0},... | collective-permute-start | bytes 245768 | tf_op jit(solution)/shard_map/ppermute | solution.py:25
  21.5 0.1 collective-permute-start.9
  21.6 2.2 %collective-permute-done.7 = bf16[160,256]{1,0:T(8,128)(2,1)S(1)} collective-permute-done((bf16[160,256]{1,0:T(8,128)(2,1)S(1)}, bf16[160,256]{1,0:T(8,128)(2,1)S(1)}, u32[]{:S(2)}, u32[]{:S(2)}) %collective-permute-start.7) | collective-permute-done | bytes 81952 | tf_op jit(solution)/shard_map/ppermute | solution.py:25
  23.8 3.0 %collective-permute-start.8 = (bf16[192,256]{1,0:T(8,128)(2,1)S(1)}, bf16[192,256]{1,0:T(8,128)(2,1)S(1)}, u32[]{:S(2)}, u32[]{:S(2)}) collective-permute-start(bf16[192,256]{1,0:T(8,128)(2,1)S(1)} %pad_maximum_fusion.1), channel_id=1, source_target_pairs={{0,5},{1,2},{2,1},{3,6},{4,7},{5,0},{6,3},{7,4},{8,11},{9,12},{10,... | collective-permute-start | bytes 294920 | tf_op jit(solution)/shard_map/ppermute | solution.py:25
  26.8 0.0 collective-permute-done.9.others
  26.8 0.0 copy-done.1
  26.8 0.0 copy-done
  26.8 2.9 %columns.3 = (f32[512,256]{1,0:T(8,128)}, f32[512,256]{1,0:T(8,128)}) custom-call(f32[512,256]{1,0:T(8,128)S(1)} %copy-done, f32[512,256]{1,0:T(8,128)S(1)} %copy-done.1, bf16[512,256]{1,0:T(8,128)(2,1)S(1)} %get-tuple-element.24.columns, f32[2,4,32,512]{3,2,1,0:T(8,128)S(1)} %get-tuple-element.23.sent_0, f32[2,4,32,512]{3,2,1,0:T(8,128)} %get-tuple-element.27.sent_1, ...), custom_call_target="tpu_custom_call" | custom-call | flops 134217728 | bytes 2097152 | tf_op jit(solution)/shard_map/columns/pallas_call | solution.py:234
  29.8 0.0 collective-permute-done.8
  29.9 0.0 copy-start.3
  29.9 1.6 %collective-permute-start.10 = (bf16[4,32,256]{2,1,0:T(8,128)(2,1)S(1)}, bf16[4,32,256]{2,1,0:T(8,128)(2,1)S(1)}, u32[]{:S(2)}, u32[]{:S(2)}) collective-permute-start(bf16[4,32,256]{2,1,0:T(8,128)(2,1)S(1)} %fusion.3.refs_0_), channel_id=1, source_target_pairs={{0,3},{1,4},{2,7},{3,0},{4,1},{5,6},{6,5},{7,2},{8,13},{9,10},{10,... | collective-permute-start | bytes 196616 | tf_op jit(solution)/shard_map/ppermute | solution.py:25
  31.5 0.0 collective-permute-start.11
  31.5 2.1 %collective-permute-done.10.refs_1_ = bf16[4,32,256]{2,1,0:T(8,128)(2,1)S(1)} collective-permute-done((bf16[4,32,256]{2,1,0:T(8,128)(2,1)S(1)}, bf16[4,32,256]{2,1,0:T(8,128)(2,1)S(1)}, u32[]{:S(2)}, u32[]{:S(2)}) %collective-permute-start.10) | collective-permute-done | bytes 65568 | tf_op jit(solution)/shard_map/ppermute | solution.py:25
  33.7 0.4 %collective-permute-start.12 = (bf16[4,32,256]{2,1,0:T(8,128)(2,1)S(1)}, bf16[4,32,256]{2,1,0:T(8,128)(2,1)S(1)}, u32[]{:S(2)}, u32[]{:S(2)}) collective-permute-start(bf16[4,32,256]{2,1,0:T(8,128)(2,1)S(1)} %collective-permute-done.10.refs_1_), channel_id=1, source_target_pairs={{0,1},{1,0},{2,3},{3,2},{4,5},{5,4},{6,7},{7,6},{8,9},{9,8},{10,11... | collective-permute-start | bytes 196616 | tf_op jit(solution)/shard_map/ppermute | solution.py:25
  34.1 0.0 copy-done.3
  34.1 0.6 %fusion.6 = (f32[32,256]{1,0:T(8,128)}, f32[32,256]{1,0:T(8,128)}) fusion(f32[32,256]{1,0:T(8,128)S(1)} %copy-done.3, f32[4,32,256]{2,1,0:T(8,128)S(1)} %bitcast.67, s32[]{:T(128)S(6)} %select_n.83, f32[32,256]{1,0:T(8,128)S(1)} %copy-done.2), kind=kLoop, calls=%fused_computation.19 | loop fusion | flops 40960 | bytes 163844 | tf_op jit(solution)/shard_map/sub | solution.py:247
  34.7 0.0 collective-permute-done.11.refs_2_
  34.7 0.3 collective-permute-done.12.refs_3_
  35.0 0.7 %place.1 = bf16[2,2,2,2,32,256]{5,4,3,2,1,0:T(8,128)(2,1)} custom-call(bf16[4,32,256]{2,1,0:T(8,128)(2,1)S(1)} %fusion.3.refs_0_, bf16[4,32,256]{2,1,0:T(8,128)(2,1)S(1)} %collective-permute-done.10.refs_1_, bf16[4,32,256]{2,1,0:T(8,128)(2,1)S(1)} %collective-permute-done.11.refs_2_, bf16[4,32,256]{2,1,0:T(8,128)(2,1)S(1)} %collective-permute-done.12.refs_3_), custom_call_target="tpu_custom_call" | custom-call | tf_op jit(solution)/shard_map/place/pallas_call | solution.py:255
  (21 shorter events, 0.2 us)
Async XLA Ops:
  0.6 6.3 %collective-permute-start = (f32[1,32,256]{2,1,0:T(8,128)}, f32[1,32,256]{2,1,0:T(8,128)S(1)}, u32[]{:S(2)}, u32[]{:S(2)}) collective-permute-start(f32[1,32,256]{2,1,0:T(8,128)} %bitcast.70), channel_id=1, source_target_pairs={{0,9},{1,8},{2,11},{3,10},{4,13},{5,12},{6,15},{7,14},{8,1},{9,0},... | collective-permute-start | bytes 98312 | tf_op jit(solution)/shard_map/ppermute | solution.py:25
  6.9 3.5 %collective-permute-start.1 = (bf16[2,32,256]{2,1,0:T(8,128)(2,1)S(1)}, bf16[2,32,256]{2,1,0:T(8,128)(2,1)S(1)}, u32[]{:S(2)}, u32[]{:S(2)}) collective-permute-start(bf16[2,32,256]{2,1,0:T(8,128)(2,1)S(1)} %maximum_bitcast_fusion), channel_id=1, source_target_pairs={{0,5},{1,2},{2,1},{3,6},{4,7},{5,0},{6,3},{7,4},{8,11},{9,12},{10,... | collective-permute-start | bytes 98312 | tf_op jit(solution)/shard_map/ppermute | solution.py:25
  8.9 7.8 %collective-permute-start.2 = (f32[2,4,32,512]{3,2,1,0:T(8,128)S(1)}, f32[2,4,32,512]{3,2,1,0:T(8,128)S(1)}, u32[]{:S(2)}, u32[]{:S(2)}) collective-permute-start(f32[2,4,32,512]{3,2,1,0:T(8,128)S(1)} %get-tuple-element.23.sent_0), channel_id=1, source_target_pairs={{0,1},{1,0},{2,3},{3,2},{4,5},{5,4},{6,7},{7,6},{8,9},{9,8},{10,11... | collective-permute-start | bytes 1572872 | tf_op jit(solution)/shard_map/ppermute | solution.py:25
  8.9 5.4 %collective-permute-start.3 = (bf16[512,256]{1,0:T(8,128)(2,1)S(1)}, bf16[512,256]{1,0:T(8,128)(2,1)S(1)}, u32[]{:S(2)}, u32[]{:S(2)}) collective-permute-start(bf16[512,256]{1,0:T(8,128)(2,1)S(1)} %get-tuple-element.24.columns), channel_id=1, source_target_pairs={{0,1},{1,0},{2,3},{3,2},{4,5},{5,4},{6,7},{7,6},{8,9},{9,8},{10,11... | collective-permute-start | bytes 786440 | tf_op jit(solution)/shard_map/ppermute | solution.py:25
  9.4 4.9 %collective-permute-start.5 = (f32[2,4,32,512]{3,2,1,0:T(8,128)}, f32[2,4,32,512]{3,2,1,0:T(8,128)S(1)}, u32[]{:S(2)}, u32[]{:S(2)}) collective-permute-start(f32[2,4,32,512]{3,2,1,0:T(8,128)} %get-tuple-element.27.sent_1), channel_id=1, source_target_pairs={{0,1},{1,0},{2,3},{3,2},{4,5},{5,4},{6,7},{7,6},{8,9},{9,8},{10,11... | collective-permute-start | bytes 1572872 | tf_op jit(solution)/shard_map/ppermute | solution.py:25
  10.5 3.8 %collective-permute-start.4 = (bf16[128,256]{1,0:T(8,128)(2,1)S(1)}, bf16[128,256]{1,0:T(8,128)(2,1)S(1)}, u32[]{:S(2)}, u32[]{:S(2)}) collective-permute-start(bf16[128,256]{1,0:T(8,128)(2,1)S(1)} %bitcast.61), channel_id=1, source_target_pairs={{0,3},{1,4},{2,7},{3,0},{4,1},{5,6},{6,5},{7,2},{8,13},{9,10},{10,... | collective-permute-start | bytes 196616 | tf_op jit(solution)/shard_map/ppermute | solution.py:25
  14.9 1.8 %copy-start.2 = (f32[32,256]{1,0:T(8,128)S(1)}, f32[32,256]{1,0:T(8,128)}, u32[]{:S(2)}) copy-start(f32[32,256]{1,0:T(8,128)} %param.11) | copy-start | bytes 98308
  14.9 3.8 %collective-permute-start.6 = (bf16[128,256]{1,0:T(8,128)(2,1)S(1)}, bf16[128,256]{1,0:T(8,128)(2,1)S(1)}, u32[]{:S(2)}, u32[]{:S(2)}) collective-permute-start(bf16[128,256]{1,0:T(8,128)(2,1)S(1)} %convert_element_type.49), channel_id=1, source_target_pairs={{0,3},{1,4},{2,7},{3,0},{4,1},{5,6},{6,5},{7,2},{8,13},{9,10},{10,... | collective-permute-start | bytes 196616 | tf_op jit(solution)/shard_map/ppermute | solution.py:25
  18.7 8.1 %copy-start.1 = (f32[512,256]{1,0:T(8,128)S(1)}, f32[512,256]{1,0:T(8,128)}, u32[]{:S(2)}) copy-start(f32[512,256]{1,0:T(8,128)} %history.1) | copy-start | bytes 1572868
  18.7 8.1 %copy-start = (f32[512,256]{1,0:T(8,128)S(1)}, f32[512,256]{1,0:T(8,128)}, u32[]{:S(2)}) copy-start(f32[512,256]{1,0:T(8,128)} %master.1) | copy-start | bytes 1572868
  18.7 5.0 %collective-permute-start.7 = (bf16[160,256]{1,0:T(8,128)(2,1)S(1)}, bf16[160,256]{1,0:T(8,128)(2,1)S(1)}, u32[]{:S(2)}, u32[]{:S(2)}) collective-permute-start(bf16[160,256]{1,0:T(8,128)(2,1)S(1)} %pad_maximum_fusion.2), channel_id=1, source_target_pairs={{0,9},{1,8},{2,11},{3,10},{4,13},{5,12},{6,15},{7,14},{8,1},{9,0},... | collective-permute-start | bytes 245768 | tf_op jit(solution)/shard_map/ppermute | solution.py:25
  21.5 5.3 %collective-permute-start.9 = (bf16[256,256]{1,0:T(8,128)(2,1)S(1)}, bf16[256,256]{1,0:T(8,128)(2,1)S(1)}, u32[]{:S(2)}, u32[]{:S(2)}) collective-permute-start(bf16[256,256]{1,0:T(8,128)(2,1)S(1)} %pad_maximum_fusion), channel_id=1, source_target_pairs={{0,1},{1,0},{2,3},{3,2},{4,5},{5,4},{6,7},{7,6},{8,9},{9,8},{10,11... | collective-permute-start | bytes 393224 | tf_op jit(solution)/shard_map/ppermute | solution.py:25
  23.8 5.9 %collective-permute-start.8 = (bf16[192,256]{1,0:T(8,128)(2,1)S(1)}, bf16[192,256]{1,0:T(8,128)(2,1)S(1)}, u32[]{:S(2)}, u32[]{:S(2)}) collective-permute-start(bf16[192,256]{1,0:T(8,128)(2,1)S(1)} %pad_maximum_fusion.1), channel_id=1, source_target_pairs={{0,5},{1,2},{2,1},{3,6},{4,7},{5,0},{6,3},{7,4},{8,11},{9,12},{10,... | collective-permute-start | bytes 294920 | tf_op jit(solution)/shard_map/ppermute | solution.py:25
  29.9 4.2 %copy-start.3 = (f32[32,256]{1,0:T(8,128)S(1)}, f32[32,256]{1,0:T(8,128)}, u32[]{:S(2)}) copy-start(f32[32,256]{1,0:T(8,128)} %rows.3) | copy-start | bytes 98308
  29.9 3.8 %collective-permute-start.10 = (bf16[4,32,256]{2,1,0:T(8,128)(2,1)S(1)}, bf16[4,32,256]{2,1,0:T(8,128)(2,1)S(1)}, u32[]{:S(2)}, u32[]{:S(2)}) collective-permute-start(bf16[4,32,256]{2,1,0:T(8,128)(2,1)S(1)} %fusion.3.refs_0_), channel_id=1, source_target_pairs={{0,3},{1,4},{2,7},{3,0},{4,1},{5,6},{6,5},{7,2},{8,13},{9,10},{10,... | collective-permute-start | bytes 196616 | tf_op jit(solution)/shard_map/ppermute | solution.py:25
  31.5 3.2 %collective-permute-start.11 = (bf16[4,32,256]{2,1,0:T(8,128)(2,1)S(1)}, bf16[4,32,256]{2,1,0:T(8,128)(2,1)S(1)}, u32[]{:S(2)}, u32[]{:S(2)}) collective-permute-start(bf16[4,32,256]{2,1,0:T(8,128)(2,1)S(1)} %fusion.3.refs_0_), channel_id=1, source_target_pairs={{0,1},{1,0},{2,3},{3,2},{4,5},{5,4},{6,7},{7,6},{8,9},{9,8},{10,11... | collective-permute-start | bytes 196616 | tf_op jit(solution)/shard_map/ppermute | solution.py:25
  33.7 1.3 %collective-permute-start.12 = (bf16[4,32,256]{2,1,0:T(8,128)(2,1)S(1)}, bf16[4,32,256]{2,1,0:T(8,128)(2,1)S(1)}, u32[]{:S(2)}, u32[]{:S(2)}) collective-permute-start(bf16[4,32,256]{2,1,0:T(8,128)(2,1)S(1)} %collective-permute-done.10.refs_1_), channel_id=1, source_target_pairs={{0,1},{1,0},{2,3},{3,2},{4,5},{5,4},{6,7},{7,6},{8,9},{9,8},{10,11... | collective-permute-start | bytes 196616 | tf_op jit(solution)/shard_map/ppermute | solution.py:25

commit v8 on v7

--- a/solution.py
+++ b/solution.py
@@ -15,9 +15,17 @@
 
 
 def parity(value):
-    for shift in (8, 4, 2, 1):
+    for shift in (4, 2, 1):
         value = value ^ (value >> shift)
     return value & 1
+
+
+def top_bits(size):
+    return [size >> k for k in range(1, size.bit_length() - 3)]
+
+
+def last_bit(me):
+    return ((me >> 2) ^ (parity(me) & ((me >> 1) ^ (me >> 2)))) & 1
 
 
 def hop(value, bits, size):
@@ -52,9 +60,9 @@
         pl.loop(0, count)(body)
 
 
-def prepare_kernel(counts, row_totals, column_totals, columns, rows, *refs):
-    kept_0, kept_1, sent_0, sent_1, column_copy, row_copy = refs[:6]
-    near_counts, near_rows, near_columns, near_copy, row_terms, sems = refs[6:]
+def prepare_kernel(counts, row_totals, column_totals, columns, rows, history, *refs):
+    kept_0, kept_1, sent_0, sent_1, column_copy, row_copy, history_copy, upper = refs[:8]
+    near_counts, near_rows, near_columns, near_copy, near_history, row_terms, sems = refs[8:]
     groups = kept_0.shape[1]
     copies = [
         pltpu.make_async_copy(row_totals, near_rows, sems.at[0]),
@@ -62,9 +70,14 @@
         pltpu.make_async_copy(counts, near_counts, sems.at[2]),
         pltpu.make_async_copy(columns, near_copy, sems.at[3]),
         pltpu.make_async_copy(rows, row_copy, sems.at[4]),
+        pltpu.make_async_copy(history, near_history, sems.at[5]),
     ]
     for copy in copies:
         copy.start()
+    me = lax.axis_index("col")
+    changed = [(me // bit) & 1 for bit in top_bits(8 * counts.shape[0])] + [last_bit(me)]
+    step = lax.broadcasted_iota(jnp.int32, upper.shape, 0)
+    upper[...] = sum(jnp.where(step == k, bit, 0) for k, bit in enumerate(changed)).astype(jnp.float32)
     copies[0].wait()
     row_floats = near_rows[...].astype(jnp.float32)
     terms = jnp.log(jnp.sum(row_floats, axis=1, keepdims=True)) - jnp.log(row_floats)
@@ -91,6 +104,8 @@
     copies[3].wait()
     column_copy[...] = near_copy[...].astype(jnp.bfloat16)
     copies[4].wait()
+    copies[5].wait()
+    history_copy[...] = near_history[...].astype(jnp.bfloat16)
 
 
 def slopes_of(rows, columns, terms, step, chunk):
@@ -166,24 +181,20 @@
     chunk = 128
     terms_type = pltpu.VMEM((2, group, own, block_columns), jnp.float32)
 
-    odd = parity(me)
-    last = jnp.where(odd == 1, me >> 1, me >> 2) & 1
-    place = (me >> 3) * 2 + last
-    top = [size >> k for k in range(1, size.bit_length() - 3)]
-    steps = [((bit, bit), (me & bit) != 0) for bit in top] + [(SUM, last != 0)]
     grid = (group // 2, 2, 2, 2, own)
-    kept_0, kept_1, sent_0, sent_1, column_copy, row_copy = pl.pallas_call(
+    kept_0, kept_1, sent_0, sent_1, column_copy, row_copy, history, side = pl.pallas_call(
         prepare_kernel,
-        out_shape=(terms_type,) * 4 + (pltpu.VMEM(column_master.shape, jnp.bfloat16), pltpu.VMEM(row_master.shape, jnp.float32)),
-        in_specs=[HBM] * 5,
-        out_specs=[VMEM] * 6,
+        out_shape=(terms_type,) * 4 + (pltpu.VMEM(column_master.shape, jnp.bfloat16), pltpu.VMEM(row_master.shape, jnp.float32), pltpu.VMEM(row_master.shape, jnp.bfloat16), pltpu.VMEM((8, width), jnp.float32)),
+        in_specs=[HBM] * 6,
+        out_specs=[VMEM] * 8,
         scratch_shapes=[
             pltpu.VMEM(grid + (block_columns,), jnp.int32),
             pltpu.VMEM((1, total_rows), jnp.int32),
             pltpu.VMEM((1, block_columns), jnp.int32),
             pltpu.VMEM(column_master.shape, jnp.float32),
+            pltpu.VMEM(row_history.shape, jnp.float32),
             pltpu.VMEM(grid + (128,), jnp.float32),
-            pltpu.SemaphoreType.DMA((5,)),
+            pltpu.SemaphoreType.DMA((6,)),
         ],
         compiler_params=PARAMS,
         cost_estimate=pl.CostEstimate(flops=8 * counts.size, bytes_accessed=4 * counts.size, transcendentals=2 * counts.size),
@@ -194,9 +205,12 @@
         far(column_totals.reshape(1, block_columns)),
         far(column_master),
         far(row_master),
+        far(row_history),
     )
     other_columns = hop(column_copy, CORE, size)
     received_0, received_1 = hop(sent_0, CORE, size), hop(sent_1, CORE, size)
+    steps = [((bit, bit), side[k] > 0) for k, bit in enumerate(top_bits(size))]
+    steps.append((SUM, side[len(steps)] > 0))
     first_hop = hop(row_master[None], steps[0][0], size)
     master, other = row_copy[None], first_hop
     for k, (bits, upper) in enumerate(steps):
@@ -205,7 +219,6 @@
         master = joined(master, other, upper).astype(jnp.bfloat16)
     mine = master.reshape(group_rows, width)
     beside = hop(mine, SPLIT, size)
-
     def gradient_of(rows, kept, received, *after):
         return pl.pallas_call(
             functools.partial(rows_kernel, chunk),
@@ -218,18 +231,14 @@
         )(*[near(v) for v in (rows, kept, received, column_copy, other_columns)], *after)
 
     part_early, slopes_0 = gradient_of(mine, kept_0, received_0, first_hop)
+    history, part_early = lax.optimization_barrier((history[None], part_early))
+    for bits, upper in steps[:-1]:
+        history = joined(history, hop(history, bits, size), upper)
     part_late, slopes_1 = gradient_of(beside, kept_1, received_1)
     own_rows, part_late = lax.optimization_barrier((jnp.concatenate([mine, beside]), part_late))
     others = hop(own_rows, CORE, size)
 
     part = part_early + hop(part_late.astype(jnp.bfloat16), SPLIT, size).astype(jnp.float32)
-    history = row_history.astype(jnp.bfloat16)[None]
-    for bits, upper in steps:
-        rounded = part.astype(jnp.bfloat16)
-        other = hop(jnp.concatenate([rounded, history.reshape(-1, width)]), bits, size)
-        part = rounded.astype(jnp.float32) + other[:group_rows].astype(jnp.float32)
-        history = joined(history, other[group_rows:].reshape(history.shape), upper)
-
     struct = jax.ShapeDtypeStruct(column_master.shape, jnp.float32)
     new_columns, new_column_history = pl.pallas_call(
         functools.partial(columns_kernel, total_rows, chunk),
@@ -242,15 +251,21 @@
         name="columns",
     )(*[near(v) for v in (column_master, column_history, column_copy, sent_0, sent_1, mine, beside, others, slopes_0, slopes_1)])
 
+    history, new_columns = lax.optimization_barrier((history, new_columns))
+    last_history = hop(history, SUM, size)
+    for bits, upper in steps:
+        rounded = part.astype(jnp.bfloat16)
+        part = rounded.astype(jnp.float32) + hop(rounded, bits, size).astype(jnp.float32)
+    history = joined(history, last_history, steps[-1][1])
+
     def adagrad(master, history, gradient):
         updated = history + gradient * gradient
         return master - step_size * gradient * lax.rsqrt(updated), updated
 
     gradient = part.reshape(group, own, width) / all_columns
-    own_gradient = lax.dynamic_index_in_dim(gradient, place, 0, keepdims=False)
+    own_gradient = lax.dynamic_index_in_dim(gradient, (me >> 3) * 2 + last_bit(me), 0, keepdims=False)
     new_rows, new_row_history = adagrad(row_master, row_history, own_gradient)
     copy = adagrad(master.astype(jnp.float32), history.astype(jnp.float32), gradient)[0].astype(jnp.bfloat16)
-    copy, new_columns = lax.optimization_barrier((copy, new_columns))
     beside = hop(copy, SPLIT, size)
     grid_rows = pl.pallas_call(
         place_kernel,

time: 35.9 us -> 35.6 us (level)
  Pallas kernels: 7.58 us -> 5.74 us
  waiting for transfers between devices: 9.1 us -> 10.1 us
  starting transfers between devices: 17.3 us -> 17.9 us
    pallas_call x1, Pallas kernels: 2.92 us -> 1.88 us  [per_device(): pl.pallas_call(functools.partial(columns_kernel, total_rows, chunk), out_...]
    ppermute x13 -> x15, waiting for transfers between devices: 9.1 us -> 10.1 us  [hop(): return lax.ppermute(value, 'col', pairs)]
    pallas_call x1, Pallas kernels: 2.72 us -> 1.92 us  [per_device(): pl.pallas_call(prepare_kernel, out_shape=(terms_type,) * 4 + (pltpu.VMEM(...]
    ppermute x13 -> x15, starting transfers between devices: 17.3 us -> 17.9 us  [hop(): return lax.ppermute(value, 'col', pairs)]
  transfers between devices with their start and end apart: 13 -> 15, of which waited for: 6 -> 8; matrix products, arithmetic and copies ran while one was open for 2% -> 2% of each run, Pallas kernels for 19% -> 14%
where the time goes in v8:
time: 35.6 us; the launch traced here: 35.4 us
  starting transfers between devices  17.9 us (50%)
  waiting for transfers between devices  10.1 us (28%)
  Pallas kernels  5.74 us (16%)
  other arithmetic  0.85 us (2%)
  between operations  0.82 us (2%)
    ppermute x15, starting transfers between devices, hop(): return lax.ppermute(value, 'col', pairs)  17.9 us
    ppermute x15, waiting for transfers between devices, hop(): return lax.ppermute(value, 'col', pairs)  10.1 us
    pallas_call x1, Pallas kernels, per_device(): pl.pallas_call(prepare_kernel, out_shape=(terms_type,) * 4 + (pltpu.VMEM(...  1.92 us
    pallas_call x1, Pallas kernels, per_device(): pl.pallas_call(functools.partial(columns_kernel, total_rows, chunk), out_...  1.88 us
    pallas_call x2, Pallas kernels, gradient_of(): pl.pallas_call(functools.partial(rows_kernel, chunk), out_shape=(pltpu.VM...  1.21 us
    pallas_call x1, Pallas kernels, per_device(): pl.pallas_call(place_kernel, out_shape=jax.ShapeDtypeStruct(grid + (width...  0.72 us
  transfers between devices with their start and end apart: 15, of which 8 were waited for; matrix products, arithmetic and copies ran while one was open for 2% of the time, Pallas kernels for 14%

profile of v8, /device:TPU:0, one launch (start us, length us, event | category | flops | bytes accessed | tf_op | source)
XLA Modules:
  0.0 35.4 jit_solution(16874911774193438063)
XLA Ops:
  0.6 3.5 %collective-permute-start = (f32[1,32,256]{2,1,0:T(8,128)}, f32[1,32,256]{2,1,0:T(8,128)S(1)}, u32[]{:S(2)}, u32[]{:S(2)}) collective-permute-start(f32[1,32,256]{2,1,0:T(8,128)} %bitcast.74), channel_id=1, source_target_pairs={{0,9},{1,8},{2,11},{3,10},{4,13},{5,12},{6,15},{7,14},{8,1},{9,0},... | collective-permute-start | bytes 98312 | tf_op jit(solution)/shard_map/ppermute | solution.py:33
  4.2 1.9 %prepare.1 = (f32[2,4,32,512]{3,2,1,0:T(8,128)S(1)}, f32[2,4,32,512]{3,2,1,0:T(8,128)S(1)}, f32[2,4,32,512]{3,2,1,0:T(8,128)S(1)}, f32[2,4,32,512]{3,2,1,0:T(8,1...) custom-call(s32[2,2,2,2,32,512]{5,4,3,2,1,0:T(8,128)} %bitcast.69, ...), custom_call_target="tpu_custom_call" | custom-call | flops 2097152 | bytes 1048576 | tf_op jit(solution)/shard_map/prepare/pallas_call | solution.py:185
  6.1 0.7 %collective-permute-start.2 = (f32[2,4,32,512]{3,2,1,0:T(8,128)S(1)}, f32[2,4,32,512]{3,2,1,0:T(8,128)S(1)}, u32[]{:S(2)}, u32[]{:S(2)}) collective-permute-start(f32[2,4,32,512]{3,2,1,0:T(8,128)S(1)} %get-tuple-element.29.sent_0), channel_id=1, source_target_pairs={{0,1},{1,0},{2,3},{3,2},{4,5},{5,4},{6,7},{7,6},{8,9},{9,8},{10,11... | collective-permute-start | bytes 1572872 | tf_op jit(solution)/shard_map/ppermute | solution.py:33
  6.9 0.0 collective-permute-done.refs_0_
  6.9 1.3 %collective-permute-start.1 = (bf16[2,32,256]{2,1,0:T(8,128)(2,1)S(1)}, bf16[2,32,256]{2,1,0:T(8,128)(2,1)S(1)}, u32[]{:S(2)}, u32[]{:S(2)}) collective-permute-start(bf16[2,32,256]{2,1,0:T(8,128)(2,1)S(1)} %maximum_bitcast_fusion), channel_id=1, source_target_pairs={{0,5},{1,2},{2,1},{3,6},{4,7},{5,0},{6,3},{7,4},{8,11},{9,12},{10,... | collective-permute-start | bytes 98312 | tf_op jit(solution)/shard_map/ppermute | solution.py:33
  8.2 0.4 %collective-permute-start.3 = (bf16[512,256]{1,0:T(8,128)(2,1)S(1)}, bf16[512,256]{1,0:T(8,128)(2,1)S(1)}, u32[]{:S(2)}, u32[]{:S(2)}) collective-permute-start(bf16[512,256]{1,0:T(8,128)(2,1)S(1)} %get-tuple-element.30.columns), channel_id=1, source_target_pairs={{0,1},{1,0},{2,3},{3,2},{4,5},{5,4},{6,7},{7,6},{8,9},{9,8},{10,11... | collective-permute-start | bytes 786440 | tf_op jit(solution)/shard_map/ppermute | solution.py:33
  8.6 0.1 collective-permute-start.5
  8.7 1.6 %collective-permute-done.1 = bf16[2,32,256]{2,1,0:T(8,128)(2,1)S(1)} collective-permute-done((bf16[2,32,256]{2,1,0:T(8,128)(2,1)S(1)}, bf16[2,32,256]{2,1,0:T(8,128)(2,1)S(1)}, u32[]{:S(2)}, u32[]{:S(2)}) %collective-permute-start.1) | collective-permute-done | bytes 32800 | tf_op jit(solution)/shard_map/ppermute | solution.py:33
  10.4 1.3 %collective-permute-start.4 = (bf16[128,256]{1,0:T(8,128)(2,1)S(1)}, bf16[128,256]{1,0:T(8,128)(2,1)S(1)}, u32[]{:S(2)}, u32[]{:S(2)}) collective-permute-start(bf16[128,256]{1,0:T(8,128)(2,1)S(1)} %bitcast.63), channel_id=1, source_target_pairs={{0,3},{1,4},{2,7},{3,0},{4,1},{5,6},{6,5},{7,2},{8,13},{9,10},{10,... | collective-permute-start | bytes 196616 | tf_op jit(solution)/shard_map/ppermute | solution.py:33
  11.7 0.0 collective-permute-done.3.other_columns
  11.7 0.0 collective-permute-done.2.received
  11.7 0.6 %rows.4 = (f32[128,256]{1,0:T(8,128)S(1)}, bf16[128,512]{1,0:T(8,128)(2,1)S(1)}) custom-call(bf16[128,256]{1,0:T(8,128)(2,1)S(1)} %bitcast.64, f32[2,4,32,512]{3,2,1,0:T(8,128)S(1)} %get-tuple-element.28.kept, f32[2,4,32,512]{3,2,1,0:T(8,128)S(1)} %collective-permute-done.2.received, bf16[512,256]{1,0:T(8,128)(2,1)S(1)} %get-tuple-element.30.columns, ...), custom_call_target="tpu_custom_call" | custom-call | flops 134217728 | tf_op jit(solution)/shard_map/rows/pallas_call | solution.py:223
  12.3 2.9 %collective-permute-start.9 = (bf16[1,32,256]{2,1,0:T(8,128)(2,1)S(1)}, bf16[1,32,256]{2,1,0:T(8,128)(2,1)S(1)}, u32[]{:S(2)}, u32[]{:S(2)}) collective-permute-start(bf16[1,32,256]{2,1,0:T(8,128)(2,1)S(1)} %bitcast.67), channel_id=1, source_target_pairs={{0,9},{1,8},{2,11},{3,10},{4,13},{5,12},{6,15},{7,14},{8,1},{9,0},... | collective-permute-start | bytes 49160 | tf_op jit(solution)/shard_map/ppermute | solution.py:33
  15.1 0.0 collective-permute-done.4.rows.beside
  15.2 0.0 collective-permute-done.5.received
  15.2 0.0 copy-start.1
  15.2 0.6 %rows.5 = (f32[128,256]{1,0:T(8,128)S(1)}, bf16[128,512]{1,0:T(8,128)(2,1)S(1)}) custom-call(bf16[128,256]{1,0:T(8,128)(2,1)S(1)} %collective-permute-done.4.rows.beside, f32[2,4,32,512]{3,2,1,0:T(8,128)S(1)} %get-tuple-element.33.kept, f32[2,4,32,512]{3,2,1,0:T(8,128)S(1)} %collective-permute-done.5.received, ...), custom_call_target="tpu_custom_call" | custom-call | flops 134217728 | tf_op jit(solution)/shard_map/rows/pallas_call | solution.py:223
  15.8 0.0 copy-start
  15.8 0.6 %collective-permute-start.6 = (bf16[128,256]{1,0:T(8,128)(2,1)S(1)}, bf16[128,256]{1,0:T(8,128)(2,1)S(1)}, u32[]{:S(2)}, u32[]{:S(2)}) collective-permute-start(bf16[128,256]{1,0:T(8,128)(2,1)S(1)} %convert_element_type.46), channel_id=1, source_target_pairs={{0,3},{1,4},{2,7},{3,0},{4,1},{5,6},{6,5},{7,2},{8,13},{9,10},{10,... | collective-permute-start | bytes 196616 | tf_op jit(solution)/shard_map/ppermute | solution.py:33
  16.4 0.2 collective-permute-start.10
  16.6 0.1 collective-permute-done.9
  16.7 2.8 %collective-permute-done.6 = bf16[128,256]{1,0:T(8,128)(2,1)S(1)} collective-permute-done((bf16[128,256]{1,0:T(8,128)(2,1)S(1)}, bf16[128,256]{1,0:T(8,128)(2,1)S(1)}, u32[]{:S(2)}, u32[]{:S(2)}) %collective-permute-start.6) | collective-permute-done | bytes 65568 | tf_op jit(solution)/shard_map/ppermute | solution.py:33
  19.6 1.8 %collective-permute-start.7 = (bf16[128,256]{1,0:T(8,128)(2,1)S(1)}, bf16[128,256]{1,0:T(8,128)(2,1)S(1)}, u32[]{:S(2)}, u32[]{:S(2)}) collective-permute-start(bf16[128,256]{1,0:T(8,128)(2,1)S(1)} %add_convert_fusion.1), channel_id=1, source_target_pairs={{0,9},{1,8},{2,11},{3,10},{4,13},{5,12},{6,15},{7,14},{8,1},{9,0},... | collective-permute-start | bytes 196616 | tf_op jit(solution)/shard_map/ppermute | solution.py:33
  21.4 0.0 collective-permute-done.10.others
  21.4 0.0 copy-done.1
  21.5 0.0 copy-done
  21.5 1.9 %columns.3 = (f32[512,256]{1,0:T(8,128)}, f32[512,256]{1,0:T(8,128)}) custom-call(f32[512,256]{1,0:T(8,128)S(1)} %copy-done, f32[512,256]{1,0:T(8,128)S(1)} %copy-done.1, bf16[512,256]{1,0:T(8,128)(2,1)S(1)} %get-tuple-element.30.columns, f32[2,4,32,512]{3,2,1,0:T(8,128)S(1)} %get-tuple-element.29.sent_0, f32[2,4,32,512]{3,2,1,0:T(8,128)S(1)} %get-tuple-element.34.sent_1, ...), custom_call_target="tpu_custom_call" | custom-call | flops 134217728 | bytes 2097152 | tf_op jit(solution)/shard_map/columns/pallas_call | solution.py:243
  23.3 1.7 %collective-permute-start.11 = (bf16[2,32,256]{2,1,0:T(8,128)(2,1)S(1)}, bf16[2,32,256]{2,1,0:T(8,128)(2,1)S(1)}, u32[]{:S(2)}, u32[]{:S(2)}) collective-permute-start(bf16[2,32,256]{2,1,0:T(8,128)(2,1)S(1)} %maximum_bitcast_fusion.1), channel_id=1, source_target_pairs={{0,5},{1,2},{2,1},{3,6},{4,7},{5,0},{6,3},{7,4},{8,11},{9,12},{10,... | collective-permute-start | bytes 98312 | tf_op jit(solution)/shard_map/ppermute | solution.py:33
  25.1 0.2 collective-permute-done.7
  25.3 0.9 %collective-permute-start.8 = (bf16[128,256]{1,0:T(8,128)(2,1)S(1)}, bf16[128,256]{1,0:T(8,128)(2,1)S(1)}, u32[]{:S(2)}, u32[]{:S(2)}) collective-permute-start(bf16[128,256]{1,0:T(8,128)(2,1)S(1)} %add_convert_fusion), channel_id=1, source_target_pairs={{0,5},{1,2},{2,1},{3,6},{4,7},{5,0},{6,3},{7,4},{8,11},{9,12},{10,... | collective-permute-start | bytes 196616 | tf_op jit(solution)/shard_map/ppermute | solution.py:33
  26.2 0.5 %collective-permute-done.11 = bf16[2,32,256]{2,1,0:T(8,128)(2,1)S(1)} collective-permute-done((bf16[2,32,256]{2,1,0:T(8,128)(2,1)S(1)}, bf16[2,32,256]{2,1,0:T(8,128)(2,1)S(1)}, u32[]{:S(2)}, u32[]{:S(2)}) %collective-permute-start.11) | collective-permute-done | bytes 32800 | tf_op jit(solution)/shard_map/ppermute | solution.py:33
  26.8 2.3 %collective-permute-done.8 = bf16[128,256]{1,0:T(8,128)(2,1)S(1)} collective-permute-done((bf16[128,256]{1,0:T(8,128)(2,1)S(1)}, bf16[128,256]{1,0:T(8,128)(2,1)S(1)}, u32[]{:S(2)}, u32[]{:S(2)}) %collective-permute-start.8) | collective-permute-done | bytes 65568 | tf_op jit(solution)/shard_map/ppermute | solution.py:33
  29.1 0.0 copy-start.3
  29.1 0.0 copy-start.2
  29.1 1.1 %collective-permute-start.12 = (bf16[4,32,256]{2,1,0:T(8,128)(2,1)S(1)}, bf16[4,32,256]{2,1,0:T(8,128)(2,1)S(1)}, u32[]{:S(2)}, u32[]{:S(2)}) collective-permute-start(bf16[4,32,256]{2,1,0:T(8,128)(2,1)S(1)} %fusion.3.refs_0_), channel_id=1, source_target_pairs={{0,3},{1,4},{2,7},{3,0},{4,1},{5,6},{6,5},{7,2},{8,13},{9,10},{10,... | collective-permute-start | bytes 196616 | tf_op jit(solution)/shard_map/ppermute | solution.py:33
  30.2 0.4 %collective-permute-start.13 = (bf16[4,32,256]{2,1,0:T(8,128)(2,1)S(1)}, bf16[4,32,256]{2,1,0:T(8,128)(2,1)S(1)}, u32[]{:S(2)}, u32[]{:S(2)}) collective-permute-start(bf16[4,32,256]{2,1,0:T(8,128)(2,1)S(1)} %fusion.3.refs_0_), channel_id=1, source_target_pairs={{0,1},{1,0},{2,3},{3,2},{4,5},{5,4},{6,7},{7,6},{8,9},{9,8},{10,11... | collective-permute-start | bytes 196616 | tf_op jit(solution)/shard_map/ppermute | solution.py:33
  30.6 2.3 %collective-permute-done.12.refs_1_ = bf16[4,32,256]{2,1,0:T(8,128)(2,1)S(1)} collective-permute-done((bf16[4,32,256]{2,1,0:T(8,128)(2,1)S(1)}, bf16[4,32,256]{2,1,0:T(8,128)(2,1)S(1)}, u32[]{:S(2)}, u32[]{:S(2)}) %collective-permute-start.12) | collective-permute-done | bytes 65568 | tf_op jit(solution)/shard_map/ppermute | solution.py:33
  32.9 0.9 %collective-permute-start.14 = (bf16[4,32,256]{2,1,0:T(8,128)(2,1)S(1)}, bf16[4,32,256]{2,1,0:T(8,128)(2,1)S(1)}, u32[]{:S(2)}, u32[]{:S(2)}) collective-permute-start(bf16[4,32,256]{2,1,0:T(8,128)(2,1)S(1)} %collective-permute-done.12.refs_1_), channel_id=1, source_target_pairs={{0,1},{1,0},{2,3},{3,2},{4,5},{5,4},{6,7},{7,6},{8,9},{9,8},{10,11... | collective-permute-start | bytes 196616 | tf_op jit(solution)/shard_map/ppermute | solution.py:33
  33.8 0.0 copy-done.3
  33.8 0.0 copy-done.2
  33.8 0.6 %fusion.6 = (f32[32,256]{1,0:T(8,128)}, f32[32,256]{1,0:T(8,128)}) fusion(f32[32,256]{1,0:T(8,128)S(1)} %copy-done.2, f32[4,32,256]{2,1,0:T(8,128)S(1)} %bitcast.71, s32[]{:T(128)S(6)} %select_n.39, f32[32,256]{1,0:T(8,128)S(1)} %copy-done.3), kind=kLoop, calls=%fused_computation.17 | loop fusion | flops 40960 | bytes 163844 | tf_op jit(solution)/shard_map/sub | solution.py:263
  34.4 0.0 collective-permute-done.13.refs_2_
  34.4 0.3 collective-permute-done.14.refs_3_
  34.7 0.7 %place.1 = bf16[2,2,2,2,32,256]{5,4,3,2,1,0:T(8,128)(2,1)} custom-call(bf16[4,32,256]{2,1,0:T(8,128)(2,1)S(1)} %fusion.3.refs_0_, bf16[4,32,256]{2,1,0:T(8,128)(2,1)S(1)} %collective-permute-done.12.refs_1_, bf16[4,32,256]{2,1,0:T(8,128)(2,1)S(1)} %collective-permute-done.13.refs_2_, bf16[4,32,256]{2,1,0:T(8,128)(2,1)S(1)} %collective-permute-done.14.refs_3_), custom_call_target="tpu_custom_call" | custom-call | tf_op jit(solution)/shard_map/place/pallas_call | solution.py:270
  (18 shorter events, 0.2 us)
Async XLA Ops:
  0.6 6.2 %collective-permute-start = (f32[1,32,256]{2,1,0:T(8,128)}, f32[1,32,256]{2,1,0:T(8,128)S(1)}, u32[]{:S(2)}, u32[]{:S(2)}) collective-permute-start(f32[1,32,256]{2,1,0:T(8,128)} %bitcast.74), channel_id=1, source_target_pairs={{0,9},{1,8},{2,11},{3,10},{4,13},{5,12},{6,15},{7,14},{8,1},{9,0},... | collective-permute-start | bytes 98312 | tf_op jit(solution)/shard_map/ppermute | solution.py:33
  6.1 5.6 %collective-permute-start.2 = (f32[2,4,32,512]{3,2,1,0:T(8,128)S(1)}, f32[2,4,32,512]{3,2,1,0:T(8,128)S(1)}, u32[]{:S(2)}, u32[]{:S(2)}) collective-permute-start(f32[2,4,32,512]{3,2,1,0:T(8,128)S(1)} %get-tuple-element.29.sent_0), channel_id=1, source_target_pairs={{0,1},{1,0},{2,3},{3,2},{4,5},{5,4},{6,7},{7,6},{8,9},{9,8},{10,11... | collective-permute-start | bytes 1572872 | tf_op jit(solution)/shard_map/ppermute | solution.py:33
  6.9 3.4 %collective-permute-start.1 = (bf16[2,32,256]{2,1,0:T(8,128)(2,1)S(1)}, bf16[2,32,256]{2,1,0:T(8,128)(2,1)S(1)}, u32[]{:S(2)}, u32[]{:S(2)}) collective-permute-start(bf16[2,32,256]{2,1,0:T(8,128)(2,1)S(1)} %maximum_bitcast_fusion), channel_id=1, source_target_pairs={{0,5},{1,2},{2,1},{3,6},{4,7},{5,0},{6,3},{7,4},{8,11},{9,12},{10,... | collective-permute-start | bytes 98312 | tf_op jit(solution)/shard_map/ppermute | solution.py:33
  8.2 3.5 %collective-permute-start.3 = (bf16[512,256]{1,0:T(8,128)(2,1)S(1)}, bf16[512,256]{1,0:T(8,128)(2,1)S(1)}, u32[]{:S(2)}, u32[]{:S(2)}) collective-permute-start(bf16[512,256]{1,0:T(8,128)(2,1)S(1)} %get-tuple-element.30.columns), channel_id=1, source_target_pairs={{0,1},{1,0},{2,3},{3,2},{4,5},{5,4},{6,7},{7,6},{8,9},{9,8},{10,11... | collective-permute-start | bytes 786440 | tf_op jit(solution)/shard_map/ppermute | solution.py:33
  8.6 6.6 %collective-permute-start.5 = (f32[2,4,32,512]{3,2,1,0:T(8,128)S(1)}, f32[2,4,32,512]{3,2,1,0:T(8,128)S(1)}, u32[]{:S(2)}, u32[]{:S(2)}) collective-permute-start(f32[2,4,32,512]{3,2,1,0:T(8,128)S(1)} %get-tuple-element.34.sent_1), channel_id=1, source_target_pairs={{0,1},{1,0},{2,3},{3,2},{4,5},{5,4},{6,7},{7,6},{8,9},{9,8},{10,11... | collective-permute-start | bytes 1572872 | tf_op jit(solution)/shard_map/ppermute | solution.py:33
  10.4 4.8 %collective-permute-start.4 = (bf16[128,256]{1,0:T(8,128)(2,1)S(1)}, bf16[128,256]{1,0:T(8,128)(2,1)S(1)}, u32[]{:S(2)}, u32[]{:S(2)}) collective-permute-start(bf16[128,256]{1,0:T(8,128)(2,1)S(1)} %bitcast.63), channel_id=1, source_target_pairs={{0,3},{1,4},{2,7},{3,0},{4,1},{5,6},{6,5},{7,2},{8,13},{9,10},{10,... | collective-permute-start | bytes 196616 | tf_op jit(solution)/shard_map/ppermute | solution.py:33
  12.3 4.5 %collective-permute-start.9 = (bf16[1,32,256]{2,1,0:T(8,128)(2,1)S(1)}, bf16[1,32,256]{2,1,0:T(8,128)(2,1)S(1)}, u32[]{:S(2)}, u32[]{:S(2)}) collective-permute-start(bf16[1,32,256]{2,1,0:T(8,128)(2,1)S(1)} %bitcast.67), channel_id=1, source_target_pairs={{0,9},{1,8},{2,11},{3,10},{4,13},{5,12},{6,15},{7,14},{8,1},{9,0},... | collective-permute-start | bytes 49160 | tf_op jit(solution)/shard_map/ppermute | solution.py:33
  15.2 6.3 %copy-start.1 = (f32[512,256]{1,0:T(8,128)S(1)}, f32[512,256]{1,0:T(8,128)}, u32[]{:S(2)}) copy-start(f32[512,256]{1,0:T(8,128)} %history.3) | copy-start | bytes 1572868
  15.8 5.7 %copy-start = (f32[512,256]{1,0:T(8,128)S(1)}, f32[512,256]{1,0:T(8,128)}, u32[]{:S(2)}) copy-start(f32[512,256]{1,0:T(8,128)} %master.1) | copy-start | bytes 1572868
  15.8 3.8 %collective-permute-start.6 = (bf16[128,256]{1,0:T(8,128)(2,1)S(1)}, bf16[128,256]{1,0:T(8,128)(2,1)S(1)}, u32[]{:S(2)}, u32[]{:S(2)}) collective-permute-start(bf16[128,256]{1,0:T(8,128)(2,1)S(1)} %convert_element_type.46), channel_id=1, source_target_pairs={{0,3},{1,4},{2,7},{3,0},{4,1},{5,6},{6,5},{7,2},{8,13},{9,10},{10,... | collective-permute-start | bytes 196616 | tf_op jit(solution)/shard_map/ppermute | solution.py:33
  16.4 5.0 %collective-permute-start.10 = (bf16[256,256]{1,0:T(8,128)(2,1)S(1)}, bf16[256,256]{1,0:T(8,128)(2,1)S(1)}, u32[]{:S(2)}, u32[]{:S(2)}) collective-permute-start(bf16[256,256]{1,0:T(8,128)(2,1)S(1)} %pad_maximum_fusion), channel_id=1, source_target_pairs={{0,1},{1,0},{2,3},{3,2},{4,5},{5,4},{6,7},{7,6},{8,9},{9,8},{10,11... | collective-permute-start | bytes 393224 | tf_op jit(solution)/shard_map/ppermute | solution.py:33
  19.6 5.7 %collective-permute-start.7 = (bf16[128,256]{1,0:T(8,128)(2,1)S(1)}, bf16[128,256]{1,0:T(8,128)(2,1)S(1)}, u32[]{:S(2)}, u32[]{:S(2)}) collective-permute-start(bf16[128,256]{1,0:T(8,128)(2,1)S(1)} %add_convert_fusion.1), channel_id=1, source_target_pairs={{0,9},{1,8},{2,11},{3,10},{4,13},{5,12},{6,15},{7,14},{8,1},{9,0},... | collective-permute-start | bytes 196616 | tf_op jit(solution)/shard_map/ppermute | solution.py:33
  23.3 3.4 %collective-permute-start.11 = (bf16[2,32,256]{2,1,0:T(8,128)(2,1)S(1)}, bf16[2,32,256]{2,1,0:T(8,128)(2,1)S(1)}, u32[]{:S(2)}, u32[]{:S(2)}) collective-permute-start(bf16[2,32,256]{2,1,0:T(8,128)(2,1)S(1)} %maximum_bitcast_fusion.1), channel_id=1, source_target_pairs={{0,5},{1,2},{2,1},{3,6},{4,7},{5,0},{6,3},{7,4},{8,11},{9,12},{10,... | collective-permute-start | bytes 98312 | tf_op jit(solution)/shard_map/ppermute | solution.py:33
  25.3 3.8 %collective-permute-start.8 = (bf16[128,256]{1,0:T(8,128)(2,1)S(1)}, bf16[128,256]{1,0:T(8,128)(2,1)S(1)}, u32[]{:S(2)}, u32[]{:S(2)}) collective-permute-start(bf16[128,256]{1,0:T(8,128)(2,1)S(1)} %add_convert_fusion), channel_id=1, source_target_pairs={{0,5},{1,2},{2,1},{3,6},{4,7},{5,0},{6,3},{7,4},{8,11},{9,12},{10,... | collective-permute-start | bytes 196616 | tf_op jit(solution)/shard_map/ppermute | solution.py:33
  29.1 4.7 %copy-start.3 = (f32[32,256]{1,0:T(8,128)S(1)}, f32[32,256]{1,0:T(8,128)}, u32[]{:S(2)}) copy-start(f32[32,256]{1,0:T(8,128)} %history.2) | copy-start | bytes 98308
  29.1 4.7 %copy-start.2 = (f32[32,256]{1,0:T(8,128)S(1)}, f32[32,256]{1,0:T(8,128)}, u32[]{:S(2)}) copy-start(f32[32,256]{1,0:T(8,128)} %rows.3) | copy-start | bytes 98308
  29.1 3.8 %collective-permute-start.12 = (bf16[4,32,256]{2,1,0:T(8,128)(2,1)S(1)}, bf16[4,32,256]{2,1,0:T(8,128)(2,1)S(1)}, u32[]{:S(2)}, u32[]{:S(2)}) collective-permute-start(bf16[4,32,256]{2,1,0:T(8,128)(2,1)S(1)} %fusion.3.refs_0_), channel_id=1, source_target_pairs={{0,3},{1,4},{2,7},{3,0},{4,1},{5,6},{6,5},{7,2},{8,13},{9,10},{10,... | collective-permute-start | bytes 196616 | tf_op jit(solution)/shard_map/ppermute | solution.py:33
  30.2 4.2 %collective-permute-start.13 = (bf16[4,32,256]{2,1,0:T(8,128)(2,1)S(1)}, bf16[4,32,256]{2,1,0:T(8,128)(2,1)S(1)}, u32[]{:S(2)}, u32[]{:S(2)}) collective-permute-start(bf16[4,32,256]{2,1,0:T(8,128)(2,1)S(1)} %fusion.3.refs_0_), channel_id=1, source_target_pairs={{0,1},{1,0},{2,3},{3,2},{4,5},{5,4},{6,7},{7,6},{8,9},{9,8},{10,11... | collective-permute-start | bytes 196616 | tf_op jit(solution)/shard_map/ppermute | solution.py:33
  32.9 1.8 %collective-permute-start.14 = (bf16[4,32,256]{2,1,0:T(8,128)(2,1)S(1)}, bf16[4,32,256]{2,1,0:T(8,128)(2,1)S(1)}, u32[]{:S(2)}, u32[]{:S(2)}) collective-permute-start(bf16[4,32,256]{2,1,0:T(8,128)(2,1)S(1)} %collective-permute-done.12.refs_1_), channel_id=1, source_target_pairs={{0,1},{1,0},{2,3},{3,2},{4,5},{5,4},{6,7},{7,6},{8,9},{9,8},{10,11... | collective-permute-start | bytes 196616 | tf_op jit(solution)/shard_map/ppermute | solution.py:33

commit v9 on v8

--- a/solution.py
+++ b/solution.py
@@ -219,6 +219,10 @@
         master = joined(master, other, upper).astype(jnp.bfloat16)
     mine = master.reshape(group_rows, width)
     beside = hop(mine, SPLIT, size)
+    history, _ = lax.optimization_barrier((history[None], mine))
+    for bits, upper in steps[:-1]:
+        history = joined(history, hop(history, bits, size), upper)
+
     def gradient_of(rows, kept, received, *after):
         return pl.pallas_call(
             functools.partial(rows_kernel, chunk),
@@ -230,11 +234,8 @@
             name="rows",
         )(*[near(v) for v in (rows, kept, received, column_copy, other_columns)], *after)
 
+    part_late, slopes_1 = gradient_of(beside, kept_1, received_1)
     part_early, slopes_0 = gradient_of(mine, kept_0, received_0, first_hop)
-    history, part_early = lax.optimization_barrier((history[None], part_early))
-    for bits, upper in steps[:-1]:
-        history = joined(history, hop(history, bits, size), upper)
-    part_late, slopes_1 = gradient_of(beside, kept_1, received_1)
     own_rows, part_late = lax.optimization_barrier((jnp.concatenate([mine, beside]), part_late))
     others = hop(own_rows, CORE, size)
 

time: 35.6 us -> 35.1 us (0.986)
  waiting for transfers between devices: 10.1 us -> 7.6 us
  starting transfers between devices: 17.9 us -> 19.9 us
    ppermute x15, waiting for transfers between devices: 10.1 us -> 7.6 us  [hop(): return lax.ppermute(value, 'col', pairs)]
    ppermute x15, starting transfers between devices: 17.9 us -> 19.9 us  [hop(): return lax.ppermute(value, 'col', pairs)]
  transfers between devices with their start and end apart: 15 -> 15, of which waited for: 8 -> 7; matrix products, arithmetic and copies ran while one was open for 2% -> 2% of each run, Pallas kernels for 14% -> 14%
where the time goes in v9:
time: 35.1 us; the launch traced here: 34.9 us
  starting transfers between devices  19.9 us (57%)
  waiting for transfers between devices  7.6 us (22%)
  Pallas kernels  5.74 us (16%)
  other arithmetic  0.85 us (2%)
  between operations  0.79 us (2%)
    ppermute x15, starting transfers between devices, hop(): return lax.ppermute(value, 'col', pairs)  19.9 us
    ppermute x15, waiting for transfers between devices, hop(): return lax.ppermute(value, 'col', pairs)  7.6 us
    pallas_call x1, Pallas kernels, per_device(): pl.pallas_call(prepare_kernel, out_shape=(terms_type,) * 4 + (pltpu.VMEM(...  1.92 us
    pallas_call x1, Pallas kernels, per_device(): pl.pallas_call(functools.partial(columns_kernel, total_rows, chunk), out_...  1.88 us
    pallas_call x2, Pallas kernels, gradient_of(): pl.pallas_call(functools.partial(rows_kernel, chunk), out_shape=(pltpu.VM...  1.21 us
    pallas_call x1, Pallas kernels, per_device(): pl.pallas_call(place_kernel, out_shape=jax.ShapeDtypeStruct(grid + (width...  0.72 us
  transfers between devices with their start and end apart: 15, of which 7 were waited for; matrix products, arithmetic and copies ran while one was open for 2% of the time, Pallas kernels for 14%

profile of v9, /device:TPU:0, one launch (start us, length us, event | category | flops | bytes accessed | tf_op | source)
XLA Modules:
  0.0 34.9 jit_solution(7386322844137637749)
XLA Ops:
  0.6 3.5 %collective-permute-start = (f32[1,32,256]{2,1,0:T(8,128)}, f32[1,32,256]{2,1,0:T(8,128)S(1)}, u32[]{:S(2)}, u32[]{:S(2)}) collective-permute-start(f32[1,32,256]{2,1,0:T(8,128)} %bitcast.74), channel_id=1, source_target_pairs={{0,9},{1,8},{2,11},{3,10},{4,13},{5,12},{6,15},{7,14},{8,1},{9,0},... | collective-permute-start | bytes 98312 | tf_op jit(solution)/shard_map/ppermute | solution.py:33
  4.2 1.9 %prepare.1 = (f32[2,4,32,512]{3,2,1,0:T(8,128)S(1)}, f32[2,4,32,512]{3,2,1,0:T(8,128)S(1)}, f32[2,4,32,512]{3,2,1,0:T(8,128)S(1)}, f32[2,4,32,512]{3,2,1,0:T(8,1...) custom-call(s32[2,2,2,2,32,512]{5,4,3,2,1,0:T(8,128)} %bitcast.69, ...), custom_call_target="tpu_custom_call" | custom-call | flops 2097152 | bytes 1048576 | tf_op jit(solution)/shard_map/prepare/pallas_call | solution.py:185
  6.1 0.1 collective-permute-done.refs_0_
  6.3 1.8 %collective-permute-start.1 = (bf16[2,32,256]{2,1,0:T(8,128)(2,1)S(1)}, bf16[2,32,256]{2,1,0:T(8,128)(2,1)S(1)}, u32[]{:S(2)}, u32[]{:S(2)}) collective-permute-start(bf16[2,32,256]{2,1,0:T(8,128)(2,1)S(1)} %maximum_bitcast_fusion), channel_id=1, source_target_pairs={{0,5},{1,2},{2,1},{3,6},{4,7},{5,0},{6,3},{7,4},{8,11},{9,12},{10,... | collective-permute-start | bytes 98312 | tf_op jit(solution)/shard_map/ppermute | solution.py:33
  8.1 0.3 collective-permute-start.2
  8.4 0.2 collective-permute-start.3
  8.6 0.3 collective-permute-start.5
  8.9 0.8 %collective-permute-done.1 = bf16[2,32,256]{2,1,0:T(8,128)(2,1)S(1)} collective-permute-done((bf16[2,32,256]{2,1,0:T(8,128)(2,1)S(1)}, bf16[2,32,256]{2,1,0:T(8,128)(2,1)S(1)}, u32[]{:S(2)}, u32[]{:S(2)}) %collective-permute-start.1) | collective-permute-done | bytes 32800 | tf_op jit(solution)/shard_map/ppermute | solution.py:33
  9.7 1.7 %collective-permute-start.4 = (bf16[128,256]{1,0:T(8,128)(2,1)S(1)}, bf16[128,256]{1,0:T(8,128)(2,1)S(1)}, u32[]{:S(2)}, u32[]{:S(2)}) collective-permute-start(bf16[128,256]{1,0:T(8,128)(2,1)S(1)} %bitcast.63), channel_id=1, source_target_pairs={{0,3},{1,4},{2,7},{3,0},{4,1},{5,6},{6,5},{7,2},{8,13},{9,10},{10,... | collective-permute-start | bytes 196616 | tf_op jit(solution)/shard_map/ppermute | solution.py:33
  11.5 3.0 %collective-permute-start.9 = (bf16[1,32,256]{2,1,0:T(8,128)(2,1)S(1)}, bf16[1,32,256]{2,1,0:T(8,128)(2,1)S(1)}, u32[]{:S(2)}, u32[]{:S(2)}) collective-permute-start(bf16[1,32,256]{2,1,0:T(8,128)(2,1)S(1)} %bitcast.67), channel_id=1, source_target_pairs={{0,9},{1,8},{2,11},{3,10},{4,13},{5,12},{6,15},{7,14},{8,1},{9,0},... | collective-permute-start | bytes 49160 | tf_op jit(solution)/shard_map/ppermute | solution.py:33
  14.4 0.0 collective-permute-done.4.rows.beside
  14.5 0.0 collective-permute-done.3.other_columns
  14.5 0.0 collective-permute-done.5.received
  14.5 0.6 %rows.5 = (f32[128,256]{1,0:T(8,128)S(1)}, bf16[128,512]{1,0:T(8,128)(2,1)S(1)}) custom-call(bf16[128,256]{1,0:T(8,128)(2,1)S(1)} %collective-permute-done.4.rows.beside, f32[2,4,32,512]{3,2,1,0:T(8,128)S(1)} %get-tuple-element.30.kept, f32[2,4,32,512]{3,2,1,0:T(8,128)S(1)} %collective-permute-done.5.received, ...), custom_call_target="tpu_custom_call" | custom-call | flops 134217728 | tf_op jit(solution)/shard_map/rows/pallas_call | solution.py:227
  15.1 0.8 %collective-permute-start.6 = (bf16[128,256]{1,0:T(8,128)(2,1)S(1)}, bf16[128,256]{1,0:T(8,128)(2,1)S(1)}, u32[]{:S(2)}, u32[]{:S(2)}) collective-permute-start(bf16[128,256]{1,0:T(8,128)(2,1)S(1)} %convert_element_type.46), channel_id=1, source_target_pairs={{0,3},{1,4},{2,7},{3,0},{4,1},{5,6},{6,5},{7,2},{8,13},{9,10},{10,... | collective-permute-start | bytes 196616 | tf_op jit(solution)/shard_map/ppermute | solution.py:33
  15.9 0.0 collective-permute-done.9
  15.9 0.7 %collective-permute-start.10 = (bf16[256,256]{1,0:T(8,128)(2,1)S(1)}, bf16[256,256]{1,0:T(8,128)(2,1)S(1)}, u32[]{:S(2)}, u32[]{:S(2)}) collective-permute-start(bf16[256,256]{1,0:T(8,128)(2,1)S(1)} %pad_maximum_fusion), channel_id=1, source_target_pairs={{0,1},{1,0},{2,3},{3,2},{4,5},{5,4},{6,7},{7,6},{8,9},{9,8},{10,11... | collective-permute-start | bytes 393224 | tf_op jit(solution)/shard_map/ppermute | solution.py:33
  16.6 0.0 collective-permute-done.2.received
  16.6 0.0 copy-start
  16.6 0.0 copy-start.1
  16.6 0.6 %rows.4 = (f32[128,256]{1,0:T(8,128)S(1)}, bf16[128,512]{1,0:T(8,128)(2,1)S(1)}) custom-call(bf16[128,256]{1,0:T(8,128)(2,1)S(1)} %bitcast.65, f32[2,4,32,512]{3,2,1,0:T(8,128)S(1)} %get-tuple-element.26.kept, f32[2,4,32,512]{3,2,1,0:T(8,128)S(1)} %collective-permute-done.2.received, bf16[512,256]{1,0:T(8,128)(2,1)S(1)} %get-tuple-element.28.columns, ...), custom_call_target="tpu_custom_call" | custom-call | flops 134217728 | tf_op jit(solution)/shard_map/rows/pallas_call | solution.py:227
  17.2 1.7 %collective-permute-done.6 = bf16[128,256]{1,0:T(8,128)(2,1)S(1)} collective-permute-done((bf16[128,256]{1,0:T(8,128)(2,1)S(1)}, bf16[128,256]{1,0:T(8,128)(2,1)S(1)}, u32[]{:S(2)}, u32[]{:S(2)}) %collective-permute-start.6) | collective-permute-done | bytes 65568 | tf_op jit(solution)/shard_map/ppermute | solution.py:33
  18.9 2.5 %collective-permute-start.7 = (bf16[128,256]{1,0:T(8,128)(2,1)S(1)}, bf16[128,256]{1,0:T(8,128)(2,1)S(1)}, u32[]{:S(2)}, u32[]{:S(2)}) collective-permute-start(bf16[128,256]{1,0:T(8,128)(2,1)S(1)} %add_convert_fusion.1), channel_id=1, source_target_pairs={{0,9},{1,8},{2,11},{3,10},{4,13},{5,12},{6,15},{7,14},{8,1},{9,0},... | collective-permute-start | bytes 196616 | tf_op jit(solution)/shard_map/ppermute | solution.py:33
  21.4 0.0 collective-permute-done.10.others
  21.4 0.0 copy-done
  21.4 0.0 copy-done.1
  21.4 1.9 %columns.3 = (f32[512,256]{1,0:T(8,128)}, f32[512,256]{1,0:T(8,128)}) custom-call(f32[512,256]{1,0:T(8,128)S(1)} %copy-done, f32[512,256]{1,0:T(8,128)S(1)} %copy-done.1, bf16[512,256]{1,0:T(8,128)(2,1)S(1)} %get-tuple-element.28.columns, f32[2,4,32,512]{3,2,1,0:T(8,128)S(1)} %get-tuple-element.27.sent_0, f32[2,4,32,512]{3,2,1,0:T(8,128)S(1)} %get-tuple-element.31.sent_1, ...), custom_call_target="tpu_custom_call" | custom-call | flops 134217728 | bytes 2097152 | tf_op jit(solution)/shard_map/columns/pallas_call | solution.py:244
  23.3 1.7 %collective-permute-start.11 = (bf16[2,32,256]{2,1,0:T(8,128)(2,1)S(1)}, bf16[2,32,256]{2,1,0:T(8,128)(2,1)S(1)}, u32[]{:S(2)}, u32[]{:S(2)}) collective-permute-start(bf16[2,32,256]{2,1,0:T(8,128)(2,1)S(1)} %maximum_bitcast_fusion.1), channel_id=1, source_target_pairs={{0,5},{1,2},{2,1},{3,6},{4,7},{5,0},{6,3},{7,4},{8,11},{9,12},{10,... | collective-permute-start | bytes 98312 | tf_op jit(solution)/shard_map/ppermute | solution.py:33
  25.1 0.0 collective-permute-done.7
  25.1 0.9 %collective-permute-start.8 = (bf16[128,256]{1,0:T(8,128)(2,1)S(1)}, bf16[128,256]{1,0:T(8,128)(2,1)S(1)}, u32[]{:S(2)}, u32[]{:S(2)}) collective-permute-start(bf16[128,256]{1,0:T(8,128)(2,1)S(1)} %add_convert_fusion), channel_id=1, source_target_pairs={{0,5},{1,2},{2,1},{3,6},{4,7},{5,0},{6,3},{7,4},{8,11},{9,12},{10,... | collective-permute-start | bytes 196616 | tf_op jit(solution)/shard_map/ppermute | solution.py:33
  26.0 0.7 %collective-permute-done.11 = bf16[2,32,256]{2,1,0:T(8,128)(2,1)S(1)} collective-permute-done((bf16[2,32,256]{2,1,0:T(8,128)(2,1)S(1)}, bf16[2,32,256]{2,1,0:T(8,128)(2,1)S(1)}, u32[]{:S(2)}, u32[]{:S(2)}) %collective-permute-start.11) | collective-permute-done | bytes 32800 | tf_op jit(solution)/shard_map/ppermute | solution.py:33
  26.7 2.1 %collective-permute-done.8 = bf16[128,256]{1,0:T(8,128)(2,1)S(1)} collective-permute-done((bf16[128,256]{1,0:T(8,128)(2,1)S(1)}, bf16[128,256]{1,0:T(8,128)(2,1)S(1)}, u32[]{:S(2)}, u32[]{:S(2)}) %collective-permute-start.8) | collective-permute-done | bytes 65568 | tf_op jit(solution)/shard_map/ppermute | solution.py:33
  28.9 0.0 copy-start.3
  28.9 0.0 copy-start.2
  29.0 1.9 %collective-permute-start.12 = (bf16[4,32,256]{2,1,0:T(8,128)(2,1)S(1)}, bf16[4,32,256]{2,1,0:T(8,128)(2,1)S(1)}, u32[]{:S(2)}, u32[]{:S(2)}) collective-permute-start(bf16[4,32,256]{2,1,0:T(8,128)(2,1)S(1)} %fusion.3.refs_0_), channel_id=1, source_target_pairs={{0,3},{1,4},{2,7},{3,0},{4,1},{5,6},{6,5},{7,2},{8,13},{9,10},{10,... | collective-permute-start | bytes 196616 | tf_op jit(solution)/shard_map/ppermute | solution.py:33
  30.8 0.0 collective-permute-start.13
  30.8 1.9 %collective-permute-done.12.refs_1_ = bf16[4,32,256]{2,1,0:T(8,128)(2,1)S(1)} collective-permute-done((bf16[4,32,256]{2,1,0:T(8,128)(2,1)S(1)}, bf16[4,32,256]{2,1,0:T(8,128)(2,1)S(1)}, u32[]{:S(2)}, u32[]{:S(2)}) %collective-permute-start.12) | collective-permute-done | bytes 65568 | tf_op jit(solution)/shard_map/ppermute | solution.py:33
  32.8 0.5 %collective-permute-start.14 = (bf16[4,32,256]{2,1,0:T(8,128)(2,1)S(1)}, bf16[4,32,256]{2,1,0:T(8,128)(2,1)S(1)}, u32[]{:S(2)}, u32[]{:S(2)}) collective-permute-start(bf16[4,32,256]{2,1,0:T(8,128)(2,1)S(1)} %collective-permute-done.12.refs_1_), channel_id=1, source_target_pairs={{0,1},{1,0},{2,3},{3,2},{4,5},{5,4},{6,7},{7,6},{8,9},{9,8},{10,11... | collective-permute-start | bytes 196616 | tf_op jit(solution)/shard_map/ppermute | solution.py:33
  33.3 0.0 copy-done.3
  33.3 0.0 copy-done.2
  33.3 0.6 %fusion.6 = (f32[32,256]{1,0:T(8,128)}, f32[32,256]{1,0:T(8,128)}) fusion(f32[32,256]{1,0:T(8,128)S(1)} %copy-done.2, f32[4,32,256]{2,1,0:T(8,128)S(1)} %bitcast.71, s32[]{:T(128)S(6)} %select_n.39, f32[32,256]{1,0:T(8,128)S(1)} %copy-done.3), kind=kLoop, calls=%fused_computation.17 | loop fusion | flops 40960 | bytes 163844 | tf_op jit(solution)/shard_map/sub | solution.py:264
  33.9 0.0 collective-permute-done.13.refs_2_
  33.9 0.3 collective-permute-done.14.refs_3_
  34.2 0.7 %place.1 = bf16[2,2,2,2,32,256]{5,4,3,2,1,0:T(8,128)(2,1)} custom-call(bf16[4,32,256]{2,1,0:T(8,128)(2,1)S(1)} %fusion.3.refs_0_, bf16[4,32,256]{2,1,0:T(8,128)(2,1)S(1)} %collective-permute-done.12.refs_1_, bf16[4,32,256]{2,1,0:T(8,128)(2,1)S(1)} %collective-permute-done.13.refs_2_, bf16[4,32,256]{2,1,0:T(8,128)(2,1)S(1)} %collective-permute-done.14.refs_3_), custom_call_target="tpu_custom_call" | custom-call | tf_op jit(solution)/shard_map/place/pallas_call | solution.py:271
  (18 shorter events, 0.2 us)
Async XLA Ops:
  0.6 5.6 %collective-permute-start = (f32[1,32,256]{2,1,0:T(8,128)}, f32[1,32,256]{2,1,0:T(8,128)S(1)}, u32[]{:S(2)}, u32[]{:S(2)}) collective-permute-start(f32[1,32,256]{2,1,0:T(8,128)} %bitcast.74), channel_id=1, source_target_pairs={{0,9},{1,8},{2,11},{3,10},{4,13},{5,12},{6,15},{7,14},{8,1},{9,0},... | collective-permute-start | bytes 98312 | tf_op jit(solution)/shard_map/ppermute | solution.py:33
  6.3 3.4 %collective-permute-start.1 = (bf16[2,32,256]{2,1,0:T(8,128)(2,1)S(1)}, bf16[2,32,256]{2,1,0:T(8,128)(2,1)S(1)}, u32[]{:S(2)}, u32[]{:S(2)}) collective-permute-start(bf16[2,32,256]{2,1,0:T(8,128)(2,1)S(1)} %maximum_bitcast_fusion), channel_id=1, source_target_pairs={{0,5},{1,2},{2,1},{3,6},{4,7},{5,0},{6,3},{7,4},{8,11},{9,12},{10,... | collective-permute-start | bytes 98312 | tf_op jit(solution)/shard_map/ppermute | solution.py:33
  8.1 8.5 %collective-permute-start.2 = (f32[2,4,32,512]{3,2,1,0:T(8,128)S(1)}, f32[2,4,32,512]{3,2,1,0:T(8,128)S(1)}, u32[]{:S(2)}, u32[]{:S(2)}) collective-permute-start(f32[2,4,32,512]{3,2,1,0:T(8,128)S(1)} %get-tuple-element.27.sent_0), channel_id=1, source_target_pairs={{0,1},{1,0},{2,3},{3,2},{4,5},{5,4},{6,7},{7,6},{8,9},{9,8},{10,11... | collective-permute-start | bytes 1572872 | tf_op jit(solution)/shard_map/ppermute | solution.py:33
  8.4 6.1 %collective-permute-start.3 = (bf16[512,256]{1,0:T(8,128)(2,1)S(1)}, bf16[512,256]{1,0:T(8,128)(2,1)S(1)}, u32[]{:S(2)}, u32[]{:S(2)}) collective-permute-start(bf16[512,256]{1,0:T(8,128)(2,1)S(1)} %get-tuple-element.28.columns), channel_id=1, source_target_pairs={{0,1},{1,0},{2,3},{3,2},{4,5},{5,4},{6,7},{7,6},{8,9},{9,8},{10,11... | collective-permute-start | bytes 786440 | tf_op jit(solution)/shard_map/ppermute | solution.py:33
  8.6 5.9 %collective-permute-start.5 = (f32[2,4,32,512]{3,2,1,0:T(8,128)S(1)}, f32[2,4,32,512]{3,2,1,0:T(8,128)S(1)}, u32[]{:S(2)}, u32[]{:S(2)}) collective-permute-start(f32[2,4,32,512]{3,2,1,0:T(8,128)S(1)} %get-tuple-element.31.sent_1), channel_id=1, source_target_pairs={{0,1},{1,0},{2,3},{3,2},{4,5},{5,4},{6,7},{7,6},{8,9},{9,8},{10,11... | collective-permute-start | bytes 1572872 | tf_op jit(solution)/shard_map/ppermute | solution.py:33
  9.7 4.7 %collective-permute-start.4 = (bf16[128,256]{1,0:T(8,128)(2,1)S(1)}, bf16[128,256]{1,0:T(8,128)(2,1)S(1)}, u32[]{:S(2)}, u32[]{:S(2)}) collective-permute-start(bf16[128,256]{1,0:T(8,128)(2,1)S(1)} %bitcast.63), channel_id=1, source_target_pairs={{0,3},{1,4},{2,7},{3,0},{4,1},{5,6},{6,5},{7,2},{8,13},{9,10},{10,... | collective-permute-start | bytes 196616 | tf_op jit(solution)/shard_map/ppermute | solution.py:33
  11.5 4.4 %collective-permute-start.9 = (bf16[1,32,256]{2,1,0:T(8,128)(2,1)S(1)}, bf16[1,32,256]{2,1,0:T(8,128)(2,1)S(1)}, u32[]{:S(2)}, u32[]{:S(2)}) collective-permute-start(bf16[1,32,256]{2,1,0:T(8,128)(2,1)S(1)} %bitcast.67), channel_id=1, source_target_pairs={{0,9},{1,8},{2,11},{3,10},{4,13},{5,12},{6,15},{7,14},{8,1},{9,0},... | collective-permute-start | bytes 49160 | tf_op jit(solution)/shard_map/ppermute | solution.py:33
  15.1 3.8 %collective-permute-start.6 = (bf16[128,256]{1,0:T(8,128)(2,1)S(1)}, bf16[128,256]{1,0:T(8,128)(2,1)S(1)}, u32[]{:S(2)}, u32[]{:S(2)}) collective-permute-start(bf16[128,256]{1,0:T(8,128)(2,1)S(1)} %convert_element_type.46), channel_id=1, source_target_pairs={{0,3},{1,4},{2,7},{3,0},{4,1},{5,6},{6,5},{7,2},{8,13},{9,10},{10,... | collective-permute-start | bytes 196616 | tf_op jit(solution)/shard_map/ppermute | solution.py:33
  15.9 5.5 %collective-permute-start.10 = (bf16[256,256]{1,0:T(8,128)(2,1)S(1)}, bf16[256,256]{1,0:T(8,128)(2,1)S(1)}, u32[]{:S(2)}, u32[]{:S(2)}) collective-permute-start(bf16[256,256]{1,0:T(8,128)(2,1)S(1)} %pad_maximum_fusion), channel_id=1, source_target_pairs={{0,1},{1,0},{2,3},{3,2},{4,5},{5,4},{6,7},{7,6},{8,9},{9,8},{10,11... | collective-permute-start | bytes 393224 | tf_op jit(solution)/shard_map/ppermute | solution.py:33
  16.6 4.8 %copy-start = (f32[512,256]{1,0:T(8,128)S(1)}, f32[512,256]{1,0:T(8,128)}, u32[]{:S(2)}) copy-start(f32[512,256]{1,0:T(8,128)} %master.1) | copy-start | bytes 1572868
  16.6 4.8 %copy-start.1 = (f32[512,256]{1,0:T(8,128)S(1)}, f32[512,256]{1,0:T(8,128)}, u32[]{:S(2)}) copy-start(f32[512,256]{1,0:T(8,128)} %history.3) | copy-start | bytes 1572868
  18.9 6.2 %collective-permute-start.7 = (bf16[128,256]{1,0:T(8,128)(2,1)S(1)}, bf16[128,256]{1,0:T(8,128)(2,1)S(1)}, u32[]{:S(2)}, u32[]{:S(2)}) collective-permute-start(bf16[128,256]{1,0:T(8,128)(2,1)S(1)} %add_convert_fusion.1), channel_id=1, source_target_pairs={{0,9},{1,8},{2,11},{3,10},{4,13},{5,12},{6,15},{7,14},{8,1},{9,0},... | collective-permute-start | bytes 196616 | tf_op jit(solution)/shard_map/ppermute | solution.py:33
  23.3 3.3 %collective-permute-start.11 = (bf16[2,32,256]{2,1,0:T(8,128)(2,1)S(1)}, bf16[2,32,256]{2,1,0:T(8,128)(2,1)S(1)}, u32[]{:S(2)}, u32[]{:S(2)}) collective-permute-start(bf16[2,32,256]{2,1,0:T(8,128)(2,1)S(1)} %maximum_bitcast_fusion.1), channel_id=1, source_target_pairs={{0,5},{1,2},{2,1},{3,6},{4,7},{5,0},{6,3},{7,4},{8,11},{9,12},{10,... | collective-permute-start | bytes 98312 | tf_op jit(solution)/shard_map/ppermute | solution.py:33
  25.1 3.8 %collective-permute-start.8 = (bf16[128,256]{1,0:T(8,128)(2,1)S(1)}, bf16[128,256]{1,0:T(8,128)(2,1)S(1)}, u32[]{:S(2)}, u32[]{:S(2)}) collective-permute-start(bf16[128,256]{1,0:T(8,128)(2,1)S(1)} %add_convert_fusion), channel_id=1, source_target_pairs={{0,5},{1,2},{2,1},{3,6},{4,7},{5,0},{6,3},{7,4},{8,11},{9,12},{10,... | collective-permute-start | bytes 196616 | tf_op jit(solution)/shard_map/ppermute | solution.py:33
  28.9 4.4 %copy-start.3 = (f32[32,256]{1,0:T(8,128)S(1)}, f32[32,256]{1,0:T(8,128)}, u32[]{:S(2)}) copy-start(f32[32,256]{1,0:T(8,128)} %history.2) | copy-start | bytes 98308
  28.9 4.3 %copy-start.2 = (f32[32,256]{1,0:T(8,128)S(1)}, f32[32,256]{1,0:T(8,128)}, u32[]{:S(2)}) copy-start(f32[32,256]{1,0:T(8,128)} %rows.3) | copy-start | bytes 98308
  29.0 3.8 %collective-permute-start.12 = (bf16[4,32,256]{2,1,0:T(8,128)(2,1)S(1)}, bf16[4,32,256]{2,1,0:T(8,128)(2,1)S(1)}, u32[]{:S(2)}, u32[]{:S(2)}) collective-permute-start(bf16[4,32,256]{2,1,0:T(8,128)(2,1)S(1)} %fusion.3.refs_0_), channel_id=1, source_target_pairs={{0,3},{1,4},{2,7},{3,0},{4,1},{5,6},{6,5},{7,2},{8,13},{9,10},{10,... | collective-permute-start | bytes 196616 | tf_op jit(solution)/shard_map/ppermute | solution.py:33
  30.8 3.1 %collective-permute-start.13 = (bf16[4,32,256]{2,1,0:T(8,128)(2,1)S(1)}, bf16[4,32,256]{2,1,0:T(8,128)(2,1)S(1)}, u32[]{:S(2)}, u32[]{:S(2)}) collective-permute-start(bf16[4,32,256]{2,1,0:T(8,128)(2,1)S(1)} %fusion.3.refs_0_), channel_id=1, source_target_pairs={{0,1},{1,0},{2,3},{3,2},{4,5},{5,4},{6,7},{7,6},{8,9},{9,8},{10,11... | collective-permute-start | bytes 196616 | tf_op jit(solution)/shard_map/ppermute | solution.py:33
  32.8 1.4 %collective-permute-start.14 = (bf16[4,32,256]{2,1,0:T(8,128)(2,1)S(1)}, bf16[4,32,256]{2,1,0:T(8,128)(2,1)S(1)}, u32[]{:S(2)}, u32[]{:S(2)}) collective-permute-start(bf16[4,32,256]{2,1,0:T(8,128)(2,1)S(1)} %collective-permute-done.12.refs_1_), channel_id=1, source_target_pairs={{0,1},{1,0},{2,3},{3,2},{4,5},{5,4},{6,7},{7,6},{8,9},{9,8},{10,11... | collective-permute-start | bytes 196616 | tf_op jit(solution)/shard_map/ppermute | solution.py:33

commit v10 on v9

--- a/solution.py
+++ b/solution.py
@@ -108,25 +108,32 @@
     history_copy[...] = near_history[...].astype(jnp.bfloat16)
 
 
-def slopes_of(rows, columns, terms, step, chunk):
+def slopes_of(rows, columns, terms, step, chunk, at_columns=slice(None)):
     group = chunk // terms.shape[2]
     at = pl.ds(step * group, group)
     scores = lax.dot_general(rows, columns, (((1,), (1,)), ((), ())), preferred_element_type=jnp.float32)
-    gap = scores - terms[0, at].reshape(scores.shape)
-    confidence = terms[1, at].reshape(scores.shape)
+    gap = scores - terms[0, at, :, at_columns].reshape(scores.shape)
+    confidence = terms[1, at, :, at_columns].reshape(scores.shape)
     return jnp.where(confidence > 0, confidence * gap, jax.nn.sigmoid(gap)).astype(jnp.bfloat16)
 
 
 def rows_kernel(chunk, rows, kept, received, columns, other_columns, *refs):
     gradient, slopes = refs[-2:]
+    half = columns.shape[0] // 2
 
     def body(step):
         at = pl.ds(pl.multiple_of(step * chunk, chunk), chunk)
-        own = slopes_of(rows[at, :], columns[...], kept, step, chunk)
-        slopes[at, :] = own
-        gradient[at, :] = jnp.dot(own, columns[...], preferred_element_type=jnp.float32)
-        other = slopes_of(rows[at, :], other_columns[...], received, step, chunk)
-        gradient[at, :] += jnp.dot(other, other_columns[...], preferred_element_type=jnp.float32)
+        total = None
+        for terms, source in ((kept, columns), (received, other_columns)):
+            for first in (0, half):
+                at_columns = slice(first, first + half)
+                block = source[at_columns, :]
+                part = slopes_of(rows[at, :], block, terms, step, chunk, at_columns)
+                if source is columns:
+                    slopes[at, at_columns] = part
+                part = jnp.dot(part, block, preferred_element_type=jnp.float32)
+                total = part if total is None else total + part
+        gradient[at, :] = total.astype(gradient.dtype)
 
     steps_of(rows.shape[0] // chunk, body)
 
@@ -223,10 +230,10 @@
     for bits, upper in steps[:-1]:
         history = joined(history, hop(history, bits, size), upper)
 
-    def gradient_of(rows, kept, received, *after):
+    def gradient_of(kind, rows, kept, received, *after):
         return pl.pallas_call(
             functools.partial(rows_kernel, chunk),
-            out_shape=(pltpu.VMEM((group_rows, width), jnp.float32), pltpu.VMEM((group_rows, block_columns), jnp.bfloat16)),
+            out_shape=(pltpu.VMEM((group_rows, width), kind), pltpu.VMEM((group_rows, block_columns), jnp.bfloat16)),
             in_specs=[VMEM] * 5 + [ANY] * len(after),
             out_specs=[VMEM] * 2,
             compiler_params=PARAMS,
@@ -234,12 +241,13 @@
             name="rows",
         )(*[near(v) for v in (rows, kept, received, column_copy, other_columns)], *after)
 
-    part_late, slopes_1 = gradient_of(beside, kept_1, received_1)
-    part_early, slopes_0 = gradient_of(mine, kept_0, received_0, first_hop)
+    part_late, slopes_1 = gradient_of(jnp.bfloat16, beside, kept_1, received_1)
+    part_early, slopes_0 = gradient_of(jnp.float32, mine, kept_0, received_0, first_hop)
     own_rows, part_late = lax.optimization_barrier((jnp.concatenate([mine, beside]), part_late))
     others = hop(own_rows, CORE, size)
-
-    part = part_early + hop(part_late.astype(jnp.bfloat16), SPLIT, size).astype(jnp.float32)
+    others, history = lax.optimization_barrier((others, history))
+
+    part = part_early + hop(part_late, SPLIT, size).astype(jnp.float32)
     struct = jax.ShapeDtypeStruct(column_master.shape, jnp.float32)
     new_columns, new_column_history = pl.pallas_call(
         functools.partial(columns_kernel, total_rows, chunk),
@@ -252,7 +260,6 @@
         name="columns",
     )(*[near(v) for v in (column_master, column_history, column_copy, sent_0, sent_1, mine, beside, others, slopes_0, slopes_1)])
 
-    history, new_columns = lax.optimization_barrier((history, new_columns))
     last_history = hop(history, SUM, size)
     for bits, upper in steps:
         rounded = part.astype(jnp.bfloat16)
@@ -268,6 +275,7 @@
     new_rows, new_row_history = adagrad(row_master, row_history, own_gradient)
     copy = adagrad(master.astype(jnp.float32), history.astype(jnp.float32), gradient)[0].astype(jnp.bfloat16)
     beside = hop(copy, SPLIT, size)
+    beside, new_columns = lax.optimization_barrier((beside, new_columns))
     grid_rows = pl.pallas_call(
         place_kernel,
         out_shape=jax.ShapeDtypeStruct(grid + (width,), jnp.bfloat16),

time: 35.1 us -> 34.9 us (level)
  starting transfers between devices: 19.9 us -> 22.4 us
  waiting for transfers between devices: 7.6 us -> 5.15 us
    ppermute x15, starting transfers between devices: 19.9 us -> 22.4 us  [hop(): return lax.ppermute(value, 'col', pairs)]
    ppermute x15, waiting for transfers between devices: 7.6 us -> 5.15 us  [hop(): return lax.ppermute(value, 'col', pairs)]
where the time goes in v10:
time: 34.9 us; the launch traced here: 34.7 us
  starting transfers between devices  22.4 us (64%)
  Pallas kernels  5.54 us (16%)
  waiting for transfers between devices  5.15 us (15%)
  other arithmetic  0.84 us (2%)
  between operations  0.78 us (2%)
    ppermute x15, starting transfers between devices, hop(): return lax.ppermute(value, 'col', pairs)  22.4 us
    ppermute x15, waiting for transfers between devices, hop(): return lax.ppermute(value, 'col', pairs)  5.15 us
    pallas_call x1, Pallas kernels, per_device(): pl.pallas_call(prepare_kernel, out_shape=(terms_type,) * 4 + (pltpu.VMEM(...  1.92 us
    pallas_call x1, Pallas kernels, per_device(): pl.pallas_call(functools.partial(columns_kernel, total_rows, chunk), out_...  1.88 us
    pallas_call x2, Pallas kernels, gradient_of(): pl.pallas_call(functools.partial(rows_kernel, chunk), out_shape=(pltpu.VM...  1.01 us
    pallas_call x1, Pallas kernels, per_device(): pl.pallas_call(place_kernel, out_shape=jax.ShapeDtypeStruct(grid + (width...  0.72 us
  transfers between devices with their start and end apart: 15, of which 7 were waited for; matrix products, arithmetic and copies ran while one was open for 2% of the time, Pallas kernels for 14%

profile of v10, /device:TPU:0, one launch (start us, length us, event | category | flops | bytes accessed | tf_op | source)
XLA Modules:
  0.0 34.7 jit_solution(411734039408905280)
XLA Ops:
  0.6 3.5 %collective-permute-start = (f32[1,32,256]{2,1,0:T(8,128)}, f32[1,32,256]{2,1,0:T(8,128)S(1)}, u32[]{:S(2)}, u32[]{:S(2)}) collective-permute-start(f32[1,32,256]{2,1,0:T(8,128)} %bitcast.74), channel_id=1, source_target_pairs={{0,9},{1,8},{2,11},{3,10},{4,13},{5,12},{6,15},{7,14},{8,1},{9,0},... | collective-permute-start | bytes 98312 | tf_op jit(solution)/shard_map/ppermute | solution.py:33
  4.2 1.9 %prepare.1 = (f32[2,4,32,512]{3,2,1,0:T(8,128)S(1)}, f32[2,4,32,512]{3,2,1,0:T(8,128)S(1)}, f32[2,4,32,512]{3,2,1,0:T(8,128)S(1)}, f32[2,4,32,512]{3,2,1,0:T(8,1...) custom-call(s32[2,2,2,2,32,512]{5,4,3,2,1,0:T(8,128)} %bitcast.69, ...), custom_call_target="tpu_custom_call" | custom-call | flops 2097152 | bytes 1048576 | tf_op jit(solution)/shard_map/prepare/pallas_call | solution.py:192
  6.1 0.1 collective-permute-done.refs_0_
  6.3 1.8 %collective-permute-start.1 = (bf16[2,32,256]{2,1,0:T(8,128)(2,1)S(1)}, bf16[2,32,256]{2,1,0:T(8,128)(2,1)S(1)}, u32[]{:S(2)}, u32[]{:S(2)}) collective-permute-start(bf16[2,32,256]{2,1,0:T(8,128)(2,1)S(1)} %maximum_bitcast_fusion), channel_id=1, source_target_pairs={{0,5},{1,2},{2,1},{3,6},{4,7},{5,0},{6,3},{7,4},{8,11},{9,12},{10,... | collective-permute-start | bytes 98312 | tf_op jit(solution)/shard_map/ppermute | solution.py:33
  8.1 0.3 collective-permute-start.2
  8.4 0.2 collective-permute-start.3
  8.6 0.3 collective-permute-start.5
  8.9 0.8 %collective-permute-done.1 = bf16[2,32,256]{2,1,0:T(8,128)(2,1)S(1)} collective-permute-done((bf16[2,32,256]{2,1,0:T(8,128)(2,1)S(1)}, bf16[2,32,256]{2,1,0:T(8,128)(2,1)S(1)}, u32[]{:S(2)}, u32[]{:S(2)}) %collective-permute-start.1) | collective-permute-done | bytes 32800 | tf_op jit(solution)/shard_map/ppermute | solution.py:33
  9.7 1.7 %collective-permute-start.4 = (bf16[128,256]{1,0:T(8,128)(2,1)S(1)}, bf16[128,256]{1,0:T(8,128)(2,1)S(1)}, u32[]{:S(2)}, u32[]{:S(2)}) collective-permute-start(bf16[128,256]{1,0:T(8,128)(2,1)S(1)} %bitcast.63), channel_id=1, source_target_pairs={{0,3},{1,4},{2,7},{3,0},{4,1},{5,6},{6,5},{7,2},{8,13},{9,10},{10,... | collective-permute-start | bytes 196616 | tf_op jit(solution)/shard_map/ppermute | solution.py:33
  11.5 3.0 %collective-permute-start.10 = (bf16[1,32,256]{2,1,0:T(8,128)(2,1)S(1)}, bf16[1,32,256]{2,1,0:T(8,128)(2,1)S(1)}, u32[]{:S(2)}, u32[]{:S(2)}) collective-permute-start(bf16[1,32,256]{2,1,0:T(8,128)(2,1)S(1)} %bitcast.67), channel_id=1, source_target_pairs={{0,9},{1,8},{2,11},{3,10},{4,13},{5,12},{6,15},{7,14},{8,1},{9,0},... | collective-permute-start | bytes 49160 | tf_op jit(solution)/shard_map/ppermute | solution.py:33
  14.4 0.0 collective-permute-done.4.rows.beside
  14.5 0.0 collective-permute-done.3.other_columns
  14.5 0.0 collective-permute-done.5.received
  14.5 0.5 %rows.5 = (bf16[128,256]{1,0:T(8,128)(2,1)S(1)}, bf16[128,512]{1,0:T(8,128)(2,1)S(1)}) custom-call(bf16[128,256]{1,0:T(8,128)(2,1)S(1)} %collective-permute-done.4.rows.beside, f32[2,4,32,512]{3,2,1,0:T(8,128)S(1)} %get-tuple-element.32.kept, f32[2,4,32,512]{3,2,1,0:T(8,128)S(1)} %collective-permute-done.5.received, ...), custom_call_target="tpu_custom_call" | custom-call | flops 134217728 | tf_op jit(solution)/shard_map/rows/pallas_call | solution.py:234
  15.0 0.8 %collective-permute-start.6 = (bf16[128,256]{1,0:T(8,128)(2,1)S(1)}, bf16[128,256]{1,0:T(8,128)(2,1)S(1)}, u32[]{:S(2)}, u32[]{:S(2)}) collective-permute-start(bf16[128,256]{1,0:T(8,128)(2,1)S(1)} %get-tuple-element.35), channel_id=1, source_target_pairs={{0,3},{1,4},{2,7},{3,0},{4,1},{5,6},{6,5},{7,2},{8,13},{9,10},{10,... | collective-permute-start | bytes 196616 | tf_op jit(solution)/shard_map/ppermute | solution.py:33
  15.8 0.1 collective-permute-done.10
  15.9 0.7 %collective-permute-start.9 = (bf16[256,256]{1,0:T(8,128)(2,1)S(1)}, bf16[256,256]{1,0:T(8,128)(2,1)S(1)}, u32[]{:S(2)}, u32[]{:S(2)}) collective-permute-start(bf16[256,256]{1,0:T(8,128)(2,1)S(1)} %pad_maximum_fusion), channel_id=1, source_target_pairs={{0,1},{1,0},{2,3},{3,2},{4,5},{5,4},{6,7},{7,6},{8,9},{9,8},{10,11... | collective-permute-start | bytes 393224 | tf_op jit(solution)/shard_map/ppermute | solution.py:33
  16.6 0.0 collective-permute-done.2.received
  16.6 0.5 %rows.4 = (f32[128,256]{1,0:T(8,128)S(1)}, bf16[128,512]{1,0:T(8,128)(2,1)S(1)}) custom-call(bf16[128,256]{1,0:T(8,128)(2,1)S(1)} %bitcast.65, f32[2,4,32,512]{3,2,1,0:T(8,128)S(1)} %get-tuple-element.28.kept, f32[2,4,32,512]{3,2,1,0:T(8,128)S(1)} %collective-permute-done.2.received, bf16[512,256]{1,0:T(8,128)(2,1)S(1)} %get-tuple-element.30.columns, ...), custom_call_target="tpu_custom_call" | custom-call | flops 134217728 | tf_op jit(solution)/shard_map/rows/pallas_call | solution.py:234
  17.1 1.7 %collective-permute-done.6 = bf16[128,256]{1,0:T(8,128)(2,1)S(1)} collective-permute-done((bf16[128,256]{1,0:T(8,128)(2,1)S(1)}, bf16[128,256]{1,0:T(8,128)(2,1)S(1)}, u32[]{:S(2)}, u32[]{:S(2)}) %collective-permute-start.6) | collective-permute-done | bytes 65568 | tf_op jit(solution)/shard_map/ppermute | solution.py:33
  18.8 2.5 %collective-permute-start.7 = (bf16[128,256]{1,0:T(8,128)(2,1)S(1)}, bf16[128,256]{1,0:T(8,128)(2,1)S(1)}, u32[]{:S(2)}, u32[]{:S(2)}) collective-permute-start(bf16[128,256]{1,0:T(8,128)(2,1)S(1)} %add_convert_fusion.1), channel_id=1, source_target_pairs={{0,9},{1,8},{2,11},{3,10},{4,13},{5,12},{6,15},{7,14},{8,1},{9,0},... | collective-permute-start | bytes 196616 | tf_op jit(solution)/shard_map/ppermute | solution.py:33
  21.3 0.0 collective-permute-done.9.others
  21.3 1.8 %collective-permute-start.11 = (bf16[2,32,256]{2,1,0:T(8,128)(2,1)S(1)}, bf16[2,32,256]{2,1,0:T(8,128)(2,1)S(1)}, u32[]{:S(2)}, u32[]{:S(2)}) collective-permute-start(bf16[2,32,256]{2,1,0:T(8,128)(2,1)S(1)} %maximum_bitcast_fusion.1), channel_id=1, source_target_pairs={{0,5},{1,2},{2,1},{3,6},{4,7},{5,0},{6,3},{7,4},{8,11},{9,12},{10,... | collective-permute-start | bytes 98312 | tf_op jit(solution)/shard_map/ppermute | solution.py:33
  23.1 0.3 collective-permute-done.7
  23.5 2.4 %collective-permute-start.8 = (bf16[128,256]{1,0:T(8,128)(2,1)S(1)}, bf16[128,256]{1,0:T(8,128)(2,1)S(1)}, u32[]{:S(2)}, u32[]{:S(2)}) collective-permute-start(bf16[128,256]{1,0:T(8,128)(2,1)S(1)} %add_convert_fusion), channel_id=1, source_target_pairs={{0,5},{1,2},{2,1},{3,6},{4,7},{5,0},{6,3},{7,4},{8,11},{9,12},{10,... | collective-permute-start | bytes 196616 | tf_op jit(solution)/shard_map/ppermute | solution.py:33
  25.9 0.0 collective-permute-done.11
  25.9 0.0 copy-start.1
  26.0 0.0 copy-start
  26.0 1.9 %collective-permute-done.8 = bf16[128,256]{1,0:T(8,128)(2,1)S(1)} collective-permute-done((bf16[128,256]{1,0:T(8,128)(2,1)S(1)}, bf16[128,256]{1,0:T(8,128)(2,1)S(1)}, u32[]{:S(2)}, u32[]{:S(2)}) %collective-permute-start.8) | collective-permute-done | bytes 65568 | tf_op jit(solution)/shard_map/ppermute | solution.py:33
  27.9 1.5 %collective-permute-start.12 = (bf16[4,32,256]{2,1,0:T(8,128)(2,1)S(1)}, bf16[4,32,256]{2,1,0:T(8,128)(2,1)S(1)}, u32[]{:S(2)}, u32[]{:S(2)}) collective-permute-start(bf16[4,32,256]{2,1,0:T(8,128)(2,1)S(1)} %fusion.3.refs_0_), channel_id=1, source_target_pairs={{0,3},{1,4},{2,7},{3,0},{4,1},{5,6},{6,5},{7,2},{8,13},{9,10},{10,... | collective-permute-start | bytes 196616 | tf_op jit(solution)/shard_map/ppermute | solution.py:33
  29.5 0.0 copy-done.1
  29.5 0.0 copy-done
  29.5 0.0 copy-start.2
  29.5 0.0 copy-start.3
  29.5 1.9 %columns.3 = (f32[512,256]{1,0:T(8,128)}, f32[512,256]{1,0:T(8,128)}) custom-call(f32[512,256]{1,0:T(8,128)S(1)} %copy-done, f32[512,256]{1,0:T(8,128)S(1)} %copy-done.1, bf16[512,256]{1,0:T(8,128)(2,1)S(1)} %get-tuple-element.30.columns, f32[2,4,32,512]{3,2,1,0:T(8,128)S(1)} %get-tuple-element.29.sent_0, f32[2,4,32,512]{3,2,1,0:T(8,128)S(1)} %get-tuple-element.33.sent_1, ...), custom_call_target="tpu_custom_call" | custom-call | flops 134217728 | bytes 2097152 | tf_op jit(solution)/shard_map/columns/pallas_call | solution.py:252
  31.4 0.7 %collective-permute-start.13 = (bf16[4,32,256]{2,1,0:T(8,128)(2,1)S(1)}, bf16[4,32,256]{2,1,0:T(8,128)(2,1)S(1)}, u32[]{:S(2)}, u32[]{:S(2)}) collective-permute-start(bf16[4,32,256]{2,1,0:T(8,128)(2,1)S(1)} %fusion.3.refs_0_), channel_id=1, source_target_pairs={{0,1},{1,0},{2,3},{3,2},{4,5},{5,4},{6,7},{7,6},{8,9},{9,8},{10,11... | collective-permute-start | bytes 196616 | tf_op jit(solution)/shard_map/ppermute | solution.py:33
  32.1 0.0 collective-permute-done.12.refs_1_
  32.1 1.0 %collective-permute-start.14 = (bf16[4,32,256]{2,1,0:T(8,128)(2,1)S(1)}, bf16[4,32,256]{2,1,0:T(8,128)(2,1)S(1)}, u32[]{:S(2)}, u32[]{:S(2)}) collective-permute-start(bf16[4,32,256]{2,1,0:T(8,128)(2,1)S(1)} %collective-permute-done.12.refs_1_), channel_id=1, source_target_pairs={{0,1},{1,0},{2,3},{3,2},{4,5},{5,4},{6,7},{7,6},{8,9},{9,8},{10,11... | collective-permute-start | bytes 196616 | tf_op jit(solution)/shard_map/ppermute | solution.py:33
  33.1 0.0 copy-done.2
  33.1 0.0 copy-done.3
  33.1 0.6 %fusion.6 = (f32[32,256]{1,0:T(8,128)}, f32[32,256]{1,0:T(8,128)}) fusion(f32[32,256]{1,0:T(8,128)S(1)} %copy-done.2, f32[4,32,256]{2,1,0:T(8,128)S(1)} %bitcast.71, s32[]{:T(128)S(6)} %select_n.39, f32[32,256]{1,0:T(8,128)S(1)} %copy-done.3), kind=kLoop, calls=%fused_computation.17 | loop fusion | flops 40960 | bytes 163844 | tf_op jit(solution)/shard_map/sub | solution.py:271
  33.7 0.0 collective-permute-done.13.refs_2_
  33.7 0.3 collective-permute-done.14.refs_3_
  34.0 0.7 %place.1 = bf16[2,2,2,2,32,256]{5,4,3,2,1,0:T(8,128)(2,1)} custom-call(bf16[4,32,256]{2,1,0:T(8,128)(2,1)S(1)} %fusion.3.refs_0_, bf16[4,32,256]{2,1,0:T(8,128)(2,1)S(1)} %collective-permute-done.12.refs_1_, bf16[4,32,256]{2,1,0:T(8,128)(2,1)S(1)} %collective-permute-done.13.refs_2_, bf16[4,32,256]{2,1,0:T(8,128)(2,1)S(1)} %collective-permute-done.14.refs_3_), custom_call_target="tpu_custom_call" | custom-call | tf_op jit(solution)/shard_map/place/pallas_call | solution.py:279
  (17 shorter events, 0.2 us)
Async XLA Ops:
  0.6 5.6 %collective-permute-start = (f32[1,32,256]{2,1,0:T(8,128)}, f32[1,32,256]{2,1,0:T(8,128)S(1)}, u32[]{:S(2)}, u32[]{:S(2)}) collective-permute-start(f32[1,32,256]{2,1,0:T(8,128)} %bitcast.74), channel_id=1, source_target_pairs={{0,9},{1,8},{2,11},{3,10},{4,13},{5,12},{6,15},{7,14},{8,1},{9,0},... | collective-permute-start | bytes 98312 | tf_op jit(solution)/shard_map/ppermute | solution.py:33
  6.3 3.4 %collective-permute-start.1 = (bf16[2,32,256]{2,1,0:T(8,128)(2,1)S(1)}, bf16[2,32,256]{2,1,0:T(8,128)(2,1)S(1)}, u32[]{:S(2)}, u32[]{:S(2)}) collective-permute-start(bf16[2,32,256]{2,1,0:T(8,128)(2,1)S(1)} %maximum_bitcast_fusion), channel_id=1, source_target_pairs={{0,5},{1,2},{2,1},{3,6},{4,7},{5,0},{6,3},{7,4},{8,11},{9,12},{10,... | collective-permute-start | bytes 98312 | tf_op jit(solution)/shard_map/ppermute | solution.py:33
  8.1 8.5 %collective-permute-start.2 = (f32[2,4,32,512]{3,2,1,0:T(8,128)S(1)}, f32[2,4,32,512]{3,2,1,0:T(8,128)S(1)}, u32[]{:S(2)}, u32[]{:S(2)}) collective-permute-start(f32[2,4,32,512]{3,2,1,0:T(8,128)S(1)} %get-tuple-element.29.sent_0), channel_id=1, source_target_pairs={{0,1},{1,0},{2,3},{3,2},{4,5},{5,4},{6,7},{7,6},{8,9},{9,8},{10,11... | collective-permute-start | bytes 1572872 | tf_op jit(solution)/shard_map/ppermute | solution.py:33
  8.4 6.1 %collective-permute-start.3 = (bf16[512,256]{1,0:T(8,128)(2,1)S(1)}, bf16[512,256]{1,0:T(8,128)(2,1)S(1)}, u32[]{:S(2)}, u32[]{:S(2)}) collective-permute-start(bf16[512,256]{1,0:T(8,128)(2,1)S(1)} %get-tuple-element.30.columns), channel_id=1, source_target_pairs={{0,1},{1,0},{2,3},{3,2},{4,5},{5,4},{6,7},{7,6},{8,9},{9,8},{10,11... | collective-permute-start | bytes 786440 | tf_op jit(solution)/shard_map/ppermute | solution.py:33
  8.6 5.9 %collective-permute-start.5 = (f32[2,4,32,512]{3,2,1,0:T(8,128)S(1)}, f32[2,4,32,512]{3,2,1,0:T(8,128)S(1)}, u32[]{:S(2)}, u32[]{:S(2)}) collective-permute-start(f32[2,4,32,512]{3,2,1,0:T(8,128)S(1)} %get-tuple-element.33.sent_1), channel_id=1, source_target_pairs={{0,1},{1,0},{2,3},{3,2},{4,5},{5,4},{6,7},{7,6},{8,9},{9,8},{10,11... | collective-permute-start | bytes 1572872 | tf_op jit(solution)/shard_map/ppermute | solution.py:33
  9.7 4.7 %collective-permute-start.4 = (bf16[128,256]{1,0:T(8,128)(2,1)S(1)}, bf16[128,256]{1,0:T(8,128)(2,1)S(1)}, u32[]{:S(2)}, u32[]{:S(2)}) collective-permute-start(bf16[128,256]{1,0:T(8,128)(2,1)S(1)} %bitcast.63), channel_id=1, source_target_pairs={{0,3},{1,4},{2,7},{3,0},{4,1},{5,6},{6,5},{7,2},{8,13},{9,10},{10,... | collective-permute-start | bytes 196616 | tf_op jit(solution)/shard_map/ppermute | solution.py:33
  11.5 4.4 %collective-permute-start.10 = (bf16[1,32,256]{2,1,0:T(8,128)(2,1)S(1)}, bf16[1,32,256]{2,1,0:T(8,128)(2,1)S(1)}, u32[]{:S(2)}, u32[]{:S(2)}) collective-permute-start(bf16[1,32,256]{2,1,0:T(8,128)(2,1)S(1)} %bitcast.67), channel_id=1, source_target_pairs={{0,9},{1,8},{2,11},{3,10},{4,13},{5,12},{6,15},{7,14},{8,1},{9,0},... | collective-permute-start | bytes 49160 | tf_op jit(solution)/shard_map/ppermute | solution.py:33
  15.0 3.8 %collective-permute-start.6 = (bf16[128,256]{1,0:T(8,128)(2,1)S(1)}, bf16[128,256]{1,0:T(8,128)(2,1)S(1)}, u32[]{:S(2)}, u32[]{:S(2)}) collective-permute-start(bf16[128,256]{1,0:T(8,128)(2,1)S(1)} %get-tuple-element.35), channel_id=1, source_target_pairs={{0,3},{1,4},{2,7},{3,0},{4,1},{5,6},{6,5},{7,2},{8,13},{9,10},{10,... | collective-permute-start | bytes 196616 | tf_op jit(solution)/shard_map/ppermute | solution.py:33
  15.9 5.4 %collective-permute-start.9 = (bf16[256,256]{1,0:T(8,128)(2,1)S(1)}, bf16[256,256]{1,0:T(8,128)(2,1)S(1)}, u32[]{:S(2)}, u32[]{:S(2)}) collective-permute-start(bf16[256,256]{1,0:T(8,128)(2,1)S(1)} %pad_maximum_fusion), channel_id=1, source_target_pairs={{0,1},{1,0},{2,3},{3,2},{4,5},{5,4},{6,7},{7,6},{8,9},{9,8},{10,11... | collective-permute-start | bytes 393224 | tf_op jit(solution)/shard_map/ppermute | solution.py:33
  18.8 4.7 %collective-permute-start.7 = (bf16[128,256]{1,0:T(8,128)(2,1)S(1)}, bf16[128,256]{1,0:T(8,128)(2,1)S(1)}, u32[]{:S(2)}, u32[]{:S(2)}) collective-permute-start(bf16[128,256]{1,0:T(8,128)(2,1)S(1)} %add_convert_fusion.1), channel_id=1, source_target_pairs={{0,9},{1,8},{2,11},{3,10},{4,13},{5,12},{6,15},{7,14},{8,1},{9,0},... | collective-permute-start | bytes 196616 | tf_op jit(solution)/shard_map/ppermute | solution.py:33
  21.3 4.6 %collective-permute-start.11 = (bf16[2,32,256]{2,1,0:T(8,128)(2,1)S(1)}, bf16[2,32,256]{2,1,0:T(8,128)(2,1)S(1)}, u32[]{:S(2)}, u32[]{:S(2)}) collective-permute-start(bf16[2,32,256]{2,1,0:T(8,128)(2,1)S(1)} %maximum_bitcast_fusion.1), channel_id=1, source_target_pairs={{0,5},{1,2},{2,1},{3,6},{4,7},{5,0},{6,3},{7,4},{8,11},{9,12},{10,... | collective-permute-start | bytes 98312 | tf_op jit(solution)/shard_map/ppermute | solution.py:33
  23.5 4.4 %collective-permute-start.8 = (bf16[128,256]{1,0:T(8,128)(2,1)S(1)}, bf16[128,256]{1,0:T(8,128)(2,1)S(1)}, u32[]{:S(2)}, u32[]{:S(2)}) collective-permute-start(bf16[128,256]{1,0:T(8,128)(2,1)S(1)} %add_convert_fusion), channel_id=1, source_target_pairs={{0,5},{1,2},{2,1},{3,6},{4,7},{5,0},{6,3},{7,4},{8,11},{9,12},{10,... | collective-permute-start | bytes 196616 | tf_op jit(solution)/shard_map/ppermute | solution.py:33
  25.9 3.5 %copy-start.1 = (f32[512,256]{1,0:T(8,128)S(1)}, f32[512,256]{1,0:T(8,128)}, u32[]{:S(2)}) copy-start(f32[512,256]{1,0:T(8,128)} %history.3) | copy-start | bytes 1572868
  26.0 3.5 %copy-start = (f32[512,256]{1,0:T(8,128)S(1)}, f32[512,256]{1,0:T(8,128)}, u32[]{:S(2)}) copy-start(f32[512,256]{1,0:T(8,128)} %master.1) | copy-start | bytes 1572868
  27.9 4.2 %collective-permute-start.12 = (bf16[4,32,256]{2,1,0:T(8,128)(2,1)S(1)}, bf16[4,32,256]{2,1,0:T(8,128)(2,1)S(1)}, u32[]{:S(2)}, u32[]{:S(2)}) collective-permute-start(bf16[4,32,256]{2,1,0:T(8,128)(2,1)S(1)} %fusion.3.refs_0_), channel_id=1, source_target_pairs={{0,3},{1,4},{2,7},{3,0},{4,1},{5,6},{6,5},{7,2},{8,13},{9,10},{10,... | collective-permute-start | bytes 196616 | tf_op jit(solution)/shard_map/ppermute | solution.py:33
  29.5 3.6 %copy-start.2 = (f32[32,256]{1,0:T(8,128)S(1)}, f32[32,256]{1,0:T(8,128)}, u32[]{:S(2)}) copy-start(f32[32,256]{1,0:T(8,128)} %rows.3) | copy-start | bytes 98308
  29.5 3.6 %copy-start.3 = (f32[32,256]{1,0:T(8,128)S(1)}, f32[32,256]{1,0:T(8,128)}, u32[]{:S(2)}) copy-start(f32[32,256]{1,0:T(8,128)} %history.2) | copy-start | bytes 98308
  31.4 2.4 %collective-permute-start.13 = (bf16[4,32,256]{2,1,0:T(8,128)(2,1)S(1)}, bf16[4,32,256]{2,1,0:T(8,128)(2,1)S(1)}, u32[]{:S(2)}, u32[]{:S(2)}) collective-permute-start(bf16[4,32,256]{2,1,0:T(8,128)(2,1)S(1)} %fusion.3.refs_0_), channel_id=1, source_target_pairs={{0,1},{1,0},{2,3},{3,2},{4,5},{5,4},{6,7},{7,6},{8,9},{9,8},{10,11... | collective-permute-start | bytes 196616 | tf_op jit(solution)/shard_map/ppermute | solution.py:33
  32.1 1.9 %collective-permute-start.14 = (bf16[4,32,256]{2,1,0:T(8,128)(2,1)S(1)}, bf16[4,32,256]{2,1,0:T(8,128)(2,1)S(1)}, u32[]{:S(2)}, u32[]{:S(2)}) collective-permute-start(bf16[4,32,256]{2,1,0:T(8,128)(2,1)S(1)} %collective-permute-done.12.refs_1_), channel_id=1, source_target_pairs={{0,1},{1,0},{2,3},{3,2},{4,5},{5,4},{6,7},{7,6},{8,9},{9,8},{10,11... | collective-permute-start | bytes 196616 | tf_op jit(solution)/shard_map/ppermute | solution.py:33

commit v11 on v10

--- a/solution.py
+++ b/solution.py
@@ -61,8 +61,8 @@
 
 
 def prepare_kernel(counts, row_totals, column_totals, columns, rows, history, *refs):
-    kept_0, kept_1, sent_0, sent_1, column_copy, row_copy, history_copy, upper = refs[:8]
-    near_counts, near_rows, near_columns, near_copy, near_history, row_terms, sems = refs[8:]
+    kept_0, kept_1, sent_0, sent_1, column_copy, row_copy, history_copy, upper, turned = refs[:9]
+    near_counts, near_rows, near_columns, near_copy, near_history, row_terms, sems = refs[9:]
     groups = kept_0.shape[1]
     copies = [
         pltpu.make_async_copy(row_totals, near_rows, sems.at[0]),
@@ -103,6 +103,7 @@
             pl.loop(0, groups)(body)
     copies[3].wait()
     column_copy[...] = near_copy[...].astype(jnp.bfloat16)
+    turned[...] = near_copy[...].T.astype(jnp.bfloat16)
     copies[4].wait()
     copies[5].wait()
     history_copy[...] = near_history[...].astype(jnp.bfloat16)
@@ -111,56 +112,64 @@
 def slopes_of(rows, columns, terms, step, chunk, at_columns=slice(None)):
     group = chunk // terms.shape[2]
     at = pl.ds(step * group, group)
-    scores = lax.dot_general(rows, columns, (((1,), (1,)), ((), ())), preferred_element_type=jnp.float32)
+    scores = jnp.dot(rows, columns, preferred_element_type=jnp.float32)
     gap = scores - terms[0, at, :, at_columns].reshape(scores.shape)
     confidence = terms[1, at, :, at_columns].reshape(scores.shape)
     return jnp.where(confidence > 0, confidence * gap, jax.nn.sigmoid(gap)).astype(jnp.bfloat16)
 
 
-def rows_kernel(chunk, rows, kept, received, columns, other_columns, *refs):
+def rows_kernel(chunk, rows, kept, received, columns, other_columns, turned, *refs):
     gradient, slopes = refs[-2:]
     half = columns.shape[0] // 2
 
     def body(step):
         at = pl.ds(pl.multiple_of(step * chunk, chunk), chunk)
         total = None
-        for terms, source in ((kept, columns), (received, other_columns)):
+        for terms, source, across in ((kept, columns, turned), (received, other_columns, other_columns[...].T)):
             for first in (0, half):
                 at_columns = slice(first, first + half)
-                block = source[at_columns, :]
-                part = slopes_of(rows[at, :], block, terms, step, chunk, at_columns)
+                part = slopes_of(rows[at, :], across[:, at_columns], terms, step, chunk, at_columns)
                 if source is columns:
                     slopes[at, at_columns] = part
-                part = jnp.dot(part, block, preferred_element_type=jnp.float32)
+                part = jnp.dot(part, source[at_columns, :], preferred_element_type=jnp.float32)
                 total = part if total is None else total + part
         gradient[at, :] = total.astype(gradient.dtype)
 
     steps_of(rows.shape[0] // chunk, body)
 
 
-def columns_kernel(total_rows, chunk, master, history, columns, sent_0, sent_1, mine, beside, others, slopes_0, slopes_1, *outs):
-    new_master, new_history, total = outs
-    group_rows = mine.shape[0]
-    total[...] = jnp.zeros_like(total)
+def columns_kernel(total_rows, chunk, master, history, turned, sent_0, sent_1, mine, beside, others, slopes_0, slopes_1, *refs):
+    new_master, new_history, far_slopes, near_master, near_history, sems = refs
+    group_rows, half, block = mine.shape[0], turned.shape[1] // 2, 128
 
     def body(step):
         first = pl.multiple_of(step * chunk, chunk)
-        at = pl.ds(first, chunk)
-        part = total[...]
         for place in range(2):
-            rows = (mine, beside)[place][at, :]
-            own = (slopes_0, slopes_1)[place][at, :]
-            part += lax.dot_general(own, rows, (((0,), (0,)), ((), ())), preferred_element_type=jnp.float32)
-            rows = others[pl.ds(place * group_rows + first, chunk), :]
-            own = slopes_of(rows, columns[...], (sent_0, sent_1)[place], step, chunk)
-            part += lax.dot_general(own, rows, (((0,), (0,)), ((), ())), preferred_element_type=jnp.float32)
-        total[...] = part
+            at = pl.ds(place * group_rows + first, chunk)
+            for start in (0, half):
+                at_columns = slice(start, start + half)
+                far_slopes[at, at_columns] = slopes_of(
+                    others[at, :], turned[:, at_columns], (sent_0, sent_1)[place], step, chunk, at_columns
+                )
 
     steps_of(group_rows // chunk, body)
-    gradient = total[...] / total_rows
-    updated = history[...] + gradient * gradient
-    new_history[...] = updated
-    new_master[...] = master[...] - step_size * gradient * lax.rsqrt(updated)
+    copies = []
+    for k in range(turned.shape[1] // block):
+        at = slice(k * block, (k + 1) * block)
+        total = None
+        for rows, slopes in ((mine, slopes_0), (beside, slopes_1), (others, far_slopes)):
+            part = lax.dot_general(slopes[:, at], rows[...], (((0,), (0,)), ((), ())), preferred_element_type=jnp.float32)
+            total = part if total is None else total + part
+        gradient = total / total_rows
+        updated = history[at, :] + gradient * gradient
+        near_history[at, :] = updated
+        near_master[at, :] = master[at, :] - step_size * gradient * lax.rsqrt(updated)
+        copies.append(pltpu.make_async_copy(near_history.at[at, :], new_history.at[at, :], sems.at[2 * k]))
+        copies.append(pltpu.make_async_copy(near_master.at[at, :], new_master.at[at, :], sems.at[2 * k + 1]))
+        copies[-2].start()
+        copies[-1].start()
+    for copy in copies:
+        copy.wait()
 
 
 def place_kernel(*refs):
@@ -189,11 +198,11 @@
     terms_type = pltpu.VMEM((2, group, own, block_columns), jnp.float32)
 
     grid = (group // 2, 2, 2, 2, own)
-    kept_0, kept_1, sent_0, sent_1, column_copy, row_copy, history, side = pl.pallas_call(
+    kept_0, kept_1, sent_0, sent_1, column_copy, row_copy, history, side, turned = pl.pallas_call(
         prepare_kernel,
-        out_shape=(terms_type,) * 4 + (pltpu.VMEM(column_master.shape, jnp.bfloat16), pltpu.VMEM(row_master.shape, jnp.float32), pltpu.VMEM(row_master.shape, jnp.bfloat16), pltpu.VMEM((8, width), jnp.float32)),
+        out_shape=(terms_type,) * 4 + (pltpu.VMEM(column_master.shape, jnp.bfloat16), pltpu.VMEM(row_master.shape, jnp.float32), pltpu.VMEM(row_master.shape, jnp.bfloat16), pltpu.VMEM((8, width), jnp.float32), pltpu.VMEM((width, block_columns), jnp.bfloat16)),
         in_specs=[HBM] * 6,
-        out_specs=[VMEM] * 8,
+        out_specs=[VMEM] * 9,
         scratch_shapes=[
             pltpu.VMEM(grid + (block_columns,), jnp.int32),
             pltpu.VMEM((1, total_rows), jnp.int32),
@@ -234,12 +243,12 @@
         return pl.pallas_call(
             functools.partial(rows_kernel, chunk),
             out_shape=(pltpu.VMEM((group_rows, width), kind), pltpu.VMEM((group_rows, block_columns), jnp.bfloat16)),
-            in_specs=[VMEM] * 5 + [ANY] * len(after),
+            in_specs=[VMEM] * 6 + [ANY] * len(after),
             out_specs=[VMEM] * 2,
             compiler_params=PARAMS,
             cost_estimate=pl.CostEstimate(flops=8 * group_rows * block_columns * width, bytes_accessed=0, transcendentals=4 * group_rows * block_columns),
             name="rows",
-        )(*[near(v) for v in (rows, kept, received, column_copy, other_columns)], *after)
+        )(*[near(v) for v in (rows, kept, received, column_copy, other_columns, turned)], *after)
 
     part_late, slopes_1 = gradient_of(jnp.bfloat16, beside, kept_1, received_1)
     part_early, slopes_0 = gradient_of(jnp.float32, mine, kept_0, received_0, first_hop)
@@ -253,12 +262,17 @@
         functools.partial(columns_kernel, total_rows, chunk),
         out_shape=(struct, struct),
         in_specs=[VMEM] * 10,
-        out_specs=[VMEM] * 2,
-        scratch_shapes=[pltpu.VMEM(column_master.shape, jnp.float32)],
+        out_specs=[HBM] * 2,
+        scratch_shapes=[
+            pltpu.VMEM((2 * group_rows, block_columns), jnp.bfloat16),
+            pltpu.VMEM(column_master.shape, jnp.float32),
+            pltpu.VMEM(column_master.shape, jnp.float32),
+            pltpu.SemaphoreType.DMA((2 * (block_columns // 128),)),
+        ],
         compiler_params=PARAMS,
         cost_estimate=pl.CostEstimate(flops=2 * total_rows * block_columns * width, bytes_accessed=4 * column_master.size * 4, transcendentals=0),
         name="columns",
-    )(*[near(v) for v in (column_master, column_history, column_copy, sent_0, sent_1, mine, beside, others, slopes_0, slopes_1)])
+    )(*[near(v) for v in (column_master, column_history, turned, sent_0, sent_1, mine, beside, others, slopes_0, slopes_1)])
 
     last_history = hop(history, SUM, size)
     for bits, upper in steps:

time: 34.9 us -> 35 us (level)
  starting transfers between devices: 22.4 us -> 22.8 us
    ppermute x15, starting transfers between devices: 22.4 us -> 22.8 us  [hop(): return lax.ppermute(value, 'col', pairs)]
    pallas_call x1, Pallas kernels: 1.88 us -> 1.51 us  [per_device(): pl.pallas_call(functools.partial(columns_kernel, total_rows, chunk), out_...]
  transfers between devices with their start and end apart: 15 -> 15, of which waited for: 7 -> 5; matrix products, arithmetic and copies ran while one was open for 2% -> 2% of each run, Pallas kernels for 14% -> 13%
where the time goes in v11:
time: 35 us; the launch traced here: 34.8 us
  starting transfers between devices  22.8 us (65%)
  Pallas kernels  5.21 us (15%)
  waiting for transfers between devices  5.07 us (14%)
  other arithmetic  0.84 us (2%)
  between operations  0.8 us (2%)
    ppermute x15, starting transfers between devices, hop(): return lax.ppermute(value, 'col', pairs)  22.8 us
    ppermute x15, waiting for transfers between devices, hop(): return lax.ppermute(value, 'col', pairs)  5.07 us
    pallas_call x1, Pallas kernels, per_device(): pl.pallas_call(prepare_kernel, out_shape=(terms_type,) * 4 + (pltpu.VMEM(...  2.04 us
    pallas_call x1, Pallas kernels, per_device(): pl.pallas_call(functools.partial(columns_kernel, total_rows, chunk), out_...  1.51 us
    pallas_call x2, Pallas kernels, gradient_of(): pl.pallas_call(functools.partial(rows_kernel, chunk), out_shape=(pltpu.VM...  0.94 us
    pallas_call x1, Pallas kernels, per_device(): pl.pallas_call(place_kernel, out_shape=jax.ShapeDtypeStruct(grid + (width...  0.72 us
  transfers between devices with their start and end apart: 15, of which 5 were waited for; matrix products, arithmetic and copies ran while one was open for 2% of the time, Pallas kernels for 13%

profile of v11, /device:TPU:0, one launch (start us, length us, event | category | flops | bytes accessed | tf_op | source)
XLA Modules:
  0.0 34.8 jit_solution(17893204828007085460)
XLA Ops:
  0.6 3.5 %collective-permute-start = (f32[1,32,256]{2,1,0:T(8,128)}, f32[1,32,256]{2,1,0:T(8,128)S(1)}, u32[]{:S(2)}, u32[]{:S(2)}) collective-permute-start(f32[1,32,256]{2,1,0:T(8,128)} %bitcast.74), channel_id=1, source_target_pairs={{0,9},{1,8},{2,11},{3,10},{4,13},{5,12},{6,15},{7,14},{8,1},{9,0},... | collective-permute-start | bytes 98312 | tf_op jit(solution)/shard_map/ppermute | solution.py:33
  4.2 2.0 %prepare.1 = (f32[2,4,32,512]{3,2,1,0:T(8,128)S(1)}, f32[2,4,32,512]{3,2,1,0:T(8,128)S(1)}, f32[2,4,32,512]{3,2,1,0:T(8,128)S(1)}, f32[2,4,32,512]{3,2,1,0:T(8,1...) custom-call(s32[2,2,2,2,32,512]{5,4,3,2,1,0:T(8,128)} %bitcast.69, ...), custom_call_target="tpu_custom_call" | custom-call | flops 2097152 | bytes 1048576 | tf_op jit(solution)/shard_map/prepare/pallas_call | solution.py:201
  6.2 0.0 collective-permute-done.refs_0_
  6.3 1.9 %collective-permute-start.1 = (bf16[2,32,256]{2,1,0:T(8,128)(2,1)S(1)}, bf16[2,32,256]{2,1,0:T(8,128)(2,1)S(1)}, u32[]{:S(2)}, u32[]{:S(2)}) collective-permute-start(bf16[2,32,256]{2,1,0:T(8,128)(2,1)S(1)} %maximum_bitcast_fusion), channel_id=1, source_target_pairs={{0,5},{1,2},{2,1},{3,6},{4,7},{5,0},{6,3},{7,4},{8,11},{9,12},{10,... | collective-permute-start | bytes 98312 | tf_op jit(solution)/shard_map/ppermute | solution.py:33
  8.2 0.2 collective-permute-start.2
  8.4 0.3 collective-permute-start.3
  8.7 0.2 collective-permute-start.5
  8.9 0.9 %collective-permute-done.1 = bf16[2,32,256]{2,1,0:T(8,128)(2,1)S(1)} collective-permute-done((bf16[2,32,256]{2,1,0:T(8,128)(2,1)S(1)}, bf16[2,32,256]{2,1,0:T(8,128)(2,1)S(1)}, u32[]{:S(2)}, u32[]{:S(2)}) %collective-permute-start.1) | collective-permute-done | bytes 32800 | tf_op jit(solution)/shard_map/ppermute | solution.py:33
  9.9 1.7 %collective-permute-start.4 = (bf16[128,256]{1,0:T(8,128)(2,1)S(1)}, bf16[128,256]{1,0:T(8,128)(2,1)S(1)}, u32[]{:S(2)}, u32[]{:S(2)}) collective-permute-start(bf16[128,256]{1,0:T(8,128)(2,1)S(1)} %bitcast.63), channel_id=1, source_target_pairs={{0,3},{1,4},{2,7},{3,0},{4,1},{5,6},{6,5},{7,2},{8,13},{9,10},{10,... | collective-permute-start | bytes 196616 | tf_op jit(solution)/shard_map/ppermute | solution.py:33
  11.6 2.8 %collective-permute-start.10 = (bf16[1,32,256]{2,1,0:T(8,128)(2,1)S(1)}, bf16[1,32,256]{2,1,0:T(8,128)(2,1)S(1)}, u32[]{:S(2)}, u32[]{:S(2)}) collective-permute-start(bf16[1,32,256]{2,1,0:T(8,128)(2,1)S(1)} %bitcast.67), channel_id=1, source_target_pairs={{0,9},{1,8},{2,11},{3,10},{4,13},{5,12},{6,15},{7,14},{8,1},{9,0},... | collective-permute-start | bytes 49160 | tf_op jit(solution)/shard_map/ppermute | solution.py:33
  14.4 0.0 collective-permute-done.4.rows.beside
  14.5 0.0 collective-permute-done.3.other_columns
  14.5 0.0 collective-permute-done.5.received
  14.5 0.5 %rows.5 = (bf16[128,256]{1,0:T(8,128)(2,1)S(1)}, bf16[128,512]{1,0:T(8,128)(2,1)S(1)}) custom-call(bf16[128,256]{1,0:T(8,128)(2,1)S(1)} %collective-permute-done.4.rows.beside, f32[2,4,32,512]{3,2,1,0:T(8,128)S(1)} %get-tuple-element.34.kept, f32[2,4,32,512]{3,2,1,0:T(8,128)S(1)} %collective-permute-done.5.received, ...), custom_call_target="tpu_custom_call" | custom-call | flops 134217728 | tf_op jit(solution)/shard_map/rows/pallas_call | solution.py:243
  15.0 0.9 %collective-permute-start.6 = (bf16[128,256]{1,0:T(8,128)(2,1)S(1)}, bf16[128,256]{1,0:T(8,128)(2,1)S(1)}, u32[]{:S(2)}, u32[]{:S(2)}) collective-permute-start(bf16[128,256]{1,0:T(8,128)(2,1)S(1)} %get-tuple-element.37), channel_id=1, source_target_pairs={{0,3},{1,4},{2,7},{3,0},{4,1},{5,6},{6,5},{7,2},{8,13},{9,10},{10,... | collective-permute-start | bytes 196616 | tf_op jit(solution)/shard_map/ppermute | solution.py:33
  15.9 0.0 collective-permute-done.10
  15.9 0.7 %collective-permute-start.9 = (bf16[256,256]{1,0:T(8,128)(2,1)S(1)}, bf16[256,256]{1,0:T(8,128)(2,1)S(1)}, u32[]{:S(2)}, u32[]{:S(2)}) collective-permute-start(bf16[256,256]{1,0:T(8,128)(2,1)S(1)} %pad_maximum_fusion), channel_id=1, source_target_pairs={{0,1},{1,0},{2,3},{3,2},{4,5},{5,4},{6,7},{7,6},{8,9},{9,8},{10,11... | collective-permute-start | bytes 393224 | tf_op jit(solution)/shard_map/ppermute | solution.py:33
  16.6 0.0 collective-permute-done.2.received
  16.6 0.5 %rows.4 = (f32[128,256]{1,0:T(8,128)S(1)}, bf16[128,512]{1,0:T(8,128)(2,1)S(1)}) custom-call(bf16[128,256]{1,0:T(8,128)(2,1)S(1)} %bitcast.65, f32[2,4,32,512]{3,2,1,0:T(8,128)S(1)} %get-tuple-element.29.kept, f32[2,4,32,512]{3,2,1,0:T(8,128)S(1)} %collective-permute-done.2.received, bf16[512,256]{1,0:T(8,128)(2,1)S(1)} %get-tuple-element.31.columns, ...), custom_call_target="tpu_custom_call" | custom-call | flops 134217728 | tf_op jit(solution)/shard_map/rows/pallas_call | solution.py:243
  17.1 1.7 %collective-permute-done.6 = bf16[128,256]{1,0:T(8,128)(2,1)S(1)} collective-permute-done((bf16[128,256]{1,0:T(8,128)(2,1)S(1)}, bf16[128,256]{1,0:T(8,128)(2,1)S(1)}, u32[]{:S(2)}, u32[]{:S(2)}) %collective-permute-start.6) | collective-permute-done | bytes 65568 | tf_op jit(solution)/shard_map/ppermute | solution.py:33
  18.7 2.5 %collective-permute-start.7 = (bf16[128,256]{1,0:T(8,128)(2,1)S(1)}, bf16[128,256]{1,0:T(8,128)(2,1)S(1)}, u32[]{:S(2)}, u32[]{:S(2)}) collective-permute-start(bf16[128,256]{1,0:T(8,128)(2,1)S(1)} %add_convert_fusion.1), channel_id=1, source_target_pairs={{0,9},{1,8},{2,11},{3,10},{4,13},{5,12},{6,15},{7,14},{8,1},{9,0},... | collective-permute-start | bytes 196616 | tf_op jit(solution)/shard_map/ppermute | solution.py:33
  21.3 0.0 collective-permute-done.9.others
  21.3 1.8 %collective-permute-start.11 = (bf16[2,32,256]{2,1,0:T(8,128)(2,1)S(1)}, bf16[2,32,256]{2,1,0:T(8,128)(2,1)S(1)}, u32[]{:S(2)}, u32[]{:S(2)}) collective-permute-start(bf16[2,32,256]{2,1,0:T(8,128)(2,1)S(1)} %maximum_bitcast_fusion.1), channel_id=1, source_target_pairs={{0,5},{1,2},{2,1},{3,6},{4,7},{5,0},{6,3},{7,4},{8,11},{9,12},{10,... | collective-permute-start | bytes 98312 | tf_op jit(solution)/shard_map/ppermute | solution.py:33
  23.1 0.3 collective-permute-done.7
  23.4 2.4 %collective-permute-start.8 = (bf16[128,256]{1,0:T(8,128)(2,1)S(1)}, bf16[128,256]{1,0:T(8,128)(2,1)S(1)}, u32[]{:S(2)}, u32[]{:S(2)}) collective-permute-start(bf16[128,256]{1,0:T(8,128)(2,1)S(1)} %add_convert_fusion), channel_id=1, source_target_pairs={{0,5},{1,2},{2,1},{3,6},{4,7},{5,0},{6,3},{7,4},{8,11},{9,12},{10,... | collective-permute-start | bytes 196616 | tf_op jit(solution)/shard_map/ppermute | solution.py:33
  25.9 0.0 collective-permute-done.11
  25.9 0.0 copy-start.1
  25.9 0.0 copy-start
  25.9 1.9 %collective-permute-done.8 = bf16[128,256]{1,0:T(8,128)(2,1)S(1)} collective-permute-done((bf16[128,256]{1,0:T(8,128)(2,1)S(1)}, bf16[128,256]{1,0:T(8,128)(2,1)S(1)}, u32[]{:S(2)}, u32[]{:S(2)}) %collective-permute-start.8) | collective-permute-done | bytes 65568 | tf_op jit(solution)/shard_map/ppermute | solution.py:33
  27.9 1.5 %collective-permute-start.12 = (bf16[4,32,256]{2,1,0:T(8,128)(2,1)S(1)}, bf16[4,32,256]{2,1,0:T(8,128)(2,1)S(1)}, u32[]{:S(2)}, u32[]{:S(2)}) collective-permute-start(bf16[4,32,256]{2,1,0:T(8,128)(2,1)S(1)} %fusion.3.refs_0_), channel_id=1, source_target_pairs={{0,3},{1,4},{2,7},{3,0},{4,1},{5,6},{6,5},{7,2},{8,13},{9,10},{10,... | collective-permute-start | bytes 196616 | tf_op jit(solution)/shard_map/ppermute | solution.py:33
  29.4 0.0 copy-done.1
  29.4 0.0 copy-done
  29.4 0.0 copy-start.2
  29.4 0.0 copy-start.3
  29.4 1.5 %columns.3 = (f32[512,256]{1,0:T(8,128)}, f32[512,256]{1,0:T(8,128)}) custom-call(f32[512,256]{1,0:T(8,128)S(1)} %copy-done, f32[512,256]{1,0:T(8,128)S(1)} %copy-done.1, bf16[256,512]{1,0:T(8,128)(2,1)S(1)} %get-tuple-element.32.turned, f32[2,4,32,512]{3,2,1,0:T(8,128)S(1)} %get-tuple-element.30.sent_0, f32[2,4,32,512]{3,2,1,0:T(8,128)S(1)} %get-tuple-element.35.sent_1, ...), custom_call_target="tpu_custom_call" | custom-call | flops 134217728 | bytes 2097152 | tf_op jit(solution)/shard_map/columns/pallas_call | solution.py:261
  31.0 0.8 %collective-permute-start.13 = (bf16[4,32,256]{2,1,0:T(8,128)(2,1)S(1)}, bf16[4,32,256]{2,1,0:T(8,128)(2,1)S(1)}, u32[]{:S(2)}, u32[]{:S(2)}) collective-permute-start(bf16[4,32,256]{2,1,0:T(8,128)(2,1)S(1)} %fusion.3.refs_0_), channel_id=1, source_target_pairs={{0,1},{1,0},{2,3},{3,2},{4,5},{5,4},{6,7},{7,6},{8,9},{9,8},{10,11... | collective-permute-start | bytes 196616 | tf_op jit(solution)/shard_map/ppermute | solution.py:33
  31.7 0.0 collective-permute-done.12.refs_1_
  31.7 1.4 %collective-permute-start.14 = (bf16[4,32,256]{2,1,0:T(8,128)(2,1)S(1)}, bf16[4,32,256]{2,1,0:T(8,128)(2,1)S(1)}, u32[]{:S(2)}, u32[]{:S(2)}) collective-permute-start(bf16[4,32,256]{2,1,0:T(8,128)(2,1)S(1)} %collective-permute-done.12.refs_1_), channel_id=1, source_target_pairs={{0,1},{1,0},{2,3},{3,2},{4,5},{5,4},{6,7},{7,6},{8,9},{9,8},{10,11... | collective-permute-start | bytes 196616 | tf_op jit(solution)/shard_map/ppermute | solution.py:33
  33.2 0.0 copy-done.2
  33.2 0.0 copy-done.3
  33.2 0.6 %fusion.6 = (f32[32,256]{1,0:T(8,128)}, f32[32,256]{1,0:T(8,128)}) fusion(f32[32,256]{1,0:T(8,128)S(1)} %copy-done.2, f32[4,32,256]{2,1,0:T(8,128)S(1)} %bitcast.71, s32[]{:T(128)S(6)} %select_n.39, f32[32,256]{1,0:T(8,128)S(1)} %copy-done.3), kind=kLoop, calls=%fused_computation.17 | loop fusion | flops 40960 | bytes 163844 | tf_op jit(solution)/shard_map/sub | solution.py:285
  33.8 0.0 collective-permute-done.13.refs_2_
  33.8 0.3 collective-permute-done.14.refs_3_
  34.1 0.7 %place.1 = bf16[2,2,2,2,32,256]{5,4,3,2,1,0:T(8,128)(2,1)} custom-call(bf16[4,32,256]{2,1,0:T(8,128)(2,1)S(1)} %fusion.3.refs_0_, bf16[4,32,256]{2,1,0:T(8,128)(2,1)S(1)} %collective-permute-done.12.refs_1_, bf16[4,32,256]{2,1,0:T(8,128)(2,1)S(1)} %collective-permute-done.13.refs_2_, bf16[4,32,256]{2,1,0:T(8,128)(2,1)S(1)} %collective-permute-done.14.refs_3_), custom_call_target="tpu_custom_call" | custom-call | tf_op jit(solution)/shard_map/place/pallas_call | solution.py:293
  (17 shorter events, 0.2 us)
Async XLA Ops:
  0.6 5.6 %collective-permute-start = (f32[1,32,256]{2,1,0:T(8,128)}, f32[1,32,256]{2,1,0:T(8,128)S(1)}, u32[]{:S(2)}, u32[]{:S(2)}) collective-permute-start(f32[1,32,256]{2,1,0:T(8,128)} %bitcast.74), channel_id=1, source_target_pairs={{0,9},{1,8},{2,11},{3,10},{4,13},{5,12},{6,15},{7,14},{8,1},{9,0},... | collective-permute-start | bytes 98312 | tf_op jit(solution)/shard_map/ppermute | solution.py:33
  6.3 3.5 %collective-permute-start.1 = (bf16[2,32,256]{2,1,0:T(8,128)(2,1)S(1)}, bf16[2,32,256]{2,1,0:T(8,128)(2,1)S(1)}, u32[]{:S(2)}, u32[]{:S(2)}) collective-permute-start(bf16[2,32,256]{2,1,0:T(8,128)(2,1)S(1)} %maximum_bitcast_fusion), channel_id=1, source_target_pairs={{0,5},{1,2},{2,1},{3,6},{4,7},{5,0},{6,3},{7,4},{8,11},{9,12},{10,... | collective-permute-start | bytes 98312 | tf_op jit(solution)/shard_map/ppermute | solution.py:33
  8.2 8.4 %collective-permute-start.2 = (f32[2,4,32,512]{3,2,1,0:T(8,128)S(1)}, f32[2,4,32,512]{3,2,1,0:T(8,128)S(1)}, u32[]{:S(2)}, u32[]{:S(2)}) collective-permute-start(f32[2,4,32,512]{3,2,1,0:T(8,128)S(1)} %get-tuple-element.30.sent_0), channel_id=1, source_target_pairs={{0,1},{1,0},{2,3},{3,2},{4,5},{5,4},{6,7},{7,6},{8,9},{9,8},{10,11... | collective-permute-start | bytes 1572872 | tf_op jit(solution)/shard_map/ppermute | solution.py:33
  8.4 6.1 %collective-permute-start.3 = (bf16[512,256]{1,0:T(8,128)(2,1)S(1)}, bf16[512,256]{1,0:T(8,128)(2,1)S(1)}, u32[]{:S(2)}, u32[]{:S(2)}) collective-permute-start(bf16[512,256]{1,0:T(8,128)(2,1)S(1)} %get-tuple-element.31.columns), channel_id=1, source_target_pairs={{0,1},{1,0},{2,3},{3,2},{4,5},{5,4},{6,7},{7,6},{8,9},{9,8},{10,11... | collective-permute-start | bytes 786440 | tf_op jit(solution)/shard_map/ppermute | solution.py:33
  8.7 5.8 %collective-permute-start.5 = (f32[2,4,32,512]{3,2,1,0:T(8,128)S(1)}, f32[2,4,32,512]{3,2,1,0:T(8,128)S(1)}, u32[]{:S(2)}, u32[]{:S(2)}) collective-permute-start(f32[2,4,32,512]{3,2,1,0:T(8,128)S(1)} %get-tuple-element.35.sent_1), channel_id=1, source_target_pairs={{0,1},{1,0},{2,3},{3,2},{4,5},{5,4},{6,7},{7,6},{8,9},{9,8},{10,11... | collective-permute-start | bytes 1572872 | tf_op jit(solution)/shard_map/ppermute | solution.py:33
  9.9 4.6 %collective-permute-start.4 = (bf16[128,256]{1,0:T(8,128)(2,1)S(1)}, bf16[128,256]{1,0:T(8,128)(2,1)S(1)}, u32[]{:S(2)}, u32[]{:S(2)}) collective-permute-start(bf16[128,256]{1,0:T(8,128)(2,1)S(1)} %bitcast.63), channel_id=1, source_target_pairs={{0,3},{1,4},{2,7},{3,0},{4,1},{5,6},{6,5},{7,2},{8,13},{9,10},{10,... | collective-permute-start | bytes 196616 | tf_op jit(solution)/shard_map/ppermute | solution.py:33
  11.6 4.3 %collective-permute-start.10 = (bf16[1,32,256]{2,1,0:T(8,128)(2,1)S(1)}, bf16[1,32,256]{2,1,0:T(8,128)(2,1)S(1)}, u32[]{:S(2)}, u32[]{:S(2)}) collective-permute-start(bf16[1,32,256]{2,1,0:T(8,128)(2,1)S(1)} %bitcast.67), channel_id=1, source_target_pairs={{0,9},{1,8},{2,11},{3,10},{4,13},{5,12},{6,15},{7,14},{8,1},{9,0},... | collective-permute-start | bytes 49160 | tf_op jit(solution)/shard_map/ppermute | solution.py:33
  15.0 3.8 %collective-permute-start.6 = (bf16[128,256]{1,0:T(8,128)(2,1)S(1)}, bf16[128,256]{1,0:T(8,128)(2,1)S(1)}, u32[]{:S(2)}, u32[]{:S(2)}) collective-permute-start(bf16[128,256]{1,0:T(8,128)(2,1)S(1)} %get-tuple-element.37), channel_id=1, source_target_pairs={{0,3},{1,4},{2,7},{3,0},{4,1},{5,6},{6,5},{7,2},{8,13},{9,10},{10,... | collective-permute-start | bytes 196616 | tf_op jit(solution)/shard_map/ppermute | solution.py:33
  15.9 5.4 %collective-permute-start.9 = (bf16[256,256]{1,0:T(8,128)(2,1)S(1)}, bf16[256,256]{1,0:T(8,128)(2,1)S(1)}, u32[]{:S(2)}, u32[]{:S(2)}) collective-permute-start(bf16[256,256]{1,0:T(8,128)(2,1)S(1)} %pad_maximum_fusion), channel_id=1, source_target_pairs={{0,1},{1,0},{2,3},{3,2},{4,5},{5,4},{6,7},{7,6},{8,9},{9,8},{10,11... | collective-permute-start | bytes 393224 | tf_op jit(solution)/shard_map/ppermute | solution.py:33
  18.7 4.7 %collective-permute-start.7 = (bf16[128,256]{1,0:T(8,128)(2,1)S(1)}, bf16[128,256]{1,0:T(8,128)(2,1)S(1)}, u32[]{:S(2)}, u32[]{:S(2)}) collective-permute-start(bf16[128,256]{1,0:T(8,128)(2,1)S(1)} %add_convert_fusion.1), channel_id=1, source_target_pairs={{0,9},{1,8},{2,11},{3,10},{4,13},{5,12},{6,15},{7,14},{8,1},{9,0},... | collective-permute-start | bytes 196616 | tf_op jit(solution)/shard_map/ppermute | solution.py:33
  21.3 4.6 %collective-permute-start.11 = (bf16[2,32,256]{2,1,0:T(8,128)(2,1)S(1)}, bf16[2,32,256]{2,1,0:T(8,128)(2,1)S(1)}, u32[]{:S(2)}, u32[]{:S(2)}) collective-permute-start(bf16[2,32,256]{2,1,0:T(8,128)(2,1)S(1)} %maximum_bitcast_fusion.1), channel_id=1, source_target_pairs={{0,5},{1,2},{2,1},{3,6},{4,7},{5,0},{6,3},{7,4},{8,11},{9,12},{10,... | collective-permute-start | bytes 98312 | tf_op jit(solution)/shard_map/ppermute | solution.py:33
  23.4 4.4 %collective-permute-start.8 = (bf16[128,256]{1,0:T(8,128)(2,1)S(1)}, bf16[128,256]{1,0:T(8,128)(2,1)S(1)}, u32[]{:S(2)}, u32[]{:S(2)}) collective-permute-start(bf16[128,256]{1,0:T(8,128)(2,1)S(1)} %add_convert_fusion), channel_id=1, source_target_pairs={{0,5},{1,2},{2,1},{3,6},{4,7},{5,0},{6,3},{7,4},{8,11},{9,12},{10,... | collective-permute-start | bytes 196616 | tf_op jit(solution)/shard_map/ppermute | solution.py:33
  25.9 3.5 %copy-start.1 = (f32[512,256]{1,0:T(8,128)S(1)}, f32[512,256]{1,0:T(8,128)}, u32[]{:S(2)}) copy-start(f32[512,256]{1,0:T(8,128)} %history.3) | copy-start | bytes 1572868
  25.9 3.5 %copy-start = (f32[512,256]{1,0:T(8,128)S(1)}, f32[512,256]{1,0:T(8,128)}, u32[]{:S(2)}) copy-start(f32[512,256]{1,0:T(8,128)} %master.1) | copy-start | bytes 1572868
  27.9 3.8 %collective-permute-start.12 = (bf16[4,32,256]{2,1,0:T(8,128)(2,1)S(1)}, bf16[4,32,256]{2,1,0:T(8,128)(2,1)S(1)}, u32[]{:S(2)}, u32[]{:S(2)}) collective-permute-start(bf16[4,32,256]{2,1,0:T(8,128)(2,1)S(1)} %fusion.3.refs_0_), channel_id=1, source_target_pairs={{0,3},{1,4},{2,7},{3,0},{4,1},{5,6},{6,5},{7,2},{8,13},{9,10},{10,... | collective-permute-start | bytes 196616 | tf_op jit(solution)/shard_map/ppermute | solution.py:33
  29.4 3.7 %copy-start.2 = (f32[32,256]{1,0:T(8,128)S(1)}, f32[32,256]{1,0:T(8,128)}, u32[]{:S(2)}) copy-start(f32[32,256]{1,0:T(8,128)} %rows.3) | copy-start | bytes 98308
  29.4 3.7 %copy-start.3 = (f32[32,256]{1,0:T(8,128)S(1)}, f32[32,256]{1,0:T(8,128)}, u32[]{:S(2)}) copy-start(f32[32,256]{1,0:T(8,128)} %history.2) | copy-start | bytes 98308
  31.0 2.8 %collective-permute-start.13 = (bf16[4,32,256]{2,1,0:T(8,128)(2,1)S(1)}, bf16[4,32,256]{2,1,0:T(8,128)(2,1)S(1)}, u32[]{:S(2)}, u32[]{:S(2)}) collective-permute-start(bf16[4,32,256]{2,1,0:T(8,128)(2,1)S(1)} %fusion.3.refs_0_), channel_id=1, source_target_pairs={{0,1},{1,0},{2,3},{3,2},{4,5},{5,4},{6,7},{7,6},{8,9},{9,8},{10,11... | collective-permute-start | bytes 196616 | tf_op jit(solution)/shard_map/ppermute | solution.py:33
  31.7 2.3 %collective-permute-start.14 = (bf16[4,32,256]{2,1,0:T(8,128)(2,1)S(1)}, bf16[4,32,256]{2,1,0:T(8,128)(2,1)S(1)}, u32[]{:S(2)}, u32[]{:S(2)}) collective-permute-start(bf16[4,32,256]{2,1,0:T(8,128)(2,1)S(1)} %collective-permute-done.12.refs_1_), channel_id=1, source_target_pairs={{0,1},{1,0},{2,3},{3,2},{4,5},{5,4},{6,7},{7,6},{8,9},{9,8},{10,11... | collective-permute-start | bytes 196616 | tf_op jit(solution)/shard_map/ppermute | solution.py:33

commit v12 on v11

--- a/solution.py
+++ b/solution.py
@@ -44,11 +44,11 @@
     return pltpu.with_memory_space_constraint(value, pltpu.HBM)
 
 
-def place_at(place, g):
+def place_at(place, g, groups):
     me = lax.axis_index("col")
     odd = parity(me) ^ (place >> 1)
     one, two = (me >> 1) & 1, (me >> 2) & 1
-    split, last, rest = (one + odd * (two - one)) ^ (place & 1), g & 1, g >> 1
+    split, last, rest = (one + odd * (two - one)) ^ (place & 1), g // (groups // 2), g % (groups // 2)
     bit_one, bit_two = split + odd * (last - split), last + odd * (split - last)
     return rest, bit_two, bit_one, odd ^ bit_one ^ bit_two ^ parity(rest)
 
@@ -88,7 +88,7 @@
     for place in range(4):
 
         def body(g, place=place):
-            at = place_at(place, g)
+            at = place_at(place, g, groups)
             amounts = near_counts[at].astype(jnp.float32)
             term = row_terms[at]
             term = jnp.concatenate([term] * (amounts.shape[1] // 128), axis=1)
@@ -176,7 +176,7 @@
     pieces, out = refs[:4], refs[4]
     for place in range(4):
         for g in range(pieces[0].shape[0]):
-            out[place_at(place, g)] = pieces[place][g]
+            out[place_at(place, g, pieces[0].shape[0])] = pieces[place][g]
 
 
 def joined(held, other, upper):
@@ -227,16 +227,17 @@
     received_0, received_1 = hop(sent_0, CORE, size), hop(sent_1, CORE, size)
     steps = [((bit, bit), side[k] > 0) for k, bit in enumerate(top_bits(size))]
     steps.append((SUM, side[len(steps)] > 0))
-    first_hop = hop(row_master[None], steps[0][0], size)
+    gathers = steps[-1:] + steps[:-1]
+    first_hop = hop(row_master[None], gathers[0][0], size)
     master, other = row_copy[None], first_hop
-    for k, (bits, upper) in enumerate(steps):
+    for k, (bits, upper) in enumerate(gathers):
         if k > 0:
             other = hop(master, bits, size)
         master = joined(master, other, upper).astype(jnp.bfloat16)
     mine = master.reshape(group_rows, width)
     beside = hop(mine, SPLIT, size)
     history, _ = lax.optimization_barrier((history[None], mine))
-    for bits, upper in steps[:-1]:
+    for bits, upper in gathers[:-1]:
         history = joined(history, hop(history, bits, size), upper)
 
     def gradient_of(kind, rows, kept, received, *after):
@@ -274,18 +275,18 @@
         name="columns",
     )(*[near(v) for v in (column_master, column_history, turned, sent_0, sent_1, mine, beside, others, slopes_0, slopes_1)])
 
-    last_history = hop(history, SUM, size)
+    last_history = hop(history, gathers[-1][0], size)
     for bits, upper in steps:
         rounded = part.astype(jnp.bfloat16)
         part = rounded.astype(jnp.float32) + hop(rounded, bits, size).astype(jnp.float32)
-    history = joined(history, last_history, steps[-1][1])
+    history = joined(history, last_history, gathers[-1][1])
 
     def adagrad(master, history, gradient):
         updated = history + gradient * gradient
         return master - step_size * gradient * lax.rsqrt(updated), updated
 
     gradient = part.reshape(group, own, width) / all_columns
-    own_gradient = lax.dynamic_index_in_dim(gradient, (me >> 3) * 2 + last_bit(me), 0, keepdims=False)
+    own_gradient = lax.dynamic_index_in_dim(gradient, last_bit(me) * (group // 2) + (me >> 3), 0, keepdims=False)
     new_rows, new_row_history = adagrad(row_master, row_history, own_gradient)
     copy = adagrad(master.astype(jnp.float32), history.astype(jnp.float32), gradient)[0].astype(jnp.bfloat16)
     beside = hop(copy, SPLIT, size)

time: 35 us -> 34.7 us (level)
  starting transfers between devices: 22.8 us -> 20.7 us
  waiting for transfers between devices: 5.07 us -> 6.9 us
    ppermute x15, starting transfers between devices: 22.8 us -> 20.7 us  [hop(): return lax.ppermute(value, 'col', pairs)]
    ppermute x15, waiting for transfers between devices: 5.07 us -> 6.9 us  [hop(): return lax.ppermute(value, 'col', pairs)]
  transfers between devices with their start and end apart: 15 -> 15, of which waited for: 5 -> 6; matrix products, arithmetic and copies ran while one was open for 2% -> 2% of each run, Pallas kernels for 13% -> 13%
where the time goes in v12:
time: 34.7 us; the launch traced here: 34.5 us
  starting transfers between devices  20.7 us (60%)
  waiting for transfers between devices  6.9 us (20%)
  Pallas kernels  5.24 us (15%)
  other arithmetic  0.84 us (2%)
  between operations  0.8 us (2%)
    ppermute x15, starting transfers between devices, hop(): return lax.ppermute(value, 'col', pairs)  20.7 us
    ppermute x15, waiting for transfers between devices, hop(): return lax.ppermute(value, 'col', pairs)  6.9 us
    pallas_call x1, Pallas kernels, per_device(): pl.pallas_call(prepare_kernel, out_shape=(terms_type,) * 4 + (pltpu.VMEM(...  2.04 us
    pallas_call x1, Pallas kernels, per_device(): pl.pallas_call(functools.partial(columns_kernel, total_rows, chunk), out_...  1.51 us
    pallas_call x2, Pallas kernels, gradient_of(): pl.pallas_call(functools.partial(rows_kernel, chunk), out_shape=(pltpu.VM...  0.94 us
    pallas_call x1, Pallas kernels, per_device(): pl.pallas_call(place_kernel, out_shape=jax.ShapeDtypeStruct(grid + (width...  0.75 us
  transfers between devices with their start and end apart: 15, of which 6 were waited for; matrix products, arithmetic and copies ran while one was open for 2% of the time, Pallas kernels for 13%

profile of v12, /device:TPU:0, one launch (start us, length us, event | category | flops | bytes accessed | tf_op | source)
XLA Modules:
  0.0 34.5 jit_solution(385820082686479036)
XLA Ops:
  0.6 2.5 %collective-permute-start = (f32[1,32,256]{2,1,0:T(8,128)}, f32[1,32,256]{2,1,0:T(8,128)S(1)}, u32[]{:S(2)}, u32[]{:S(2)}) collective-permute-start(f32[1,32,256]{2,1,0:T(8,128)} %bitcast.74), channel_id=1, source_target_pairs={{0,5},{1,2},{2,1},{3,6},{4,7},{5,0},{6,3},{7,4},{8,11},{9,12},{10,... | collective-permute-start | bytes 98312 | tf_op jit(solution)/shard_map/ppermute | solution.py:33
  3.2 2.0 %prepare.1 = (f32[2,4,32,512]{3,2,1,0:T(8,128)S(1)}, f32[2,4,32,512]{3,2,1,0:T(8,128)S(1)}, f32[2,4,32,512]{3,2,1,0:T(8,128)S(1)}, f32[2,4,32,512]{3,2,1,0:T(8,1...) custom-call(s32[2,2,2,2,32,512]{5,4,3,2,1,0:T(8,128)} %bitcast.69, ...), custom_call_target="tpu_custom_call" | custom-call | flops 2097152 | bytes 1048576 | tf_op jit(solution)/shard_map/prepare/pallas_call | solution.py:201
  5.2 0.0 collective-permute-done.refs_0_
  5.3 2.9 %collective-permute-start.1 = (bf16[2,32,256]{2,1,0:T(8,128)(2,1)S(1)}, bf16[2,32,256]{2,1,0:T(8,128)(2,1)S(1)}, u32[]{:S(2)}, u32[]{:S(2)}) collective-permute-start(bf16[2,32,256]{2,1,0:T(8,128)(2,1)S(1)} %maximum_bitcast_fusion), channel_id=1, source_target_pairs={{0,9},{1,8},{2,11},{3,10},{4,13},{5,12},{6,15},{7,14},{8,1},{9,0},... | collective-permute-start | bytes 98312 | tf_op jit(solution)/shard_map/ppermute | solution.py:33
  8.2 0.3 collective-permute-start.2
  8.5 0.2 collective-permute-start.3
  8.7 0.3 collective-permute-start.5
  9.0 0.8 %collective-permute-done.1 = bf16[2,32,256]{2,1,0:T(8,128)(2,1)S(1)} collective-permute-done((bf16[2,32,256]{2,1,0:T(8,128)(2,1)S(1)}, bf16[2,32,256]{2,1,0:T(8,128)(2,1)S(1)}, u32[]{:S(2)}, u32[]{:S(2)}) %collective-permute-start.1) | collective-permute-done | bytes 32800 | tf_op jit(solution)/shard_map/ppermute | solution.py:33
  9.9 1.6 %collective-permute-start.4 = (bf16[128,256]{1,0:T(8,128)(2,1)S(1)}, bf16[128,256]{1,0:T(8,128)(2,1)S(1)}, u32[]{:S(2)}, u32[]{:S(2)}) collective-permute-start(bf16[128,256]{1,0:T(8,128)(2,1)S(1)} %bitcast.63), channel_id=1, source_target_pairs={{0,3},{1,4},{2,7},{3,0},{4,1},{5,6},{6,5},{7,2},{8,13},{9,10},{10,... | collective-permute-start | bytes 196616 | tf_op jit(solution)/shard_map/ppermute | solution.py:33
  11.5 1.6 %collective-permute-start.10 = (bf16[1,32,256]{2,1,0:T(8,128)(2,1)S(1)}, bf16[1,32,256]{2,1,0:T(8,128)(2,1)S(1)}, u32[]{:S(2)}, u32[]{:S(2)}) collective-permute-start(bf16[1,32,256]{2,1,0:T(8,128)(2,1)S(1)} %bitcast.67), channel_id=1, source_target_pairs={{0,5},{1,2},{2,1},{3,6},{4,7},{5,0},{6,3},{7,4},{8,11},{9,12},{10,... | collective-permute-start | bytes 49160 | tf_op jit(solution)/shard_map/ppermute | solution.py:33
  13.1 0.5 %collective-permute-done.4.rows.beside = bf16[128,256]{1,0:T(8,128)(2,1)S(1)} collective-permute-done((bf16[128,256]{1,0:T(8,128)(2,1)S(1)}, bf16[128,256]{1,0:T(8,128)(2,1)S(1)}, u32[]{:S(2)}, u32[]{:S(2)}) %collective-permute-start.4) | collective-permute-done | bytes 65568 | tf_op jit(solution)/shard_map/ppermute | solution.py:33
  13.6 0.0 collective-permute-done.3.other_columns
  13.6 0.0 collective-permute-done.5.received
  13.7 0.5 %rows.5 = (bf16[128,256]{1,0:T(8,128)(2,1)S(1)}, bf16[128,512]{1,0:T(8,128)(2,1)S(1)}) custom-call(bf16[128,256]{1,0:T(8,128)(2,1)S(1)} %collective-permute-done.4.rows.beside, f32[2,4,32,512]{3,2,1,0:T(8,128)S(1)} %get-tuple-element.34.kept, f32[2,4,32,512]{3,2,1,0:T(8,128)S(1)} %collective-permute-done.5.received, ...), custom_call_target="tpu_custom_call" | custom-call | flops 134217728 | tf_op jit(solution)/shard_map/rows/pallas_call | solution.py:244
  14.1 1.6 %collective-permute-start.6 = (bf16[128,256]{1,0:T(8,128)(2,1)S(1)}, bf16[128,256]{1,0:T(8,128)(2,1)S(1)}, u32[]{:S(2)}, u32[]{:S(2)}) collective-permute-start(bf16[128,256]{1,0:T(8,128)(2,1)S(1)} %get-tuple-element.37), channel_id=1, source_target_pairs={{0,3},{1,4},{2,7},{3,0},{4,1},{5,6},{6,5},{7,2},{8,13},{9,10},{10,... | collective-permute-start | bytes 196616 | tf_op jit(solution)/shard_map/ppermute | solution.py:33
  15.8 0.0 collective-permute-done.10
  15.8 0.6 %collective-permute-start.9 = (bf16[256,256]{1,0:T(8,128)(2,1)S(1)}, bf16[256,256]{1,0:T(8,128)(2,1)S(1)}, u32[]{:S(2)}, u32[]{:S(2)}) collective-permute-start(bf16[256,256]{1,0:T(8,128)(2,1)S(1)} %pad_maximum_fusion), channel_id=1, source_target_pairs={{0,1},{1,0},{2,3},{3,2},{4,5},{5,4},{6,7},{7,6},{8,9},{9,8},{10,11... | collective-permute-start | bytes 393224 | tf_op jit(solution)/shard_map/ppermute | solution.py:33
  16.4 0.0 collective-permute-done.2.received
  16.4 0.5 %rows.4 = (f32[128,256]{1,0:T(8,128)S(1)}, bf16[128,512]{1,0:T(8,128)(2,1)S(1)}) custom-call(bf16[128,256]{1,0:T(8,128)(2,1)S(1)} %bitcast.65, f32[2,4,32,512]{3,2,1,0:T(8,128)S(1)} %get-tuple-element.29.kept, f32[2,4,32,512]{3,2,1,0:T(8,128)S(1)} %collective-permute-done.2.received, bf16[512,256]{1,0:T(8,128)(2,1)S(1)} %get-tuple-element.31.columns, ...), custom_call_target="tpu_custom_call" | custom-call | flops 134217728 | tf_op jit(solution)/shard_map/rows/pallas_call | solution.py:244
  16.8 1.1 %collective-permute-done.6 = bf16[128,256]{1,0:T(8,128)(2,1)S(1)} collective-permute-done((bf16[128,256]{1,0:T(8,128)(2,1)S(1)}, bf16[128,256]{1,0:T(8,128)(2,1)S(1)}, u32[]{:S(2)}, u32[]{:S(2)}) %collective-permute-start.6) | collective-permute-done | bytes 65568 | tf_op jit(solution)/shard_map/ppermute | solution.py:33
  17.9 3.2 %collective-permute-start.7 = (bf16[128,256]{1,0:T(8,128)(2,1)S(1)}, bf16[128,256]{1,0:T(8,128)(2,1)S(1)}, u32[]{:S(2)}, u32[]{:S(2)}) collective-permute-start(bf16[128,256]{1,0:T(8,128)(2,1)S(1)} %add_convert_fusion.1), channel_id=1, source_target_pairs={{0,9},{1,8},{2,11},{3,10},{4,13},{5,12},{6,15},{7,14},{8,1},{9,0},... | collective-permute-start | bytes 196616 | tf_op jit(solution)/shard_map/ppermute | solution.py:33
  21.1 0.0 collective-permute-done.9.others
  21.1 0.1 collective-permute-start.11
  21.2 2.4 %collective-permute-done.7 = bf16[128,256]{1,0:T(8,128)(2,1)S(1)} collective-permute-done((bf16[128,256]{1,0:T(8,128)(2,1)S(1)}, bf16[128,256]{1,0:T(8,128)(2,1)S(1)}, u32[]{:S(2)}, u32[]{:S(2)}) %collective-permute-start.7) | collective-permute-done | bytes 65568 | tf_op jit(solution)/shard_map/ppermute | solution.py:33
  23.6 3.0 %collective-permute-start.8 = (bf16[128,256]{1,0:T(8,128)(2,1)S(1)}, bf16[128,256]{1,0:T(8,128)(2,1)S(1)}, u32[]{:S(2)}, u32[]{:S(2)}) collective-permute-start(bf16[128,256]{1,0:T(8,128)(2,1)S(1)} %add_convert_fusion), channel_id=1, source_target_pairs={{0,5},{1,2},{2,1},{3,6},{4,7},{5,0},{6,3},{7,4},{8,11},{9,12},{10,... | collective-permute-start | bytes 196616 | tf_op jit(solution)/shard_map/ppermute | solution.py:33
  26.6 0.0 collective-permute-done.11
  26.7 0.0 copy-start.1
  26.7 0.0 copy-start
  26.7 1.9 %collective-permute-done.8 = bf16[128,256]{1,0:T(8,128)(2,1)S(1)} collective-permute-done((bf16[128,256]{1,0:T(8,128)(2,1)S(1)}, bf16[128,256]{1,0:T(8,128)(2,1)S(1)}, u32[]{:S(2)}, u32[]{:S(2)}) %collective-permute-start.8) | collective-permute-done | bytes 65568 | tf_op jit(solution)/shard_map/ppermute | solution.py:33
  28.7 1.9 %collective-permute-start.12 = (bf16[4,32,256]{2,1,0:T(8,128)(2,1)S(1)}, bf16[4,32,256]{2,1,0:T(8,128)(2,1)S(1)}, u32[]{:S(2)}, u32[]{:S(2)}) collective-permute-start(bf16[4,32,256]{2,1,0:T(8,128)(2,1)S(1)} %fusion.3.refs_0_), channel_id=1, source_target_pairs={{0,3},{1,4},{2,7},{3,0},{4,1},{5,6},{6,5},{7,2},{8,13},{9,10},{10,... | collective-permute-start | bytes 196616 | tf_op jit(solution)/shard_map/ppermute | solution.py:33
  30.5 0.0 copy-done.1
  30.5 0.0 copy-done
  30.5 0.0 copy-start.2
  30.5 0.0 copy-start.3
  30.5 1.5 %columns.3 = (f32[512,256]{1,0:T(8,128)}, f32[512,256]{1,0:T(8,128)}) custom-call(f32[512,256]{1,0:T(8,128)S(1)} %copy-done, f32[512,256]{1,0:T(8,128)S(1)} %copy-done.1, bf16[256,512]{1,0:T(8,128)(2,1)S(1)} %get-tuple-element.32.turned, f32[2,4,32,512]{3,2,1,0:T(8,128)S(1)} %get-tuple-element.30.sent_0, f32[2,4,32,512]{3,2,1,0:T(8,128)S(1)} %get-tuple-element.35.sent_1, ...), custom_call_target="tpu_custom_call" | custom-call | flops 134217728 | bytes 2097152 | tf_op jit(solution)/shard_map/columns/pallas_call | solution.py:262
  32.1 0.5 %collective-permute-start.13 = (bf16[4,32,256]{2,1,0:T(8,128)(2,1)S(1)}, bf16[4,32,256]{2,1,0:T(8,128)(2,1)S(1)}, u32[]{:S(2)}, u32[]{:S(2)}) collective-permute-start(bf16[4,32,256]{2,1,0:T(8,128)(2,1)S(1)} %fusion.3.refs_0_), channel_id=1, source_target_pairs={{0,1},{1,0},{2,3},{3,2},{4,5},{5,4},{6,7},{7,6},{8,9},{9,8},{10,11... | collective-permute-start | bytes 196616 | tf_op jit(solution)/shard_map/ppermute | solution.py:33
  32.5 0.0 collective-permute-done.12.refs_1_
  32.5 0.4 %collective-permute-start.14 = (bf16[4,32,256]{2,1,0:T(8,128)(2,1)S(1)}, bf16[4,32,256]{2,1,0:T(8,128)(2,1)S(1)}, u32[]{:S(2)}, u32[]{:S(2)}) collective-permute-start(bf16[4,32,256]{2,1,0:T(8,128)(2,1)S(1)} %collective-permute-done.12.refs_1_), channel_id=1, source_target_pairs={{0,1},{1,0},{2,3},{3,2},{4,5},{5,4},{6,7},{7,6},{8,9},{9,8},{10,11... | collective-permute-start | bytes 196616 | tf_op jit(solution)/shard_map/ppermute | solution.py:33
  32.9 0.0 copy-done.2
  32.9 0.0 copy-done.3
  32.9 0.6 %fusion.6 = (f32[32,256]{1,0:T(8,128)}, f32[32,256]{1,0:T(8,128)}) fusion(f32[32,256]{1,0:T(8,128)S(1)} %copy-done.2, f32[4,32,256]{2,1,0:T(8,128)S(1)} %bitcast.71, s32[]{:T(128)S(6)} %select_n.39, f32[32,256]{1,0:T(8,128)S(1)} %copy-done.3), kind=kLoop, calls=%fused_computation.17 | loop fusion | flops 40960 | bytes 163844 | tf_op jit(solution)/shard_map/sub | solution.py:286
  33.5 0.0 collective-permute-done.13.refs_2_
  33.5 0.3 collective-permute-done.14.refs_3_
  33.8 0.8 %place.1 = bf16[2,2,2,2,32,256]{5,4,3,2,1,0:T(8,128)(2,1)} custom-call(bf16[4,32,256]{2,1,0:T(8,128)(2,1)S(1)} %fusion.3.refs_0_, bf16[4,32,256]{2,1,0:T(8,128)(2,1)S(1)} %collective-permute-done.12.refs_1_, bf16[4,32,256]{2,1,0:T(8,128)(2,1)S(1)} %collective-permute-done.13.refs_2_, bf16[4,32,256]{2,1,0:T(8,128)(2,1)S(1)} %collective-permute-done.14.refs_3_), custom_call_target="tpu_custom_call" | custom-call | tf_op jit(solution)/shard_map/place/pallas_call | solution.py:294
  (17 shorter events, 0.2 us)
Async XLA Ops:
  0.6 4.6 %collective-permute-start = (f32[1,32,256]{2,1,0:T(8,128)}, f32[1,32,256]{2,1,0:T(8,128)S(1)}, u32[]{:S(2)}, u32[]{:S(2)}) collective-permute-start(f32[1,32,256]{2,1,0:T(8,128)} %bitcast.74), channel_id=1, source_target_pairs={{0,5},{1,2},{2,1},{3,6},{4,7},{5,0},{6,3},{7,4},{8,11},{9,12},{10,... | collective-permute-start | bytes 98312 | tf_op jit(solution)/shard_map/ppermute | solution.py:33
  5.3 4.5 %collective-permute-start.1 = (bf16[2,32,256]{2,1,0:T(8,128)(2,1)S(1)}, bf16[2,32,256]{2,1,0:T(8,128)(2,1)S(1)}, u32[]{:S(2)}, u32[]{:S(2)}) collective-permute-start(bf16[2,32,256]{2,1,0:T(8,128)(2,1)S(1)} %maximum_bitcast_fusion), channel_id=1, source_target_pairs={{0,9},{1,8},{2,11},{3,10},{4,13},{5,12},{6,15},{7,14},{8,1},{9,0},... | collective-permute-start | bytes 98312 | tf_op jit(solution)/shard_map/ppermute | solution.py:33
  8.2 8.2 %collective-permute-start.2 = (f32[2,4,32,512]{3,2,1,0:T(8,128)S(1)}, f32[2,4,32,512]{3,2,1,0:T(8,128)S(1)}, u32[]{:S(2)}, u32[]{:S(2)}) collective-permute-start(f32[2,4,32,512]{3,2,1,0:T(8,128)S(1)} %get-tuple-element.30.sent_0), channel_id=1, source_target_pairs={{0,1},{1,0},{2,3},{3,2},{4,5},{5,4},{6,7},{7,6},{8,9},{9,8},{10,11... | collective-permute-start | bytes 1572872 | tf_op jit(solution)/shard_map/ppermute | solution.py:33
  8.5 5.1 %collective-permute-start.3 = (bf16[512,256]{1,0:T(8,128)(2,1)S(1)}, bf16[512,256]{1,0:T(8,128)(2,1)S(1)}, u32[]{:S(2)}, u32[]{:S(2)}) collective-permute-start(bf16[512,256]{1,0:T(8,128)(2,1)S(1)} %get-tuple-element.31.columns), channel_id=1, source_target_pairs={{0,1},{1,0},{2,3},{3,2},{4,5},{5,4},{6,7},{7,6},{8,9},{9,8},{10,11... | collective-permute-start | bytes 786440 | tf_op jit(solution)/shard_map/ppermute | solution.py:33
  8.7 4.9 %collective-permute-start.5 = (f32[2,4,32,512]{3,2,1,0:T(8,128)S(1)}, f32[2,4,32,512]{3,2,1,0:T(8,128)S(1)}, u32[]{:S(2)}, u32[]{:S(2)}) collective-permute-start(f32[2,4,32,512]{3,2,1,0:T(8,128)S(1)} %get-tuple-element.35.sent_1), channel_id=1, source_target_pairs={{0,1},{1,0},{2,3},{3,2},{4,5},{5,4},{6,7},{7,6},{8,9},{9,8},{10,11... | collective-permute-start | bytes 1572872 | tf_op jit(solution)/shard_map/ppermute | solution.py:33
  9.9 3.8 %collective-permute-start.4 = (bf16[128,256]{1,0:T(8,128)(2,1)S(1)}, bf16[128,256]{1,0:T(8,128)(2,1)S(1)}, u32[]{:S(2)}, u32[]{:S(2)}) collective-permute-start(bf16[128,256]{1,0:T(8,128)(2,1)S(1)} %bitcast.63), channel_id=1, source_target_pairs={{0,3},{1,4},{2,7},{3,0},{4,1},{5,6},{6,5},{7,2},{8,13},{9,10},{10,... | collective-permute-start | bytes 196616 | tf_op jit(solution)/shard_map/ppermute | solution.py:33
  11.5 4.3 %collective-permute-start.10 = (bf16[1,32,256]{2,1,0:T(8,128)(2,1)S(1)}, bf16[1,32,256]{2,1,0:T(8,128)(2,1)S(1)}, u32[]{:S(2)}, u32[]{:S(2)}) collective-permute-start(bf16[1,32,256]{2,1,0:T(8,128)(2,1)S(1)} %bitcast.67), channel_id=1, source_target_pairs={{0,5},{1,2},{2,1},{3,6},{4,7},{5,0},{6,3},{7,4},{8,11},{9,12},{10,... | collective-permute-start | bytes 49160 | tf_op jit(solution)/shard_map/ppermute | solution.py:33
  14.1 3.8 %collective-permute-start.6 = (bf16[128,256]{1,0:T(8,128)(2,1)S(1)}, bf16[128,256]{1,0:T(8,128)(2,1)S(1)}, u32[]{:S(2)}, u32[]{:S(2)}) collective-permute-start(bf16[128,256]{1,0:T(8,128)(2,1)S(1)} %get-tuple-element.37), channel_id=1, source_target_pairs={{0,3},{1,4},{2,7},{3,0},{4,1},{5,6},{6,5},{7,2},{8,13},{9,10},{10,... | collective-permute-start | bytes 196616 | tf_op jit(solution)/shard_map/ppermute | solution.py:33
  15.8 5.3 %collective-permute-start.9 = (bf16[256,256]{1,0:T(8,128)(2,1)S(1)}, bf16[256,256]{1,0:T(8,128)(2,1)S(1)}, u32[]{:S(2)}, u32[]{:S(2)}) collective-permute-start(bf16[256,256]{1,0:T(8,128)(2,1)S(1)} %pad_maximum_fusion), channel_id=1, source_target_pairs={{0,1},{1,0},{2,3},{3,2},{4,5},{5,4},{6,7},{7,6},{8,9},{9,8},{10,11... | collective-permute-start | bytes 393224 | tf_op jit(solution)/shard_map/ppermute | solution.py:33
  17.9 5.7 %collective-permute-start.7 = (bf16[128,256]{1,0:T(8,128)(2,1)S(1)}, bf16[128,256]{1,0:T(8,128)(2,1)S(1)}, u32[]{:S(2)}, u32[]{:S(2)}) collective-permute-start(bf16[128,256]{1,0:T(8,128)(2,1)S(1)} %add_convert_fusion.1), channel_id=1, source_target_pairs={{0,9},{1,8},{2,11},{3,10},{4,13},{5,12},{6,15},{7,14},{8,1},{9,0},... | collective-permute-start | bytes 196616 | tf_op jit(solution)/shard_map/ppermute | solution.py:33
  21.1 5.5 %collective-permute-start.11 = (bf16[2,32,256]{2,1,0:T(8,128)(2,1)S(1)}, bf16[2,32,256]{2,1,0:T(8,128)(2,1)S(1)}, u32[]{:S(2)}, u32[]{:S(2)}) collective-permute-start(bf16[2,32,256]{2,1,0:T(8,128)(2,1)S(1)} %maximum_bitcast_fusion.1), channel_id=1, source_target_pairs={{0,9},{1,8},{2,11},{3,10},{4,13},{5,12},{6,15},{7,14},{8,1},{9,0},... | collective-permute-start | bytes 98312 | tf_op jit(solution)/shard_map/ppermute | solution.py:33
  23.6 5.0 %collective-permute-start.8 = (bf16[128,256]{1,0:T(8,128)(2,1)S(1)}, bf16[128,256]{1,0:T(8,128)(2,1)S(1)}, u32[]{:S(2)}, u32[]{:S(2)}) collective-permute-start(bf16[128,256]{1,0:T(8,128)(2,1)S(1)} %add_convert_fusion), channel_id=1, source_target_pairs={{0,5},{1,2},{2,1},{3,6},{4,7},{5,0},{6,3},{7,4},{8,11},{9,12},{10,... | collective-permute-start | bytes 196616 | tf_op jit(solution)/shard_map/ppermute | solution.py:33
  26.7 3.8 %copy-start.1 = (f32[512,256]{1,0:T(8,128)S(1)}, f32[512,256]{1,0:T(8,128)}, u32[]{:S(2)}) copy-start(f32[512,256]{1,0:T(8,128)} %history.3) | copy-start | bytes 1572868
  26.7 3.8 %copy-start = (f32[512,256]{1,0:T(8,128)S(1)}, f32[512,256]{1,0:T(8,128)}, u32[]{:S(2)}) copy-start(f32[512,256]{1,0:T(8,128)} %master.1) | copy-start | bytes 1572868
  28.7 3.8 %collective-permute-start.12 = (bf16[4,32,256]{2,1,0:T(8,128)(2,1)S(1)}, bf16[4,32,256]{2,1,0:T(8,128)(2,1)S(1)}, u32[]{:S(2)}, u32[]{:S(2)}) collective-permute-start(bf16[4,32,256]{2,1,0:T(8,128)(2,1)S(1)} %fusion.3.refs_0_), channel_id=1, source_target_pairs={{0,3},{1,4},{2,7},{3,0},{4,1},{5,6},{6,5},{7,2},{8,13},{9,10},{10,... | collective-permute-start | bytes 196616 | tf_op jit(solution)/shard_map/ppermute | solution.py:33
  30.5 2.3 %copy-start.2 = (f32[32,256]{1,0:T(8,128)S(1)}, f32[32,256]{1,0:T(8,128)}, u32[]{:S(2)}) copy-start(f32[32,256]{1,0:T(8,128)} %rows.3) | copy-start | bytes 98308
  30.5 2.3 %copy-start.3 = (f32[32,256]{1,0:T(8,128)S(1)}, f32[32,256]{1,0:T(8,128)}, u32[]{:S(2)}) copy-start(f32[32,256]{1,0:T(8,128)} %history.2) | copy-start | bytes 98308
  32.1 1.5 %collective-permute-start.13 = (bf16[4,32,256]{2,1,0:T(8,128)(2,1)S(1)}, bf16[4,32,256]{2,1,0:T(8,128)(2,1)S(1)}, u32[]{:S(2)}, u32[]{:S(2)}) collective-permute-start(bf16[4,32,256]{2,1,0:T(8,128)(2,1)S(1)} %fusion.3.refs_0_), channel_id=1, source_target_pairs={{0,1},{1,0},{2,3},{3,2},{4,5},{5,4},{6,7},{7,6},{8,9},{9,8},{10,11... | collective-permute-start | bytes 196616 | tf_op jit(solution)/shard_map/ppermute | solution.py:33
  32.5 1.3 %collective-permute-start.14 = (bf16[4,32,256]{2,1,0:T(8,128)(2,1)S(1)}, bf16[4,32,256]{2,1,0:T(8,128)(2,1)S(1)}, u32[]{:S(2)}, u32[]{:S(2)}) collective-permute-start(bf16[4,32,256]{2,1,0:T(8,128)(2,1)S(1)} %collective-permute-done.12.refs_1_), channel_id=1, source_target_pairs={{0,1},{1,0},{2,3},{3,2},{4,5},{5,4},{6,7},{7,6},{8,9},{9,8},{10,11... | collective-permute-start | bytes 196616 | tf_op jit(solution)/shard_map/ppermute | solution.py:33

commit v13 on v12

--- a/solution.py
+++ b/solution.py
@@ -289,8 +289,8 @@
     own_gradient = lax.dynamic_index_in_dim(gradient, last_bit(me) * (group // 2) + (me >> 3), 0, keepdims=False)
     new_rows, new_row_history = adagrad(row_master, row_history, own_gradient)
     copy = adagrad(master.astype(jnp.float32), history.astype(jnp.float32), gradient)[0].astype(jnp.bfloat16)
+    copy, new_columns = lax.optimization_barrier((copy, new_columns))
     beside = hop(copy, SPLIT, size)
-    beside, new_columns = lax.optimization_barrier((beside, new_columns))
     grid_rows = pl.pallas_call(
         place_kernel,
         out_shape=jax.ShapeDtypeStruct(grid + (width,), jnp.bfloat16),

time: 34.7 us -> 34.8 us (level)
  transfers between devices with their start and end apart: 15 -> 15, of which waited for: 6 -> 7; matrix products, arithmetic and copies ran while one was open for 2% -> 2% of each run, Pallas kernels for 13% -> 13%
where the time goes in v13:
time: 34.8 us; the launch traced here: 34.5 us
  starting transfers between devices  20.7 us (59%)
  waiting for transfers between devices  6.93 us (20%)
  Pallas kernels  5.22 us (15%)
  other arithmetic  0.85 us (2%)
  between operations  0.81 us (2%)
    ppermute x15, starting transfers between devices, hop(): return lax.ppermute(value, 'col', pairs)  20.7 us
    ppermute x15, waiting for transfers between devices, hop(): return lax.ppermute(value, 'col', pairs)  6.93 us
    pallas_call x1, Pallas kernels, per_device(): pl.pallas_call(prepare_kernel, out_shape=(terms_type,) * 4 + (pltpu.VMEM(...  2.04 us
    pallas_call x1, Pallas kernels, per_device(): pl.pallas_call(functools.partial(columns_kernel, total_rows, chunk), out_...  1.5 us
    pallas_call x2, Pallas kernels, gradient_of(): pl.pallas_call(functools.partial(rows_kernel, chunk), out_shape=(pltpu.VM...  0.94 us
    pallas_call x1, Pallas kernels, per_device(): pl.pallas_call(place_kernel, out_shape=jax.ShapeDtypeStruct(grid + (width...  0.74 us
  transfers between devices with their start and end apart: 15, of which 7 were waited for; matrix products, arithmetic and copies ran while one was open for 2% of the time, Pallas kernels for 13%

profile of v13, /device:TPU:0, one launch (start us, length us, event | category | flops | bytes accessed | tf_op | source)
XLA Modules:
  0.0 34.5 jit_solution(3766430697905530211)
XLA Ops:
  0.6 2.5 %collective-permute-start = (f32[1,32,256]{2,1,0:T(8,128)}, f32[1,32,256]{2,1,0:T(8,128)S(1)}, u32[]{:S(2)}, u32[]{:S(2)}) collective-permute-start(f32[1,32,256]{2,1,0:T(8,128)} %bitcast.74), channel_id=1, source_target_pairs={{0,5},{1,2},{2,1},{3,6},{4,7},{5,0},{6,3},{7,4},{8,11},{9,12},{10,... | collective-permute-start | bytes 98312 | tf_op jit(solution)/shard_map/ppermute | solution.py:33
  3.2 2.0 %prepare.1 = (f32[2,4,32,512]{3,2,1,0:T(8,128)S(1)}, f32[2,4,32,512]{3,2,1,0:T(8,128)S(1)}, f32[2,4,32,512]{3,2,1,0:T(8,128)S(1)}, f32[2,4,32,512]{3,2,1,0:T(8,1...) custom-call(s32[2,2,2,2,32,512]{5,4,3,2,1,0:T(8,128)} %bitcast.69, ...), custom_call_target="tpu_custom_call" | custom-call | flops 2097152 | bytes 1048576 | tf_op jit(solution)/shard_map/prepare/pallas_call | solution.py:201
  5.2 0.0 collective-permute-done.refs_0_
  5.3 2.9 %collective-permute-start.1 = (bf16[2,32,256]{2,1,0:T(8,128)(2,1)S(1)}, bf16[2,32,256]{2,1,0:T(8,128)(2,1)S(1)}, u32[]{:S(2)}, u32[]{:S(2)}) collective-permute-start(bf16[2,32,256]{2,1,0:T(8,128)(2,1)S(1)} %maximum_bitcast_fusion), channel_id=1, source_target_pairs={{0,9},{1,8},{2,11},{3,10},{4,13},{5,12},{6,15},{7,14},{8,1},{9,0},... | collective-permute-start | bytes 98312 | tf_op jit(solution)/shard_map/ppermute | solution.py:33
  8.2 0.3 collective-permute-start.2
  8.5 0.2 collective-permute-start.3
  8.7 0.3 collective-permute-start.5
  9.0 0.8 %collective-permute-done.1 = bf16[2,32,256]{2,1,0:T(8,128)(2,1)S(1)} collective-permute-done((bf16[2,32,256]{2,1,0:T(8,128)(2,1)S(1)}, bf16[2,32,256]{2,1,0:T(8,128)(2,1)S(1)}, u32[]{:S(2)}, u32[]{:S(2)}) %collective-permute-start.1) | collective-permute-done | bytes 32800 | tf_op jit(solution)/shard_map/ppermute | solution.py:33
  9.9 1.6 %collective-permute-start.4 = (bf16[128,256]{1,0:T(8,128)(2,1)S(1)}, bf16[128,256]{1,0:T(8,128)(2,1)S(1)}, u32[]{:S(2)}, u32[]{:S(2)}) collective-permute-start(bf16[128,256]{1,0:T(8,128)(2,1)S(1)} %bitcast.63), channel_id=1, source_target_pairs={{0,3},{1,4},{2,7},{3,0},{4,1},{5,6},{6,5},{7,2},{8,13},{9,10},{10,... | collective-permute-start | bytes 196616 | tf_op jit(solution)/shard_map/ppermute | solution.py:33
  11.5 1.6 %collective-permute-start.10 = (bf16[1,32,256]{2,1,0:T(8,128)(2,1)S(1)}, bf16[1,32,256]{2,1,0:T(8,128)(2,1)S(1)}, u32[]{:S(2)}, u32[]{:S(2)}) collective-permute-start(bf16[1,32,256]{2,1,0:T(8,128)(2,1)S(1)} %bitcast.67), channel_id=1, source_target_pairs={{0,5},{1,2},{2,1},{3,6},{4,7},{5,0},{6,3},{7,4},{8,11},{9,12},{10,... | collective-permute-start | bytes 49160 | tf_op jit(solution)/shard_map/ppermute | solution.py:33
  13.1 0.5 %collective-permute-done.4.rows.beside = bf16[128,256]{1,0:T(8,128)(2,1)S(1)} collective-permute-done((bf16[128,256]{1,0:T(8,128)(2,1)S(1)}, bf16[128,256]{1,0:T(8,128)(2,1)S(1)}, u32[]{:S(2)}, u32[]{:S(2)}) %collective-permute-start.4) | collective-permute-done | bytes 65568 | tf_op jit(solution)/shard_map/ppermute | solution.py:33
  13.6 0.0 collective-permute-done.3.other_columns
  13.6 0.0 collective-permute-done.5.received
  13.7 0.5 %rows.5 = (bf16[128,256]{1,0:T(8,128)(2,1)S(1)}, bf16[128,512]{1,0:T(8,128)(2,1)S(1)}) custom-call(bf16[128,256]{1,0:T(8,128)(2,1)S(1)} %collective-permute-done.4.rows.beside, f32[2,4,32,512]{3,2,1,0:T(8,128)S(1)} %get-tuple-element.34.kept, f32[2,4,32,512]{3,2,1,0:T(8,128)S(1)} %collective-permute-done.5.received, ...), custom_call_target="tpu_custom_call" | custom-call | flops 134217728 | tf_op jit(solution)/shard_map/rows/pallas_call | solution.py:244
  14.1 1.6 %collective-permute-start.6 = (bf16[128,256]{1,0:T(8,128)(2,1)S(1)}, bf16[128,256]{1,0:T(8,128)(2,1)S(1)}, u32[]{:S(2)}, u32[]{:S(2)}) collective-permute-start(bf16[128,256]{1,0:T(8,128)(2,1)S(1)} %get-tuple-element.37), channel_id=1, source_target_pairs={{0,3},{1,4},{2,7},{3,0},{4,1},{5,6},{6,5},{7,2},{8,13},{9,10},{10,... | collective-permute-start | bytes 196616 | tf_op jit(solution)/shard_map/ppermute | solution.py:33
  15.8 0.0 collective-permute-done.10
  15.8 0.6 %collective-permute-start.9 = (bf16[256,256]{1,0:T(8,128)(2,1)S(1)}, bf16[256,256]{1,0:T(8,128)(2,1)S(1)}, u32[]{:S(2)}, u32[]{:S(2)}) collective-permute-start(bf16[256,256]{1,0:T(8,128)(2,1)S(1)} %pad_maximum_fusion), channel_id=1, source_target_pairs={{0,1},{1,0},{2,3},{3,2},{4,5},{5,4},{6,7},{7,6},{8,9},{9,8},{10,11... | collective-permute-start | bytes 393224 | tf_op jit(solution)/shard_map/ppermute | solution.py:33
  16.4 0.0 collective-permute-done.2.received
  16.4 0.0 copy-start.1
  16.4 0.5 %rows.4 = (f32[128,256]{1,0:T(8,128)S(1)}, bf16[128,512]{1,0:T(8,128)(2,1)S(1)}) custom-call(bf16[128,256]{1,0:T(8,128)(2,1)S(1)} %bitcast.65, f32[2,4,32,512]{3,2,1,0:T(8,128)S(1)} %get-tuple-element.29.kept, f32[2,4,32,512]{3,2,1,0:T(8,128)S(1)} %collective-permute-done.2.received, bf16[512,256]{1,0:T(8,128)(2,1)S(1)} %get-tuple-element.31.columns, ...), custom_call_target="tpu_custom_call" | custom-call | flops 134217728 | tf_op jit(solution)/shard_map/rows/pallas_call | solution.py:244
  16.8 0.0 copy-start
  16.9 1.0 %collective-permute-done.6 = bf16[128,256]{1,0:T(8,128)(2,1)S(1)} collective-permute-done((bf16[128,256]{1,0:T(8,128)(2,1)S(1)}, bf16[128,256]{1,0:T(8,128)(2,1)S(1)}, u32[]{:S(2)}, u32[]{:S(2)}) %collective-permute-start.6) | collective-permute-done | bytes 65568 | tf_op jit(solution)/shard_map/ppermute | solution.py:33
  17.9 3.2 %collective-permute-start.7 = (bf16[128,256]{1,0:T(8,128)(2,1)S(1)}, bf16[128,256]{1,0:T(8,128)(2,1)S(1)}, u32[]{:S(2)}, u32[]{:S(2)}) collective-permute-start(bf16[128,256]{1,0:T(8,128)(2,1)S(1)} %add_convert_fusion.1), channel_id=1, source_target_pairs={{0,9},{1,8},{2,11},{3,10},{4,13},{5,12},{6,15},{7,14},{8,1},{9,0},... | collective-permute-start | bytes 196616 | tf_op jit(solution)/shard_map/ppermute | solution.py:33
  21.1 0.0 collective-permute-done.9.others
  21.1 0.1 collective-permute-start.11
  21.2 2.4 %collective-permute-done.7 = bf16[128,256]{1,0:T(8,128)(2,1)S(1)} collective-permute-done((bf16[128,256]{1,0:T(8,128)(2,1)S(1)}, bf16[128,256]{1,0:T(8,128)(2,1)S(1)}, u32[]{:S(2)}, u32[]{:S(2)}) %collective-permute-start.7) | collective-permute-done | bytes 65568 | tf_op jit(solution)/shard_map/ppermute | solution.py:33
  23.6 3.0 %collective-permute-start.8 = (bf16[128,256]{1,0:T(8,128)(2,1)S(1)}, bf16[128,256]{1,0:T(8,128)(2,1)S(1)}, u32[]{:S(2)}, u32[]{:S(2)}) collective-permute-start(bf16[128,256]{1,0:T(8,128)(2,1)S(1)} %add_convert_fusion), channel_id=1, source_target_pairs={{0,5},{1,2},{2,1},{3,6},{4,7},{5,0},{6,3},{7,4},{8,11},{9,12},{10,... | collective-permute-start | bytes 196616 | tf_op jit(solution)/shard_map/ppermute | solution.py:33
  26.6 0.0 copy-done.1
  26.7 0.0 copy-done
  26.7 1.5 %columns.3 = (f32[512,256]{1,0:T(8,128)}, f32[512,256]{1,0:T(8,128)}) custom-call(f32[512,256]{1,0:T(8,128)S(1)} %copy-done, f32[512,256]{1,0:T(8,128)S(1)} %copy-done.1, bf16[256,512]{1,0:T(8,128)(2,1)S(1)} %get-tuple-element.32.turned, f32[2,4,32,512]{3,2,1,0:T(8,128)S(1)} %get-tuple-element.30.sent_0, f32[2,4,32,512]{3,2,1,0:T(8,128)S(1)} %get-tuple-element.35.sent_1, ...), custom_call_target="tpu_custom_call" | custom-call | flops 134217728 | bytes 2097152 | tf_op jit(solution)/shard_map/columns/pallas_call | solution.py:262
  28.2 0.0 collective-permute-done.11
  28.2 0.4 %collective-permute-done.8 = bf16[128,256]{1,0:T(8,128)(2,1)S(1)} collective-permute-done((bf16[128,256]{1,0:T(8,128)(2,1)S(1)}, bf16[128,256]{1,0:T(8,128)(2,1)S(1)}, u32[]{:S(2)}, u32[]{:S(2)}) %collective-permute-start.8) | collective-permute-done | bytes 65568 | tf_op jit(solution)/shard_map/ppermute | solution.py:33
  28.6 0.0 copy-start.3
  28.7 0.0 copy-start.2
  28.7 1.9 %collective-permute-start.12 = (bf16[4,32,256]{2,1,0:T(8,128)(2,1)S(1)}, bf16[4,32,256]{2,1,0:T(8,128)(2,1)S(1)}, u32[]{:S(2)}, u32[]{:S(2)}) collective-permute-start(bf16[4,32,256]{2,1,0:T(8,128)(2,1)S(1)} %fusion.3.refs_0_), channel_id=1, source_target_pairs={{0,3},{1,4},{2,7},{3,0},{4,1},{5,6},{6,5},{7,2},{8,13},{9,10},{10,... | collective-permute-start | bytes 196616 | tf_op jit(solution)/shard_map/ppermute | solution.py:33
  30.6 0.4 %collective-permute-start.13 = (bf16[4,32,256]{2,1,0:T(8,128)(2,1)S(1)}, bf16[4,32,256]{2,1,0:T(8,128)(2,1)S(1)}, u32[]{:S(2)}, u32[]{:S(2)}) collective-permute-start(bf16[4,32,256]{2,1,0:T(8,128)(2,1)S(1)} %fusion.3.refs_0_), channel_id=1, source_target_pairs={{0,1},{1,0},{2,3},{3,2},{4,5},{5,4},{6,7},{7,6},{8,9},{9,8},{10,11... | collective-permute-start | bytes 196616 | tf_op jit(solution)/shard_map/ppermute | solution.py:33
  30.9 1.6 %collective-permute-done.12.refs_1_ = bf16[4,32,256]{2,1,0:T(8,128)(2,1)S(1)} collective-permute-done((bf16[4,32,256]{2,1,0:T(8,128)(2,1)S(1)}, bf16[4,32,256]{2,1,0:T(8,128)(2,1)S(1)}, u32[]{:S(2)}, u32[]{:S(2)}) %collective-permute-start.12) | collective-permute-done | bytes 65568 | tf_op jit(solution)/shard_map/ppermute | solution.py:33
  32.5 0.4 %collective-permute-start.14 = (bf16[4,32,256]{2,1,0:T(8,128)(2,1)S(1)}, bf16[4,32,256]{2,1,0:T(8,128)(2,1)S(1)}, u32[]{:S(2)}, u32[]{:S(2)}) collective-permute-start(bf16[4,32,256]{2,1,0:T(8,128)(2,1)S(1)} %collective-permute-done.12.refs_1_), channel_id=1, source_target_pairs={{0,1},{1,0},{2,3},{3,2},{4,5},{5,4},{6,7},{7,6},{8,9},{9,8},{10,11... | collective-permute-start | bytes 196616 | tf_op jit(solution)/shard_map/ppermute | solution.py:33
  32.9 0.0 copy-done.3
  32.9 0.0 copy-done.2
  32.9 0.6 %fusion.6 = (f32[32,256]{1,0:T(8,128)}, f32[32,256]{1,0:T(8,128)}) fusion(f32[32,256]{1,0:T(8,128)S(1)} %copy-done.2, f32[4,32,256]{2,1,0:T(8,128)S(1)} %bitcast.71, s32[]{:T(128)S(6)} %select_n.39, f32[32,256]{1,0:T(8,128)S(1)} %copy-done.3), kind=kLoop, calls=%fused_computation.17 | loop fusion | flops 40960 | bytes 163844 | tf_op jit(solution)/shard_map/sub | solution.py:286
  33.5 0.0 collective-permute-done.13.refs_2_
  33.5 0.3 collective-permute-done.14.refs_3_
  33.8 0.7 %place.1 = bf16[2,2,2,2,32,256]{5,4,3,2,1,0:T(8,128)(2,1)} custom-call(bf16[4,32,256]{2,1,0:T(8,128)(2,1)S(1)} %fusion.3.refs_0_, bf16[4,32,256]{2,1,0:T(8,128)(2,1)S(1)} %collective-permute-done.12.refs_1_, bf16[4,32,256]{2,1,0:T(8,128)(2,1)S(1)} %collective-permute-done.13.refs_2_, bf16[4,32,256]{2,1,0:T(8,128)(2,1)S(1)} %collective-permute-done.14.refs_3_), custom_call_target="tpu_custom_call" | custom-call | tf_op jit(solution)/shard_map/place/pallas_call | solution.py:294
  (17 shorter events, 0.2 us)
Async XLA Ops:
  0.6 4.6 %collective-permute-start = (f32[1,32,256]{2,1,0:T(8,128)}, f32[1,32,256]{2,1,0:T(8,128)S(1)}, u32[]{:S(2)}, u32[]{:S(2)}) collective-permute-start(f32[1,32,256]{2,1,0:T(8,128)} %bitcast.74), channel_id=1, source_target_pairs={{0,5},{1,2},{2,1},{3,6},{4,7},{5,0},{6,3},{7,4},{8,11},{9,12},{10,... | collective-permute-start | bytes 98312 | tf_op jit(solution)/shard_map/ppermute | solution.py:33
  5.3 4.5 %collective-permute-start.1 = (bf16[2,32,256]{2,1,0:T(8,128)(2,1)S(1)}, bf16[2,32,256]{2,1,0:T(8,128)(2,1)S(1)}, u32[]{:S(2)}, u32[]{:S(2)}) collective-permute-start(bf16[2,32,256]{2,1,0:T(8,128)(2,1)S(1)} %maximum_bitcast_fusion), channel_id=1, source_target_pairs={{0,9},{1,8},{2,11},{3,10},{4,13},{5,12},{6,15},{7,14},{8,1},{9,0},... | collective-permute-start | bytes 98312 | tf_op jit(solution)/shard_map/ppermute | solution.py:33
  8.2 8.2 %collective-permute-start.2 = (f32[2,4,32,512]{3,2,1,0:T(8,128)S(1)}, f32[2,4,32,512]{3,2,1,0:T(8,128)S(1)}, u32[]{:S(2)}, u32[]{:S(2)}) collective-permute-start(f32[2,4,32,512]{3,2,1,0:T(8,128)S(1)} %get-tuple-element.30.sent_0), channel_id=1, source_target_pairs={{0,1},{1,0},{2,3},{3,2},{4,5},{5,4},{6,7},{7,6},{8,9},{9,8},{10,11... | collective-permute-start | bytes 1572872 | tf_op jit(solution)/shard_map/ppermute | solution.py:33
  8.5 5.1 %collective-permute-start.3 = (bf16[512,256]{1,0:T(8,128)(2,1)S(1)}, bf16[512,256]{1,0:T(8,128)(2,1)S(1)}, u32[]{:S(2)}, u32[]{:S(2)}) collective-permute-start(bf16[512,256]{1,0:T(8,128)(2,1)S(1)} %get-tuple-element.31.columns), channel_id=1, source_target_pairs={{0,1},{1,0},{2,3},{3,2},{4,5},{5,4},{6,7},{7,6},{8,9},{9,8},{10,11... | collective-permute-start | bytes 786440 | tf_op jit(solution)/shard_map/ppermute | solution.py:33
  8.7 4.9 %collective-permute-start.5 = (f32[2,4,32,512]{3,2,1,0:T(8,128)S(1)}, f32[2,4,32,512]{3,2,1,0:T(8,128)S(1)}, u32[]{:S(2)}, u32[]{:S(2)}) collective-permute-start(f32[2,4,32,512]{3,2,1,0:T(8,128)S(1)} %get-tuple-element.35.sent_1), channel_id=1, source_target_pairs={{0,1},{1,0},{2,3},{3,2},{4,5},{5,4},{6,7},{7,6},{8,9},{9,8},{10,11... | collective-permute-start | bytes 1572872 | tf_op jit(solution)/shard_map/ppermute | solution.py:33
  9.9 3.8 %collective-permute-start.4 = (bf16[128,256]{1,0:T(8,128)(2,1)S(1)}, bf16[128,256]{1,0:T(8,128)(2,1)S(1)}, u32[]{:S(2)}, u32[]{:S(2)}) collective-permute-start(bf16[128,256]{1,0:T(8,128)(2,1)S(1)} %bitcast.63), channel_id=1, source_target_pairs={{0,3},{1,4},{2,7},{3,0},{4,1},{5,6},{6,5},{7,2},{8,13},{9,10},{10,... | collective-permute-start | bytes 196616 | tf_op jit(solution)/shard_map/ppermute | solution.py:33
  11.5 4.3 %collective-permute-start.10 = (bf16[1,32,256]{2,1,0:T(8,128)(2,1)S(1)}, bf16[1,32,256]{2,1,0:T(8,128)(2,1)S(1)}, u32[]{:S(2)}, u32[]{:S(2)}) collective-permute-start(bf16[1,32,256]{2,1,0:T(8,128)(2,1)S(1)} %bitcast.67), channel_id=1, source_target_pairs={{0,5},{1,2},{2,1},{3,6},{4,7},{5,0},{6,3},{7,4},{8,11},{9,12},{10,... | collective-permute-start | bytes 49160 | tf_op jit(solution)/shard_map/ppermute | solution.py:33
  14.1 3.8 %collective-permute-start.6 = (bf16[128,256]{1,0:T(8,128)(2,1)S(1)}, bf16[128,256]{1,0:T(8,128)(2,1)S(1)}, u32[]{:S(2)}, u32[]{:S(2)}) collective-permute-start(bf16[128,256]{1,0:T(8,128)(2,1)S(1)} %get-tuple-element.37), channel_id=1, source_target_pairs={{0,3},{1,4},{2,7},{3,0},{4,1},{5,6},{6,5},{7,2},{8,13},{9,10},{10,... | collective-permute-start | bytes 196616 | tf_op jit(solution)/shard_map/ppermute | solution.py:33
  15.8 5.3 %collective-permute-start.9 = (bf16[256,256]{1,0:T(8,128)(2,1)S(1)}, bf16[256,256]{1,0:T(8,128)(2,1)S(1)}, u32[]{:S(2)}, u32[]{:S(2)}) collective-permute-start(bf16[256,256]{1,0:T(8,128)(2,1)S(1)} %pad_maximum_fusion), channel_id=1, source_target_pairs={{0,1},{1,0},{2,3},{3,2},{4,5},{5,4},{6,7},{7,6},{8,9},{9,8},{10,11... | collective-permute-start | bytes 393224 | tf_op jit(solution)/shard_map/ppermute | solution.py:33
  16.4 10.3 %copy-start.1 = (f32[512,256]{1,0:T(8,128)S(1)}, f32[512,256]{1,0:T(8,128)}, u32[]{:S(2)}) copy-start(f32[512,256]{1,0:T(8,128)} %history.3) | copy-start | bytes 1572868
  16.8 9.8 %copy-start = (f32[512,256]{1,0:T(8,128)S(1)}, f32[512,256]{1,0:T(8,128)}, u32[]{:S(2)}) copy-start(f32[512,256]{1,0:T(8,128)} %master.1) | copy-start | bytes 1572868
  17.9 5.7 %collective-permute-start.7 = (bf16[128,256]{1,0:T(8,128)(2,1)S(1)}, bf16[128,256]{1,0:T(8,128)(2,1)S(1)}, u32[]{:S(2)}, u32[]{:S(2)}) collective-permute-start(bf16[128,256]{1,0:T(8,128)(2,1)S(1)} %add_convert_fusion.1), channel_id=1, source_target_pairs={{0,9},{1,8},{2,11},{3,10},{4,13},{5,12},{6,15},{7,14},{8,1},{9,0},... | collective-permute-start | bytes 196616 | tf_op jit(solution)/shard_map/ppermute | solution.py:33
  21.1 7.0 %collective-permute-start.11 = (bf16[2,32,256]{2,1,0:T(8,128)(2,1)S(1)}, bf16[2,32,256]{2,1,0:T(8,128)(2,1)S(1)}, u32[]{:S(2)}, u32[]{:S(2)}) collective-permute-start(bf16[2,32,256]{2,1,0:T(8,128)(2,1)S(1)} %maximum_bitcast_fusion.1), channel_id=1, source_target_pairs={{0,9},{1,8},{2,11},{3,10},{4,13},{5,12},{6,15},{7,14},{8,1},{9,0},... | collective-permute-start | bytes 98312 | tf_op jit(solution)/shard_map/ppermute | solution.py:33
  23.6 5.0 %collective-permute-start.8 = (bf16[128,256]{1,0:T(8,128)(2,1)S(1)}, bf16[128,256]{1,0:T(8,128)(2,1)S(1)}, u32[]{:S(2)}, u32[]{:S(2)}) collective-permute-start(bf16[128,256]{1,0:T(8,128)(2,1)S(1)} %add_convert_fusion), channel_id=1, source_target_pairs={{0,5},{1,2},{2,1},{3,6},{4,7},{5,0},{6,3},{7,4},{8,11},{9,12},{10,... | collective-permute-start | bytes 196616 | tf_op jit(solution)/shard_map/ppermute | solution.py:33
  28.6 4.3 %copy-start.3 = (f32[32,256]{1,0:T(8,128)S(1)}, f32[32,256]{1,0:T(8,128)}, u32[]{:S(2)}) copy-start(f32[32,256]{1,0:T(8,128)} %history.2) | copy-start | bytes 98308
  28.7 4.2 %copy-start.2 = (f32[32,256]{1,0:T(8,128)S(1)}, f32[32,256]{1,0:T(8,128)}, u32[]{:S(2)}) copy-start(f32[32,256]{1,0:T(8,128)} %rows.3) | copy-start | bytes 98308
  28.7 3.8 %collective-permute-start.12 = (bf16[4,32,256]{2,1,0:T(8,128)(2,1)S(1)}, bf16[4,32,256]{2,1,0:T(8,128)(2,1)S(1)}, u32[]{:S(2)}, u32[]{:S(2)}) collective-permute-start(bf16[4,32,256]{2,1,0:T(8,128)(2,1)S(1)} %fusion.3.refs_0_), channel_id=1, source_target_pairs={{0,3},{1,4},{2,7},{3,0},{4,1},{5,6},{6,5},{7,2},{8,13},{9,10},{10,... | collective-permute-start | bytes 196616 | tf_op jit(solution)/shard_map/ppermute | solution.py:33
  30.6 3.0 %collective-permute-start.13 = (bf16[4,32,256]{2,1,0:T(8,128)(2,1)S(1)}, bf16[4,32,256]{2,1,0:T(8,128)(2,1)S(1)}, u32[]{:S(2)}, u32[]{:S(2)}) collective-permute-start(bf16[4,32,256]{2,1,0:T(8,128)(2,1)S(1)} %fusion.3.refs_0_), channel_id=1, source_target_pairs={{0,1},{1,0},{2,3},{3,2},{4,5},{5,4},{6,7},{7,6},{8,9},{9,8},{10,11... | collective-permute-start | bytes 196616 | tf_op jit(solution)/shard_map/ppermute | solution.py:33
  32.5 1.3 %collective-permute-start.14 = (bf16[4,32,256]{2,1,0:T(8,128)(2,1)S(1)}, bf16[4,32,256]{2,1,0:T(8,128)(2,1)S(1)}, u32[]{:S(2)}, u32[]{:S(2)}) collective-permute-start(bf16[4,32,256]{2,1,0:T(8,128)(2,1)S(1)} %collective-permute-done.12.refs_1_), channel_id=1, source_target_pairs={{0,1},{1,0},{2,3},{3,2},{4,5},{5,4},{6,7},{7,6},{8,9},{9,8},{10,11... | collective-permute-start | bytes 196616 | tf_op jit(solution)/shard_map/ppermute | solution.py:33
